TPU v7x, 32 devices: a whole 2x2x4 slice. The times are simulated.
32 devices in a mesh: src: 8 (over z, x), rcv: 4 (over y, core).
Axes of the slice: x: 2, y: 2, z: 4, core: 2. Of those that a mesh axis runs over, the one named last changes fastest.
Arguments:
- probes: bfloat16 [256, 128, 256], P('rcv', 'src'), may hold values from -6 to 6
- kappa: float32 [128, 256], P('src'), may hold values from 0.02 to 0.24
- footprint: bfloat16 [8, 4, 192, 128, 128], P('src', 'rcv'), may hold values from -0.109375 to 0.109375
- block_source: int32 [8, 4, 192], P('src', 'rcv'), may hold values from 0 to 31
- block_receptor: int32 [8, 4, 192], P('src', 'rcv'), may hold values from 0 to 15
- block_count: int32 [8, 4], P('src', 'rcv'), may hold values from 1 to 192, as said below
- obs_weight: float32 [8192], P('rcv'), may hold values from 1 to 8
Outputs:
- hessian_probe: float32 [256, 128, 256], P('rcv', 'src')
Inputs may be any that keep to these rules, and one draw needn't show every extreme that they name: Slots 0 to block_count - 1 of a tile and group hold its footprint blocks, later slots are unused; some tile and group uses all 192 slots.
All inputs are finite; a program needn't handle non-finite values.
Results may differ from a plain program's by a relative error of at most 0.006.
Values may be sent and summed in bfloat16 or wider, within the bound.
No kernel may reach another device: no remote copies, remote signals or barrier semaphores. Data moves between devices by JAX's collectives and lax.ppermute only.
A program may use at most 64 MiB of HBM per device.

v0:
```python
import jax
import jax.numpy as jnp
from jax import lax
from jax.sharding import PartitionSpec as P

BLK = 128
RB_LOC = 16
GROUP = 32
SMOOTH = 4


def extended(shard, sides, width):
    for axis, dim in sides:
        size, length = (lax.axis_size(axis), shard.shape[dim])
        up = [(i, (i + 1) % size) for i in range(size - 1)]
        down = [(j, i) for i, j in up]
        last = lax.slice_in_dim(shard, length - width, length, axis=dim)
        leading = lax.slice_in_dim(shard, 0, width, axis=dim)
        before = lax.ppermute(last, axis, up)
        after = lax.ppermute(leading, axis, down)
        shard = jnp.concatenate([before, shard, after], axis=dim)
    return shard


def laplacian_operator(emission_source_field):
    padded = extended(emission_source_field.astype(jnp.bfloat16), (("src", 1),), 1).astype(
        emission_source_field.dtype
    )
    padded = jnp.pad(padded, ((0, 0), (0, 0), (1, 1)))
    return (
        padded[:, 2:, 1:-1]
        + padded[:, :-2, 1:-1]
        + padded[:, 1:-1, 2:]
        + padded[:, 1:-1, :-2]
        - 4.0 * emission_source_field
    )


def run_groups(step_group, initial, slot_total):
    rounds = slot_total // GROUP
    return lax.fori_loop(
        0, rounds, lambda group_index, running: step_group(group_index * GROUP, running), initial
    )


def per_device(probes, kappa, footprint, block_source, block_receptor, block_count, obs_weight):
    probe_local, lat_rows, lon_cells = probes.shape
    smoothed = probes.astype(jnp.float32)
    for repeat in range(SMOOTH):
        smoothed = smoothed + kappa * laplacian_operator(smoothed)
    local_field = smoothed.astype(jnp.bfloat16)
    gathered = lax.all_gather(local_field, "rcv", axis=0, tiled=True)
    probe_total = gathered.shape[0]
    tile_field = gathered.reshape(probe_total, -1, BLK).transpose(1, 2, 0)
    source_blocks = tile_field.shape[0]
    blocks = footprint.reshape(footprint.shape[2:])
    sources = block_source.reshape(-1)
    receptors = block_receptor.reshape(-1)
    used_slots = block_count.reshape(())
    slot_total = blocks.shape[0]

    def slot_contents(offset):
        block_portion = lax.dynamic_slice_in_dim(blocks, offset, GROUP, 0)
        source_ids = lax.dynamic_slice_in_dim(sources, offset, GROUP, 0)
        receptor_ids = lax.dynamic_slice_in_dim(receptors, offset, GROUP, 0)
        in_use = (offset + jnp.arange(GROUP, dtype=jnp.int32) < used_slots).astype(jnp.float32)
        return (block_portion, source_ids, receptor_ids, in_use)

    def forward_group(offset, running):
        block_portion, source_ids, receptor_ids, in_use = slot_contents(offset)
        selected_entries = jnp.take(tile_field, source_ids, axis=0)
        hessian_result = jnp.einsum(
            "wlq,wqd->wld", block_portion, selected_entries, preferred_element_type=jnp.float32
        )
        return running.at[receptor_ids].add(hessian_result * in_use[:, None, None])

    evolved = run_groups(
        forward_group, jnp.zeros((RB_LOC, BLK, probe_total), jnp.float32), slot_total
    )
    sim_rows = evolved.reshape(-1, probe_total)
    receptor_all = lax.psum(sim_rows, "src")
    weighted = (obs_weight[:, None] * receptor_all).astype(jnp.bfloat16)
    weighted = weighted.reshape(RB_LOC, BLK, probe_total)

    def adjoint_group(offset, running):
        block_portion, source_ids, receptor_ids, in_use = slot_contents(offset)
        selected_entries = jnp.take(weighted, receptor_ids, axis=0)
        hessian_result = jnp.einsum(
            "grc,grp->pgc", block_portion, selected_entries, preferred_element_type=jnp.float32
        )
        return running.at[:, source_ids].add(hessian_result * in_use[None, :, None])

    adjoint_terms = run_groups(
        adjoint_group, jnp.zeros((probe_total, source_blocks, BLK), jnp.float32), slot_total
    )
    adjoint_rows = adjoint_terms.reshape(probe_total, lat_rows, lon_cells).astype(jnp.bfloat16)
    back = lax.psum_scatter(adjoint_rows, "rcv", scatter_dimension=0, tiled=True).astype(
        jnp.float32
    )
    for repeat in range(SMOOTH):
        back = back + laplacian_operator(kappa * back)
    return probes.astype(jnp.float32) + back


def solution(mesh):
    placed = (
        P("rcv", "src", None),
        P("src", None),
        P("src", "rcv", None, None, None),
        P("src", "rcv", None),
        P("src", "rcv", None),
        P("src", "rcv"),
        P("rcv"),
    )
    return jax.shard_map(
        per_device, mesh=mesh, in_specs=placed, out_specs=P("rcv", "src", None), check_vma=False
    )
```

profile of v0, /device:TPU:0, one launch (start us, length us, event | category | flops | bytes accessed | tf_op | source)
XLA Modules:
  0.0 469.9 jit_solution(10007175282225328306)
XLA Ops:
  7.7 4.8 %collective-permute-start = (bf16[64,1,256]{2,1,0:T(2,128)(2,1)S(1)}, bf16[64,1,256]{2,1,0:T(2,128)(2,1)S(1)}, u32[]{:S(2)}, u32[]{:S(2)}) collective-permute-start(bf16[64,1,256]{2,1,0:T(2,128)(2,1)S(1)} %get-tuple-element.315), channel_id=1, source_target_pairs={{0,4},{4,8},{8,12},{12,16},{16,20},{20,24},{24,28},{1,5},{5,9},{9,... | collective-permute-start | bytes 98312 | tf_op jit(solution)/shard_map/ppermute | solution.py:19
  14.5 4.3 collective-permute-done.1
  21.1 4.4 collective-permute-start.2
  27.3 4.3 collective-permute-done.3
  43.6 4.4 collective-permute-start.6
  56.2 21.9 %all-gather.2.cloned.1.call-done = bf16[256,16,256]{2,1,0:T(8,128)(2,1)} async-done(((bf16[64,16,256]{2,1,0:T(8,128)(2,1)}), bf16[256,16,256]{2,1,0:T(8,128)(2,1)}) %all-gather.2.cloned.1.call-update) | async-done | bytes 2097168 | tf_op jit(solution)/shard_map/all_gather | solution.py:52
  78.1 4.3 copy.15
  83.1 94.1 %while.26 = (s32[]{:T(128)}, f32[16,128,256]{2,1,0:T(8,128)S(1)}, s32[192]{0:T(256)S(1)}, bf16[192,128,128]{2,1,0:T(8,128)(2,1)}, s32[192]{0:T(256)S(1)}, /*inde...) while((s32[]{:T(128)}, f32[16,128,256]{2,1,0:T(8,128)S(1)}, ...), condition=%wide.region_2.3_spmd, body=%wide.region_0.2_spmd.sunk | while | flops 271582592 | bytes 24122736 | solution.py:41
  87.6 4.7 convolution_multiply_fusion.4
  92.3 6.5 %scatter_fusion = f32[16,128,256]{2,1,0:T(8,128)S(1)} fusion(f32[16,128,256]{2,1,0:T(8,128)S(1)} %get-tuple-element.427, s32[32]{0:T(128)S(1)} %compare_select_fusion.8, f32[32,128,256]{2,1,0:T(8,128)} %convolution_multiply_fusion.4), kind=kCustom, calls=%fused_computation.2.clone.1 | custom fusion | flops 1048576 | bytes 12583040 | tf_op jit(solution)/shard_map/while/body/eval_jaxpr/scatter-add | solution.py:75
  103.2 4.7 convolution_multiply_fusion.4
  107.9 6.5 %scatter_fusion = f32[16,128,256]{2,1,0:T(8,128)S(1)} fusion(f32[16,128,256]{2,1,0:T(8,128)S(1)} %get-tuple-element.427, s32[32]{0:T(128)S(1)} %compare_select_fusion.8, f32[32,128,256]{2,1,0:T(8,128)} %convolution_multiply_fusion.4), kind=kCustom, calls=%fused_computation.2.clone.1 | custom fusion | flops 1048576 | bytes 12583040 | tf_op jit(solution)/shard_map/while/body/eval_jaxpr/scatter-add | solution.py:75
  118.9 4.7 convolution_multiply_fusion.4
  123.6 6.5 %scatter_fusion = f32[16,128,256]{2,1,0:T(8,128)S(1)} fusion(f32[16,128,256]{2,1,0:T(8,128)S(1)} %get-tuple-element.427, s32[32]{0:T(128)S(1)} %compare_select_fusion.8, f32[32,128,256]{2,1,0:T(8,128)} %convolution_multiply_fusion.4), kind=kCustom, calls=%fused_computation.2.clone.1 | custom fusion | flops 1048576 | bytes 12583040 | tf_op jit(solution)/shard_map/while/body/eval_jaxpr/scatter-add | solution.py:75
  134.6 4.7 convolution_multiply_fusion.4
  139.3 6.5 %scatter_fusion = f32[16,128,256]{2,1,0:T(8,128)S(1)} fusion(f32[16,128,256]{2,1,0:T(8,128)S(1)} %get-tuple-element.427, s32[32]{0:T(128)S(1)} %compare_select_fusion.8, f32[32,128,256]{2,1,0:T(8,128)} %convolution_multiply_fusion.4), kind=kCustom, calls=%fused_computation.2.clone.1 | custom fusion | flops 1048576 | bytes 12583040 | tf_op jit(solution)/shard_map/while/body/eval_jaxpr/scatter-add | solution.py:75
  150.3 4.7 convolution_multiply_fusion.4
  155.0 6.5 %scatter_fusion = f32[16,128,256]{2,1,0:T(8,128)S(1)} fusion(f32[16,128,256]{2,1,0:T(8,128)S(1)} %get-tuple-element.427, s32[32]{0:T(128)S(1)} %compare_select_fusion.8, f32[32,128,256]{2,1,0:T(8,128)} %convolution_multiply_fusion.4), kind=kCustom, calls=%fused_computation.2.clone.1 | custom fusion | flops 1048576 | bytes 12583040 | tf_op jit(solution)/shard_map/while/body/eval_jaxpr/scatter-add | solution.py:75
  166.0 4.7 convolution_multiply_fusion.4
  170.7 6.5 %scatter_fusion = f32[16,128,256]{2,1,0:T(8,128)S(1)} fusion(f32[16,128,256]{2,1,0:T(8,128)S(1)} %get-tuple-element.427, s32[32]{0:T(128)S(1)} %compare_select_fusion.8, f32[32,128,256]{2,1,0:T(8,128)} %convolution_multiply_fusion.4), kind=kCustom, calls=%fused_computation.2.clone.1 | custom fusion | flops 1048576 | bytes 12583040 | tf_op jit(solution)/shard_map/while/body/eval_jaxpr/scatter-add | solution.py:75
  178.8 101.8 %all-reduce.10.cloned.1.call-done = f32[2048,256]{1,0:T(8,128)} async-done(((f32[2048,256]{1,0:T(8,128)}), f32[2048,256]{1,0:T(8,128)}) %all-reduce.10.cloned.1.call-update) | async-done | bytes 2097168 | tf_op jit(solution)/shard_map/psum | solution.py:81
  285.0 94.0 %while.27 = (s32[]{:T(128)}, f32[256,32,128]{2,0,1:T(8,128)}, s32[192]{0:T(256)S(1)}, s32[192]{0:T(256)S(1)}, bf16[16,128,256]{2,1,0:T(8,128)(2,1)S(1)}, /*index...) while((s32[]{:T(128)}, f32[256,32,128]{2,0,1:T(8,128)}, ...), condition=%wide.region_6.7_spmd, body=%wide.region_4.6_spmd.sunk | while | flops 271582592 | bytes 24122736 | solution.py:41
  290.7 9.9 %scatter_fusion.1 = f32[256,32,128]{2,0,1:T(8,128)} fusion(f32[256,32,128]{2,0,1:T(8,128)} %get-tuple-element.460, s32[32]{0:T(128)S(1)} %compare_select_fusion.9, f32[32,256,128]{2,1,0:T(8,128)} %convolution_multiply_fusion.5), kind=kCustom, calls=%fused_computation.3.clone.1 | custom fusion | flops 1048576 | bytes 12583040 | tf_op jit(solution)/shard_map/while/body/eval_jaxpr/scatter-add | solution.py:91
  306.4 9.9 %scatter_fusion.1 = f32[256,32,128]{2,0,1:T(8,128)} fusion(f32[256,32,128]{2,0,1:T(8,128)} %get-tuple-element.460, s32[32]{0:T(128)S(1)} %compare_select_fusion.9, f32[32,256,128]{2,1,0:T(8,128)} %convolution_multiply_fusion.5), kind=kCustom, calls=%fused_computation.3.clone.1 | custom fusion | flops 1048576 | bytes 12583040 | tf_op jit(solution)/shard_map/while/body/eval_jaxpr/scatter-add | solution.py:91
  322.0 9.9 %scatter_fusion.1 = f32[256,32,128]{2,0,1:T(8,128)} fusion(f32[256,32,128]{2,0,1:T(8,128)} %get-tuple-element.460, s32[32]{0:T(128)S(1)} %compare_select_fusion.9, f32[32,256,128]{2,1,0:T(8,128)} %convolution_multiply_fusion.5), kind=kCustom, calls=%fused_computation.3.clone.1 | custom fusion | flops 1048576 | bytes 12583040 | tf_op jit(solution)/shard_map/while/body/eval_jaxpr/scatter-add | solution.py:91
  337.6 9.8 %scatter_fusion.1 = f32[256,32,128]{2,0,1:T(8,128)} fusion(f32[256,32,128]{2,0,1:T(8,128)} %get-tuple-element.460, s32[32]{0:T(128)S(1)} %compare_select_fusion.9, f32[32,256,128]{2,1,0:T(8,128)} %convolution_multiply_fusion.5), kind=kCustom, calls=%fused_computation.3.clone.1 | custom fusion | flops 1048576 | bytes 12583040 | tf_op jit(solution)/shard_map/while/body/eval_jaxpr/scatter-add | solution.py:91
  353.2 10.0 %scatter_fusion.1 = f32[256,32,128]{2,0,1:T(8,128)} fusion(f32[256,32,128]{2,0,1:T(8,128)} %get-tuple-element.460, s32[32]{0:T(128)S(1)} %compare_select_fusion.9, f32[32,256,128]{2,1,0:T(8,128)} %convolution_multiply_fusion.5), kind=kCustom, calls=%fused_computation.3.clone.1 | custom fusion | flops 1048576 | bytes 12583040 | tf_op jit(solution)/shard_map/while/body/eval_jaxpr/scatter-add | solution.py:91
  369.0 10.0 %scatter_fusion.1 = f32[256,32,128]{2,0,1:T(8,128)} fusion(f32[256,32,128]{2,0,1:T(8,128)} %get-tuple-element.460, s32[32]{0:T(128)S(1)} %compare_select_fusion.9, f32[32,256,128]{2,1,0:T(8,128)} %convolution_multiply_fusion.5), kind=kCustom, calls=%fused_computation.3.clone.1 | custom fusion | flops 1048576 | bytes 12583040 | tf_op jit(solution)/shard_map/while/body/eval_jaxpr/scatter-add | solution.py:91
  385.1 31.1 %reduce-scatter.2.cloned.1.call-done = bf16[64,16,256]{2,1,0:T(8,128)(2,1)} async-done(((bf16[256,16,256]{2,1,0:T(8,128)(2,1)}), bf16[64,16,256]{2,1,0:T(8,128)(2,1)}) %reduce-scatter.2.cloned.1.call-update) | async-done | bytes 524304 | tf_op jit(solution)/shard_map/reduce_scatter | solution.py:97
  428.2 4.3 collective-permute-start.10
  434.4 4.3 collective-permute-done.11
  450.7 4.4 collective-permute-start.14
  (131 shorter events, 135.5 us)
Async XLA Ops:
  6.5 13.6 %copy-start.1 = (bf16[64,16,256]{2,1,0:T(8,128)(2,1)S(1)}, bf16[64,16,256]{2,1,0:T(8,128)(2,1)}, u32[]{:S(2)}) copy-start(bf16[64,16,256]{2,1,0:T(8,128)(2,1)} %param.11) | copy-start | bytes 1572868
  6.5 13.6 %copy-start.4 = (f32[16,256]{1,0:T(8,128)S(1)}, f32[16,256]{1,0:T(8,128)}, u32[]{:S(2)}) copy-start(f32[16,256]{1,0:T(8,128)} %param.12) | copy-start | bytes 49156
  6.5 71.5 %all-gather.2.cloned.1.call-start = ((), (), s32[]{:S(2)}) async-start(), calls=%async_computation.1 | async-start | bytes 2621440 | tf_op jit(solution)/shard_map/all_gather | solution.py:52
  7.7 6.7 %collective-permute-start = (bf16[64,1,256]{2,1,0:T(2,128)(2,1)S(1)}, bf16[64,1,256]{2,1,0:T(2,128)(2,1)S(1)}, u32[]{:S(2)}, u32[]{:S(2)}) collective-permute-start(bf16[64,1,256]{2,1,0:T(2,128)(2,1)S(1)} %get-tuple-element.315), channel_id=1, source_target_pairs={{0,4},{4,8},{8,12},{12,16},{16,20},{20,24},{24,28},{1,5},{5,9},{9,... | collective-permute-start | bytes 98312 | tf_op jit(solution)/shard_map/ppermute | solution.py:19
  12.6 6.2 %collective-permute-start.1 = (bf16[64,1,256]{2,1,0:T(2,128)(2,1)S(1)}, bf16[64,1,256]{2,1,0:T(2,128)(2,1)S(1)}, u32[]{:S(2)}, u32[]{:S(2)}) collective-permute-start(bf16[64,1,256]{2,1,0:T(2,128)(2,1)S(1)} %get-tuple-element.316), channel_id=1, source_target_pairs={{4,0},{8,4},{12,8},{16,12},{20,16},{24,20},{28,24},{5,1},{9,5},{13... | collective-permute-start | bytes 98312 | tf_op jit(solution)/shard_map/ppermute | solution.py:20
  21.1 6.2 %collective-permute-start.2 = (bf16[64,1,256]{2,1,0:T(2,128)(2,1)S(1)}, bf16[64,1,256]{2,1,0:T(2,128)(2,1)S(1)}, u32[]{:S(2)}, u32[]{:S(2)}) collective-permute-start(bf16[64,1,256]{2,1,0:T(2,128)(2,1)S(1)} %get-tuple-element.313), channel_id=1, source_target_pairs={{0,4},{4,8},{8,12},{12,16},{16,20},{20,24},{24,28},{1,5},{5,9},{9,... | collective-permute-start | bytes 98312 | tf_op jit(solution)/shard_map/ppermute | solution.py:19
  25.4 6.2 %collective-permute-start.3 = (bf16[64,1,256]{2,1,0:T(2,128)(2,1)S(1)}, bf16[64,1,256]{2,1,0:T(2,128)(2,1)S(1)}, u32[]{:S(2)}, u32[]{:S(2)}) collective-permute-start(bf16[64,1,256]{2,1,0:T(2,128)(2,1)S(1)} %get-tuple-element.314), channel_id=1, source_target_pairs={{4,0},{8,4},{12,8},{16,12},{20,16},{24,20},{28,24},{5,1},{9,5},{13... | collective-permute-start | bytes 98312 | tf_op jit(solution)/shard_map/ppermute | solution.py:20
  32.8 5.9 %collective-permute-start.4 = (bf16[64,1,256]{2,1,0:T(2,128)(2,1)S(1)}, bf16[64,1,256]{2,1,0:T(2,128)(2,1)S(1)}, u32[]{:S(2)}, u32[]{:S(2)}) collective-permute-start(bf16[64,1,256]{2,1,0:T(2,128)(2,1)S(1)} %get-tuple-element.311), channel_id=1, source_target_pairs={{0,4},{4,8},{8,12},{12,16},{16,20},{20,24},{24,28},{1,5},{5,9},{9,... | collective-permute-start | bytes 98312 | tf_op jit(solution)/shard_map/ppermute | solution.py:19
  36.2 6.2 %collective-permute-start.5 = (bf16[64,1,256]{2,1,0:T(2,128)(2,1)S(1)}, bf16[64,1,256]{2,1,0:T(2,128)(2,1)S(1)}, u32[]{:S(2)}, u32[]{:S(2)}) collective-permute-start(bf16[64,1,256]{2,1,0:T(2,128)(2,1)S(1)} %get-tuple-element.312), channel_id=1, source_target_pairs={{4,0},{8,4},{12,8},{16,12},{20,16},{24,20},{28,24},{5,1},{9,5},{13... | collective-permute-start | bytes 98312 | tf_op jit(solution)/shard_map/ppermute | solution.py:20
  43.6 6.2 %collective-permute-start.6 = (bf16[64,1,256]{2,1,0:T(2,128)(2,1)S(1)}, bf16[64,1,256]{2,1,0:T(2,128)(2,1)S(1)}, u32[]{:S(2)}, u32[]{:S(2)}) collective-permute-start(bf16[64,1,256]{2,1,0:T(2,128)(2,1)S(1)} %get-tuple-element.309), channel_id=1, source_target_pairs={{0,4},{4,8},{8,12},{12,16},{16,20},{20,24},{24,28},{1,5},{5,9},{9,... | collective-permute-start | bytes 98312 | tf_op jit(solution)/shard_map/ppermute | solution.py:19
  48.0 6.2 %collective-permute-start.7 = (bf16[64,1,256]{2,1,0:T(2,128)(2,1)S(1)}, bf16[64,1,256]{2,1,0:T(2,128)(2,1)S(1)}, u32[]{:S(2)}, u32[]{:S(2)}) collective-permute-start(bf16[64,1,256]{2,1,0:T(2,128)(2,1)S(1)} %get-tuple-element.310), channel_id=1, source_target_pairs={{4,0},{8,4},{12,8},{16,12},{20,16},{24,20},{28,24},{5,1},{9,5},{13... | collective-permute-start | bytes 98312 | tf_op jit(solution)/shard_map/ppermute | solution.py:20
  56.1 224.4 %all-reduce.10.cloned.1.call-start = ((), (), s32[]{:S(2)}) async-start(), calls=%async_computation.2 | async-start | bytes 4194304 | tf_op jit(solution)/shard_map/psum | solution.py:81
  82.4 0.7 copy-start.6
  82.4 0.7 copy-start.7
  177.2 1.3 copy-start
  177.2 103.3 %copy-start.5 = (f32[2048]{0:T(1024)S(1)}, f32[2048]{0:T(1024)}, u32[]{:S(2)}) copy-start(f32[2048]{0:T(1024)} %param.17) | copy-start | bytes 24580
  178.5 237.6 %reduce-scatter.2.cloned.1.call-start = ((), (), s32[]{:S(2)}) async-start(), calls=%async_computation.3 | async-start | bytes 2621440 | tf_op jit(solution)/shard_map/reduce_scatter | solution.py:97
  416.1 11.3 %copy-start.3 = (bf16[64,16,256]{2,1,0:T(8,128)(2,1)S(1)}, bf16[64,16,256]{2,1,0:T(8,128)(2,1)}, u32[]{:S(2)}) copy-start(bf16[64,16,256]{2,1,0:T(8,128)(2,1)} %reduce-scatter.2.cloned.1.call-done) | copy-start | bytes 1572868
  417.5 5.3 %collective-permute-start.8 = (bf16[64,1,256]{2,1,0:T(2,128)(2,1)S(1)}, bf16[64,1,256]{2,1,0:T(2,128)(2,1)S(1)}, u32[]{:S(2)}, u32[]{:S(2)}) collective-permute-start(bf16[64,1,256]{2,1,0:T(2,128)(2,1)S(1)} %get-tuple-element.307), channel_id=1, source_target_pairs={{0,4},{4,8},{8,12},{12,16},{16,20},{20,24},{24,28},{1,5},{5,9},{9,... | collective-permute-start | bytes 98312 | tf_op jit(solution)/shard_map/ppermute | solution.py:19
  420.9 6.2 %collective-permute-start.9 = (bf16[64,1,256]{2,1,0:T(2,128)(2,1)S(1)}, bf16[64,1,256]{2,1,0:T(2,128)(2,1)S(1)}, u32[]{:S(2)}, u32[]{:S(2)}) collective-permute-start(bf16[64,1,256]{2,1,0:T(2,128)(2,1)S(1)} %get-tuple-element.308), channel_id=1, source_target_pairs={{4,0},{8,4},{12,8},{16,12},{20,16},{24,20},{28,24},{5,1},{9,5},{13... | collective-permute-start | bytes 98312 | tf_op jit(solution)/shard_map/ppermute | solution.py:20
  428.2 6.2 %collective-permute-start.10 = (bf16[64,1,256]{2,1,0:T(2,128)(2,1)S(1)}, bf16[64,1,256]{2,1,0:T(2,128)(2,1)S(1)}, u32[]{:S(2)}, u32[]{:S(2)}) collective-permute-start(bf16[64,1,256]{2,1,0:T(2,128)(2,1)S(1)} %get-tuple-element.305), channel_id=1, source_target_pairs={{0,4},{4,8},{8,12},{12,16},{16,20},{20,24},{24,28},{1,5},{5,9},{9,... | collective-permute-start | bytes 98312 | tf_op jit(solution)/shard_map/ppermute | solution.py:19
  432.5 6.2 %collective-permute-start.11 = (bf16[64,1,256]{2,1,0:T(2,128)(2,1)S(1)}, bf16[64,1,256]{2,1,0:T(2,128)(2,1)S(1)}, u32[]{:S(2)}, u32[]{:S(2)}) collective-permute-start(bf16[64,1,256]{2,1,0:T(2,128)(2,1)S(1)} %get-tuple-element.306), channel_id=1, source_target_pairs={{4,0},{8,4},{12,8},{16,12},{20,16},{24,20},{28,24},{5,1},{9,5},{13... | collective-permute-start | bytes 98312 | tf_op jit(solution)/shard_map/ppermute | solution.py:20
  439.9 5.9 %collective-permute-start.12 = (bf16[64,1,256]{2,1,0:T(2,128)(2,1)S(1)}, bf16[64,1,256]{2,1,0:T(2,128)(2,1)S(1)}, u32[]{:S(2)}, u32[]{:S(2)}) collective-permute-start(bf16[64,1,256]{2,1,0:T(2,128)(2,1)S(1)} %get-tuple-element.303), channel_id=1, source_target_pairs={{0,4},{4,8},{8,12},{12,16},{16,20},{20,24},{24,28},{1,5},{5,9},{9,... | collective-permute-start | bytes 98312 | tf_op jit(solution)/shard_map/ppermute | solution.py:19
  443.3 6.2 %collective-permute-start.13 = (bf16[64,1,256]{2,1,0:T(2,128)(2,1)S(1)}, bf16[64,1,256]{2,1,0:T(2,128)(2,1)S(1)}, u32[]{:S(2)}, u32[]{:S(2)}) collective-permute-start(bf16[64,1,256]{2,1,0:T(2,128)(2,1)S(1)} %get-tuple-element.304), channel_id=1, source_target_pairs={{4,0},{8,4},{12,8},{16,12},{20,16},{24,20},{28,24},{5,1},{9,5},{13... | collective-permute-start | bytes 98312 | tf_op jit(solution)/shard_map/ppermute | solution.py:20
  450.6 11.1 %copy-start.2 = (bf16[64,16,256]{2,1,0:T(8,128)(2,1)S(1)}, bf16[64,16,256]{2,1,0:T(8,128)(2,1)}, u32[]{:S(2)}) copy-start(bf16[64,16,256]{2,1,0:T(8,128)(2,1)} %param.11) | copy-start | bytes 1572868
  450.7 6.3 %collective-permute-start.14 = (bf16[64,1,256]{2,1,0:T(2,128)(2,1)S(1)}, bf16[64,1,256]{2,1,0:T(2,128)(2,1)S(1)}, u32[]{:S(2)}, u32[]{:S(2)}) collective-permute-start(bf16[64,1,256]{2,1,0:T(2,128)(2,1)S(1)} %get-tuple-element.301), channel_id=1, source_target_pairs={{0,4},{4,8},{8,12},{12,16},{16,20},{20,24},{24,28},{1,5},{5,9},{9,... | collective-permute-start | bytes 98312 | tf_op jit(solution)/shard_map/ppermute | solution.py:19
  455.1 6.2 %collective-permute-start.15 = (bf16[64,1,256]{2,1,0:T(2,128)(2,1)S(1)}, bf16[64,1,256]{2,1,0:T(2,128)(2,1)S(1)}, u32[]{:S(2)}, u32[]{:S(2)}) collective-permute-start(bf16[64,1,256]{2,1,0:T(2,128)(2,1)S(1)} %get-tuple-element.302), channel_id=1, source_target_pairs={{4,0},{8,4},{12,8},{16,12},{20,16},{24,20},{28,24},{5,1},{9,5},{13... | collective-permute-start | bytes 98312 | tf_op jit(solution)/shard_map/ppermute | solution.py:20
Sparse Core Ops, SparseCore 0:
  56.2 21.8 all-gather.1
  178.6 101.8 all-reduce.9
  385.2 30.9 reduce-scatter.1
where the time goes:
time: 472 us; the launch traced here: 470 us
  waiting for transfers between devices  194 us (41%)
  other arithmetic  126 us (27%)
  matrix products  53.5 us (11%)
  starting transfers between devices  43 us (9%)
  local copies, waits for them, and re-layouts  40.5 us (9%)
  between operations  13.5 us (3%)
    psum x1, waiting for transfers between devices, per_device(): receptor_all = lax.psum(sim_rows, 'src')  102 us
    scatter-add x6, other arithmetic, adjoint_group(): return running.at[:, source_ids].add(hessian_result * in_use[None, :, None])  59.6 us
    scatter-add x6, other arithmetic, forward_group(): return running.at[receptor_ids].add(hessian_result * in_use[:, None, None])  38.9 us
    ppermute x8, waiting for transfers between devices, extended(): after = lax.ppermute(leading, axis, down)  33 us
    ppermute x8, starting transfers between devices, extended(): before = lax.ppermute(last, axis, up)  32.4 us
    reduce_scatter x1, waiting for transfers between devices, per_device(): lax.psum_scatter(adjoint_rows, 'rcv', scatter_dimension=0, tiled=True)  31.1 us
    dot_general x6, matrix products, forward_group(): jnp.einsum('wlq,wqd->wld', block_portion, selected_entries, preferred_ele...  28.1 us
    dot_general x6, matrix products, adjoint_group(): jnp.einsum('grc,grp->pgc', block_portion, selected_entries, preferred_ele...  25.4 us
  transfers between devices with their start and end apart: 19, of which 19 were waited for; matrix products, arithmetic and copies ran while one was open for 0% of the time, Pallas kernels for 0%

commit v1 on v0

v1 whole, which is shorter than its diff:
```python
import jax
import jax.numpy as jnp
from jax import lax
from jax.experimental import pallas as pl
from jax.experimental.pallas import tpu as pltpu
from jax.sharding import PartitionSpec as P

BLK = 128
RB_LOC = 16
SMOOTH = 4
SUB = 8
PIECES = 16
GROUP = 32
F32, BF16 = jnp.float32, jnp.bfloat16
VMEM = pl.BlockSpec(memory_space=pltpu.VMEM)
SMEM = pl.BlockSpec(memory_space=pltpu.SMEM)


def params(mib=32):
    return pltpu.CompilerParams(vmem_limit_bytes=mib * 1024 * 1024)


def widen(probes_ref, wide):
    for h in range(wide.shape[0]):
        wide[h] = probes_ref[:, h * BLK : (h + 1) * BLK].astype(F32)


def one_row(wide, start, size, rows):
    at = pl.ds(start, size, stride=rows)
    return jnp.concatenate([wide[h, at, :] for h in range(wide.shape[0])], axis=1)


def edge_kernel(probes_ref, kappa_ref, north_ref, south_ref, wide):
    rows, lon = kappa_ref.shape
    probe_local = probes_ref.shape[0] // rows
    widen(probes_ref, wide)
    place = lax.broadcasted_iota(jnp.int32, (PIECES, lon), 0)
    for out_ref, first in ((north_ref, 0), (south_ref, rows - SMOOTH)):
        for r in range(SMOOTH):
            out_ref[r, :probe_local, :] = one_row(wide, first + r, probe_local, rows).astype(BF16)
            whole = kappa_ref[first + r : first + r + 1, :]
            high = whole.astype(BF16).astype(F32)
            rest = whole - high
            middle = rest.astype(BF16).astype(F32)
            low = rest - middle
            pieces = jnp.where(place == 0, high, jnp.where(place == 1, middle, jnp.where(place == 2, low, 0.0)))
            out_ref[r, probe_local:, :] = pieces.astype(BF16)


def kappa_rows(kappa_ref, above_ref, below_ref, probe_local):
    def halo(ref, r):
        piece = ref[r, probe_local:, :].astype(F32)
        return piece[0:1] + piece[1:2] + piece[2:3]

    rows = kappa_ref.shape[0]
    return (
        [halo(above_ref, r) for r in range(SMOOTH)]
        + [kappa_ref[r : r + 1, :] for r in range(rows)]
        + [halo(below_ref, r) for r in range(SMOOTH)]
    )


def smooth_kernel(probes_ref, kappa_ref, above_ref, below_ref, field_ref, wide, coef, halos, result):
    rows, lon = kappa_ref.shape
    probe_local = probes_ref.shape[0] // rows
    total = rows + 2 * SMOOTH
    widen(probes_ref, wide)
    halos[0] = above_ref[:, :probe_local, :].astype(F32)
    halos[1] = below_ref[:, :probe_local, :].astype(F32)
    lane = lax.broadcasted_iota(jnp.int32, (SUB, lon), 1)
    for r, k in enumerate(kappa_rows(kappa_ref, above_ref, below_ref, probe_local)):
        k = jnp.broadcast_to(k, (SUB, lon))
        coef[0, r] = k
        coef[1, r] = jnp.where(lane > 0, k, 0.0)
        coef[2, r] = jnp.where(lane < lon - 1, k, 0.0)

    @pl.loop(0, probe_local // SUB)
    def _(c):
        base = pl.multiple_of(c * SUB, SUB)
        f = (
            [halos[0, r, pl.ds(base, SUB), :] for r in range(SMOOTH)]
            + [one_row(wide, base * rows + r, SUB, rows) for r in range(rows)]
            + [halos[1, r, pl.ds(base, SUB), :] for r in range(SMOOTH)]
        )
        for step in range(SMOOTH):
            new = list(f)
            for r in range(step + 1, total - step - 1):
                k, kl, kr = coef[0, r], coef[1, r], coef[2, r]
                g = f[r]
                new[r] = (
                    g
                    + k * (f[r - 1] + f[r + 1] - 4.0 * g)
                    + kl * pltpu.roll(g, 1, 1)
                    + kr * pltpu.roll(g, lon - 1, 1)
                )
            f = new
        for r in range(rows):
            for h in range(lon // BLK):
                result[r * (lon // BLK) + h, pl.ds(base, SUB), :] = f[r + SMOOTH][:, h * BLK : (h + 1) * BLK]

    field_ref[...] = result[...].astype(BF16)


def forward_kernel(sources, receptors, count, blocks_ref, near_ref, far_ref, out_ref, total):
    g = pl.program_id(0)

    @pl.when(g == 0)
    def _():
        total[...] = jnp.zeros_like(total)

    group = blocks_ref.shape[0]
    spare = total.shape[0] - 1
    for i in range(group):
        n = g * group + i
        j = sources[n]
        b = jnp.where(n < count[0], receptors[n], spare)
        entries = jnp.concatenate([near_ref[j], far_ref[j]], axis=0)
        total[b] += lax.dot_general(
            entries, blocks_ref[i], (((1,), (1,)), ((), ())), preferred_element_type=F32
        )

    @pl.when(g == pl.num_programs(0) - 1)
    def _():
        out_ref[...] = total[:spare].astype(BF16)


def adjoint_kernel(sources, receptors, count, blocks_ref, weighted_ref, near_ref, far_ref, total):
    g = pl.program_id(0)

    @pl.when(g == 0)
    def _():
        total[...] = jnp.zeros_like(total)

    group = blocks_ref.shape[0]
    spare = total.shape[0] - 1
    for i in range(group):
        n = g * group + i
        j = jnp.where(n < count[0], sources[n], spare)
        total[j] += jnp.dot(weighted_ref[receptors[n]], blocks_ref[i], preferred_element_type=F32)

    @pl.when(g == pl.num_programs(0) - 1)
    def _():
        half = near_ref.shape[1]
        near_ref[...] = total[:spare, :half].astype(BF16)
        far_ref[...] = total[:spare, half:].astype(BF16)


def back_kernel(
    inside, probes_ref, kappa_ref, above_ref, below_ref, own_ref, core_ref, far_ref, top_ref, bottom_ref, out_ref, wide, coef, terms, halos
):
    rows, lon = kappa_ref.shape
    probe_local = probes_ref.shape[0] // rows
    total = rows + 2 * SMOOTH
    halves = lon // BLK
    widen(probes_ref, wide)
    terms[...] = own_ref[...].astype(F32) + core_ref[...].astype(F32) + far_ref[...].astype(F32)
    halos[0] = top_ref[...].astype(F32)
    halos[1] = bottom_ref[...].astype(F32)
    lane = lax.broadcasted_iota(jnp.int32, (SUB, lon), 1)
    for r, k in enumerate(kappa_rows(kappa_ref, above_ref, below_ref, probe_local)):
        coef[r] = jnp.broadcast_to(k, (SUB, lon))
    in_grid = [inside[0]] * SMOOTH + [None] * rows + [inside[1]] * SMOOTH

    def joined(ref, first, base):
        return jnp.concatenate([ref[first + h, pl.ds(base, SUB), :] for h in range(halves)], axis=1)

    @pl.loop(0, probe_local // SUB)
    def _(c):
        base = pl.multiple_of(c * SUB, SUB)
        f = (
            [joined(halos.at[0], r * halves, base) for r in range(SMOOTH)]
            + [joined(terms, r * halves, base) for r in range(rows)]
            + [joined(halos.at[1], r * halves, base) for r in range(SMOOTH)]
        )
        for step in range(SMOOTH):
            g = [coef[r] * f[r] for r in range(total)]
            new = list(f)
            for r in range(step + 1, total - step - 1):
                west = jnp.where(lane > 0, pltpu.roll(g[r], 1, 1), 0.0)
                east = jnp.where(lane < lon - 1, pltpu.roll(g[r], lon - 1, 1), 0.0)
                lap = g[r - 1] + g[r + 1] + west + east - 4.0 * g[r]
                if in_grid[r] is not None:
                    lap = lap * in_grid[r]
                new[r] = f[r] + lap
            f = new
        for r in range(rows):
            at = pl.ds(base * rows + r, SUB, stride=rows)
            for h in range(halves):
                wide[h, at, :] += f[r + SMOOTH][:, h * BLK : (h + 1) * BLK]

    for h in range(halves):
        out_ref[:, h * BLK : (h + 1) * BLK] = wide[h]


def swap(x, axis, distance):
    size = lax.axis_size(axis)
    return lax.ppermute(x, axis, [(i, i ^ distance) for i in range(size)])


def exchange_edges(north, south):
    size = lax.axis_size("src")
    down = [(i, i + 1) for i in range(size - 1)]
    up = [(j, i) for i, j in down]
    return lax.ppermute(south, "src", down), lax.ppermute(north, "src", up)


def per_device(probes, kappa, footprint, block_source, block_receptor, block_count, obs_weight):
    probe_local, rows, lon = probes.shape
    halves = lon // BLK
    cells = rows * halves
    tiles = lax.axis_size("src")
    me = lax.axis_index("src")
    blocks = footprint.reshape(footprint.shape[2:])
    slots = blocks.shape[0]
    scalars = (block_source.reshape(-1), block_receptor.reshape(-1), block_count.reshape(-1))
    flat = probes.reshape(probe_local * rows, lon)
    pair = 2 * probe_local

    edge = jax.ShapeDtypeStruct((SMOOTH, probe_local + PIECES, lon), BF16)
    north, south = pl.pallas_call(
        edge_kernel,
        out_shape=(edge, edge),
        in_specs=[VMEM, VMEM],
        out_specs=(VMEM, VMEM),
        scratch_shapes=[pltpu.VMEM((halves, probe_local * rows, BLK), F32)],
        compiler_params=params(),
        name="edges",
    )(flat, kappa)
    above, below = exchange_edges(north, south)

    part = jax.ShapeDtypeStruct((cells, probe_local, BLK), BF16)
    own = pl.pallas_call(
        smooth_kernel,
        out_shape=part,
        in_specs=[VMEM] * 4,
        out_specs=VMEM,
        scratch_shapes=[
            pltpu.VMEM((halves, probe_local * rows, BLK), F32),
            pltpu.VMEM((3, rows + 2 * SMOOTH, SUB, lon), F32),
            pltpu.VMEM((2, SMOOTH, probe_local, lon), F32),
            pltpu.VMEM((cells, probe_local, BLK), F32),
        ],
        compiler_params=params(),
        name="smooth",
    )(flat, kappa, above, below)

    def streamed(kernel, operands, outs, total):
        whole = lambda shape: pl.BlockSpec(shape, lambda g, *_: (0,) * len(shape))
        return pl.pallas_call(
            kernel,
            out_shape=outs,
            grid_spec=pltpu.PrefetchScalarGridSpec(
                num_scalar_prefetch=3,
                grid=(slots // GROUP,),
                in_specs=[pl.BlockSpec((GROUP, BLK, BLK), lambda g, *_: (g, 0, 0))]
                + [whole(x.shape) for x in operands],
                out_specs=jax.tree.map(lambda o: whole(o.shape), outs),
                scratch_shapes=[pltpu.VMEM(total, F32)],
            ),
            compiler_params=params(),
            name=kernel.__name__,
        )(*scalars, blocks, *operands)

    def forward(near, far):
        return streamed(
            forward_kernel,
            (near, far),
            jax.ShapeDtypeStruct((RB_LOC, pair, BLK), BF16),
            (RB_LOC + 1, pair, BLK),
        )

    def adjoint(weighted):
        return streamed(adjoint_kernel, (weighted,), (part, part), (cells + 1, pair, BLK))

    share = RB_LOC * pair // tiles
    weights = jnp.broadcast_to(obs_weight.reshape(RB_LOC, 1, BLK), (RB_LOC, pair, BLK))
    weights = lax.dynamic_index_in_dim(weights.reshape(tiles, share, BLK), me, 0, False)

    def summed(evolved):
        terms = lax.all_to_all(evolved.reshape(tiles, share, BLK), "src", 0, 0)
        return (weights * jnp.sum(terms.astype(F32), axis=0)).astype(BF16)

    def spread(weighted):
        sent = jnp.broadcast_to(weighted[None], (tiles, share, BLK))
        return lax.all_to_all(sent, "src", 0, 0).reshape(RB_LOC, pair, BLK)

    other = swap(own, "rcv", 2)
    beside = swap(own, "rcv", 1)
    first = summed(forward(own, beside))
    second = summed(forward(other, swap(other, "rcv", 1)))

    to_other, to_diagonal = adjoint(spread(second))
    both = (to_other.astype(F32) + swap(to_diagonal, "rcv", 1).astype(F32)).astype(BF16)
    from_other = swap(both, "rcv", 2)
    mine, to_beside = adjoint(spread(first))
    from_beside = swap(to_beside, "rcv", 1)

    edge_cells = SMOOTH * halves

    def edge_sum(lo):
        pieces = [lax.slice_in_dim(x, lo, lo + edge_cells, axis=0).astype(F32) for x in (mine, from_beside, from_other)]
        return (pieces[0] + pieces[1] + pieces[2]).astype(BF16)

    top, bottom = exchange_edges(edge_sum(0), edge_sum(cells - edge_cells))
    inside = jnp.stack([me > 0, me < tiles - 1]).astype(F32)
    out = pl.pallas_call(
        back_kernel,
        out_shape=jax.ShapeDtypeStruct((probe_local * rows, lon), F32),
        in_specs=[SMEM] + [VMEM] * 9,
        out_specs=VMEM,
        scratch_shapes=[
            pltpu.VMEM((halves, probe_local * rows, BLK), F32),
            pltpu.VMEM((rows + 2 * SMOOTH, SUB, lon), F32),
            pltpu.VMEM((cells, probe_local, BLK), F32),
            pltpu.VMEM((2, edge_cells, probe_local, BLK), F32),
        ],
        compiler_params=params(),
        name="back",
    )(inside, flat, kappa, above, below, mine, from_beside, from_other, top, bottom)
    return out.reshape(probe_local, rows, lon)


def solution(mesh):
    placed = (
        P("rcv", "src", None),
        P("src", None),
        P("src", "rcv", None, None, None),
        P("src", "rcv", None),
        P("src", "rcv", None),
        P("src", "rcv"),
        P("rcv"),
    )
    return jax.shard_map(
        per_device, mesh=mesh, in_specs=placed, out_specs=P("rcv", "src", None), check_vma=False
    )
```

time: 472 us -> 145 us (0.31)
  waiting for transfers between devices: 194 us -> 50.4 us
  other arithmetic: 126 us -> 0.54 us
  matrix products: 53.5 us -> 0 us
  Pallas kernels: 0 us -> 30.2 us
  local copies, waits for them, and re-layouts: 40.5 us -> 15.3 us
  blocking collectives: 0 us -> 18.1 us
  starting transfers between devices: 43 us -> 28.6 us
  between operations: 13.5 us -> 0.85 us
    psum x1 -> x0, waiting for transfers between devices: 102 us -> none  [per_device(): receptor_all = lax.psum(sim_rows, 'src')]
    scatter-add x12 -> x0, other arithmetic: 98.5 us -> none  [the longest x6 59.6 us: adjoint_group(): return running.at[:, source_ids].add(hessian_result * in_use[None, :, None])]
    dot_general x12 -> x0, matrix products: 53.5 us -> none  [the longest x6 28.1 us: forward_group(): jnp.einsum('wlq,wqd->wld', block_portion, selected_entries, preferred_ele...]
    reduce_scatter x1 -> x0, waiting for transfers between devices: 31.1 us -> none  [per_device(): lax.psum_scatter(adjoint_rows, 'rcv', scatter_dimension=0, tiled=True)]
    pallas_call x0 -> x7, Pallas kernels: none -> 30.2 us  [the longest x4 21.1 us: streamed(): pl.pallas_call(kernel, out_shape=outs, grid_spec=pltpu.PrefetchScalarGrid...]
    ppermute x16 -> x10, starting transfers between devices: 42.8 us -> 15.1 us  [the longest x4 12 us: exchange_edges(): return (lax.ppermute(south, 'src', down), lax.ppermute(north, 'src', up))]
    gather x12 -> x0, local copies, waits for them, and re-layouts: 26.2 us -> none  [the longest x6 22.1 us: forward_group(): selected_entries = jnp.take(tile_field, source_ids, axis=0)]
    all_to_all x0 -> x3, waiting for transfers between devices: none -> 25.4 us  [the longest x2 18 us: summed(): terms = lax.all_to_all(evolved.reshape(tiles, share, BLK), 'src', 0, 0)]
  transfers between devices with their start and end apart: 19 -> 13, of which waited for: 19 -> 10; matrix products, arithmetic and copies ran while one was open for 0% -> 0% of each run, Pallas kernels for 0% -> 15%
where the time goes in v1:
time: 145 us; the launch traced here: 144 us
  waiting for transfers between devices  50.4 us (35%)
  Pallas kernels  30.2 us (21%)
  starting transfers between devices  28.6 us (20%)
  blocking collectives  18.1 us (12%)
  local copies, waits for them, and re-layouts  15.3 us (11%)
    pallas_call x4, Pallas kernels, streamed(): pl.pallas_call(kernel, out_shape=outs, grid_spec=pltpu.PrefetchScalarGrid...  21.1 us
    all_to_all x1, blocking collectives, spread(): return lax.all_to_all(sent, 'src', 0, 0).reshape(RB_LOC, pair, BLK)  18.1 us
    all_to_all x2, waiting for transfers between devices, summed(): terms = lax.all_to_all(evolved.reshape(tiles, share, BLK), 'src', 0, 0)  18 us
    ppermute x6, waiting for transfers between devices, swap(): return lax.ppermute(x, axis, [(i, i ^ distance) for i in range(size)])  15.1 us
    unnamed x26, local copies, waits for them, and re-layouts  14.3 us
    ppermute x4, starting transfers between devices, exchange_edges(): return (lax.ppermute(south, 'src', down), lax.ppermute(north, 'src', up))  12 us
    ppermute x4, waiting for transfers between devices, exchange_edges(): return (lax.ppermute(south, 'src', down), lax.ppermute(north, 'src', up))  9.96 us
    all_to_all x2, starting transfers between devices, summed(): terms = lax.all_to_all(evolved.reshape(tiles, share, BLK), 'src', 0, 0)  9.92 us
  transfers between devices with their start and end apart: 13, of which 10 were waited for; matrix products, arithmetic and copies ran while one was open for 0% of the time, Pallas kernels for 15%

profile of v1, /device:TPU:0, one launch (start us, length us, event | category | flops | bytes accessed | tf_op | source)
XLA Modules:
  0.0 144.0 jit_solution(741449924401710206)
XLA Ops:
  0.0 1.1 copy-done.4
  1.1 0.7 copy-done.6
  2.1 4.9 %collective-permute-start = (bf16[4,80,256]{2,1,0:T(8,128)(2,1)S(1)}, bf16[4,80,256]{2,1,0:T(8,128)(2,1)S(1)}, u32[]{:S(2)}, u32[]{:S(2)}) collective-permute-start(bf16[4,80,256]{2,1,0:T(8,128)(2,1)S(1)} %get-tuple-element.11), channel_id=1, source_target_pairs={{0,4},{4,8},{8,12},{12,16},{16,20},{20,24},{24,28},{1,5},{5,9},{9,... | collective-permute-start | bytes 491528 | tf_op jit(solution)/shard_map/ppermute | solution.py:204
  6.9 1.3 collective-permute-start.1
  8.2 2.1 %collective-permute-done.above_ref = bf16[4,80,256]{2,1,0:T(8,128)(2,1)S(1)} collective-permute-done((bf16[4,80,256]{2,1,0:T(8,128)(2,1)S(1)}, bf16[4,80,256]{2,1,0:T(8,128)(2,1)S(1)}, u32[]{:S(2)}, u32[]{:S(2)}) %collective-permute-start) | collective-permute-done | bytes 163872 | tf_op jit(solution)/shard_map/ppermute | solution.py:204
  10.4 4.1 %collective-permute-done.1.below_ref = bf16[4,80,256]{2,1,0:T(8,128)(2,1)S(1)} collective-permute-done((bf16[4,80,256]{2,1,0:T(8,128)(2,1)S(1)}, bf16[4,80,256]{2,1,0:T(8,128)(2,1)S(1)}, u32[]{:S(2)}, u32[]{:S(2)}) %collective-permute-start.1) | collective-permute-done | bytes 163872 | tf_op jit(solution)/shard_map/ppermute | solution.py:204
  14.5 3.5 %smooth.1.near_ref = bf16[32,64,128]{2,1,0:T(8,128)(2,1)S(1)} custom-call(bf16[1024,256]{1,0:T(8,128)(2,1)S(1)} %bitcast.39, f32[16,256]{1,0:T(8,128)S(1)} %copy-done.6, bf16[4,80,256]{2,1,0:T(8,128)(2,1)S(1)} %collective-permute-done.above_ref, bf16[4,80,256]{2,1,0:T(8,128)(2,1)S(1)} %collective-permute-done.1.below_ref), custom_call_target="tpu_custom_call" | custom-call | tf_op jit(solution)/shard_map/smooth/pallas_call | solution.py:232
  18.0 1.6 %collective-permute-start.4 = (bf16[32,64,128]{2,1,0:T(8,128)(2,1)S(1)}, bf16[32,64,128]{2,1,0:T(8,128)(2,1)S(1)}, u32[]{:S(2)}, u32[]{:S(2)}) collective-permute-start(bf16[32,64,128]{2,1,0:T(8,128)(2,1)S(1)} %smooth.1.near_ref), channel_id=1, source_target_pairs={{0,2},{1,3},{2,0},{3,1},{4,6},{5,7},{6,4},{7,5},{8,10},{9,11},{10,... | collective-permute-start | bytes 1572872 | tf_op jit(solution)/shard_map/ppermute | solution.py:197
  20.3 2.8 %copy-done = bf16[1,1,192,128,128]{4,3,2,1,0:T(8,128)(2,1)S(1)} copy-done((bf16[1,1,192,128,128]{4,3,2,1,0:T(8,128)(2,1)S(1)}, bf16[1,1,192,128,128]{4,3,2,1,0:T(8,128)(2,1)}, u32[]{:S(2)}) %copy-start) | copy-done | bytes 6291480
  24.4 6.7 %forward_kernel.2 = bf16[16,128,128]{2,1,0:T(8,128)(2,1)} custom-call(s32[192]{0:T(256)S(1)} %bitcast.43, s32[192]{0:T(256)S(1)} %bitcast.47, s32[1]{0:T(128)} %bitcast.30.count, bf16[192,128,128]{2,1,0:T(8,128)(2,1)S(1)} %bitcast.34, bf16[32,64,128]{2,1,0:T(8,128)(2,1)S(1)} %smooth.1.near_ref, bf16[32,64,128]{2,1,0:T(8,128)(2,1)S(1)} %collective-permute-done.2.far_ref), custom_call_target="tpu_custom_call" | custom-call | tf_op jit(solution)/shard_map/forward_kernel/pallas_call | solution.py:249
  31.1 6.3 %all-to-all-start = ((bf16[8,256,128]{2,1,0:T(8,128)(2,1)}), bf16[8,256,128]{2,1,0:T(8,128)(2,1)S(1)}, u32[]{:S(2)}, u32[]{:S(2)}) async-start(bf16[8,256,128]{2,1,0:T(8,128)(2,1)} %bitcast.9), calls=%async_computation | async-start | bytes 1048576 | tf_op jit(solution)/shard_map/all_to_all | solution.py:280
  37.5 1.9 %collective-permute-done.5.far_ref = bf16[32,64,128]{2,1,0:T(8,128)(2,1)S(1)} collective-permute-done((bf16[32,64,128]{2,1,0:T(8,128)(2,1)S(1)}, bf16[32,64,128]{2,1,0:T(8,128)(2,1)S(1)}, u32[]{:S(2)}, u32[]{:S(2)}) %collective-permute-start.5) | collective-permute-done | bytes 524320 | tf_op jit(solution)/shard_map/ppermute | solution.py:197
  39.4 2.8 %copy-done.1 = bf16[1,1,192,128,128]{4,3,2,1,0:T(8,128)(2,1)S(1)} copy-done((bf16[1,1,192,128,128]{4,3,2,1,0:T(8,128)(2,1)S(1)}, bf16[1,1,192,128,128]{4,3,2,1,0:T(8,128)(2,1)}, u32[]{:S(2)}) %copy-start.1) | copy-done | bytes 6291480
  42.2 6.7 %forward_kernel.3 = bf16[16,128,128]{2,1,0:T(8,128)(2,1)} custom-call(s32[192]{0:T(256)S(1)} %bitcast.44, s32[192]{0:T(256)S(1)} %bitcast.48, s32[1]{0:T(128)} %bitcast.32.count, bf16[192,128,128]{2,1,0:T(8,128)(2,1)S(1)} %bitcast.35, bf16[32,64,128]{2,1,0:T(8,128)(2,1)S(1)} %collective-permute-done.4.near_ref, ...), custom_call_target="tpu_custom_call" | custom-call | tf_op jit(solution)/shard_map/forward_kernel/pallas_call | solution.py:249
  48.9 3.4 %all-to-all-done = bf16[8,256,128]{2,1,0:T(8,128)(2,1)S(1)} async-done(((bf16[8,256,128]{2,1,0:T(8,128)(2,1)}), bf16[8,256,128]{2,1,0:T(8,128)(2,1)S(1)}, u32[]{:S(2)}, u32[]{:S(2)}) %all-to-all-start) | async-done | bytes 524320 | tf_op jit(solution)/shard_map/all_to_all | solution.py:280
  52.2 3.6 %all-to-all-start.2 = ((bf16[8,256,128]{2,1,0:T(8,128)(2,1)}), bf16[8,256,128]{2,1,0:T(8,128)(2,1)S(1)}, u32[]{:S(2)}, u32[]{:S(2)}) async-start(bf16[8,256,128]{2,1,0:T(8,128)(2,1)} %bitcast.13), calls=%async_computation.2 | async-start | bytes 1048576 | tf_op jit(solution)/shard_map/all_to_all | solution.py:280
  56.0 14.6 %all-to-all-done.2 = bf16[8,256,128]{2,1,0:T(8,128)(2,1)S(1)} async-done(((bf16[8,256,128]{2,1,0:T(8,128)(2,1)}), bf16[8,256,128]{2,1,0:T(8,128)(2,1)S(1)}, u32[]{:S(2)}, u32[]{:S(2)}) %all-to-all-start.2) | async-done | bytes 524320 | tf_op jit(solution)/shard_map/all_to_all | solution.py:280
  70.8 18.1 %all_to_all.20 = bf16[8,256,128]{2,1,0:T(8,128)(2,1)S(1)} all-to-all(bf16[8,256,128]{2,1,0:T(8,128)(2,1)S(1)} %broadcast_in_dim.28), channel_id=1, replica_groups=mesh['src'=8,'rcv'=4] {'src'}, dimensions={0} | all-to-all | bytes 1048576 | tf_op jit(solution)/shard_map/all_to_all | solution.py:285
  88.9 0.9 broadcast_in_dim.26
  89.8 3.6 %all-to-all-start.1 = ((bf16[8,256,128]{2,1,0:T(8,128)(2,1)}), bf16[8,256,128]{2,1,0:T(8,128)(2,1)S(1)}, u32[]{:S(2)}, u32[]{:S(2)}) async-start(bf16[8,256,128]{2,1,0:T(8,128)(2,1)} %broadcast_in_dim.26), calls=%async_computation.1 | async-start | bytes 1048576 | tf_op jit(solution)/shard_map/all_to_all | solution.py:285
  93.4 2.8 %copy-done.2 = bf16[1,1,192,128,128]{4,3,2,1,0:T(8,128)(2,1)S(1)} copy-done((bf16[1,1,192,128,128]{4,3,2,1,0:T(8,128)(2,1)S(1)}, bf16[1,1,192,128,128]{4,3,2,1,0:T(8,128)(2,1)}, u32[]{:S(2)}) %copy-start.2) | copy-done | bytes 6291480
  96.2 3.8 %adjoint_kernel.3 = (bf16[32,64,128]{2,1,0:T(8,128)(2,1)S(1)}, bf16[32,64,128]{2,1,0:T(8,128)(2,1)S(1)}) custom-call(s32[192]{0:T(256)S(1)} %bitcast.45, s32[192]{0:T(256)S(1)} %bitcast.49, s32[1]{0:T(128)} %bitcast.33.count, bf16[192,128,128]{2,1,0:T(8,128)(2,1)S(1)} %bitcast.36, bf16[16,128,128]{2,1,0:T(8,128)(2,1)S(1)} %bitcast.42), custom_call_target="tpu_custom_call" | custom-call | tf_op jit(solution)/shard_map/adjoint_kernel/pallas_call | solution.py:249
  100.1 7.5 %all-to-all-done.1 = bf16[8,256,128]{2,1,0:T(8,128)(2,1)S(1)} async-done(((bf16[8,256,128]{2,1,0:T(8,128)(2,1)}), bf16[8,256,128]{2,1,0:T(8,128)(2,1)S(1)}, u32[]{:S(2)}, u32[]{:S(2)}) %all-to-all-start.1) | async-done | bytes 524320 | tf_op jit(solution)/shard_map/all_to_all | solution.py:285
  107.6 2.8 %copy-done.3 = bf16[1,1,192,128,128]{4,3,2,1,0:T(8,128)(2,1)S(1)} copy-done((bf16[1,1,192,128,128]{4,3,2,1,0:T(8,128)(2,1)S(1)}, bf16[1,1,192,128,128]{4,3,2,1,0:T(8,128)(2,1)}, u32[]{:S(2)}) %copy-start.3) | copy-done | bytes 6291480
  110.4 3.8 %adjoint_kernel.2 = (bf16[32,64,128]{2,1,0:T(8,128)(2,1)S(1)}, bf16[32,64,128]{2,1,0:T(8,128)(2,1)S(1)}) custom-call(s32[192]{0:T(256)S(1)} %bitcast.46, s32[192]{0:T(256)S(1)} %bitcast.50, s32[1]{0:T(128)} %bitcast.31.count, bf16[192,128,128]{2,1,0:T(8,128)(2,1)S(1)} %bitcast.37, bf16[16,128,128]{2,1,0:T(8,128)(2,1)S(1)} %bitcast.41), custom_call_target="tpu_custom_call" | custom-call | tf_op jit(solution)/shard_map/adjoint_kernel/pallas_call | solution.py:249
  114.5 1.2 collective-permute-start.7
  116.2 12.7 %collective-permute-done.7.far_ref = bf16[32,64,128]{2,1,0:T(8,128)(2,1)S(1)} collective-permute-done((bf16[32,64,128]{2,1,0:T(8,128)(2,1)S(1)}, bf16[32,64,128]{2,1,0:T(8,128)(2,1)S(1)}, u32[]{:S(2)}, u32[]{:S(2)}) %collective-permute-start.7) | collective-permute-done | bytes 524320 | tf_op jit(solution)/shard_map/ppermute | solution.py:197
  129.0 1.3 collective-permute-start.9
  130.3 4.6 %collective-permute-start.8 = (bf16[8,64,128]{2,1,0:T(8,128)(2,1)S(1)}, bf16[8,64,128]{2,1,0:T(8,128)(2,1)S(1)}, u32[]{:S(2)}, u32[]{:S(2)}) collective-permute-start(bf16[8,64,128]{2,1,0:T(8,128)(2,1)S(1)} %get-tuple-element.18), channel_id=1, source_target_pairs={{0,4},{4,8},{8,12},{12,16},{16,20},{20,24},{24,28},{1,5},{5,9},{9,... | collective-permute-start | bytes 393224 | tf_op jit(solution)/shard_map/ppermute | solution.py:204
  135.0 1.1 collective-permute-done.9.bottom_ref
  136.0 2.6 %collective-permute-done.8.top_ref = bf16[8,64,128]{2,1,0:T(8,128)(2,1)S(1)} collective-permute-done((bf16[8,64,128]{2,1,0:T(8,128)(2,1)S(1)}, bf16[8,64,128]{2,1,0:T(8,128)(2,1)S(1)}, u32[]{:S(2)}, u32[]{:S(2)}) %collective-permute-start.8) | collective-permute-done | bytes 131104 | tf_op jit(solution)/shard_map/ppermute | solution.py:204
  138.7 5.3 %back.1 = f32[1024,256]{1,0:T(8,128)} custom-call(f32[2]{0:T(128)S(1)} %add_convert_fusion.3.inside, bf16[1024,256]{1,0:T(8,128)(2,1)S(1)} %bitcast.40, f32[16,256]{1,0:T(8,128)S(1)} %copy-done.7, bf16[4,80,256]{2,1,0:T(8,128)(2,1)S(1)} %collective-permute-done.above_ref, bf16[4,80,256]{2,1,0:T(8,128)(2,1)S(1)} %collective-permute-done.1.below_ref, ...), custom_call_target="tpu_custom_call" | custom-call | tf_op jit(solution)/shard_map/back/pallas_call | solution.py:306
  (37 shorter events, 3.1 us)
Async XLA Ops:
  0.0 39.4 %copy-start.9 = (s32[1,1,192]{2,1,0:T(1,128)S(1)}, s32[1,1,192]{2,1,0:T(1,128)}, u32[]{:S(2)}) copy-start(s32[1,1,192]{2,1,0:T(1,128)} %param.10) | copy-start | bytes 2308
  0.0 1.1 copy-start.4
  1.1 0.7 copy-start.6
  1.8 37.6 %copy-start.11 = (s32[1,1,192]{2,1,0:T(1,128)S(1)}, s32[1,1,192]{2,1,0:T(1,128)}, u32[]{:S(2)}) copy-start(s32[1,1,192]{2,1,0:T(1,128)} %param.11) | copy-start | bytes 2308
  2.1 8.3 %collective-permute-start = (bf16[4,80,256]{2,1,0:T(8,128)(2,1)S(1)}, bf16[4,80,256]{2,1,0:T(8,128)(2,1)S(1)}, u32[]{:S(2)}, u32[]{:S(2)}) collective-permute-start(bf16[4,80,256]{2,1,0:T(8,128)(2,1)S(1)} %get-tuple-element.11), channel_id=1, source_target_pairs={{0,4},{4,8},{8,12},{12,16},{16,20},{20,24},{24,28},{1,5},{5,9},{9,... | collective-permute-start | bytes 491528 | tf_op jit(solution)/shard_map/ppermute | solution.py:204
  6.9 7.6 %collective-permute-start.1 = (bf16[4,80,256]{2,1,0:T(8,128)(2,1)S(1)}, bf16[4,80,256]{2,1,0:T(8,128)(2,1)S(1)}, u32[]{:S(2)}, u32[]{:S(2)}) collective-permute-start(bf16[4,80,256]{2,1,0:T(8,128)(2,1)S(1)} %get-tuple-element.12), channel_id=1, source_target_pairs={{4,0},{8,4},{12,8},{16,12},{20,16},{24,20},{28,24},{5,1},{9,5},{13... | collective-permute-start | bytes 491528 | tf_op jit(solution)/shard_map/ppermute | solution.py:204
  17.9 2.3 %collective-permute-start.2 = (bf16[32,64,128]{2,1,0:T(8,128)(2,1)S(1)}, bf16[32,64,128]{2,1,0:T(8,128)(2,1)S(1)}, u32[]{:S(2)}, u32[]{:S(2)}) collective-permute-start(bf16[32,64,128]{2,1,0:T(8,128)(2,1)S(1)} %smooth.1.near_ref), channel_id=1, source_target_pairs={{0,1},{1,0},{2,3},{3,2},{4,5},{5,4},{6,7},{7,6},{8,9},{9,8},{10,11... | collective-permute-start | bytes 1572872 | tf_op jit(solution)/shard_map/ppermute | solution.py:197
  18.0 19.4 %collective-permute-start.4 = (bf16[32,64,128]{2,1,0:T(8,128)(2,1)S(1)}, bf16[32,64,128]{2,1,0:T(8,128)(2,1)S(1)}, u32[]{:S(2)}, u32[]{:S(2)}) collective-permute-start(bf16[32,64,128]{2,1,0:T(8,128)(2,1)S(1)} %smooth.1.near_ref), channel_id=1, source_target_pairs={{0,2},{1,3},{2,0},{3,1},{4,6},{5,7},{6,4},{7,5},{8,10},{9,11},{10,... | collective-permute-start | bytes 1572872 | tf_op jit(solution)/shard_map/ppermute | solution.py:197
  20.3 2.8 %copy-start = (bf16[1,1,192,128,128]{4,3,2,1,0:T(8,128)(2,1)S(1)}, bf16[1,1,192,128,128]{4,3,2,1,0:T(8,128)(2,1)}, u32[]{:S(2)}) copy-start(bf16[1,1,192,128,128]{4,3,2,1,0:T(8,128)(2,1)} %param.9) | copy-start | bytes 18874372
  23.1 0.7 copy-start.8
  23.7 0.7 copy-start.10
  31.1 39.5 %copy-start.12 = (f32[2048]{0:T(1024)S(1)}, f32[2048]{0:T(1024)}, u32[]{:S(2)}) copy-start(f32[2048]{0:T(1024)} %param.13) | copy-start | bytes 24580
  31.1 21.1 %all-to-all-start = ((bf16[8,256,128]{2,1,0:T(8,128)(2,1)}), bf16[8,256,128]{2,1,0:T(8,128)(2,1)S(1)}, u32[]{:S(2)}, u32[]{:S(2)}) async-start(bf16[8,256,128]{2,1,0:T(8,128)(2,1)} %bitcast.9), calls=%async_computation | async-start | bytes 1048576 | tf_op jit(solution)/shard_map/all_to_all | solution.py:280
  37.4 2.0 %collective-permute-start.5 = (bf16[32,64,128]{2,1,0:T(8,128)(2,1)S(1)}, bf16[32,64,128]{2,1,0:T(8,128)(2,1)S(1)}, u32[]{:S(2)}, u32[]{:S(2)}) collective-permute-start(bf16[32,64,128]{2,1,0:T(8,128)(2,1)S(1)} %collective-permute-done.4.near_ref), channel_id=1, source_target_pairs={{0,1},{1,0},{2,3},{3,2},{4,5},{5,4},{6,7},{7,6},{8,9},{9,8},{10,11... | collective-permute-start | bytes 1572872 | tf_op jit(solution)/shard_map/ppermute | solution.py:197
  39.4 2.8 %copy-start.1 = (bf16[1,1,192,128,128]{4,3,2,1,0:T(8,128)(2,1)S(1)}, bf16[1,1,192,128,128]{4,3,2,1,0:T(8,128)(2,1)}, u32[]{:S(2)}) copy-start(bf16[1,1,192,128,128]{4,3,2,1,0:T(8,128)(2,1)} %param.9) | copy-start | bytes 18874372
  52.2 18.3 %all-to-all-start.2 = ((bf16[8,256,128]{2,1,0:T(8,128)(2,1)}), bf16[8,256,128]{2,1,0:T(8,128)(2,1)S(1)}, u32[]{:S(2)}, u32[]{:S(2)}) async-start(bf16[8,256,128]{2,1,0:T(8,128)(2,1)} %bitcast.13), calls=%async_computation.2 | async-start | bytes 1048576 | tf_op jit(solution)/shard_map/all_to_all | solution.py:280
  89.8 17.8 %all-to-all-start.1 = ((bf16[8,256,128]{2,1,0:T(8,128)(2,1)}), bf16[8,256,128]{2,1,0:T(8,128)(2,1)S(1)}, u32[]{:S(2)}, u32[]{:S(2)}) async-start(bf16[8,256,128]{2,1,0:T(8,128)(2,1)} %broadcast_in_dim.26), calls=%async_computation.1 | async-start | bytes 1048576 | tf_op jit(solution)/shard_map/all_to_all | solution.py:285
  93.4 2.8 %copy-start.2 = (bf16[1,1,192,128,128]{4,3,2,1,0:T(8,128)(2,1)S(1)}, bf16[1,1,192,128,128]{4,3,2,1,0:T(8,128)(2,1)}, u32[]{:S(2)}) copy-start(bf16[1,1,192,128,128]{4,3,2,1,0:T(8,128)(2,1)} %param.9) | copy-start | bytes 18874372
  96.2 42.5 %copy-start.5 = (bf16[64,16,256]{2,1,0:T(8,128)(2,1)S(1)}, bf16[64,16,256]{2,1,0:T(8,128)(2,1)}, u32[]{:S(2)}) copy-start(bf16[64,16,256]{2,1,0:T(8,128)(2,1)} %param.7) | copy-start | bytes 1572868
  96.2 42.5 %copy-start.7 = (f32[16,256]{1,0:T(8,128)S(1)}, f32[16,256]{1,0:T(8,128)}, u32[]{:S(2)}) copy-start(f32[16,256]{1,0:T(8,128)} %kappa_ref.5) | copy-start | bytes 49156
  100.1 14.3 %collective-permute-start.6 = (bf16[32,64,128]{2,1,0:T(8,128)(2,1)S(1)}, bf16[32,64,128]{2,1,0:T(8,128)(2,1)S(1)}, u32[]{:S(2)}, u32[]{:S(2)}) collective-permute-start(bf16[32,64,128]{2,1,0:T(8,128)(2,1)S(1)} %get-tuple-element.16), channel_id=1, source_target_pairs={{0,1},{1,0},{2,3},{3,2},{4,5},{5,4},{6,7},{7,6},{8,9},{9,8},{10,11... | collective-permute-start | bytes 1572872 | tf_op jit(solution)/shard_map/ppermute | solution.py:197
  107.6 2.8 %copy-start.3 = (bf16[1,1,192,128,128]{4,3,2,1,0:T(8,128)(2,1)S(1)}, bf16[1,1,192,128,128]{4,3,2,1,0:T(8,128)(2,1)}, u32[]{:S(2)}) copy-start(bf16[1,1,192,128,128]{4,3,2,1,0:T(8,128)(2,1)} %param.9) | copy-start | bytes 18874372
  114.3 2.0 %collective-permute-start.3 = (bf16[32,64,128]{2,1,0:T(8,128)(2,1)S(1)}, bf16[32,64,128]{2,1,0:T(8,128)(2,1)S(1)}, u32[]{:S(2)}, u32[]{:S(2)}) collective-permute-start(bf16[32,64,128]{2,1,0:T(8,128)(2,1)S(1)} %get-tuple-element.14), channel_id=1, source_target_pairs={{0,1},{1,0},{2,3},{3,2},{4,5},{5,4},{6,7},{7,6},{8,9},{9,8},{10,11... | collective-permute-start | bytes 1572872 | tf_op jit(solution)/shard_map/ppermute | solution.py:197
  114.5 14.4 %collective-permute-start.7 = (bf16[32,64,128]{2,1,0:T(8,128)(2,1)S(1)}, bf16[32,64,128]{2,1,0:T(8,128)(2,1)S(1)}, u32[]{:S(2)}, u32[]{:S(2)}) collective-permute-start(bf16[32,64,128]{2,1,0:T(8,128)(2,1)S(1)} %add_convert_fusion), channel_id=1, source_target_pairs={{0,2},{1,3},{2,0},{3,1},{4,6},{5,7},{6,4},{7,5},{8,10},{9,11},{10,... | collective-permute-start | bytes 1572872 | tf_op jit(solution)/shard_map/ppermute | solution.py:197
  129.0 7.0 %collective-permute-start.9 = (bf16[8,64,128]{2,1,0:T(8,128)(2,1)S(1)}, bf16[8,64,128]{2,1,0:T(8,128)(2,1)S(1)}, u32[]{:S(2)}, u32[]{:S(2)}) collective-permute-start(bf16[8,64,128]{2,1,0:T(8,128)(2,1)S(1)} %get-tuple-element.17), channel_id=1, source_target_pairs={{4,0},{8,4},{12,8},{16,12},{20,16},{24,20},{28,24},{5,1},{9,5},{13... | collective-permute-start | bytes 393224 | tf_op jit(solution)/shard_map/ppermute | solution.py:204
  130.3 8.3 %collective-permute-start.8 = (bf16[8,64,128]{2,1,0:T(8,128)(2,1)S(1)}, bf16[8,64,128]{2,1,0:T(8,128)(2,1)S(1)}, u32[]{:S(2)}, u32[]{:S(2)}) collective-permute-start(bf16[8,64,128]{2,1,0:T(8,128)(2,1)S(1)} %get-tuple-element.18), channel_id=1, source_target_pairs={{0,4},{4,8},{8,12},{12,16},{16,20},{20,24},{24,28},{1,5},{5,9},{9,... | collective-permute-start | bytes 393224 | tf_op jit(solution)/shard_map/ppermute | solution.py:204

commit v2 on v1

--- a/solution.py
+++ b/solution.py
@@ -16,7 +16,7 @@
 SMEM = pl.BlockSpec(memory_space=pltpu.SMEM)
 
 
-def params(mib=32):
+def params(mib=24):
     return pltpu.CompilerParams(vmem_limit_bytes=mib * 1024 * 1024)
 
 
@@ -101,48 +101,61 @@
     field_ref[...] = result[...].astype(BF16)
 
 
-def forward_kernel(sources, receptors, count, blocks_ref, near_ref, far_ref, out_ref, total):
-    g = pl.program_id(0)
-
-    @pl.when(g == 0)
-    def _():
-        total[...] = jnp.zeros_like(total)
-
-    group = blocks_ref.shape[0]
+def hold_kernel(blocks_ref, after_ref, held_ref, arrived):
+    copy = pltpu.make_async_copy(blocks_ref, held_ref, arrived)
+    copy.start()
+    copy.wait()
+
+
+def each_slot(slots, body):
+    @pl.loop(0, slots // GROUP)
+    def _(g):
+        for i in range(GROUP):
+            body(g * GROUP + i)
+
+
+def forward_kernel(
+    sources, receptors, count, place, held, near_ref, far_ref, keep_ref, give_ref, turned, total
+):
+    total[...] = jnp.zeros_like(total)
+    for j in range(turned.shape[0]):
+        turned[j] = jnp.concatenate([near_ref[j], far_ref[j]], axis=0).T
+
     spare = total.shape[0] - 1
-    for i in range(group):
-        n = g * group + i
-        j = sources[n]
+
+    def slot(n):
         b = jnp.where(n < count[0], receptors[n], spare)
-        entries = jnp.concatenate([near_ref[j], far_ref[j]], axis=0)
-        total[b] += lax.dot_general(
-            entries, blocks_ref[i], (((1,), (1,)), ((), ())), preferred_element_type=F32
-        )
-
-    @pl.when(g == pl.num_programs(0) - 1)
-    def _():
-        out_ref[...] = total[:spare].astype(BF16)
-
-
-def adjoint_kernel(sources, receptors, count, blocks_ref, weighted_ref, near_ref, far_ref, total):
-    g = pl.program_id(0)
-
-    @pl.when(g == 0)
-    def _():
-        total[...] = jnp.zeros_like(total)
-
-    group = blocks_ref.shape[0]
+        total[b] += jnp.dot(held[n], turned[sources[n]], preferred_element_type=F32)
+
+    each_slot(held.shape[0], slot)
+    half = keep_ref.shape[0]
+    for out_ref, side in ((keep_ref, place[0]), (give_ref, 1 - place[0])):
+        for b in range(half):
+            out_ref[b] = total[side * half + b].T.astype(BF16)
+
+
+def adjoint_kernel(
+    sources, receptors, count, place, held, mine_ref, theirs_ref, near_ref, far_ref, weighted, total
+):
+    total[...] = jnp.zeros_like(total)
+    pieces, share = mine_ref.shape[:2]
+    for side_ref, side in ((mine_ref, place[0]), (theirs_ref, 1 - place[0])):
+        for k in range(pieces):
+            row = (side * pieces + lax.bitwise_xor(place[1], k)) * share
+            weighted[pl.ds(pl.multiple_of(row, share), share), :] = side_ref[k]
+
     spare = total.shape[0] - 1
-    for i in range(group):
-        n = g * group + i
+    pair = total.shape[1]
+
+    def slot(n):
         j = jnp.where(n < count[0], sources[n], spare)
-        total[j] += jnp.dot(weighted_ref[receptors[n]], blocks_ref[i], preferred_element_type=F32)
-
-    @pl.when(g == pl.num_programs(0) - 1)
-    def _():
-        half = near_ref.shape[1]
-        near_ref[...] = total[:spare, :half].astype(BF16)
-        far_ref[...] = total[:spare, half:].astype(BF16)
+        entries = weighted[pl.ds(pl.multiple_of(receptors[n] * pair, pair), pair), :]
+        total[j] += jnp.dot(entries, held[n], preferred_element_type=F32)
+
+    each_slot(held.shape[0], slot)
+    half = near_ref.shape[1]
+    near_ref[...] = total[:spare, :half].astype(BF16)
+    far_ref[...] = total[:spare, half:].astype(BF16)
 
 
 def back_kernel(
@@ -197,6 +210,10 @@
     return lax.ppermute(x, axis, [(i, i ^ distance) for i in range(size)])
 
 
+def far_first(size):
+    return sorted(range(1, size), key=lambda k: -k.bit_length())
+
+
 def exchange_edges(north, south):
     size = lax.axis_size("src")
     down = [(i, i + 1) for i in range(size - 1)]
@@ -212,7 +229,6 @@
     me = lax.axis_index("src")
     blocks = footprint.reshape(footprint.shape[2:])
     slots = blocks.shape[0]
-    scalars = (block_source.reshape(-1), block_receptor.reshape(-1), block_count.reshape(-1))
     flat = probes.reshape(probe_local * rows, lon)
     pair = 2 * probe_local
 
@@ -227,6 +243,18 @@
         name="edges",
     )(flat, kappa)
     above, below = exchange_edges(north, south)
+
+    def hold(after):
+        return pl.pallas_call(
+            hold_kernel,
+            out_shape=jax.ShapeDtypeStruct(blocks.shape, BF16),
+            in_specs=[pl.BlockSpec(memory_space=pltpu.HBM), pl.BlockSpec(memory_space=pl.ANY)],
+            out_specs=VMEM,
+            scratch_shapes=[pltpu.SemaphoreType.DMA],
+            compiler_params=params(),
+            cost_estimate=pl.CostEstimate(flops=0, bytes_accessed=4 * slots * BLK * BLK, transcendentals=0),
+            name="hold",
+        )(blocks, after)
 
     part = jax.ShapeDtypeStruct((cells, probe_local, BLK), BF16)
     own = pl.pallas_call(
@@ -244,55 +272,83 @@
         name="smooth",
     )(flat, kappa, above, below)
 
-    def streamed(kernel, operands, outs, total):
-        whole = lambda shape: pl.BlockSpec(shape, lambda g, *_: (0,) * len(shape))
+    side, row = me % 2, me // 2
+    place = jnp.stack([side, row]).astype(jnp.int32)
+    scalars = (block_source.reshape(-1), block_receptor.reshape(-1), block_count.reshape(-1), place)
+    spread_over = tiles // 2
+    share = RB_LOC * pair // tiles
+
+    def over_slots(kernel, held, operands, outs, scratch):
         return pl.pallas_call(
             kernel,
             out_shape=outs,
-            grid_spec=pltpu.PrefetchScalarGridSpec(
-                num_scalar_prefetch=3,
-                grid=(slots // GROUP,),
-                in_specs=[pl.BlockSpec((GROUP, BLK, BLK), lambda g, *_: (g, 0, 0))]
-                + [whole(x.shape) for x in operands],
-                out_specs=jax.tree.map(lambda o: whole(o.shape), outs),
-                scratch_shapes=[pltpu.VMEM(total, F32)],
+            in_specs=[SMEM] * len(scalars) + [VMEM] * (1 + len(operands)),
+            out_specs=jax.tree.map(lambda _: VMEM, outs),
+            scratch_shapes=scratch,
+            compiler_params=params(),
+            cost_estimate=pl.CostEstimate(
+                flops=2 * slots * BLK * BLK * pair, bytes_accessed=2 * slots * BLK * BLK, transcendentals=0
             ),
-            compiler_params=params(),
             name=kernel.__name__,
-        )(*scalars, blocks, *operands)
-
-    def forward(near, far):
-        return streamed(
+        )(*scalars, held, *operands)
+
+    def forward(held, near, far):
+        half = jax.ShapeDtypeStruct((RB_LOC // 2, pair, BLK), BF16)
+        return over_slots(
             forward_kernel,
+            held,
             (near, far),
-            jax.ShapeDtypeStruct((RB_LOC, pair, BLK), BF16),
-            (RB_LOC + 1, pair, BLK),
+            (half, half),
+            [pltpu.VMEM((cells, BLK, pair), BF16), pltpu.VMEM((RB_LOC + 1, BLK, pair), F32)],
         )
 
-    def adjoint(weighted):
-        return streamed(adjoint_kernel, (weighted,), (part, part), (cells + 1, pair, BLK))
-
-    share = RB_LOC * pair // tiles
+    def adjoint(held, mine, theirs):
+        return over_slots(
+            adjoint_kernel,
+            held,
+            (mine, theirs),
+            (part, part),
+            [pltpu.VMEM((RB_LOC * pair, BLK), BF16), pltpu.VMEM((cells + 1, pair, BLK), F32)],
+        )
+
     weights = jnp.broadcast_to(obs_weight.reshape(RB_LOC, 1, BLK), (RB_LOC, pair, BLK))
-    weights = lax.dynamic_index_in_dim(weights.reshape(tiles, share, BLK), me, 0, False)
-
-    def summed(evolved):
-        terms = lax.all_to_all(evolved.reshape(tiles, share, BLK), "src", 0, 0)
-        return (weights * jnp.sum(terms.astype(F32), axis=0)).astype(BF16)
+    weights = lax.dynamic_index_in_dim(weights.reshape(2, spread_over, share, BLK), side, 0, False)
+    weights = lax.dynamic_index_in_dim(weights, row, 0, False)
+
+    def summed(keep, give):
+        got = swap(give, "src", 1)
+        pairs = (keep.astype(F32) + got.astype(F32)).astype(BF16).reshape(spread_over, share, BLK)
+        picked = lambda k: lax.dynamic_index_in_dim(pairs, lax.bitwise_xor(row, k), 0, False)
+        total = picked(0).astype(F32)
+        for k in far_first(spread_over):
+            total = total + swap(picked(k), "src", 2 * k).astype(F32)
+        return (weights * total).astype(BF16)
+
+    def gathered(weighted):
+        pieces = {k: swap(weighted, "src", 2 * k) for k in far_first(spread_over)}
+        return jnp.stack([weighted] + [pieces[k] for k in range(1, spread_over)])
 
     def spread(weighted):
-        sent = jnp.broadcast_to(weighted[None], (tiles, share, BLK))
-        return lax.all_to_all(sent, "src", 0, 0).reshape(RB_LOC, pair, BLK)
+        mine = gathered(weighted)
+        return mine, swap(mine, "src", 1)
 
     other = swap(own, "rcv", 2)
     beside = swap(own, "rcv", 1)
-    first = summed(forward(own, beside))
-    second = summed(forward(other, swap(other, "rcv", 1)))
-
-    to_other, to_diagonal = adjoint(spread(second))
+    held = hold(own)
+    near_keep, near_give = forward(held, own, beside)
+    other, near_give = lax.optimization_barrier((other, near_give))
+    first = summed(near_keep, near_give)
+    second = summed(*forward(held, other, swap(other, "rcv", 1)))
+
+    held = hold(second)
+    second_halves = spread(second)
+    first, _ = lax.optimization_barrier((first, second_halves[0]))
+    first_mine = gathered(first)
+    to_other, to_diagonal = adjoint(held, *second_halves)
     both = (to_other.astype(F32) + swap(to_diagonal, "rcv", 1).astype(F32)).astype(BF16)
+    first_mine, both = lax.optimization_barrier((first_mine, both))
     from_other = swap(both, "rcv", 2)
-    mine, to_beside = adjoint(spread(first))
+    mine, to_beside = adjoint(held, first_mine, swap(first_mine, "src", 1))
     from_beside = swap(to_beside, "rcv", 1)
 
     edge_cells = SMOOTH * halves

time: 145 us -> 120 us (0.83)
  blocking collectives: 18.1 us -> 0 us
  starting transfers between devices: 28.6 us -> 38.3 us
  waiting for transfers between devices: 50.4 us -> 41 us
  Pallas kernels: 30.2 us -> 25.6 us
  local copies, waits for them, and re-layouts: 15.3 us -> 13.2 us
    all_to_all x3 -> x0, waiting for transfers between devices: 25.4 us -> none  [the longest x2 18 us: summed(): terms = lax.all_to_all(evolved.reshape(tiles, share, BLK), 'src', 0, 0)]
    ppermute x6 -> x22, starting transfers between devices: 3.09 us -> 27.3 us  [swap(): return lax.ppermute(x, axis, [(i, i ^ distance) for i in range(size)])]
    all_to_all x1 -> x0, blocking collectives: 18.1 us -> none  [spread(): return lax.all_to_all(sent, 'src', 0, 0).reshape(RB_LOC, pair, BLK)]
    ppermute x6 -> x22, waiting for transfers between devices: 15.1 us -> 29 us  [swap(): return lax.ppermute(x, axis, [(i, i ^ distance) for i in range(size)])]
    all_to_all x3 -> x0, starting transfers between devices: 13.6 us -> none  [the longest x2 9.92 us: summed(): terms = lax.all_to_all(evolved.reshape(tiles, share, BLK), 'src', 0, 0)]
    pallas_call x4 -> x6, Pallas kernels: 21.1 us -> 16.5 us  [the longest x4 15.6 us: over_slots(): pl.pallas_call(kernel, out_shape=outs, in_specs=[SMEM] * len(scalars) + [...]
    ppermute x4, waiting for transfers between devices: 9.96 us -> 12 us  [exchange_edges(): return (lax.ppermute(south, 'src', down), lax.ppermute(north, 'src', up))]
    unnamed x26 -> x22, local copies, waits for them, and re-layouts: 14.3 us -> 13 us
  transfers between devices with their start and end apart: 13 -> 26, of which waited for: 10 -> 17; matrix products, arithmetic and copies ran while one was open for 0% -> 0% of each run, Pallas kernels for 15% -> 11%
where the time goes in v2:
time: 120 us
  waiting for transfers between devices  41 us (34%)
  starting transfers between devices  38.3 us (32%)
  Pallas kernels  25.6 us (21%)
  local copies, waits for them, and re-layouts  13.2 us (11%)
    ppermute x22, waiting for transfers between devices, swap(): return lax.ppermute(x, axis, [(i, i ^ distance) for i in range(size)])  29 us
    ppermute x22, starting transfers between devices, swap(): return lax.ppermute(x, axis, [(i, i ^ distance) for i in range(size)])  27.3 us
    pallas_call x4, Pallas kernels, over_slots(): pl.pallas_call(kernel, out_shape=outs, in_specs=[SMEM] * len(scalars) + [...  15.6 us
    unnamed x22, local copies, waits for them, and re-layouts  13 us
    ppermute x4, waiting for transfers between devices, exchange_edges(): return (lax.ppermute(south, 'src', down), lax.ppermute(north, 'src', up))  12 us
    ppermute x4, starting transfers between devices, exchange_edges(): return (lax.ppermute(south, 'src', down), lax.ppermute(north, 'src', up))  11 us
    pallas_call x1, Pallas kernels, per_device(): pl.pallas_call(back_kernel, out_shape=jax.ShapeDtypeStruct((probe_local *...  5.34 us
    pallas_call x1, Pallas kernels, per_device(): pl.pallas_call(smooth_kernel, out_shape=part, in_specs=[VMEM] * 4, out_sp...  3.45 us
  transfers between devices with their start and end apart: 26, of which 17 were waited for; matrix products, arithmetic and copies ran while one was open for 0% of the time, Pallas kernels for 11%

profile of v2, /device:TPU:0, one launch (start us, length us, event | category | flops | bytes accessed | tf_op | source)
XLA Modules:
  0.0 119.7 jit_solution(13024798119946647296)
XLA Ops:
  2.1 4.9 %collective-permute-start = (bf16[4,80,256]{2,1,0:T(8,128)(2,1)S(1)}, bf16[4,80,256]{2,1,0:T(8,128)(2,1)S(1)}, u32[]{:S(2)}, u32[]{:S(2)}) collective-permute-start(bf16[4,80,256]{2,1,0:T(8,128)(2,1)S(1)} %get-tuple-element.20), channel_id=1, source_target_pairs={{0,4},{4,8},{8,12},{12,16},{16,20},{20,24},{24,28},{1,5},{5,9},{9,... | collective-permute-start | bytes 491528 | tf_op jit(solution)/shard_map/ppermute | solution.py:221
  8.2 2.1 %collective-permute-done.above_ref = bf16[4,80,256]{2,1,0:T(8,128)(2,1)S(1)} collective-permute-done((bf16[4,80,256]{2,1,0:T(8,128)(2,1)S(1)}, bf16[4,80,256]{2,1,0:T(8,128)(2,1)S(1)}, u32[]{:S(2)}, u32[]{:S(2)}) %collective-permute-start) | collective-permute-done | bytes 163872 | tf_op jit(solution)/shard_map/ppermute | solution.py:221
  10.3 4.1 %collective-permute-done.1.below_ref = bf16[4,80,256]{2,1,0:T(8,128)(2,1)S(1)} collective-permute-done((bf16[4,80,256]{2,1,0:T(8,128)(2,1)S(1)}, bf16[4,80,256]{2,1,0:T(8,128)(2,1)S(1)}, u32[]{:S(2)}, u32[]{:S(2)}) %collective-permute-start.1) | collective-permute-done | bytes 163872 | tf_op jit(solution)/shard_map/ppermute | solution.py:221
  14.5 3.5 %smooth.1.after_ref.near_ref = bf16[32,64,128]{2,1,0:T(8,128)(2,1)S(1)} custom-call(bf16[1024,256]{1,0:T(8,128)(2,1)S(1)} %bitcast.50, f32[16,256]{1,0:T(8,128)S(1)} %copy-done.6, bf16[4,80,256]{2,1,0:T(8,128)(2,1)S(1)} %collective-permute-done.above_ref, bf16[4,80,256]{2,1,0:T(8,128)(2,1)S(1)} %collective-permute-done.1.below_ref), custom_call_target="tpu_custom_call" | custom-call | tf_op jit(solution)/shard_map/smooth/pallas_call | solution.py:260
  18.0 1.6 %collective-permute-start.2 = (bf16[32,64,128]{2,1,0:T(8,128)(2,1)S(1)}, bf16[32,64,128]{2,1,0:T(8,128)(2,1)S(1)}, u32[]{:S(2)}, u32[]{:S(2)}) collective-permute-start(bf16[32,64,128]{2,1,0:T(8,128)(2,1)S(1)} %smooth.1.after_ref.near_ref), channel_id=1, source_target_pairs={{0,2},{1,3},{2,0},{3,1},{4,6},{5,7},{6,4},{7,5},{8,10},{9,11},{10,... | collective-permute-start | bytes 1572872 | tf_op jit(solution)/shard_map/ppermute | solution.py:210
  20.3 2.8 %copy-done.2 = bf16[1,1,192,128,128]{4,3,2,1,0:T(8,128)(2,1)S(1)} copy-done((bf16[1,1,192,128,128]{4,3,2,1,0:T(8,128)(2,1)S(1)}, bf16[1,1,192,128,128]{4,3,2,1,0:T(8,128)(2,1)}, u32[]{:S(2)}) %copy-start.2) | copy-done | bytes 6291480
  23.8 4.1 %forward_kernel.2 = (bf16[8,128,128]{2,1,0:T(8,128)(2,1)S(1)}, bf16[8,128,128]{2,1,0:T(8,128)(2,1)S(1)}) custom-call(s32[192]{0:T(256)S(1)} %bitcast.53, s32[192]{0:T(256)S(1)} %bitcast.57, s32[1]{0:T(128)} %bitcast.43.count, s32[2]{0:T(128)S(1)} %pad_add_fusion.place, bf16[192,128,128]{2,1,0:T(8,128)(2,1)S(1)} %hold.2.held, ...), custom_call_target="tpu_custom_call" | custom-call | flops 805306368 | bytes 6291456 | tf_op jit(solution)/shard_map/forward_kernel/pallas_call | solution.py:282
  27.9 2.7 %copy-done = bf16[192,128,128]{2,1,0:T(8,128)(2,1)} copy-done((bf16[192,128,128]{2,1,0:T(8,128)(2,1)}, bf16[192,128,128]{2,1,0:T(8,128)(2,1)S(1)}, u32[]{:S(2)}) %copy-start) | copy-done | bytes 6291480
  30.6 1.7 %collective-permute-done.2.near_ref = bf16[32,64,128]{2,1,0:T(8,128)(2,1)S(1)} collective-permute-done((bf16[32,64,128]{2,1,0:T(8,128)(2,1)S(1)}, bf16[32,64,128]{2,1,0:T(8,128)(2,1)S(1)}, u32[]{:S(2)}, u32[]{:S(2)}) %collective-permute-start.2) | collective-permute-done | bytes 524320 | tf_op jit(solution)/shard_map/ppermute | solution.py:210
  32.3 2.4 %collective-permute-start.9 = (bf16[8,128,128]{2,1,0:T(8,128)(2,1)S(1)}, bf16[8,128,128]{2,1,0:T(8,128)(2,1)S(1)}, u32[]{:S(2)}, u32[]{:S(2)}) collective-permute-start(bf16[8,128,128]{2,1,0:T(8,128)(2,1)S(1)} %get-tuple-element.27), channel_id=1, source_target_pairs={{0,4},{4,0},{8,12},{12,8},{16,20},{20,16},{24,28},{28,24},{1,5},{5... | collective-permute-start | bytes 786440 | tf_op jit(solution)/shard_map/ppermute | solution.py:210
  34.8 2.8 %copy-done.1 = bf16[192,128,128]{2,1,0:T(8,128)(2,1)S(1)} copy-done((bf16[192,128,128]{2,1,0:T(8,128)(2,1)S(1)}, bf16[192,128,128]{2,1,0:T(8,128)(2,1)}, u32[]{:S(2)}) %copy-start.1) | copy-done | bytes 6291480
  37.6 4.0 %forward_kernel.3 = (bf16[8,128,128]{2,1,0:T(8,128)(2,1)S(1)}, bf16[8,128,128]{2,1,0:T(8,128)(2,1)S(1)}) custom-call(s32[192]{0:T(256)S(1)} %bitcast.54, s32[192]{0:T(256)S(1)} %bitcast.58, s32[1]{0:T(128)} %bitcast.44.count, s32[2]{0:T(128)S(1)} %pad_add_fusion.place, bf16[192,128,128]{2,1,0:T(8,128)(2,1)S(1)} %copy-done.1, ...), custom_call_target="tpu_custom_call" | custom-call | flops 805306368 | bytes 6291456 | tf_op jit(solution)/shard_map/forward_kernel/pallas_call | solution.py:282
  41.6 2.0 %collective-permute-start.5 = (bf16[8,128,128]{2,1,0:T(8,128)(2,1)S(1)}, bf16[8,128,128]{2,1,0:T(8,128)(2,1)S(1)}, u32[]{:S(2)}, u32[]{:S(2)}) collective-permute-start(bf16[8,128,128]{2,1,0:T(8,128)(2,1)S(1)} %get-tuple-element.25), channel_id=1, source_target_pairs={{0,4},{4,0},{8,12},{12,8},{16,20},{20,16},{24,28},{28,24},{1,5},{5... | collective-permute-start | bytes 786440 | tf_op jit(solution)/shard_map/ppermute | solution.py:210
  43.7 2.6 %collective-permute-start.10 = (bf16[256,128]{1,0:T(8,128)(2,1)S(1)}, bf16[256,128]{1,0:T(8,128)(2,1)S(1)}, u32[]{:S(2)}, u32[]{:S(2)}) collective-permute-start(bf16[256,128]{1,0:T(8,128)(2,1)S(1)} %get-tuple-element.39), channel_id=1, source_target_pairs={{0,16},{4,20},{8,24},{12,28},{16,0},{20,4},{24,8},{28,12},{1,17},{... | collective-permute-start | bytes 196616 | tf_op jit(solution)/shard_map/ppermute | solution.py:210
  47.7 2.5 %collective-permute-done.5 = bf16[8,128,128]{2,1,0:T(8,128)(2,1)S(1)} collective-permute-done((bf16[8,128,128]{2,1,0:T(8,128)(2,1)S(1)}, bf16[8,128,128]{2,1,0:T(8,128)(2,1)S(1)}, u32[]{:S(2)}, u32[]{:S(2)}) %collective-permute-start.5) | collective-permute-done | bytes 262176 | tf_op jit(solution)/shard_map/ppermute | solution.py:210
  50.2 3.2 %collective-permute-start.6 = (bf16[256,128]{1,0:T(8,128)(2,1)S(1)}, bf16[256,128]{1,0:T(8,128)(2,1)S(1)}, u32[]{:S(2)}, u32[]{:S(2)}) collective-permute-start(bf16[256,128]{1,0:T(8,128)(2,1)S(1)} %get-tuple-element.42), channel_id=1, source_target_pairs={{0,16},{4,20},{8,24},{12,28},{16,0},{20,4},{24,8},{28,12},{1,17},{... | collective-permute-start | bytes 196616 | tf_op jit(solution)/shard_map/ppermute | solution.py:210
  56.2 3.5 %collective-permute-done.7 = bf16[256,128]{1,0:T(8,128)(2,1)S(1)} collective-permute-done((bf16[256,128]{1,0:T(8,128)(2,1)S(1)}, bf16[256,128]{1,0:T(8,128)(2,1)S(1)}, u32[]{:S(2)}, u32[]{:S(2)}) %collective-permute-start.7) | collective-permute-done | bytes 65568 | tf_op jit(solution)/shard_map/ppermute | solution.py:210
  60.5 2.5 %collective-permute-start.14 = (bf16[256,128]{1,0:T(8,128)(2,1)S(1)}, bf16[256,128]{1,0:T(8,128)(2,1)S(1)}, u32[]{:S(2)}, u32[]{:S(2)}) collective-permute-start(bf16[256,128]{1,0:T(8,128)(2,1)S(1)} %get-tuple-element.38.after_ref), channel_id=1, source_target_pairs={{0,16},{4,20},{8,24},{12,28},{16,0},{20,4},{24,8},{28,12},{1,17},{... | collective-permute-start | bytes 196616 | tf_op jit(solution)/shard_map/ppermute | solution.py:210
  64.5 3.4 %collective-permute-done.14 = bf16[256,128]{1,0:T(8,128)(2,1)S(1)} collective-permute-done((bf16[256,128]{1,0:T(8,128)(2,1)S(1)}, bf16[256,128]{1,0:T(8,128)(2,1)S(1)}, u32[]{:S(2)}, u32[]{:S(2)}) %collective-permute-start.14) | collective-permute-done | bytes 65568 | tf_op jit(solution)/shard_map/ppermute | solution.py:210
  70.2 2.8 %copy-done.3 = bf16[1,1,192,128,128]{4,3,2,1,0:T(8,128)(2,1)S(1)} copy-done((bf16[1,1,192,128,128]{4,3,2,1,0:T(8,128)(2,1)S(1)}, bf16[1,1,192,128,128]{4,3,2,1,0:T(8,128)(2,1)}, u32[]{:S(2)}) %copy-start.3) | copy-done | bytes 6291480
  73.4 2.2 %collective-permute-done.19.theirs_ref = bf16[4,256,128]{2,1,0:T(8,128)(2,1)S(1)} collective-permute-done((bf16[4,256,128]{2,1,0:T(8,128)(2,1)S(1)}, bf16[4,256,128]{2,1,0:T(8,128)(2,1)S(1)}, u32[]{:S(2)}, u32[]{:S(2)}) %collective-permute-start.19) | collective-permute-done | bytes 262176 | tf_op jit(solution)/shard_map/ppermute | solution.py:210
  75.6 3.8 %adjoint_kernel.2 = (bf16[32,64,128]{2,1,0:T(8,128)(2,1)S(1)}, bf16[32,64,128]{2,1,0:T(8,128)(2,1)S(1)}) custom-call(s32[192]{0:T(256)S(1)} %bitcast.55, s32[192]{0:T(256)S(1)} %bitcast.59, s32[1]{0:T(128)} %bitcast.45.count, s32[2]{0:T(128)S(1)} %pad_add_fusion.place, bf16[192,128,128]{2,1,0:T(8,128)(2,1)S(1)} %hold.3.held, ...), custom_call_target="tpu_custom_call" | custom-call | flops 805306368 | bytes 6291456 | tf_op jit(solution)/shard_map/adjoint_kernel/pallas_call | solution.py:282
  81.0 2.0 %collective-permute-start.17 = (bf16[256,128]{1,0:T(8,128)(2,1)S(1)}, bf16[256,128]{1,0:T(8,128)(2,1)S(1)}, u32[]{:S(2)}, u32[]{:S(2)}) collective-permute-start(bf16[256,128]{1,0:T(8,128)(2,1)S(1)} %get-tuple-element.28), channel_id=1, source_target_pairs={{0,16},{4,20},{8,24},{12,28},{16,0},{20,4},{24,8},{28,12},{1,17},{... | collective-permute-start | bytes 196616 | tf_op jit(solution)/shard_map/ppermute | solution.py:210
  84.3 1.8 %collective-permute-done.17 = bf16[256,128]{1,0:T(8,128)(2,1)S(1)} collective-permute-done((bf16[256,128]{1,0:T(8,128)(2,1)S(1)}, bf16[256,128]{1,0:T(8,128)(2,1)S(1)}, u32[]{:S(2)}, u32[]{:S(2)}) %collective-permute-start.17) | collective-permute-done | bytes 65568 | tf_op jit(solution)/shard_map/ppermute | solution.py:210
  86.1 3.5 %collective-permute-done.18 = bf16[256,128]{1,0:T(8,128)(2,1)S(1)} collective-permute-done((bf16[256,128]{1,0:T(8,128)(2,1)S(1)}, bf16[256,128]{1,0:T(8,128)(2,1)S(1)}, u32[]{:S(2)}, u32[]{:S(2)}) %collective-permute-start.18) | collective-permute-done | bytes 65568 | tf_op jit(solution)/shard_map/ppermute | solution.py:210
  90.3 1.6 %collective-permute-start.23 = (bf16[32,64,128]{2,1,0:T(8,128)(2,1)S(1)}, bf16[32,64,128]{2,1,0:T(8,128)(2,1)S(1)}, u32[]{:S(2)}, u32[]{:S(2)}) collective-permute-start(bf16[32,64,128]{2,1,0:T(8,128)(2,1)S(1)} %add_convert_fusion), channel_id=1, source_target_pairs={{0,2},{1,3},{2,0},{3,1},{4,6},{5,7},{6,4},{7,5},{8,10},{9,11},{10,... | collective-permute-start | bytes 1572872 | tf_op jit(solution)/shard_map/ppermute | solution.py:210
  91.9 5.9 %collective-permute-done.21.theirs_ref = bf16[4,256,128]{2,1,0:T(8,128)(2,1)S(1)} collective-permute-done((bf16[4,256,128]{2,1,0:T(8,128)(2,1)S(1)}, bf16[4,256,128]{2,1,0:T(8,128)(2,1)S(1)}, u32[]{:S(2)}, u32[]{:S(2)}) %collective-permute-start.21) | collective-permute-done | bytes 262176 | tf_op jit(solution)/shard_map/ppermute | solution.py:210
  97.8 3.8 %adjoint_kernel.3 = (bf16[32,64,128]{2,1,0:T(8,128)(2,1)S(1)}, bf16[32,64,128]{2,1,0:T(8,128)(2,1)S(1)}) custom-call(s32[192]{0:T(256)S(1)} %bitcast.56, s32[192]{0:T(256)S(1)} %bitcast.60, s32[1]{0:T(128)} %bitcast.46.count, s32[2]{0:T(128)S(1)} %pad_add_fusion.place, bf16[192,128,128]{2,1,0:T(8,128)(2,1)S(1)} %hold.3.held, ...), custom_call_target="tpu_custom_call" | custom-call | flops 805306368 | bytes 6291456 | tf_op jit(solution)/shard_map/adjoint_kernel/pallas_call | solution.py:282
  101.6 1.8 %collective-permute-done.23.far_ref = bf16[32,64,128]{2,1,0:T(8,128)(2,1)S(1)} collective-permute-done((bf16[32,64,128]{2,1,0:T(8,128)(2,1)S(1)}, bf16[32,64,128]{2,1,0:T(8,128)(2,1)S(1)}, u32[]{:S(2)}, u32[]{:S(2)}) %collective-permute-start.23) | collective-permute-done | bytes 524320 | tf_op jit(solution)/shard_map/ppermute | solution.py:210
  103.7 3.5 %collective-permute-start.24 = (bf16[8,64,128]{2,1,0:T(8,128)(2,1)S(1)}, bf16[8,64,128]{2,1,0:T(8,128)(2,1)S(1)}, u32[]{:S(2)}, u32[]{:S(2)}) collective-permute-start(bf16[8,64,128]{2,1,0:T(8,128)(2,1)S(1)} %get-tuple-element.36), channel_id=1, source_target_pairs={{0,4},{4,8},{8,12},{12,16},{16,20},{20,24},{24,28},{1,5},{5,9},{9,... | collective-permute-start | bytes 393224 | tf_op jit(solution)/shard_map/ppermute | solution.py:221
  109.7 4.6 %collective-permute-done.25.bottom_ref = bf16[8,64,128]{2,1,0:T(8,128)(2,1)S(1)} collective-permute-done((bf16[8,64,128]{2,1,0:T(8,128)(2,1)S(1)}, bf16[8,64,128]{2,1,0:T(8,128)(2,1)S(1)}, u32[]{:S(2)}, u32[]{:S(2)}) %collective-permute-start.25) | collective-permute-done | bytes 131104 | tf_op jit(solution)/shard_map/ppermute | solution.py:221
  114.3 5.3 %back.1 = f32[1024,256]{1,0:T(8,128)} custom-call(f32[2]{0:T(128)S(1)} %add_convert_fusion.5.inside, bf16[1024,256]{1,0:T(8,128)(2,1)S(1)} %bitcast.51, f32[16,256]{1,0:T(8,128)S(1)} %copy-done.7, bf16[4,80,256]{2,1,0:T(8,128)(2,1)S(1)} %collective-permute-done.above_ref, bf16[4,80,256]{2,1,0:T(8,128)(2,1)S(1)} %collective-permute-done.1.below_ref, ...), custom_call_target="tpu_custom_call" | custom-call | tf_op jit(solution)/shard_map/back/pallas_call | solution.py:362
  (63 shorter events, 19.6 us)
Async XLA Ops:
  2.1 8.3 %collective-permute-start = (bf16[4,80,256]{2,1,0:T(8,128)(2,1)S(1)}, bf16[4,80,256]{2,1,0:T(8,128)(2,1)S(1)}, u32[]{:S(2)}, u32[]{:S(2)}) collective-permute-start(bf16[4,80,256]{2,1,0:T(8,128)(2,1)S(1)} %get-tuple-element.20), channel_id=1, source_target_pairs={{0,4},{4,8},{8,12},{12,16},{16,20},{20,24},{24,28},{1,5},{5,9},{9,... | collective-permute-start | bytes 491528 | tf_op jit(solution)/shard_map/ppermute | solution.py:221
  6.9 7.6 %collective-permute-start.1 = (bf16[4,80,256]{2,1,0:T(8,128)(2,1)S(1)}, bf16[4,80,256]{2,1,0:T(8,128)(2,1)S(1)}, u32[]{:S(2)}, u32[]{:S(2)}) collective-permute-start(bf16[4,80,256]{2,1,0:T(8,128)(2,1)S(1)} %get-tuple-element.21), channel_id=1, source_target_pairs={{4,0},{8,4},{12,8},{16,12},{20,16},{24,20},{28,24},{5,1},{9,5},{13... | collective-permute-start | bytes 491528 | tf_op jit(solution)/shard_map/ppermute | solution.py:221
  17.9 5.6 %collective-permute-start.3 = (bf16[32,64,128]{2,1,0:T(8,128)(2,1)S(1)}, bf16[32,64,128]{2,1,0:T(8,128)(2,1)S(1)}, u32[]{:S(2)}, u32[]{:S(2)}) collective-permute-start(bf16[32,64,128]{2,1,0:T(8,128)(2,1)S(1)} %smooth.1.after_ref.near_ref), channel_id=1, source_target_pairs={{0,1},{1,0},{2,3},{3,2},{4,5},{5,4},{6,7},{7,6},{8,9},{9,8},{10,11... | collective-permute-start | bytes 1572872 | tf_op jit(solution)/shard_map/ppermute | solution.py:210
  18.0 14.3 %collective-permute-start.2 = (bf16[32,64,128]{2,1,0:T(8,128)(2,1)S(1)}, bf16[32,64,128]{2,1,0:T(8,128)(2,1)S(1)}, u32[]{:S(2)}, u32[]{:S(2)}) collective-permute-start(bf16[32,64,128]{2,1,0:T(8,128)(2,1)S(1)} %smooth.1.after_ref.near_ref), channel_id=1, source_target_pairs={{0,2},{1,3},{2,0},{3,1},{4,6},{5,7},{6,4},{7,5},{8,10},{9,11},{10,... | collective-permute-start | bytes 1572872 | tf_op jit(solution)/shard_map/ppermute | solution.py:210
  20.3 2.8 %copy-start.2 = (bf16[1,1,192,128,128]{4,3,2,1,0:T(8,128)(2,1)S(1)}, bf16[1,1,192,128,128]{4,3,2,1,0:T(8,128)(2,1)}, u32[]{:S(2)}) copy-start(bf16[1,1,192,128,128]{4,3,2,1,0:T(8,128)(2,1)} %param.9) | copy-start | bytes 18874372
  30.6 29.2 %copy-start.10 = (f32[2048]{0:T(1024)S(1)}, f32[2048]{0:T(1024)}, u32[]{:S(2)}) copy-start(f32[2048]{0:T(1024)} %param.13) | copy-start | bytes 24580
  32.3 2.4 %collective-permute-start.4 = (bf16[32,64,128]{2,1,0:T(8,128)(2,1)S(1)}, bf16[32,64,128]{2,1,0:T(8,128)(2,1)S(1)}, u32[]{:S(2)}, u32[]{:S(2)}) collective-permute-start(bf16[32,64,128]{2,1,0:T(8,128)(2,1)S(1)} %collective-permute-done.2.near_ref), channel_id=1, source_target_pairs={{0,1},{1,0},{2,3},{3,2},{4,5},{5,4},{6,7},{7,6},{8,9},{9,8},{10,11... | collective-permute-start | bytes 1572872 | tf_op jit(solution)/shard_map/ppermute | solution.py:210
  32.3 11.2 %collective-permute-start.9 = (bf16[8,128,128]{2,1,0:T(8,128)(2,1)S(1)}, bf16[8,128,128]{2,1,0:T(8,128)(2,1)S(1)}, u32[]{:S(2)}, u32[]{:S(2)}) collective-permute-start(bf16[8,128,128]{2,1,0:T(8,128)(2,1)S(1)} %get-tuple-element.27), channel_id=1, source_target_pairs={{0,4},{4,0},{8,12},{12,8},{16,20},{20,16},{24,28},{28,24},{1,5},{5... | collective-permute-start | bytes 786440 | tf_op jit(solution)/shard_map/ppermute | solution.py:210
  34.8 2.8 %copy-start.1 = (bf16[192,128,128]{2,1,0:T(8,128)(2,1)S(1)}, bf16[192,128,128]{2,1,0:T(8,128)(2,1)}, u32[]{:S(2)}) copy-start(bf16[192,128,128]{2,1,0:T(8,128)(2,1)} %copy-done) | copy-start | bytes 18874372
  41.6 8.6 %collective-permute-start.5 = (bf16[8,128,128]{2,1,0:T(8,128)(2,1)S(1)}, bf16[8,128,128]{2,1,0:T(8,128)(2,1)S(1)}, u32[]{:S(2)}, u32[]{:S(2)}) collective-permute-start(bf16[8,128,128]{2,1,0:T(8,128)(2,1)S(1)} %get-tuple-element.25), channel_id=1, source_target_pairs={{0,4},{4,0},{8,12},{12,8},{16,20},{20,16},{24,28},{28,24},{1,5},{5... | collective-permute-start | bytes 786440 | tf_op jit(solution)/shard_map/ppermute | solution.py:210
  43.7 11.2 %collective-permute-start.10 = (bf16[256,128]{1,0:T(8,128)(2,1)S(1)}, bf16[256,128]{1,0:T(8,128)(2,1)S(1)}, u32[]{:S(2)}, u32[]{:S(2)}) collective-permute-start(bf16[256,128]{1,0:T(8,128)(2,1)S(1)} %get-tuple-element.39), channel_id=1, source_target_pairs={{0,16},{4,20},{8,24},{12,28},{16,0},{20,4},{24,8},{28,12},{1,17},{... | collective-permute-start | bytes 196616 | tf_op jit(solution)/shard_map/ppermute | solution.py:210
  46.3 8.8 %collective-permute-start.11 = (bf16[256,128]{1,0:T(8,128)(2,1)S(1)}, bf16[256,128]{1,0:T(8,128)(2,1)S(1)}, u32[]{:S(2)}, u32[]{:S(2)}) collective-permute-start(bf16[256,128]{1,0:T(8,128)(2,1)S(1)} %get-tuple-element.41), channel_id=1, source_target_pairs={{0,24},{4,28},{8,16},{12,20},{16,8},{20,12},{24,0},{28,4},{1,25},{... | collective-permute-start | bytes 196616 | tf_op jit(solution)/shard_map/ppermute | solution.py:210
  47.6 7.4 %collective-permute-start.12 = (bf16[256,128]{1,0:T(8,128)(2,1)S(1)}, bf16[256,128]{1,0:T(8,128)(2,1)S(1)}, u32[]{:S(2)}, u32[]{:S(2)}) collective-permute-start(bf16[256,128]{1,0:T(8,128)(2,1)S(1)} %get-tuple-element.40), channel_id=1, source_target_pairs={{0,8},{4,12},{8,0},{12,4},{16,24},{20,28},{24,16},{28,20},{1,9},{5... | collective-permute-start | bytes 196616 | tf_op jit(solution)/shard_map/ppermute | solution.py:210
  50.2 5.9 %collective-permute-start.6 = (bf16[256,128]{1,0:T(8,128)(2,1)S(1)}, bf16[256,128]{1,0:T(8,128)(2,1)S(1)}, u32[]{:S(2)}, u32[]{:S(2)}) collective-permute-start(bf16[256,128]{1,0:T(8,128)(2,1)S(1)} %get-tuple-element.42), channel_id=1, source_target_pairs={{0,16},{4,20},{8,24},{12,28},{16,0},{20,4},{24,8},{28,12},{1,17},{... | collective-permute-start | bytes 196616 | tf_op jit(solution)/shard_map/ppermute | solution.py:210
  53.5 6.2 %collective-permute-start.7 = (bf16[256,128]{1,0:T(8,128)(2,1)S(1)}, bf16[256,128]{1,0:T(8,128)(2,1)S(1)}, u32[]{:S(2)}, u32[]{:S(2)}) collective-permute-start(bf16[256,128]{1,0:T(8,128)(2,1)S(1)} %get-tuple-element.44), channel_id=1, source_target_pairs={{0,24},{4,28},{8,16},{12,20},{16,8},{20,12},{24,0},{28,4},{1,25},{... | collective-permute-start | bytes 196616 | tf_op jit(solution)/shard_map/ppermute | solution.py:210
  54.9 5.0 %collective-permute-start.8 = (bf16[256,128]{1,0:T(8,128)(2,1)S(1)}, bf16[256,128]{1,0:T(8,128)(2,1)S(1)}, u32[]{:S(2)}, u32[]{:S(2)}) collective-permute-start(bf16[256,128]{1,0:T(8,128)(2,1)S(1)} %get-tuple-element.43), channel_id=1, source_target_pairs={{0,8},{4,12},{8,0},{12,4},{16,24},{20,28},{24,16},{28,20},{1,9},{5... | collective-permute-start | bytes 196616 | tf_op jit(solution)/shard_map/ppermute | solution.py:210
  60.0 4.5 %collective-permute-start.13 = (bf16[256,128]{1,0:T(8,128)(2,1)S(1)}, bf16[256,128]{1,0:T(8,128)(2,1)S(1)}, u32[]{:S(2)}, u32[]{:S(2)}) collective-permute-start(bf16[256,128]{1,0:T(8,128)(2,1)S(1)} %get-tuple-element.38.after_ref), channel_id=1, source_target_pairs={{0,8},{4,12},{8,0},{12,4},{16,24},{20,28},{24,16},{28,20},{1,9},{5... | collective-permute-start | bytes 196616 | tf_op jit(solution)/shard_map/ppermute | solution.py:210
  60.5 7.4 %collective-permute-start.14 = (bf16[256,128]{1,0:T(8,128)(2,1)S(1)}, bf16[256,128]{1,0:T(8,128)(2,1)S(1)}, u32[]{:S(2)}, u32[]{:S(2)}) collective-permute-start(bf16[256,128]{1,0:T(8,128)(2,1)S(1)} %get-tuple-element.38.after_ref), channel_id=1, source_target_pairs={{0,16},{4,20},{8,24},{12,28},{16,0},{20,4},{24,8},{28,12},{1,17},{... | collective-permute-start | bytes 196616 | tf_op jit(solution)/shard_map/ppermute | solution.py:210
  63.0 6.2 %collective-permute-start.15 = (bf16[256,128]{1,0:T(8,128)(2,1)S(1)}, bf16[256,128]{1,0:T(8,128)(2,1)S(1)}, u32[]{:S(2)}, u32[]{:S(2)}) collective-permute-start(bf16[256,128]{1,0:T(8,128)(2,1)S(1)} %get-tuple-element.38.after_ref), channel_id=1, source_target_pairs={{0,24},{4,28},{8,16},{12,20},{16,8},{20,12},{24,0},{28,4},{1,25},{... | collective-permute-start | bytes 196616 | tf_op jit(solution)/shard_map/ppermute | solution.py:210
  69.2 6.4 %collective-permute-start.19 = (bf16[4,256,128]{2,1,0:T(8,128)(2,1)S(1)}, bf16[4,256,128]{2,1,0:T(8,128)(2,1)S(1)}, u32[]{:S(2)}, u32[]{:S(2)}) collective-permute-start(bf16[4,256,128]{2,1,0:T(8,128)(2,1)S(1)} %pad_maximum_fusion.mine_ref), channel_id=1, source_target_pairs={{0,4},{4,0},{8,12},{12,8},{16,20},{20,16},{24,28},{28,24},{1,5},{5... | collective-permute-start | bytes 786440 | tf_op jit(solution)/shard_map/ppermute | solution.py:210
  70.2 2.8 %copy-start.3 = (bf16[1,1,192,128,128]{4,3,2,1,0:T(8,128)(2,1)S(1)}, bf16[1,1,192,128,128]{4,3,2,1,0:T(8,128)(2,1)}, u32[]{:S(2)}) copy-start(bf16[1,1,192,128,128]{4,3,2,1,0:T(8,128)(2,1)} %param.9) | copy-start | bytes 18874372
  79.4 34.9 %copy-start.5 = (bf16[64,16,256]{2,1,0:T(8,128)(2,1)S(1)}, bf16[64,16,256]{2,1,0:T(8,128)(2,1)}, u32[]{:S(2)}) copy-start(bf16[64,16,256]{2,1,0:T(8,128)(2,1)} %param.7) | copy-start | bytes 1572868
  79.4 34.9 %copy-start.7 = (f32[16,256]{1,0:T(8,128)S(1)}, f32[16,256]{1,0:T(8,128)}, u32[]{:S(2)}) copy-start(f32[16,256]{1,0:T(8,128)} %kappa_ref.5) | copy-start | bytes 49156
  79.4 10.3 %collective-permute-start.20 = (bf16[32,64,128]{2,1,0:T(8,128)(2,1)S(1)}, bf16[32,64,128]{2,1,0:T(8,128)(2,1)S(1)}, u32[]{:S(2)}, u32[]{:S(2)}) collective-permute-start(bf16[32,64,128]{2,1,0:T(8,128)(2,1)S(1)} %get-tuple-element.30), channel_id=1, source_target_pairs={{0,1},{1,0},{2,3},{3,2},{4,5},{5,4},{6,7},{7,6},{8,9},{9,8},{10,11... | collective-permute-start | bytes 1572872 | tf_op jit(solution)/shard_map/ppermute | solution.py:210
  79.5 4.8 %collective-permute-start.16 = (bf16[256,128]{1,0:T(8,128)(2,1)S(1)}, bf16[256,128]{1,0:T(8,128)(2,1)S(1)}, u32[]{:S(2)}, u32[]{:S(2)}) collective-permute-start(bf16[256,128]{1,0:T(8,128)(2,1)S(1)} %get-tuple-element.28), channel_id=1, source_target_pairs={{0,8},{4,12},{8,0},{12,4},{16,24},{20,28},{24,16},{28,20},{1,9},{5... | collective-permute-start | bytes 196616 | tf_op jit(solution)/shard_map/ppermute | solution.py:210
  81.0 5.2 %collective-permute-start.17 = (bf16[256,128]{1,0:T(8,128)(2,1)S(1)}, bf16[256,128]{1,0:T(8,128)(2,1)S(1)}, u32[]{:S(2)}, u32[]{:S(2)}) collective-permute-start(bf16[256,128]{1,0:T(8,128)(2,1)S(1)} %get-tuple-element.28), channel_id=1, source_target_pairs={{0,16},{4,20},{8,24},{12,28},{16,0},{20,4},{24,8},{28,12},{1,17},{... | collective-permute-start | bytes 196616 | tf_op jit(solution)/shard_map/ppermute | solution.py:210
  82.9 6.7 %collective-permute-start.18 = (bf16[256,128]{1,0:T(8,128)(2,1)S(1)}, bf16[256,128]{1,0:T(8,128)(2,1)S(1)}, u32[]{:S(2)}, u32[]{:S(2)}) collective-permute-start(bf16[256,128]{1,0:T(8,128)(2,1)S(1)} %get-tuple-element.28), channel_id=1, source_target_pairs={{0,24},{4,28},{8,16},{12,20},{16,8},{20,12},{24,0},{28,4},{1,25},{... | collective-permute-start | bytes 196616 | tf_op jit(solution)/shard_map/ppermute | solution.py:210
  89.9 7.9 %collective-permute-start.21 = (bf16[4,256,128]{2,1,0:T(8,128)(2,1)S(1)}, bf16[4,256,128]{2,1,0:T(8,128)(2,1)S(1)}, u32[]{:S(2)}, u32[]{:S(2)}) collective-permute-start(bf16[4,256,128]{2,1,0:T(8,128)(2,1)S(1)} %pad_maximum_fusion.1.mine_ref), channel_id=1, source_target_pairs={{0,4},{4,0},{8,12},{12,8},{16,20},{20,16},{24,28},{28,24},{1,5},{5... | collective-permute-start | bytes 786440 | tf_op jit(solution)/shard_map/ppermute | solution.py:210
  90.3 13.2 %collective-permute-start.23 = (bf16[32,64,128]{2,1,0:T(8,128)(2,1)S(1)}, bf16[32,64,128]{2,1,0:T(8,128)(2,1)S(1)}, u32[]{:S(2)}, u32[]{:S(2)}) collective-permute-start(bf16[32,64,128]{2,1,0:T(8,128)(2,1)S(1)} %add_convert_fusion), channel_id=1, source_target_pairs={{0,2},{1,3},{2,0},{3,1},{4,6},{5,7},{6,4},{7,5},{8,10},{9,11},{10,... | collective-permute-start | bytes 1572872 | tf_op jit(solution)/shard_map/ppermute | solution.py:210
  101.6 2.0 %collective-permute-start.22 = (bf16[32,64,128]{2,1,0:T(8,128)(2,1)S(1)}, bf16[32,64,128]{2,1,0:T(8,128)(2,1)S(1)}, u32[]{:S(2)}, u32[]{:S(2)}) collective-permute-start(bf16[32,64,128]{2,1,0:T(8,128)(2,1)S(1)} %get-tuple-element.33), channel_id=1, source_target_pairs={{0,1},{1,0},{2,3},{3,2},{4,5},{5,4},{6,7},{7,6},{8,9},{9,8},{10,11... | collective-permute-start | bytes 1572872 | tf_op jit(solution)/shard_map/ppermute | solution.py:210
  103.7 6.0 %collective-permute-start.24 = (bf16[8,64,128]{2,1,0:T(8,128)(2,1)S(1)}, bf16[8,64,128]{2,1,0:T(8,128)(2,1)S(1)}, u32[]{:S(2)}, u32[]{:S(2)}) collective-permute-start(bf16[8,64,128]{2,1,0:T(8,128)(2,1)S(1)} %get-tuple-element.36), channel_id=1, source_target_pairs={{0,4},{4,8},{8,12},{12,16},{16,20},{20,24},{24,28},{1,5},{5,9},{9,... | collective-permute-start | bytes 393224 | tf_op jit(solution)/shard_map/ppermute | solution.py:221
  107.2 7.1 %collective-permute-start.25 = (bf16[8,64,128]{2,1,0:T(8,128)(2,1)S(1)}, bf16[8,64,128]{2,1,0:T(8,128)(2,1)S(1)}, u32[]{:S(2)}, u32[]{:S(2)}) collective-permute-start(bf16[8,64,128]{2,1,0:T(8,128)(2,1)S(1)} %get-tuple-element.35), channel_id=1, source_target_pairs={{4,0},{8,4},{12,8},{16,12},{20,16},{24,20},{28,24},{5,1},{9,5},{13... | collective-permute-start | bytes 393224 | tf_op jit(solution)/shard_map/ppermute | solution.py:221
  (5 other events, 5.8 us)

commit v3 on v2

--- a/solution.py
+++ b/solution.py
@@ -60,43 +60,82 @@
     )
 
 
-def smooth_kernel(probes_ref, kappa_ref, above_ref, below_ref, field_ref, wide, coef, halos, result):
-    rows, lon = kappa_ref.shape
-    probe_local = probes_ref.shape[0] // rows
-    total = rows + 2 * SMOOTH
-    widen(probes_ref, wide)
-    halos[0] = above_ref[:, :probe_local, :].astype(F32)
-    halos[1] = below_ref[:, :probe_local, :].astype(F32)
+def put_row(ref, blk, at, row):
+    for h in range(row.shape[1] // BLK):
+        ref[blk + h, at, :] = row[:, h * BLK : (h + 1) * BLK]
+
+
+def smooth_step(f, coef, lon, r):
+    k, kl, kr = coef[0, r], coef[1, r], coef[2, r]
+    g = f[r]
+    return g + k * (f[r - 1] + f[r + 1] - 4.0 * g) + kl * pltpu.roll(g, 1, 1) + kr * pltpu.roll(g, lon - 1, 1)
+
+
+def smooth_coefficients(coef, kappas, lon):
     lane = lax.broadcasted_iota(jnp.int32, (SUB, lon), 1)
-    for r, k in enumerate(kappa_rows(kappa_ref, above_ref, below_ref, probe_local)):
+    for r, k in enumerate(kappas):
         k = jnp.broadcast_to(k, (SUB, lon))
         coef[0, r] = k
         coef[1, r] = jnp.where(lane > 0, k, 0.0)
         coef[2, r] = jnp.where(lane < lon - 1, k, 0.0)
 
+
+def keep_state(state_ref, step, f, at):
+    rows = len(f)
+    for i in range(2):
+        state_ref[0, step, i, at, :] = f[step + i]
+        state_ref[1, step, i, at, :] = f[rows - 2 - step + i]
+
+
+def smooth_inner_kernel(probes_ref, kappa_ref, field_ref, state_ref, wide, coef, result):
+    rows, lon = kappa_ref.shape
+    probe_local = probes_ref.shape[0] // rows
+    halves = lon // BLK
+    widen(probes_ref, wide)
+    smooth_coefficients(coef, [kappa_ref[r : r + 1, :] for r in range(rows)], lon)
+
     @pl.loop(0, probe_local // SUB)
     def _(c):
         base = pl.multiple_of(c * SUB, SUB)
-        f = (
-            [halos[0, r, pl.ds(base, SUB), :] for r in range(SMOOTH)]
-            + [one_row(wide, base * rows + r, SUB, rows) for r in range(rows)]
-            + [halos[1, r, pl.ds(base, SUB), :] for r in range(SMOOTH)]
-        )
+        at = pl.ds(base, SUB)
+        f = [one_row(wide, base * rows + r, SUB, rows) for r in range(rows)]
         for step in range(SMOOTH):
-            new = list(f)
-            for r in range(step + 1, total - step - 1):
-                k, kl, kr = coef[0, r], coef[1, r], coef[2, r]
-                g = f[r]
-                new[r] = (
-                    g
-                    + k * (f[r - 1] + f[r + 1] - 4.0 * g)
-                    + kl * pltpu.roll(g, 1, 1)
-                    + kr * pltpu.roll(g, lon - 1, 1)
-                )
-            f = new
-        for r in range(rows):
-            for h in range(lon // BLK):
-                result[r * (lon // BLK) + h, pl.ds(base, SUB), :] = f[r + SMOOTH][:, h * BLK : (h + 1) * BLK]
+            keep_state(state_ref, step, f, at)
+            f = [smooth_step(f, coef, lon, r) if step < r < rows - 1 - step else f[r] for r in range(rows)]
+        for r in range(SMOOTH, rows - SMOOTH):
+            put_row(result, (r - SMOOTH) * halves, at, f[r])
+
+    field_ref[...] = result[...].astype(BF16)
+
+
+def side_rows(state_ref, side, step, mine, at):
+    inner = [state_ref[side, step, i, at, :] for i in range(2)]
+    return mine + inner if side == 0 else inner + mine
+
+
+def smooth_outer_kernel(kappa_ref, above_ref, below_ref, state_ref, field_ref, coef, halos, result):
+    rows, lon = kappa_ref.shape
+    probe_local = state_ref.shape[3]
+    halves = lon // BLK
+    halos[0] = above_ref[:, :probe_local, :].astype(F32)
+    halos[1] = below_ref[:, :probe_local, :].astype(F32)
+    smooth_coefficients(coef, kappa_rows(kappa_ref, above_ref, below_ref, probe_local), lon)
+    total = rows + 2 * SMOOTH
+
+    @pl.loop(0, probe_local // SUB)
+    def _(c):
+        base = pl.multiple_of(c * SUB, SUB)
+        at = pl.ds(base, SUB)
+        for side in range(2):
+            mine = [halos[side, r, at, :] for r in range(SMOOTH)]
+            for step in range(SMOOTH):
+                f = side_rows(state_ref, side, step, mine, at)
+                first = step if side == 0 else total - 6 - step
+                rows_at = dict(enumerate(f, first))
+                new = range(first + 1, first + 5)
+                mine = [smooth_step(rows_at, coef, lon, r) for r in new]
+            for r in range(SMOOTH):
+                put_row(result, (side * SMOOTH + r) * halves, at, mine[r])
 
     field_ref[...] = result[...].astype(BF16)
 
@@ -115,11 +154,17 @@
 
 
 def forward_kernel(
-    sources, receptors, count, place, held, near_ref, far_ref, keep_ref, give_ref, turned, total
+    sources, receptors, count, place, held, near_in, near_out, far_in, far_out, keep_ref, give_ref, turned, total
 ):
     total[...] = jnp.zeros_like(total)
+    edge = near_out.shape[0] // 2
     for j in range(turned.shape[0]):
-        turned[j] = jnp.concatenate([near_ref[j], far_ref[j]], axis=0).T
+        if edge <= j < turned.shape[0] - edge:
+            near, far = near_in[j - edge], far_in[j - edge]
+        else:
+            at = j if j < edge else j - near_in.shape[0]
+            near, far = near_out[at], far_out[at]
+        turned[j] = jnp.concatenate([near, far], axis=0).T
 
     spare = total.shape[0] - 1
 
@@ -135,7 +180,7 @@
 
 
 def adjoint_kernel(
-    sources, receptors, count, place, held, mine_ref, theirs_ref, near_ref, far_ref, weighted, total
+    sources, receptors, count, place, held, mine_ref, theirs_ref, near_in, near_out, far_in, far_out, weighted, total
 ):
     total[...] = jnp.zeros_like(total)
     pieces, share = mine_ref.shape[:2]
@@ -153,53 +198,88 @@
         total[j] += jnp.dot(entries, held[n], preferred_element_type=F32)
 
     each_slot(held.shape[0], slot)
-    half = near_ref.shape[1]
-    near_ref[...] = total[:spare, :half].astype(BF16)
-    far_ref[...] = total[:spare, half:].astype(BF16)
-
-
-def back_kernel(
-    inside, probes_ref, kappa_ref, above_ref, below_ref, own_ref, core_ref, far_ref, top_ref, bottom_ref, out_ref, wide, coef, terms, halos
+    half = near_in.shape[1]
+    edge = near_out.shape[0] // 2
+    for at, in_ref, out_ref in ((pl.ds(0, half), near_in, near_out), (pl.ds(half, half), far_in, far_out)):
+        out_ref[:edge] = total[:edge, at].astype(BF16)
+        in_ref[...] = total[edge : spare - edge, at].astype(BF16)
+        out_ref[edge:] = total[spare - edge : spare, at].astype(BF16)
+
+
+def joined(ref, first, at, halves):
+    return jnp.concatenate([ref[first + h, at, :] for h in range(halves)], axis=1)
+
+
+def back_step(f, g, lane, r):
+    lon = lane.shape[1]
+    west = jnp.where(lane > 0, pltpu.roll(g[r], 1, 1), 0.0)
+    east = jnp.where(lane < lon - 1, pltpu.roll(g[r], lon - 1, 1), 0.0)
+    return g[r - 1] + g[r + 1] + west + east - 4.0 * g[r]
+
+
+def back_inner_kernel(
+    probes_ref, kappa_ref, own_in, core_in, far_in, own_out, core_out, far_out, wide, state_ref, coef, terms
 ):
     rows, lon = kappa_ref.shape
     probe_local = probes_ref.shape[0] // rows
+    halves = lon // BLK
+    edge = own_out.shape[0] // 2
+    widen(probes_ref, wide)
+    inner = own_in[...].astype(F32) + core_in[...].astype(F32) + far_in[...].astype(F32)
+    outer = own_out[...].astype(F32) + core_out[...].astype(F32) + far_out[...].astype(F32)
+    terms[:edge] = outer[:edge]
+    terms[edge : terms.shape[0] - edge] = inner
+    terms[terms.shape[0] - edge :] = outer[edge:]
+    lane = lax.broadcasted_iota(jnp.int32, (SUB, lon), 1)
+    for r in range(rows):
+        coef[r] = jnp.broadcast_to(kappa_ref[r : r + 1, :], (SUB, lon))
+
+    @pl.loop(0, probe_local // SUB)
+    def _(c):
+        base = pl.multiple_of(c * SUB, SUB)
+        at = pl.ds(base, SUB)
+        f = [joined(terms, r * halves, at, halves) for r in range(rows)]
+        for step in range(SMOOTH):
+            keep_state(state_ref, step, f, at)
+            g = {r: coef[r] * f[r] for r in range(step, rows - step)}
+            f = [f[r] + back_step(f, g, lane, r) if step < r < rows - 1 - step else f[r] for r in range(rows)]
+        for r in range(SMOOTH, rows - SMOOTH):
+            for h in range(halves):
+                wide[h, pl.ds(base * rows + r, SUB, stride=rows), :] += f[r][:, h * BLK : (h + 1) * BLK]
+
+
+def back_outer_kernel(
+    inside, kappa_ref, above_ref, below_ref, top_ref, bottom_ref, state_ref, done_ref, out_ref, wide, coef, halos
+):
+    rows, lon = kappa_ref.shape
+    probe_local = state_ref.shape[3]
+    halves = lon // BLK
     total = rows + 2 * SMOOTH
-    halves = lon // BLK
-    widen(probes_ref, wide)
-    terms[...] = own_ref[...].astype(F32) + core_ref[...].astype(F32) + far_ref[...].astype(F32)
+    wide[...] = done_ref[...]
     halos[0] = top_ref[...].astype(F32)
     halos[1] = bottom_ref[...].astype(F32)
     lane = lax.broadcasted_iota(jnp.int32, (SUB, lon), 1)
     for r, k in enumerate(kappa_rows(kappa_ref, above_ref, below_ref, probe_local)):
         coef[r] = jnp.broadcast_to(k, (SUB, lon))
-    in_grid = [inside[0]] * SMOOTH + [None] * rows + [inside[1]] * SMOOTH
-
-    def joined(ref, first, base):
-        return jnp.concatenate([ref[first + h, pl.ds(base, SUB), :] for h in range(halves)], axis=1)
 
     @pl.loop(0, probe_local // SUB)
     def _(c):
         base = pl.multiple_of(c * SUB, SUB)
-        f = (
-            [joined(halos.at[0], r * halves, base) for r in range(SMOOTH)]
-            + [joined(terms, r * halves, base) for r in range(rows)]
-            + [joined(halos.at[1], r * halves, base) for r in range(SMOOTH)]
-        )
-        for step in range(SMOOTH):
-            g = [coef[r] * f[r] for r in range(total)]
-            new = list(f)
-            for r in range(step + 1, total - step - 1):
-                west = jnp.where(lane > 0, pltpu.roll(g[r], 1, 1), 0.0)
-                east = jnp.where(lane < lon - 1, pltpu.roll(g[r], lon - 1, 1), 0.0)
-                lap = g[r - 1] + g[r + 1] + west + east - 4.0 * g[r]
-                if in_grid[r] is not None:
-                    lap = lap * in_grid[r]
-                new[r] = f[r] + lap
-            f = new
-        for r in range(rows):
-            at = pl.ds(base * rows + r, SUB, stride=rows)
-            for h in range(halves):
-                wide[h, at, :] += f[r + SMOOTH][:, h * BLK : (h + 1) * BLK]
+        at = pl.ds(base, SUB)
+        for side in range(2):
+            mine = [joined(halos.at[side], r * halves, at, halves) for r in range(SMOOTH)]
+            for step in range(SMOOTH):
+                first = step if side == 0 else total - 6 - step
+                f = dict(enumerate(side_rows(state_ref, side, step, mine, at), first))
+                g = {r: coef[r] * f[r] for r in f}
+                mine = []
+                for r in range(first + 1, first + 5):
+                    lap = back_step(f, g, lane, r)
+                    mine.append(f[r] + (lap if SMOOTH <= r < total - SMOOTH else lap * inside[side]))
+            for r in range(SMOOTH):
+                row = r if side == 0 else rows - SMOOTH + r
+                for h in range(halves):
+                    wide[h, pl.ds(base * rows + row, SUB, stride=rows), :] += mine[r][:, h * BLK : (h + 1) * BLK]
 
     for h in range(halves):
         out_ref[:, h * BLK : (h + 1) * BLK] = wide[h]
@@ -256,21 +336,38 @@
             name="hold",
         )(blocks, after)
 
-    part = jax.ShapeDtypeStruct((cells, probe_local, BLK), BF16)
-    own = pl.pallas_call(
-        smooth_kernel,
-        out_shape=part,
+    edge_cells = SMOOTH * halves
+    inner_part = jax.ShapeDtypeStruct((cells - 2 * edge_cells, probe_local, BLK), BF16)
+    outer_part = jax.ShapeDtypeStruct((2 * edge_cells, probe_local, BLK), BF16)
+    state = jax.ShapeDtypeStruct((2, SMOOTH, 2, probe_local, lon), F32)
+    by_half = (halves, probe_local * rows, BLK)
+    halo_rows = rows + 2 * SMOOTH
+    own_in, smooth_state = pl.pallas_call(
+        smooth_inner_kernel,
+        out_shape=(inner_part, state),
+        in_specs=[VMEM] * 2,
+        out_specs=(VMEM, VMEM),
+        scratch_shapes=[
+            pltpu.VMEM(by_half, F32),
+            pltpu.VMEM((3, rows, SUB, lon), F32),
+            pltpu.VMEM(inner_part.shape, F32),
+        ],
+        compiler_params=params(),
+        name="smooth_inner",
+    )(flat, kappa)
+    own_out = pl.pallas_call(
+        smooth_outer_kernel,
+        out_shape=outer_part,
         in_specs=[VMEM] * 4,
         out_specs=VMEM,
         scratch_shapes=[
-            pltpu.VMEM((halves, probe_local * rows, BLK), F32),
-            pltpu.VMEM((3, rows + 2 * SMOOTH, SUB, lon), F32),
+            pltpu.VMEM((3, halo_rows, SUB, lon), F32),
             pltpu.VMEM((2, SMOOTH, probe_local, lon), F32),
-            pltpu.VMEM((cells, probe_local, BLK), F32),
+            pltpu.VMEM(outer_part.shape, F32),
         ],
         compiler_params=params(),
-        name="smooth",
-    )(flat, kappa, above, below)
+        name="smooth_outer",
+    )(kappa, above, below, smooth_state)
 
     side, row = me % 2, me // 2
     place = jnp.stack([side, row]).astype(jnp.int32)
@@ -292,12 +389,12 @@
             name=kernel.__name__,
         )(*scalars, held, *operands)
 
-    def forward(held, near, far):
+    def forward(held, *fields):
         half = jax.ShapeDtypeStruct((RB_LOC // 2, pair, BLK), BF16)
         return over_slots(
             forward_kernel,
             held,
-            (near, far),
+            fields,
             (half, half),
             [pltpu.VMEM((cells, BLK, pair), BF16), pltpu.VMEM((RB_LOC + 1, BLK, pair), F32)],
         )
@@ -307,7 +404,7 @@
             adjoint_kernel,
             held,
             (mine, theirs),
-            (part, part),
+            (inner_part, outer_part) * 2,
             [pltpu.VMEM((RB_LOC * pair, BLK), BF16), pltpu.VMEM((cells + 1, pair, BLK), F32)],
         )
 
@@ -332,47 +429,50 @@
         mine = gathered(weighted)
         return mine, swap(mine, "src", 1)
 
-    other = swap(own, "rcv", 2)
-    beside = swap(own, "rcv", 1)
-    held = hold(own)
-    near_keep, near_give = forward(held, own, beside)
-    other, near_give = lax.optimization_barrier((other, near_give))
+    own = (own_in, own_out)
+    other = [swap(x, "rcv", 2) for x in own]
+    beside = [swap(x, "rcv", 1) for x in own]
+    held = hold(own_out)
+    near_keep, near_give = forward(held, *own, *beside)
+    other[1], near_give = lax.optimization_barrier((other[1], near_give))
     first = summed(near_keep, near_give)
-    second = summed(*forward(held, other, swap(other, "rcv", 1)))
+    second = summed(*forward(held, *other, *[swap(x, "rcv", 1) for x in other]))
 
     held = hold(second)
     second_halves = spread(second)
-    first, _ = lax.optimization_barrier((first, second_halves[0]))
-    first_mine = gathered(first)
-    to_other, to_diagonal = adjoint(held, *second_halves)
-    both = (to_other.astype(F32) + swap(to_diagonal, "rcv", 1).astype(F32)).astype(BF16)
-    first_mine, both = lax.optimization_barrier((first_mine, both))
-    from_other = swap(both, "rcv", 2)
-    mine, to_beside = adjoint(held, first_mine, swap(first_mine, "src", 1))
-    from_beside = swap(to_beside, "rcv", 1)
-
-    edge_cells = SMOOTH * halves
-
-    def edge_sum(lo):
-        pieces = [lax.slice_in_dim(x, lo, lo + edge_cells, axis=0).astype(F32) for x in (mine, from_beside, from_other)]
-        return (pieces[0] + pieces[1] + pieces[2]).astype(BF16)
-
-    top, bottom = exchange_edges(edge_sum(0), edge_sum(cells - edge_cells))
+    first_halves = spread(first)
+    mine_in, mine_out, *to_beside = adjoint(held, *first_halves)
+    beside_in, beside_out = [swap(x, "rcv", 1) for x in to_beside]
+    other_in, other_out, diagonal_in, diagonal_out = adjoint(held, *second_halves)
+    both = lambda here, there: (here.astype(F32) + swap(there, "rcv", 1).astype(F32)).astype(BF16)
+    far_out = swap(both(other_out, diagonal_out), "rcv", 2)
+    far_in = swap(both(other_in, diagonal_in), "rcv", 2)
+
+    edges = (mine_out.astype(F32) + beside_out.astype(F32) + far_out.astype(F32)).astype(BF16)
+    top, bottom = exchange_edges(edges[:edge_cells], edges[edge_cells:])
     inside = jnp.stack([me > 0, me < tiles - 1]).astype(F32)
+    inner, back_state = pl.pallas_call(
+        back_inner_kernel,
+        out_shape=(jax.ShapeDtypeStruct(by_half, F32), state),
+        in_specs=[VMEM] * 8,
+        out_specs=(VMEM, VMEM),
+        scratch_shapes=[pltpu.VMEM((rows, SUB, lon), F32), pltpu.VMEM((cells, probe_local, BLK), F32)],
+        compiler_params=params(),
+        name="back_inner",
+    )(flat, kappa, mine_in, beside_in, far_in, mine_out, beside_out, far_out)
     out = pl.pallas_call(
-        back_kernel,
+        back_outer_kernel,
         out_shape=jax.ShapeDtypeStruct((probe_local * rows, lon), F32),
-        in_specs=[SMEM] + [VMEM] * 9,
+        in_specs=[SMEM] + [VMEM] * 7,
         out_specs=VMEM,
         scratch_shapes=[
-            pltpu.VMEM((halves, probe_local * rows, BLK), F32),
-            pltpu.VMEM((rows + 2 * SMOOTH, SUB, lon), F32),
-            pltpu.VMEM((cells, probe_local, BLK), F32),
+            pltpu.VMEM(by_half, F32),
+            pltpu.VMEM((halo_rows, SUB, lon), F32),
             pltpu.VMEM((2, edge_cells, probe_local, BLK), F32),
         ],
         compiler_params=params(),
-        name="back",
-    )(inside, flat, kappa, above, below, mine, from_beside, from_other, top, bottom)
+        name="back_outer",
+    )(inside, kappa, above, below, top, bottom, back_state, inner)
     return out.reshape(probe_local, rows, lon)
 
 

time: 120 us -> 112 us (0.933)
  waiting for transfers between devices: 41 us -> 26.5 us
  Pallas kernels: 25.6 us -> 30.3 us
  starting transfers between devices: 38.3 us -> 39.9 us
    ppermute x4, waiting for transfers between devices: 12 us -> 2.06 us  [exchange_edges(): return (lax.ppermute(south, 'src', down), lax.ppermute(north, 'src', up))]
    pallas_call x2 -> x4, Pallas kernels: 8.79 us -> 13.5 us  [the longest x1 4.27 us: per_device(): pl.pallas_call(back_outer_kernel, out_shape=jax.ShapeDtypeStruct((probe_l...]
    ppermute x22 -> x28, waiting for transfers between devices: 29 us -> 24.4 us  [swap(): return lax.ppermute(x, axis, [(i, i ^ distance) for i in range(size)])]
    ppermute x22 -> x28, starting transfers between devices: 27.3 us -> 30.1 us  [swap(): return lax.ppermute(x, axis, [(i, i ^ distance) for i in range(size)])]
  transfers between devices with their start and end apart: 26 -> 32, of which waited for: 17 -> 12; matrix products, arithmetic and copies ran while one was open for 0% -> 1% of each run, Pallas kernels for 11% -> 23%
where the time goes in v3:
time: 112 us; the launch traced here: 111 us
  starting transfers between devices  39.9 us (36%)
  Pallas kernels  30.3 us (27%)
  waiting for transfers between devices  26.5 us (24%)
  local copies, waits for them, and re-layouts  13 us (12%)
    ppermute x28, starting transfers between devices, swap(): return lax.ppermute(x, axis, [(i, i ^ distance) for i in range(size)])  30.1 us
    ppermute x28, waiting for transfers between devices, swap(): return lax.ppermute(x, axis, [(i, i ^ distance) for i in range(size)])  24.4 us
    pallas_call x4, Pallas kernels, over_slots(): pl.pallas_call(kernel, out_shape=outs, in_specs=[SMEM] * len(scalars) + [...  15.7 us
    unnamed x22, local copies, waits for them, and re-layouts  12.8 us
    ppermute x4, starting transfers between devices, exchange_edges(): return (lax.ppermute(south, 'src', down), lax.ppermute(north, 'src', up))  9.76 us
    pallas_call x1, Pallas kernels, per_device(): pl.pallas_call(back_outer_kernel, out_shape=jax.ShapeDtypeStruct((probe_l...  4.27 us
    pallas_call x1, Pallas kernels, per_device(): pl.pallas_call(back_inner_kernel, out_shape=(jax.ShapeDtypeStruct(by_half...  3.53 us
    pallas_call x1, Pallas kernels, per_device(): pl.pallas_call(smooth_inner_kernel, out_shape=(inner_part, state), in_spe...  3.15 us
  transfers between devices with their start and end apart: 32, of which 12 were waited for; matrix products, arithmetic and copies ran while one was open for 1% of the time, Pallas kernels for 23%

profile of v3, /device:TPU:0, one launch (start us, length us, event | category | flops | bytes accessed | tf_op | source)
XLA Modules:
  0.0 111.2 jit_solution(4803639426853885618)
XLA Ops:
  2.1 4.9 %collective-permute-start = (bf16[4,80,256]{2,1,0:T(8,128)(2,1)S(1)}, bf16[4,80,256]{2,1,0:T(8,128)(2,1)S(1)}, u32[]{:S(2)}, u32[]{:S(2)}) collective-permute-start(bf16[4,80,256]{2,1,0:T(8,128)(2,1)S(1)} %get-tuple-element.25), channel_id=1, source_target_pairs={{0,4},{4,8},{8,12},{12,16},{16,20},{20,24},{24,28},{1,5},{5,9},{9,... | collective-permute-start | bytes 491528 | tf_op jit(solution)/shard_map/ppermute | solution.py:301
  8.2 3.1 %smooth_inner.1 = (bf16[16,64,128]{2,1,0:T(8,128)(2,1)S(1)}, f32[2,4,2,64,256]{4,3,2,1,0:T(8,128)S(1)}) custom-call(bf16[1024,256]{1,0:T(8,128)(2,1)S(1)} %bitcast.50, f32[16,256]{1,0:T(8,128)S(1)} %copy-done.6), custom_call_target="tpu_custom_call" | custom-call | tf_op jit(solution)/shard_map/smooth_inner/pallas_call | solution.py:345
  11.4 1.6 %collective-permute-start.2 = (bf16[16,64,128]{2,1,0:T(8,128)(2,1)S(1)}, bf16[16,64,128]{2,1,0:T(8,128)(2,1)S(1)}, u32[]{:S(2)}, u32[]{:S(2)}) collective-permute-start(bf16[16,64,128]{2,1,0:T(8,128)(2,1)S(1)} %get-tuple-element.28.near_in), channel_id=1, source_target_pairs={{0,2},{1,3},{2,0},{3,1},{4,6},{5,7},{6,4},{7,5},{8,10},{9,11},{10,... | collective-permute-start | bytes 786440 | tf_op jit(solution)/shard_map/ppermute | solution.py:290
  14.5 2.5 %smooth_outer.1.after_ref.near_out = bf16[16,64,128]{2,1,0:T(8,128)(2,1)S(1)} custom-call(f32[16,256]{1,0:T(8,128)S(1)} %copy-done.6, bf16[4,80,256]{2,1,0:T(8,128)(2,1)S(1)} %collective-permute-done.above_ref, bf16[4,80,256]{2,1,0:T(8,128)(2,1)S(1)} %collective-permute-done.1.below_ref, f32[2,4,2,64,256]{4,3,2,1,0:T(8,128)S(1)} %get-tuple-element.27.state_ref), custom_call_target="tpu_custom_call" | custom-call | tf_op jit(solution)/shard_map/smooth_outer/pallas_call | solution.py:358
  17.1 1.6 %collective-permute-start.3 = (bf16[16,64,128]{2,1,0:T(8,128)(2,1)S(1)}, bf16[16,64,128]{2,1,0:T(8,128)(2,1)S(1)}, u32[]{:S(2)}, u32[]{:S(2)}) collective-permute-start(bf16[16,64,128]{2,1,0:T(8,128)(2,1)S(1)} %smooth_outer.1.after_ref.near_out), channel_id=1, source_target_pairs={{0,2},{1,3},{2,0},{3,1},{4,6},{5,7},{6,4},{7,5},{8,10},{9,11},{10,... | collective-permute-start | bytes 786440 | tf_op jit(solution)/shard_map/ppermute | solution.py:290
  19.4 2.8 %copy-done.2 = bf16[1,1,192,128,128]{4,3,2,1,0:T(8,128)(2,1)S(1)} copy-done((bf16[1,1,192,128,128]{4,3,2,1,0:T(8,128)(2,1)S(1)}, bf16[1,1,192,128,128]{4,3,2,1,0:T(8,128)(2,1)}, u32[]{:S(2)}) %copy-start.2) | copy-done | bytes 6291480
  22.9 4.1 %forward_kernel.2 = (bf16[8,128,128]{2,1,0:T(8,128)(2,1)S(1)}, bf16[8,128,128]{2,1,0:T(8,128)(2,1)S(1)}) custom-call(s32[192]{0:T(256)S(1)} %bitcast.53, s32[192]{0:T(256)S(1)} %bitcast.57, s32[1]{0:T(128)} %bitcast.43.count, s32[2]{0:T(128)S(1)} %pad_add_fusion.place, bf16[192,128,128]{2,1,0:T(8,128)(2,1)S(1)} %hold.2.held, ...), custom_call_target="tpu_custom_call" | custom-call | flops 805306368 | bytes 6291456 | tf_op jit(solution)/shard_map/forward_kernel/pallas_call | solution.py:379
  27.0 2.7 %copy-done = bf16[192,128,128]{2,1,0:T(8,128)(2,1)} copy-done((bf16[192,128,128]{2,1,0:T(8,128)(2,1)}, bf16[192,128,128]{2,1,0:T(8,128)(2,1)S(1)}, u32[]{:S(2)}) %copy-start) | copy-done | bytes 6291480
  30.0 2.5 %collective-permute-start.12 = (bf16[8,128,128]{2,1,0:T(8,128)(2,1)S(1)}, bf16[8,128,128]{2,1,0:T(8,128)(2,1)S(1)}, u32[]{:S(2)}, u32[]{:S(2)}) collective-permute-start(bf16[8,128,128]{2,1,0:T(8,128)(2,1)S(1)} %get-tuple-element.34), channel_id=1, source_target_pairs={{0,4},{4,0},{8,12},{12,8},{16,20},{20,16},{24,28},{28,24},{1,5},{5... | collective-permute-start | bytes 786440 | tf_op jit(solution)/shard_map/ppermute | solution.py:290
  32.5 2.8 %copy-done.1 = bf16[192,128,128]{2,1,0:T(8,128)(2,1)S(1)} copy-done((bf16[192,128,128]{2,1,0:T(8,128)(2,1)S(1)}, bf16[192,128,128]{2,1,0:T(8,128)(2,1)}, u32[]{:S(2)}) %copy-start.1) | copy-done | bytes 6291480
  35.3 4.0 %forward_kernel.3 = (bf16[8,128,128]{2,1,0:T(8,128)(2,1)S(1)}, bf16[8,128,128]{2,1,0:T(8,128)(2,1)S(1)}) custom-call(s32[192]{0:T(256)S(1)} %bitcast.54, s32[192]{0:T(256)S(1)} %bitcast.58, s32[1]{0:T(128)} %bitcast.44.count, s32[2]{0:T(128)S(1)} %pad_add_fusion.place, bf16[192,128,128]{2,1,0:T(8,128)(2,1)S(1)} %copy-done.1, ...), custom_call_target="tpu_custom_call" | custom-call | flops 805306368 | bytes 6291456 | tf_op jit(solution)/shard_map/forward_kernel/pallas_call | solution.py:379
  40.6 2.7 %collective-permute-start.13 = (bf16[256,128]{1,0:T(8,128)(2,1)S(1)}, bf16[256,128]{1,0:T(8,128)(2,1)S(1)}, u32[]{:S(2)}, u32[]{:S(2)}) collective-permute-start(bf16[256,128]{1,0:T(8,128)(2,1)S(1)} %get-tuple-element.49), channel_id=1, source_target_pairs={{0,16},{4,20},{8,24},{12,28},{16,0},{20,4},{24,8},{28,12},{1,17},{... | collective-permute-start | bytes 196616 | tf_op jit(solution)/shard_map/ppermute | solution.py:290
  44.7 2.8 %collective-permute-done.8 = bf16[8,128,128]{2,1,0:T(8,128)(2,1)S(1)} collective-permute-done((bf16[8,128,128]{2,1,0:T(8,128)(2,1)S(1)}, bf16[8,128,128]{2,1,0:T(8,128)(2,1)S(1)}, u32[]{:S(2)}, u32[]{:S(2)}) %collective-permute-start.8) | collective-permute-done | bytes 262176 | tf_op jit(solution)/shard_map/ppermute | solution.py:290
  47.6 4.1 %collective-permute-start.10 = (bf16[256,128]{1,0:T(8,128)(2,1)S(1)}, bf16[256,128]{1,0:T(8,128)(2,1)S(1)}, u32[]{:S(2)}, u32[]{:S(2)}) collective-permute-start(bf16[256,128]{1,0:T(8,128)(2,1)S(1)} %get-tuple-element.54), channel_id=1, source_target_pairs={{0,24},{4,28},{8,16},{12,20},{16,8},{20,12},{24,0},{28,4},{1,25},{... | collective-permute-start | bytes 196616 | tf_op jit(solution)/shard_map/ppermute | solution.py:290
  52.3 2.0 %collective-permute-done.10 = bf16[256,128]{1,0:T(8,128)(2,1)S(1)} collective-permute-done((bf16[256,128]{1,0:T(8,128)(2,1)S(1)}, bf16[256,128]{1,0:T(8,128)(2,1)S(1)}, u32[]{:S(2)}, u32[]{:S(2)}) %collective-permute-start.10) | collective-permute-done | bytes 65568 | tf_op jit(solution)/shard_map/ppermute | solution.py:290
  54.3 1.9 %collective-permute-done.11 = bf16[256,128]{1,0:T(8,128)(2,1)S(1)} collective-permute-done((bf16[256,128]{1,0:T(8,128)(2,1)S(1)}, bf16[256,128]{1,0:T(8,128)(2,1)S(1)}, u32[]{:S(2)}, u32[]{:S(2)}) %collective-permute-start.11) | collective-permute-done | bytes 65568 | tf_op jit(solution)/shard_map/ppermute | solution.py:290
  57.2 1.9 %collective-permute-start.21 = (bf16[256,128]{1,0:T(8,128)(2,1)S(1)}, bf16[256,128]{1,0:T(8,128)(2,1)S(1)}, u32[]{:S(2)}, u32[]{:S(2)}) collective-permute-start(bf16[256,128]{1,0:T(8,128)(2,1)S(1)} %get-tuple-element.46.after_ref), channel_id=1, source_target_pairs={{0,8},{4,12},{8,0},{12,4},{16,24},{20,28},{24,16},{28,20},{1,9},{5... | collective-permute-start | bytes 196616 | tf_op jit(solution)/shard_map/ppermute | solution.py:290
  59.1 1.7 %collective-permute-start.22 = (bf16[256,128]{1,0:T(8,128)(2,1)S(1)}, bf16[256,128]{1,0:T(8,128)(2,1)S(1)}, u32[]{:S(2)}, u32[]{:S(2)}) collective-permute-start(bf16[256,128]{1,0:T(8,128)(2,1)S(1)} %get-tuple-element.46.after_ref), channel_id=1, source_target_pairs={{0,16},{4,20},{8,24},{12,28},{16,0},{20,4},{24,8},{28,12},{1,17},{... | collective-permute-start | bytes 196616 | tf_op jit(solution)/shard_map/ppermute | solution.py:290
  61.7 3.6 %collective-permute-done.22 = bf16[256,128]{1,0:T(8,128)(2,1)S(1)} collective-permute-done((bf16[256,128]{1,0:T(8,128)(2,1)S(1)}, bf16[256,128]{1,0:T(8,128)(2,1)S(1)}, u32[]{:S(2)}, u32[]{:S(2)}) %collective-permute-start.22) | collective-permute-done | bytes 65568 | tf_op jit(solution)/shard_map/ppermute | solution.py:290
  65.3 1.9 %collective-permute-done.23 = bf16[256,128]{1,0:T(8,128)(2,1)S(1)} collective-permute-done((bf16[256,128]{1,0:T(8,128)(2,1)S(1)}, bf16[256,128]{1,0:T(8,128)(2,1)S(1)}, u32[]{:S(2)}, u32[]{:S(2)}) %collective-permute-start.23) | collective-permute-done | bytes 65568 | tf_op jit(solution)/shard_map/ppermute | solution.py:290
  67.4 1.5 %collective-permute-start.17 = (bf16[256,128]{1,0:T(8,128)(2,1)S(1)}, bf16[256,128]{1,0:T(8,128)(2,1)S(1)}, u32[]{:S(2)}, u32[]{:S(2)}) collective-permute-start(bf16[256,128]{1,0:T(8,128)(2,1)S(1)} %get-tuple-element.45), channel_id=1, source_target_pairs={{0,16},{4,20},{8,24},{12,28},{16,0},{20,4},{24,8},{28,12},{1,17},{... | collective-permute-start | bytes 196616 | tf_op jit(solution)/shard_map/ppermute | solution.py:290
  69.0 2.9 %collective-permute-start.18 = (bf16[256,128]{1,0:T(8,128)(2,1)S(1)}, bf16[256,128]{1,0:T(8,128)(2,1)S(1)}, u32[]{:S(2)}, u32[]{:S(2)}) collective-permute-start(bf16[256,128]{1,0:T(8,128)(2,1)S(1)} %get-tuple-element.45), channel_id=1, source_target_pairs={{0,24},{4,28},{8,16},{12,20},{16,8},{20,12},{24,0},{28,4},{1,25},{... | collective-permute-start | bytes 196616 | tf_op jit(solution)/shard_map/ppermute | solution.py:290
  72.6 2.5 %collective-permute-done.18 = bf16[256,128]{1,0:T(8,128)(2,1)S(1)} collective-permute-done((bf16[256,128]{1,0:T(8,128)(2,1)S(1)}, bf16[256,128]{1,0:T(8,128)(2,1)S(1)}, u32[]{:S(2)}, u32[]{:S(2)}) %collective-permute-start.18) | collective-permute-done | bytes 65568 | tf_op jit(solution)/shard_map/ppermute | solution.py:290
  75.1 1.7 %collective-permute-start.19 = (bf16[4,256,128]{2,1,0:T(8,128)(2,1)S(1)}, bf16[4,256,128]{2,1,0:T(8,128)(2,1)S(1)}, u32[]{:S(2)}, u32[]{:S(2)}) collective-permute-start(bf16[4,256,128]{2,1,0:T(8,128)(2,1)S(1)} %pad_maximum_fusion.mine_ref), channel_id=1, source_target_pairs={{0,4},{4,0},{8,12},{12,8},{16,20},{20,16},{24,28},{28,24},{1,5},{5... | collective-permute-start | bytes 786440 | tf_op jit(solution)/shard_map/ppermute | solution.py:290
  76.8 2.8 %copy-done.3 = bf16[1,1,192,128,128]{4,3,2,1,0:T(8,128)(2,1)S(1)} copy-done((bf16[1,1,192,128,128]{4,3,2,1,0:T(8,128)(2,1)S(1)}, bf16[1,1,192,128,128]{4,3,2,1,0:T(8,128)(2,1)}, u32[]{:S(2)}) %copy-start.3) | copy-done | bytes 6291480
  80.0 3.8 %adjoint_kernel.3 = (bf16[16,64,128]{2,1,0:T(8,128)(2,1)S(1)}, bf16[16,64,128]{2,1,0:T(8,128)(2,1)S(1)}, bf16[16,64,128]{2,1,0:T(8,128)(2,1)S(1)}, bf16[16,64,128]{2,1,0:T(8,128)(2,1)S(1)}) custom-call(s32[192]{0:T(256)S(1)} %bitcast.55, s32[192]{0:T(256)S(1)} %bitcast.59, s32[1]{0:T(128)} %bitcast.46.count, s32[2]{0:T(128)S(1)} %pad_add_fusion.place, ...), custom_call_target="tpu_custom_call" | custom-call | flops 805306368 | bytes 6291456 | tf_op jit(solution)/shard_map/adjoint_kernel/pallas_call | solution.py:379
  84.4 3.8 %adjoint_kernel.2 = (bf16[16,64,128]{2,1,0:T(8,128)(2,1)S(1)}, bf16[16,64,128]{2,1,0:T(8,128)(2,1)S(1)}, bf16[16,64,128]{2,1,0:T(8,128)(2,1)S(1)}, bf16[16,64,128]{2,1,0:T(8,128)(2,1)S(1)}) custom-call(s32[192]{0:T(256)S(1)} %bitcast.56, s32[192]{0:T(256)S(1)} %bitcast.60, s32[1]{0:T(128)} %bitcast.45.count, s32[2]{0:T(128)S(1)} %pad_add_fusion.place, ...), custom_call_target="tpu_custom_call" | custom-call | flops 805306368 | bytes 6291456 | tf_op jit(solution)/shard_map/adjoint_kernel/pallas_call | solution.py:379
  89.3 1.5 %collective-permute-start.31 = (bf16[16,64,128]{2,1,0:T(8,128)(2,1)S(1)}, bf16[16,64,128]{2,1,0:T(8,128)(2,1)S(1)}, u32[]{:S(2)}, u32[]{:S(2)}) collective-permute-start(bf16[16,64,128]{2,1,0:T(8,128)(2,1)S(1)} %add_convert_fusion), channel_id=1, source_target_pairs={{0,2},{1,3},{2,0},{3,1},{4,6},{5,7},{6,4},{7,5},{8,10},{9,11},{10,... | collective-permute-start | bytes 786440 | tf_op jit(solution)/shard_map/ppermute | solution.py:290
  90.8 6.8 %collective-permute-done.26.far_out = bf16[16,64,128]{2,1,0:T(8,128)(2,1)S(1)} collective-permute-done((bf16[16,64,128]{2,1,0:T(8,128)(2,1)S(1)}, bf16[16,64,128]{2,1,0:T(8,128)(2,1)S(1)}, u32[]{:S(2)}, u32[]{:S(2)}) %collective-permute-start.26) | collective-permute-done | bytes 262176 | tf_op jit(solution)/shard_map/ppermute | solution.py:290
  97.8 2.3 %collective-permute-start.27 = (bf16[8,64,128]{2,1,0:T(8,128)(2,1)S(1)}, bf16[8,64,128]{2,1,0:T(8,128)(2,1)S(1)}, u32[]{:S(2)}, u32[]{:S(2)}) collective-permute-start(bf16[8,64,128]{2,1,0:T(8,128)(2,1)S(1)} %get-tuple-element.48), channel_id=1, source_target_pairs={{0,4},{4,8},{8,12},{12,16},{16,20},{20,24},{24,28},{1,5},{5,9},{9,... | collective-permute-start | bytes 393224 | tf_op jit(solution)/shard_map/ppermute | solution.py:301
  102.8 3.5 %back_inner.1 = (f32[2,1024,128]{2,1,0:T(8,128)S(1)}, f32[2,4,2,64,256]{4,3,2,1,0:T(8,128)S(1)}) custom-call(bf16[1024,256]{1,0:T(8,128)(2,1)S(1)} %bitcast.51, f32[16,256]{1,0:T(8,128)S(1)} %copy-done.7, bf16[16,64,128]{2,1,0:T(8,128)(2,1)S(1)} %get-tuple-element.39.own_in, bf16[16,64,128]{2,1,0:T(8,128)(2,1)S(1)} %collective-permute-done.29.core_in, ...), custom_call_target="tpu_custom_call" | custom-call | tf_op jit(solution)/shard_map/back_inner/pallas_call | solution.py:454
  106.9 4.3 %back_outer.1 = f32[1024,256]{1,0:T(8,128)} custom-call(f32[2]{0:T(128)S(1)} %add_convert_fusion.5.inside, f32[16,256]{1,0:T(8,128)S(1)} %copy-done.7, bf16[4,80,256]{2,1,0:T(8,128)(2,1)S(1)} %collective-permute-done.above_ref, bf16[4,80,256]{2,1,0:T(8,128)(2,1)S(1)} %collective-permute-done.1.below_ref, ...), custom_call_target="tpu_custom_call" | custom-call | tf_op jit(solution)/shard_map/back_outer/pallas_call | solution.py:463
  (79 shorter events, 17.9 us)
Async XLA Ops:
  2.1 11.0 %collective-permute-start = (bf16[4,80,256]{2,1,0:T(8,128)(2,1)S(1)}, bf16[4,80,256]{2,1,0:T(8,128)(2,1)S(1)}, u32[]{:S(2)}, u32[]{:S(2)}) collective-permute-start(bf16[4,80,256]{2,1,0:T(8,128)(2,1)S(1)} %get-tuple-element.25), channel_id=1, source_target_pairs={{0,4},{4,8},{8,12},{12,16},{16,20},{20,24},{24,28},{1,5},{5,9},{9,... | collective-permute-start | bytes 491528 | tf_op jit(solution)/shard_map/ppermute | solution.py:301
  6.9 7.6 %collective-permute-start.1 = (bf16[4,80,256]{2,1,0:T(8,128)(2,1)S(1)}, bf16[4,80,256]{2,1,0:T(8,128)(2,1)S(1)}, u32[]{:S(2)}, u32[]{:S(2)}) collective-permute-start(bf16[4,80,256]{2,1,0:T(8,128)(2,1)S(1)} %get-tuple-element.26), channel_id=1, source_target_pairs={{4,0},{8,4},{12,8},{16,12},{20,16},{24,20},{28,24},{5,1},{9,5},{13... | collective-permute-start | bytes 491528 | tf_op jit(solution)/shard_map/ppermute | solution.py:301
  11.4 11.5 %collective-permute-start.4 = (bf16[16,64,128]{2,1,0:T(8,128)(2,1)S(1)}, bf16[16,64,128]{2,1,0:T(8,128)(2,1)S(1)}, u32[]{:S(2)}, u32[]{:S(2)}) collective-permute-start(bf16[16,64,128]{2,1,0:T(8,128)(2,1)S(1)} %get-tuple-element.28.near_in), channel_id=1, source_target_pairs={{0,1},{1,0},{2,3},{3,2},{4,5},{5,4},{6,7},{7,6},{8,9},{9,8},{10,11... | collective-permute-start | bytes 786440 | tf_op jit(solution)/shard_map/ppermute | solution.py:290
  11.4 11.2 %collective-permute-start.2 = (bf16[16,64,128]{2,1,0:T(8,128)(2,1)S(1)}, bf16[16,64,128]{2,1,0:T(8,128)(2,1)S(1)}, u32[]{:S(2)}, u32[]{:S(2)}) collective-permute-start(bf16[16,64,128]{2,1,0:T(8,128)(2,1)S(1)} %get-tuple-element.28.near_in), channel_id=1, source_target_pairs={{0,2},{1,3},{2,0},{3,1},{4,6},{5,7},{6,4},{7,5},{8,10},{9,11},{10,... | collective-permute-start | bytes 786440 | tf_op jit(solution)/shard_map/ppermute | solution.py:290
  17.0 5.9 %collective-permute-start.5 = (bf16[16,64,128]{2,1,0:T(8,128)(2,1)S(1)}, bf16[16,64,128]{2,1,0:T(8,128)(2,1)S(1)}, u32[]{:S(2)}, u32[]{:S(2)}) collective-permute-start(bf16[16,64,128]{2,1,0:T(8,128)(2,1)S(1)} %smooth_outer.1.after_ref.near_out), channel_id=1, source_target_pairs={{0,1},{1,0},{2,3},{3,2},{4,5},{5,4},{6,7},{7,6},{8,9},{9,8},{10,11... | collective-permute-start | bytes 786440 | tf_op jit(solution)/shard_map/ppermute | solution.py:290
  17.1 12.6 %collective-permute-start.3 = (bf16[16,64,128]{2,1,0:T(8,128)(2,1)S(1)}, bf16[16,64,128]{2,1,0:T(8,128)(2,1)S(1)}, u32[]{:S(2)}, u32[]{:S(2)}) collective-permute-start(bf16[16,64,128]{2,1,0:T(8,128)(2,1)S(1)} %smooth_outer.1.after_ref.near_out), channel_id=1, source_target_pairs={{0,2},{1,3},{2,0},{3,1},{4,6},{5,7},{6,4},{7,5},{8,10},{9,11},{10,... | collective-permute-start | bytes 786440 | tf_op jit(solution)/shard_map/ppermute | solution.py:290
  22.6 9.9 %collective-permute-start.6 = (bf16[16,64,128]{2,1,0:T(8,128)(2,1)S(1)}, bf16[16,64,128]{2,1,0:T(8,128)(2,1)S(1)}, u32[]{:S(2)}, u32[]{:S(2)}) collective-permute-start(bf16[16,64,128]{2,1,0:T(8,128)(2,1)S(1)} %collective-permute-done.2.near_in), channel_id=1, source_target_pairs={{0,1},{1,0},{2,3},{3,2},{4,5},{5,4},{6,7},{7,6},{8,9},{9,8},{10,11... | collective-permute-start | bytes 786440 | tf_op jit(solution)/shard_map/ppermute | solution.py:290
  29.7 2.8 %collective-permute-start.7 = (bf16[16,64,128]{2,1,0:T(8,128)(2,1)S(1)}, bf16[16,64,128]{2,1,0:T(8,128)(2,1)S(1)}, u32[]{:S(2)}, u32[]{:S(2)}) collective-permute-start(bf16[16,64,128]{2,1,0:T(8,128)(2,1)S(1)} %collective-permute-done.3.near_out), channel_id=1, source_target_pairs={{0,1},{1,0},{2,3},{3,2},{4,5},{5,4},{6,7},{7,6},{8,9},{9,8},{10,11... | collective-permute-start | bytes 786440 | tf_op jit(solution)/shard_map/ppermute | solution.py:290
  30.0 10.5 %collective-permute-start.12 = (bf16[8,128,128]{2,1,0:T(8,128)(2,1)S(1)}, bf16[8,128,128]{2,1,0:T(8,128)(2,1)S(1)}, u32[]{:S(2)}, u32[]{:S(2)}) collective-permute-start(bf16[8,128,128]{2,1,0:T(8,128)(2,1)S(1)} %get-tuple-element.34), channel_id=1, source_target_pairs={{0,4},{4,0},{8,12},{12,8},{16,20},{20,16},{24,28},{28,24},{1,5},{5... | collective-permute-start | bytes 786440 | tf_op jit(solution)/shard_map/ppermute | solution.py:290
  39.3 8.2 %collective-permute-start.8 = (bf16[8,128,128]{2,1,0:T(8,128)(2,1)S(1)}, bf16[8,128,128]{2,1,0:T(8,128)(2,1)S(1)}, u32[]{:S(2)}, u32[]{:S(2)}) collective-permute-start(bf16[8,128,128]{2,1,0:T(8,128)(2,1)S(1)} %get-tuple-element.32), channel_id=1, source_target_pairs={{0,4},{4,0},{8,12},{12,8},{16,20},{20,16},{24,28},{28,24},{1,5},{5... | collective-permute-start | bytes 786440 | tf_op jit(solution)/shard_map/ppermute | solution.py:290
  40.6 11.1 %collective-permute-start.13 = (bf16[256,128]{1,0:T(8,128)(2,1)S(1)}, bf16[256,128]{1,0:T(8,128)(2,1)S(1)}, u32[]{:S(2)}, u32[]{:S(2)}) collective-permute-start(bf16[256,128]{1,0:T(8,128)(2,1)S(1)} %get-tuple-element.49), channel_id=1, source_target_pairs={{0,16},{4,20},{8,24},{12,28},{16,0},{20,4},{24,8},{28,12},{1,17},{... | collective-permute-start | bytes 196616 | tf_op jit(solution)/shard_map/ppermute | solution.py:290
  43.3 9.1 %collective-permute-start.14 = (bf16[256,128]{1,0:T(8,128)(2,1)S(1)}, bf16[256,128]{1,0:T(8,128)(2,1)S(1)}, u32[]{:S(2)}, u32[]{:S(2)}) collective-permute-start(bf16[256,128]{1,0:T(8,128)(2,1)S(1)} %get-tuple-element.51), channel_id=1, source_target_pairs={{0,24},{4,28},{8,16},{12,20},{16,8},{20,12},{24,0},{28,4},{1,25},{... | collective-permute-start | bytes 196616 | tf_op jit(solution)/shard_map/ppermute | solution.py:290
  44.6 7.7 %collective-permute-start.15 = (bf16[256,128]{1,0:T(8,128)(2,1)S(1)}, bf16[256,128]{1,0:T(8,128)(2,1)S(1)}, u32[]{:S(2)}, u32[]{:S(2)}) collective-permute-start(bf16[256,128]{1,0:T(8,128)(2,1)S(1)} %get-tuple-element.50), channel_id=1, source_target_pairs={{0,8},{4,12},{8,0},{12,4},{16,24},{20,28},{24,16},{28,20},{1,9},{5... | collective-permute-start | bytes 196616 | tf_op jit(solution)/shard_map/ppermute | solution.py:290
  47.6 6.7 %collective-permute-start.10 = (bf16[256,128]{1,0:T(8,128)(2,1)S(1)}, bf16[256,128]{1,0:T(8,128)(2,1)S(1)}, u32[]{:S(2)}, u32[]{:S(2)}) collective-permute-start(bf16[256,128]{1,0:T(8,128)(2,1)S(1)} %get-tuple-element.54), channel_id=1, source_target_pairs={{0,24},{4,28},{8,16},{12,20},{16,8},{20,12},{24,0},{28,4},{1,25},{... | collective-permute-start | bytes 196616 | tf_op jit(solution)/shard_map/ppermute | solution.py:290
  51.7 4.5 %collective-permute-start.11 = (bf16[256,128]{1,0:T(8,128)(2,1)S(1)}, bf16[256,128]{1,0:T(8,128)(2,1)S(1)}, u32[]{:S(2)}, u32[]{:S(2)}) collective-permute-start(bf16[256,128]{1,0:T(8,128)(2,1)S(1)} %get-tuple-element.53), channel_id=1, source_target_pairs={{0,8},{4,12},{8,0},{12,4},{16,24},{20,28},{24,16},{28,20},{1,9},{5... | collective-permute-start | bytes 196616 | tf_op jit(solution)/shard_map/ppermute | solution.py:290
  51.7 5.3 %collective-permute-start.9 = (bf16[256,128]{1,0:T(8,128)(2,1)S(1)}, bf16[256,128]{1,0:T(8,128)(2,1)S(1)}, u32[]{:S(2)}, u32[]{:S(2)}) collective-permute-start(bf16[256,128]{1,0:T(8,128)(2,1)S(1)} %get-tuple-element.52), channel_id=1, source_target_pairs={{0,16},{4,20},{8,24},{12,28},{16,0},{20,4},{24,8},{28,12},{1,17},{... | collective-permute-start | bytes 196616 | tf_op jit(solution)/shard_map/ppermute | solution.py:290
  57.2 4.5 %collective-permute-start.21 = (bf16[256,128]{1,0:T(8,128)(2,1)S(1)}, bf16[256,128]{1,0:T(8,128)(2,1)S(1)}, u32[]{:S(2)}, u32[]{:S(2)}) collective-permute-start(bf16[256,128]{1,0:T(8,128)(2,1)S(1)} %get-tuple-element.46.after_ref), channel_id=1, source_target_pairs={{0,8},{4,12},{8,0},{12,4},{16,24},{20,28},{24,16},{28,20},{1,9},{5... | collective-permute-start | bytes 196616 | tf_op jit(solution)/shard_map/ppermute | solution.py:290
  59.1 6.2 %collective-permute-start.22 = (bf16[256,128]{1,0:T(8,128)(2,1)S(1)}, bf16[256,128]{1,0:T(8,128)(2,1)S(1)}, u32[]{:S(2)}, u32[]{:S(2)}) collective-permute-start(bf16[256,128]{1,0:T(8,128)(2,1)S(1)} %get-tuple-element.46.after_ref), channel_id=1, source_target_pairs={{0,16},{4,20},{8,24},{12,28},{16,0},{20,4},{24,8},{28,12},{1,17},{... | collective-permute-start | bytes 196616 | tf_op jit(solution)/shard_map/ppermute | solution.py:290
  60.8 6.4 %collective-permute-start.23 = (bf16[256,128]{1,0:T(8,128)(2,1)S(1)}, bf16[256,128]{1,0:T(8,128)(2,1)S(1)}, u32[]{:S(2)}, u32[]{:S(2)}) collective-permute-start(bf16[256,128]{1,0:T(8,128)(2,1)S(1)} %get-tuple-element.46.after_ref), channel_id=1, source_target_pairs={{0,24},{4,28},{8,16},{12,20},{16,8},{20,12},{24,0},{28,4},{1,25},{... | collective-permute-start | bytes 196616 | tf_op jit(solution)/shard_map/ppermute | solution.py:290
  67.2 12.8 %collective-permute-start.24 = (bf16[4,256,128]{2,1,0:T(8,128)(2,1)S(1)}, bf16[4,256,128]{2,1,0:T(8,128)(2,1)S(1)}, u32[]{:S(2)}, u32[]{:S(2)}) collective-permute-start(bf16[4,256,128]{2,1,0:T(8,128)(2,1)S(1)} %pad_maximum_fusion.1.mine_ref), channel_id=1, source_target_pairs={{0,4},{4,0},{8,12},{12,8},{16,20},{20,16},{24,28},{28,24},{1,5},{5... | collective-permute-start | bytes 786440 | tf_op jit(solution)/shard_map/ppermute | solution.py:290
  67.4 4.4 %collective-permute-start.16 = (bf16[256,128]{1,0:T(8,128)(2,1)S(1)}, bf16[256,128]{1,0:T(8,128)(2,1)S(1)}, u32[]{:S(2)}, u32[]{:S(2)}) collective-permute-start(bf16[256,128]{1,0:T(8,128)(2,1)S(1)} %get-tuple-element.45), channel_id=1, source_target_pairs={{0,8},{4,12},{8,0},{12,4},{16,24},{20,28},{24,16},{28,20},{1,9},{5... | collective-permute-start | bytes 196616 | tf_op jit(solution)/shard_map/ppermute | solution.py:290
  67.4 5.2 %collective-permute-start.17 = (bf16[256,128]{1,0:T(8,128)(2,1)S(1)}, bf16[256,128]{1,0:T(8,128)(2,1)S(1)}, u32[]{:S(2)}, u32[]{:S(2)}) collective-permute-start(bf16[256,128]{1,0:T(8,128)(2,1)S(1)} %get-tuple-element.45), channel_id=1, source_target_pairs={{0,16},{4,20},{8,24},{12,28},{16,0},{20,4},{24,8},{28,12},{1,17},{... | collective-permute-start | bytes 196616 | tf_op jit(solution)/shard_map/ppermute | solution.py:290
  69.0 6.1 %collective-permute-start.18 = (bf16[256,128]{1,0:T(8,128)(2,1)S(1)}, bf16[256,128]{1,0:T(8,128)(2,1)S(1)}, u32[]{:S(2)}, u32[]{:S(2)}) collective-permute-start(bf16[256,128]{1,0:T(8,128)(2,1)S(1)} %get-tuple-element.45), channel_id=1, source_target_pairs={{0,24},{4,28},{8,16},{12,20},{16,8},{20,12},{24,0},{28,4},{1,25},{... | collective-permute-start | bytes 196616 | tf_op jit(solution)/shard_map/ppermute | solution.py:290
  75.1 9.3 %collective-permute-start.19 = (bf16[4,256,128]{2,1,0:T(8,128)(2,1)S(1)}, bf16[4,256,128]{2,1,0:T(8,128)(2,1)S(1)}, u32[]{:S(2)}, u32[]{:S(2)}) collective-permute-start(bf16[4,256,128]{2,1,0:T(8,128)(2,1)S(1)} %pad_maximum_fusion.mine_ref), channel_id=1, source_target_pairs={{0,4},{4,0},{8,12},{12,8},{16,20},{20,16},{24,28},{28,24},{1,5},{5... | collective-permute-start | bytes 786440 | tf_op jit(solution)/shard_map/ppermute | solution.py:290
  83.8 4.5 %collective-permute-start.25 = (bf16[16,64,128]{2,1,0:T(8,128)(2,1)S(1)}, bf16[16,64,128]{2,1,0:T(8,128)(2,1)S(1)}, u32[]{:S(2)}, u32[]{:S(2)}) collective-permute-start(bf16[16,64,128]{2,1,0:T(8,128)(2,1)S(1)} %get-tuple-element.38), channel_id=1, source_target_pairs={{0,1},{1,0},{2,3},{3,2},{4,5},{5,4},{6,7},{7,6},{8,9},{9,8},{10,11... | collective-permute-start | bytes 786440 | tf_op jit(solution)/shard_map/ppermute | solution.py:290
  83.9 5.3 %collective-permute-start.30 = (bf16[16,64,128]{2,1,0:T(8,128)(2,1)S(1)}, bf16[16,64,128]{2,1,0:T(8,128)(2,1)S(1)}, u32[]{:S(2)}, u32[]{:S(2)}) collective-permute-start(bf16[16,64,128]{2,1,0:T(8,128)(2,1)S(1)} %get-tuple-element.42), channel_id=1, source_target_pairs={{0,1},{1,0},{2,3},{3,2},{4,5},{5,4},{6,7},{7,6},{8,9},{9,8},{10,11... | collective-permute-start | bytes 786440 | tf_op jit(solution)/shard_map/ppermute | solution.py:290
  88.2 2.6 %collective-permute-start.20 = (bf16[16,64,128]{2,1,0:T(8,128)(2,1)S(1)}, bf16[16,64,128]{2,1,0:T(8,128)(2,1)S(1)}, u32[]{:S(2)}, u32[]{:S(2)}) collective-permute-start(bf16[16,64,128]{2,1,0:T(8,128)(2,1)S(1)} %get-tuple-element.36), channel_id=1, source_target_pairs={{0,1},{1,0},{2,3},{3,2},{4,5},{5,4},{6,7},{7,6},{8,9},{9,8},{10,11... | collective-permute-start | bytes 786440 | tf_op jit(solution)/shard_map/ppermute | solution.py:290
  88.4 9.2 %collective-permute-start.26 = (bf16[16,64,128]{2,1,0:T(8,128)(2,1)S(1)}, bf16[16,64,128]{2,1,0:T(8,128)(2,1)S(1)}, u32[]{:S(2)}, u32[]{:S(2)}) collective-permute-start(bf16[16,64,128]{2,1,0:T(8,128)(2,1)S(1)} %add_convert_fusion.2), channel_id=1, source_target_pairs={{0,2},{1,3},{2,0},{3,1},{4,6},{5,7},{6,4},{7,5},{8,10},{9,11},{10,... | collective-permute-start | bytes 786440 | tf_op jit(solution)/shard_map/ppermute | solution.py:290
  89.1 12.4 %collective-permute-start.29 = (bf16[16,64,128]{2,1,0:T(8,128)(2,1)S(1)}, bf16[16,64,128]{2,1,0:T(8,128)(2,1)S(1)}, u32[]{:S(2)}, u32[]{:S(2)}) collective-permute-start(bf16[16,64,128]{2,1,0:T(8,128)(2,1)S(1)} %get-tuple-element.40), channel_id=1, source_target_pairs={{0,1},{1,0},{2,3},{3,2},{4,5},{5,4},{6,7},{7,6},{8,9},{9,8},{10,11... | collective-permute-start | bytes 786440 | tf_op jit(solution)/shard_map/ppermute | solution.py:290
  89.3 13.5 %collective-permute-start.31 = (bf16[16,64,128]{2,1,0:T(8,128)(2,1)S(1)}, bf16[16,64,128]{2,1,0:T(8,128)(2,1)S(1)}, u32[]{:S(2)}, u32[]{:S(2)}) collective-permute-start(bf16[16,64,128]{2,1,0:T(8,128)(2,1)S(1)} %add_convert_fusion), channel_id=1, source_target_pairs={{0,2},{1,3},{2,0},{3,1},{4,6},{5,7},{6,4},{7,5},{8,10},{9,11},{10,... | collective-permute-start | bytes 786440 | tf_op jit(solution)/shard_map/ppermute | solution.py:290
  97.8 8.6 %collective-permute-start.27 = (bf16[8,64,128]{2,1,0:T(8,128)(2,1)S(1)}, bf16[8,64,128]{2,1,0:T(8,128)(2,1)S(1)}, u32[]{:S(2)}, u32[]{:S(2)}) collective-permute-start(bf16[8,64,128]{2,1,0:T(8,128)(2,1)S(1)} %get-tuple-element.48), channel_id=1, source_target_pairs={{0,4},{4,8},{8,12},{12,16},{16,20},{20,24},{24,28},{1,5},{5,9},{9,... | collective-permute-start | bytes 393224 | tf_op jit(solution)/shard_map/ppermute | solution.py:301
  100.1 6.9 %collective-permute-start.28 = (bf16[8,64,128]{2,1,0:T(8,128)(2,1)S(1)}, bf16[8,64,128]{2,1,0:T(8,128)(2,1)S(1)}, u32[]{:S(2)}, u32[]{:S(2)}) collective-permute-start(bf16[8,64,128]{2,1,0:T(8,128)(2,1)S(1)} %get-tuple-element.47), channel_id=1, source_target_pairs={{4,0},{8,4},{12,8},{16,12},{20,16},{24,20},{28,24},{5,1},{9,5},{13... | collective-permute-start | bytes 393224 | tf_op jit(solution)/shard_map/ppermute | solution.py:301
  (11 other events, 79.4 us)

commit v4 on v3

--- a/solution.py
+++ b/solution.py
@@ -334,7 +334,7 @@
             compiler_params=params(),
             cost_estimate=pl.CostEstimate(flops=0, bytes_accessed=4 * slots * BLK * BLK, transcendentals=0),
             name="hold",
-        )(blocks, after)
+        )(pltpu.with_memory_space_constraint(blocks, pltpu.HBM), after)
 
     edge_cells = SMOOTH * halves
     inner_part = jax.ShapeDtypeStruct((cells - 2 * edge_cells, probe_local, BLK), BF16)
@@ -408,9 +408,10 @@
             [pltpu.VMEM((RB_LOC * pair, BLK), BF16), pltpu.VMEM((cells + 1, pair, BLK), F32)],
         )
 
-    weights = jnp.broadcast_to(obs_weight.reshape(RB_LOC, 1, BLK), (RB_LOC, pair, BLK))
-    weights = lax.dynamic_index_in_dim(weights.reshape(2, spread_over, share, BLK), side, 0, False)
-    weights = lax.dynamic_index_in_dim(weights, row, 0, False)
+    first_row = (side * spread_over + row) * share
+    held_blocks = max(share // pair, 1)
+    weights = lax.dynamic_slice_in_dim(obs_weight.reshape(RB_LOC, 1, BLK), first_row // pair, held_blocks)
+    weights = jnp.broadcast_to(weights, (held_blocks, share // held_blocks, BLK)).reshape(share, BLK)
 
     def summed(keep, give):
         got = swap(give, "src", 1)
@@ -436,13 +437,16 @@
     near_keep, near_give = forward(held, *own, *beside)
     other[1], near_give = lax.optimization_barrier((other[1], near_give))
     first = summed(near_keep, near_give)
-    second = summed(*forward(held, *other, *[swap(x, "rcv", 1) for x in other]))
-
-    held = hold(second)
-    second_halves = spread(second)
-    first_halves = spread(first)
-    mine_in, mine_out, *to_beside = adjoint(held, *first_halves)
+    second = summed(*forward(hold(near_give), *other, *[swap(x, "rcv", 1) for x in other]))
+
+    held = hold(first)
+    first_mine = gathered(first)
+    second_mine = gathered(second)
+    second_mine, _ = lax.optimization_barrier((second_mine, first_mine))
+    mine_in, mine_out, *to_beside = adjoint(held, first_mine, swap(first_mine, "src", 1))
     beside_in, beside_out = [swap(x, "rcv", 1) for x in to_beside]
+    second_halves = (second_mine, swap(second_mine, "src", 1))
+    second_halves, mine_in = lax.optimization_barrier((second_halves, mine_in))
     other_in, other_out, diagonal_in, diagonal_out = adjoint(held, *second_halves)
     both = lambda here, there: (here.astype(F32) + swap(there, "rcv", 1).astype(F32)).astype(BF16)
     far_out = swap(both(other_out, diagonal_out), "rcv", 2)

time: 112 us -> 106 us (0.946)
  local copies, waits for them, and re-layouts: 13 us -> 1.87 us
  Pallas kernels: 30.3 us -> 37.8 us
  waiting for transfers between devices: 26.5 us -> 21.8 us
  starting transfers between devices: 39.9 us -> 42.1 us
    unnamed x22 -> x14, local copies, waits for them, and re-layouts: 12.8 us -> 1.8 us
    pallas_call x2 -> x3, Pallas kernels: 0.86 us -> 8.4 us  [hold(): pl.pallas_call(hold_kernel, out_shape=jax.ShapeDtypeStruct(blocks.shape,...]
    ppermute x28, waiting for transfers between devices: 24.4 us -> 20.3 us  [swap(): return lax.ppermute(x, axis, [(i, i ^ distance) for i in range(size)])]
    ppermute x4, starting transfers between devices: 9.76 us -> 12 us  [exchange_edges(): return (lax.ppermute(south, 'src', down), lax.ppermute(north, 'src', up))]
  transfers between devices with their start and end apart: 32 -> 32, of which waited for: 12 -> 11; matrix products, arithmetic and copies ran while one was open for 1% -> 1% of each run, Pallas kernels for 23% -> 28%
where the time goes in v4:
time: 106 us; the launch traced here: 105 us
  starting transfers between devices  42.1 us (40%)
  Pallas kernels  37.8 us (36%)
  waiting for transfers between devices  21.8 us (21%)
  local copies, waits for them, and re-layouts  1.87 us (2%)
    ppermute x28, starting transfers between devices, swap(): return lax.ppermute(x, axis, [(i, i ^ distance) for i in range(size)])  30.1 us
    ppermute x28, waiting for transfers between devices, swap(): return lax.ppermute(x, axis, [(i, i ^ distance) for i in range(size)])  20.3 us
    pallas_call x4, Pallas kernels, over_slots(): pl.pallas_call(kernel, out_shape=outs, in_specs=[SMEM] * len(scalars) + [...  15.7 us
    ppermute x4, starting transfers between devices, exchange_edges(): return (lax.ppermute(south, 'src', down), lax.ppermute(north, 'src', up))  12 us
    pallas_call x3, Pallas kernels, hold(): pl.pallas_call(hold_kernel, out_shape=jax.ShapeDtypeStruct(blocks.shape,...  8.4 us
    pallas_call x1, Pallas kernels, per_device(): pl.pallas_call(back_outer_kernel, out_shape=jax.ShapeDtypeStruct((probe_l...  4.28 us
    pallas_call x1, Pallas kernels, per_device(): pl.pallas_call(back_inner_kernel, out_shape=(jax.ShapeDtypeStruct(by_half...  3.53 us
    pallas_call x1, Pallas kernels, per_device(): pl.pallas_call(smooth_inner_kernel, out_shape=(inner_part, state), in_spe...  3.15 us
  transfers between devices with their start and end apart: 32, of which 11 were waited for; matrix products, arithmetic and copies ran while one was open for 1% of the time, Pallas kernels for 28%

profile of v4, /device:TPU:0, one launch (start us, length us, event | category | flops | bytes accessed | tf_op | source)
XLA Modules:
  0.0 105.3 jit_solution(3058963334614653946)
XLA Ops:
  2.1 4.9 %collective-permute-start = (bf16[4,80,256]{2,1,0:T(8,128)(2,1)S(1)}, bf16[4,80,256]{2,1,0:T(8,128)(2,1)S(1)}, u32[]{:S(2)}, u32[]{:S(2)}) collective-permute-start(bf16[4,80,256]{2,1,0:T(8,128)(2,1)S(1)} %get-tuple-element.29), channel_id=1, source_target_pairs={{0,4},{4,8},{8,12},{12,16},{16,20},{20,24},{24,28},{1,5},{5,9},{9,... | collective-permute-start | bytes 491528 | tf_op jit(solution)/shard_map/ppermute | solution.py:301
  6.9 1.3 %collective-permute-start.1 = (bf16[4,80,256]{2,1,0:T(8,128)(2,1)S(1)}, bf16[4,80,256]{2,1,0:T(8,128)(2,1)S(1)}, u32[]{:S(2)}, u32[]{:S(2)}) collective-permute-start(bf16[4,80,256]{2,1,0:T(8,128)(2,1)S(1)} %get-tuple-element.30), channel_id=1, source_target_pairs={{4,0},{8,4},{12,8},{16,12},{20,16},{24,20},{28,24},{5,1},{9,5},{13... | collective-permute-start | bytes 491528 | tf_op jit(solution)/shard_map/ppermute | solution.py:301
  8.2 3.1 %smooth_inner.1 = (bf16[16,64,128]{2,1,0:T(8,128)(2,1)S(1)}, f32[2,4,2,64,256]{4,3,2,1,0:T(8,128)S(1)}) custom-call(bf16[1024,256]{1,0:T(8,128)(2,1)S(1)} %bitcast.54, f32[16,256]{1,0:T(8,128)S(1)} %copy-done.3), custom_call_target="tpu_custom_call" | custom-call | tf_op jit(solution)/shard_map/smooth_inner/pallas_call | solution.py:345
  11.4 1.6 %collective-permute-start.14 = (bf16[16,64,128]{2,1,0:T(8,128)(2,1)S(1)}, bf16[16,64,128]{2,1,0:T(8,128)(2,1)S(1)}, u32[]{:S(2)}, u32[]{:S(2)}) collective-permute-start(bf16[16,64,128]{2,1,0:T(8,128)(2,1)S(1)} %get-tuple-element.32.near_in), channel_id=1, source_target_pairs={{0,2},{1,3},{2,0},{3,1},{4,6},{5,7},{6,4},{7,5},{8,10},{9,11},{10,... | collective-permute-start | bytes 786440 | tf_op jit(solution)/shard_map/ppermute | solution.py:290
  13.0 1.5 %collective-permute-done.1.below_ref = bf16[4,80,256]{2,1,0:T(8,128)(2,1)S(1)} collective-permute-done((bf16[4,80,256]{2,1,0:T(8,128)(2,1)S(1)}, bf16[4,80,256]{2,1,0:T(8,128)(2,1)S(1)}, u32[]{:S(2)}, u32[]{:S(2)}) %collective-permute-start.1) | collective-permute-done | bytes 163872 | tf_op jit(solution)/shard_map/ppermute | solution.py:301
  14.5 2.5 %smooth_outer.1.after_ref.near_out = bf16[16,64,128]{2,1,0:T(8,128)(2,1)S(1)} custom-call(f32[16,256]{1,0:T(8,128)S(1)} %copy-done.3, bf16[4,80,256]{2,1,0:T(8,128)(2,1)S(1)} %collective-permute-done.above_ref, bf16[4,80,256]{2,1,0:T(8,128)(2,1)S(1)} %collective-permute-done.1.below_ref, f32[2,4,2,64,256]{4,3,2,1,0:T(8,128)S(1)} %get-tuple-element.31.state_ref), custom_call_target="tpu_custom_call" | custom-call | tf_op jit(solution)/shard_map/smooth_outer/pallas_call | solution.py:358
  17.1 1.6 %collective-permute-start.4 = (bf16[16,64,128]{2,1,0:T(8,128)(2,1)S(1)}, bf16[16,64,128]{2,1,0:T(8,128)(2,1)S(1)}, u32[]{:S(2)}, u32[]{:S(2)}) collective-permute-start(bf16[16,64,128]{2,1,0:T(8,128)(2,1)S(1)} %smooth_outer.1.after_ref.near_out), channel_id=1, source_target_pairs={{0,2},{1,3},{2,0},{3,1},{4,6},{5,7},{6,4},{7,5},{8,10},{9,11},{10,... | collective-permute-start | bytes 786440 | tf_op jit(solution)/shard_map/ppermute | solution.py:290
  19.4 2.8 %hold.3.held = bf16[192,128,128]{2,1,0:T(8,128)(2,1)S(1)} custom-call(bf16[192,128,128]{2,1,0:T(8,128)(2,1)} %bitcast.65, bf16[16,64,128]{2,1,0:T(8,128)(2,1)S(1)} %smooth_outer.1.after_ref.near_out), custom_call_target="tpu_custom_call" | custom-call | bytes 12582912 | tf_op jit(solution)/shard_map/hold/pallas_call | solution.py:328
  22.5 4.0 %forward_kernel.2 = (bf16[8,128,128]{2,1,0:T(8,128)(2,1)S(1)}, bf16[8,128,128]{2,1,0:T(8,128)(2,1)S(1)}) custom-call(s32[192]{0:T(256)S(1)} %bitcast.57, s32[192]{0:T(256)S(1)} %bitcast.61, s32[1]{0:T(128)} %bitcast.48.count, s32[2]{0:T(128)S(1)} %pad_add_fusion.place, bf16[192,128,128]{2,1,0:T(8,128)(2,1)S(1)} %hold.3.held, ...), custom_call_target="tpu_custom_call" | custom-call | flops 805306368 | bytes 6291456 | tf_op jit(solution)/shard_map/forward_kernel/pallas_call | solution.py:379
  26.9 2.4 %collective-permute-start.5 = (bf16[8,128,128]{2,1,0:T(8,128)(2,1)S(1)}, bf16[8,128,128]{2,1,0:T(8,128)(2,1)S(1)}, u32[]{:S(2)}, u32[]{:S(2)}) collective-permute-start(bf16[8,128,128]{2,1,0:T(8,128)(2,1)S(1)} %get-tuple-element.35.after_ref), channel_id=1, source_target_pairs={{0,4},{4,0},{8,12},{12,8},{16,20},{20,16},{24,28},{28,24},{1,5},{5... | collective-permute-start | bytes 786440 | tf_op jit(solution)/shard_map/ppermute | solution.py:290
  29.3 2.8 %hold.5.held = bf16[192,128,128]{2,1,0:T(8,128)(2,1)S(1)} custom-call(bf16[192,128,128]{2,1,0:T(8,128)(2,1)} %bitcast.66, bf16[8,128,128]{2,1,0:T(8,128)(2,1)S(1)} %get-tuple-element.35.after_ref), custom_call_target="tpu_custom_call" | custom-call | bytes 12582912 | tf_op jit(solution)/shard_map/hold/pallas_call | solution.py:328
  32.2 4.1 %forward_kernel.3 = (bf16[8,128,128]{2,1,0:T(8,128)(2,1)S(1)}, bf16[8,128,128]{2,1,0:T(8,128)(2,1)S(1)}) custom-call(s32[192]{0:T(256)S(1)} %bitcast.58, s32[192]{0:T(256)S(1)} %bitcast.62, s32[1]{0:T(128)} %bitcast.50.count, s32[2]{0:T(128)S(1)} %pad_add_fusion.place, bf16[192,128,128]{2,1,0:T(8,128)(2,1)S(1)} %hold.5.held, ...), custom_call_target="tpu_custom_call" | custom-call | flops 805306368 | bytes 6291456 | tf_op jit(solution)/shard_map/forward_kernel/pallas_call | solution.py:379
  36.5 3.5 %collective-permute-start.6 = (bf16[256,128]{1,0:T(8,128)(2,1)S(1)}, bf16[256,128]{1,0:T(8,128)(2,1)S(1)}, u32[]{:S(2)}, u32[]{:S(2)}) collective-permute-start(bf16[256,128]{1,0:T(8,128)(2,1)S(1)} %get-tuple-element.58), channel_id=1, source_target_pairs={{0,16},{4,20},{8,24},{12,28},{16,0},{20,4},{24,8},{28,12},{1,17},{... | collective-permute-start | bytes 196616 | tf_op jit(solution)/shard_map/ppermute | solution.py:290
  40.0 1.6 %collective-permute-start.8 = (bf16[256,128]{1,0:T(8,128)(2,1)S(1)}, bf16[256,128]{1,0:T(8,128)(2,1)S(1)}, u32[]{:S(2)}, u32[]{:S(2)}) collective-permute-start(bf16[256,128]{1,0:T(8,128)(2,1)S(1)} %get-tuple-element.59), channel_id=1, source_target_pairs={{0,8},{4,12},{8,0},{12,4},{16,24},{20,28},{24,16},{28,20},{1,9},{5... | collective-permute-start | bytes 196616 | tf_op jit(solution)/shard_map/ppermute | solution.py:290
  41.6 2.9 %collective-permute-done.17 = bf16[8,128,128]{2,1,0:T(8,128)(2,1)S(1)} collective-permute-done((bf16[8,128,128]{2,1,0:T(8,128)(2,1)S(1)}, bf16[8,128,128]{2,1,0:T(8,128)(2,1)S(1)}, u32[]{:S(2)}, u32[]{:S(2)}) %collective-permute-start.17) | collective-permute-done | bytes 262176 | tf_op jit(solution)/shard_map/ppermute | solution.py:290
  44.6 2.7 %collective-permute-start.18 = (bf16[256,128]{1,0:T(8,128)(2,1)S(1)}, bf16[256,128]{1,0:T(8,128)(2,1)S(1)}, u32[]{:S(2)}, u32[]{:S(2)}) collective-permute-start(bf16[256,128]{1,0:T(8,128)(2,1)S(1)} %get-tuple-element.55), channel_id=1, source_target_pairs={{0,16},{4,20},{8,24},{12,28},{16,0},{20,4},{24,8},{28,12},{1,17},{... | collective-permute-start | bytes 196616 | tf_op jit(solution)/shard_map/ppermute | solution.py:290
  49.9 1.9 %collective-permute-done.20 = bf16[256,128]{1,0:T(8,128)(2,1)S(1)} collective-permute-done((bf16[256,128]{1,0:T(8,128)(2,1)S(1)}, bf16[256,128]{1,0:T(8,128)(2,1)S(1)}, u32[]{:S(2)}, u32[]{:S(2)}) %collective-permute-start.20) | collective-permute-done | bytes 65568 | tf_op jit(solution)/shard_map/ppermute | solution.py:290
  51.9 2.1 %collective-permute-done.19 = bf16[256,128]{1,0:T(8,128)(2,1)S(1)} collective-permute-done((bf16[256,128]{1,0:T(8,128)(2,1)S(1)}, bf16[256,128]{1,0:T(8,128)(2,1)S(1)}, u32[]{:S(2)}, u32[]{:S(2)}) %collective-permute-start.19) | collective-permute-done | bytes 65568 | tf_op jit(solution)/shard_map/ppermute | solution.py:290
  55.4 3.2 %collective-permute-start.9 = (bf16[256,128]{1,0:T(8,128)(2,1)S(1)}, bf16[256,128]{1,0:T(8,128)(2,1)S(1)}, u32[]{:S(2)}, u32[]{:S(2)}) collective-permute-start(bf16[256,128]{1,0:T(8,128)(2,1)S(1)} %get-tuple-element.62.after_ref), channel_id=1, source_target_pairs={{0,8},{4,12},{8,0},{12,4},{16,24},{20,28},{24,16},{28,20},{1,9},{5... | collective-permute-start | bytes 196616 | tf_op jit(solution)/shard_map/ppermute | solution.py:290
  60.4 2.5 %collective-permute-start.21 = (bf16[256,128]{1,0:T(8,128)(2,1)S(1)}, bf16[256,128]{1,0:T(8,128)(2,1)S(1)}, u32[]{:S(2)}, u32[]{:S(2)}) collective-permute-start(bf16[256,128]{1,0:T(8,128)(2,1)S(1)} %get-tuple-element.61), channel_id=1, source_target_pairs={{0,8},{4,12},{8,0},{12,4},{16,24},{20,28},{24,16},{28,20},{1,9},{5... | collective-permute-start | bytes 196616 | tf_op jit(solution)/shard_map/ppermute | solution.py:290
  63.9 1.5 %collective-permute-start.12 = (bf16[4,256,128]{2,1,0:T(8,128)(2,1)S(1)}, bf16[4,256,128]{2,1,0:T(8,128)(2,1)S(1)}, u32[]{:S(2)}, u32[]{:S(2)}) collective-permute-start(bf16[4,256,128]{2,1,0:T(8,128)(2,1)S(1)} %pad_maximum_fusion.mine_ref), channel_id=1, source_target_pairs={{0,4},{4,0},{8,12},{12,8},{16,20},{20,16},{24,28},{28,24},{1,5},{5... | collective-permute-start | bytes 786440 | tf_op jit(solution)/shard_map/ppermute | solution.py:290
  65.4 1.4 %collective-permute-done.22 = bf16[256,128]{1,0:T(8,128)(2,1)S(1)} collective-permute-done((bf16[256,128]{1,0:T(8,128)(2,1)S(1)}, bf16[256,128]{1,0:T(8,128)(2,1)S(1)}, u32[]{:S(2)}, u32[]{:S(2)}) %collective-permute-start.22) | collective-permute-done | bytes 65568 | tf_op jit(solution)/shard_map/ppermute | solution.py:290
  66.8 1.5 %collective-permute-start.24 = (bf16[4,256,128]{2,1,0:T(8,128)(2,1)S(1)}, bf16[4,256,128]{2,1,0:T(8,128)(2,1)S(1)}, u32[]{:S(2)}, u32[]{:S(2)}) collective-permute-start(bf16[4,256,128]{2,1,0:T(8,128)(2,1)S(1)} %pad_maximum_fusion.1.mine_ref), channel_id=1, source_target_pairs={{0,4},{4,0},{8,12},{12,8},{16,20},{20,16},{24,28},{28,24},{1,5},{5... | collective-permute-start | bytes 786440 | tf_op jit(solution)/shard_map/ppermute | solution.py:290
  68.3 2.8 %hold.4.held = bf16[192,128,128]{2,1,0:T(8,128)(2,1)S(1)} custom-call(bf16[192,128,128]{2,1,0:T(8,128)(2,1)} %bitcast.67, bf16[256,128]{1,0:T(8,128)(2,1)S(1)} %get-tuple-element.62.after_ref), custom_call_target="tpu_custom_call" | custom-call | bytes 12582912 | tf_op jit(solution)/shard_map/hold/pallas_call | solution.py:328
  71.1 1.8 %collective-permute-done.12.theirs_ref = bf16[4,256,128]{2,1,0:T(8,128)(2,1)S(1)} collective-permute-done((bf16[4,256,128]{2,1,0:T(8,128)(2,1)S(1)}, bf16[4,256,128]{2,1,0:T(8,128)(2,1)S(1)}, u32[]{:S(2)}, u32[]{:S(2)}) %collective-permute-start.12) | collective-permute-done | bytes 262176 | tf_op jit(solution)/shard_map/ppermute | solution.py:290
  72.8 3.8 %adjoint_kernel.2 = (bf16[16,64,128]{2,1,0:T(8,128)(2,1)S(1)}, bf16[16,64,128]{2,1,0:T(8,128)(2,1)S(1)}, bf16[16,64,128]{2,1,0:T(8,128)(2,1)S(1)}, bf16[16,64,128]{2,1,0:T(8,128)(2,1)S(1)}) custom-call(s32[192]{0:T(256)S(1)} %bitcast.59, s32[192]{0:T(256)S(1)} %bitcast.63, s32[1]{0:T(128)} %bitcast.49.count, s32[2]{0:T(128)S(1)} %pad_add_fusion.place, ...), custom_call_target="tpu_custom_call" | custom-call | flops 805306368 | bytes 6291456 | tf_op jit(solution)/shard_map/adjoint_kernel/pallas_call | solution.py:379
  76.6 3.8 %adjoint_kernel.3 = (bf16[16,64,128]{2,1,0:T(8,128)(2,1)S(1)}, bf16[16,64,128]{2,1,0:T(8,128)(2,1)S(1)}, bf16[16,64,128]{2,1,0:T(8,128)(2,1)S(1)}, bf16[16,64,128]{2,1,0:T(8,128)(2,1)S(1)}) custom-call(s32[192]{0:T(256)S(1)} %bitcast.60, s32[192]{0:T(256)S(1)} %bitcast.64, s32[1]{0:T(128)} %bitcast.51.count, s32[2]{0:T(128)S(1)} %pad_add_fusion.place, ...), custom_call_target="tpu_custom_call" | custom-call | flops 805306368 | bytes 6291456 | tf_op jit(solution)/shard_map/adjoint_kernel/pallas_call | solution.py:379
  82.5 1.9 %collective-permute-start.31 = (bf16[16,64,128]{2,1,0:T(8,128)(2,1)S(1)}, bf16[16,64,128]{2,1,0:T(8,128)(2,1)S(1)}, u32[]{:S(2)}, u32[]{:S(2)}) collective-permute-start(bf16[16,64,128]{2,1,0:T(8,128)(2,1)S(1)} %add_convert_fusion), channel_id=1, source_target_pairs={{0,2},{1,3},{2,0},{3,1},{4,6},{5,7},{6,4},{7,5},{8,10},{9,11},{10,... | collective-permute-start | bytes 786440 | tf_op jit(solution)/shard_map/ppermute | solution.py:290
  84.4 7.0 %collective-permute-done.26.far_out = bf16[16,64,128]{2,1,0:T(8,128)(2,1)S(1)} collective-permute-done((bf16[16,64,128]{2,1,0:T(8,128)(2,1)S(1)}, bf16[16,64,128]{2,1,0:T(8,128)(2,1)S(1)}, u32[]{:S(2)}, u32[]{:S(2)}) %collective-permute-start.26) | collective-permute-done | bytes 262176 | tf_op jit(solution)/shard_map/ppermute | solution.py:290
  92.8 4.6 %collective-permute-start.27 = (bf16[8,64,128]{2,1,0:T(8,128)(2,1)S(1)}, bf16[8,64,128]{2,1,0:T(8,128)(2,1)S(1)}, u32[]{:S(2)}, u32[]{:S(2)}) collective-permute-start(bf16[8,64,128]{2,1,0:T(8,128)(2,1)S(1)} %get-tuple-element.54), channel_id=1, source_target_pairs={{0,4},{4,8},{8,12},{12,16},{16,20},{20,24},{24,28},{1,5},{5,9},{9,... | collective-permute-start | bytes 393224 | tf_op jit(solution)/shard_map/ppermute | solution.py:301
  97.4 3.5 %back_inner.1 = (f32[2,1024,128]{2,1,0:T(8,128)S(1)}, f32[2,4,2,64,256]{4,3,2,1,0:T(8,128)S(1)}) custom-call(bf16[1024,256]{1,0:T(8,128)(2,1)S(1)} %bitcast.55, f32[16,256]{1,0:T(8,128)S(1)} %copy-done.4, bf16[16,64,128]{2,1,0:T(8,128)(2,1)S(1)} %get-tuple-element.47.own_in, bf16[16,64,128]{2,1,0:T(8,128)(2,1)S(1)} %collective-permute-done.29.core_in, ...), custom_call_target="tpu_custom_call" | custom-call | tf_op jit(solution)/shard_map/back_inner/pallas_call | solution.py:458
  101.0 4.3 %back_outer.1 = f32[1024,256]{1,0:T(8,128)} custom-call(f32[2]{0:T(128)S(1)} %add_convert_fusion.5.inside, f32[16,256]{1,0:T(8,128)S(1)} %copy-done.4, bf16[4,80,256]{2,1,0:T(8,128)(2,1)S(1)} %collective-permute-done.above_ref, bf16[4,80,256]{2,1,0:T(8,128)(2,1)S(1)} %collective-permute-done.1.below_ref, ...), custom_call_target="tpu_custom_call" | custom-call | tf_op jit(solution)/shard_map/back_outer/pallas_call | solution.py:467
  (72 shorter events, 13.7 us)
Async XLA Ops:
  2.1 10.9 %collective-permute-start = (bf16[4,80,256]{2,1,0:T(8,128)(2,1)S(1)}, bf16[4,80,256]{2,1,0:T(8,128)(2,1)S(1)}, u32[]{:S(2)}, u32[]{:S(2)}) collective-permute-start(bf16[4,80,256]{2,1,0:T(8,128)(2,1)S(1)} %get-tuple-element.29), channel_id=1, source_target_pairs={{0,4},{4,8},{8,12},{12,16},{16,20},{20,24},{24,28},{1,5},{5,9},{9,... | collective-permute-start | bytes 491528 | tf_op jit(solution)/shard_map/ppermute | solution.py:301
  6.9 7.6 %collective-permute-start.1 = (bf16[4,80,256]{2,1,0:T(8,128)(2,1)S(1)}, bf16[4,80,256]{2,1,0:T(8,128)(2,1)S(1)}, u32[]{:S(2)}, u32[]{:S(2)}) collective-permute-start(bf16[4,80,256]{2,1,0:T(8,128)(2,1)S(1)} %get-tuple-element.30), channel_id=1, source_target_pairs={{4,0},{8,4},{12,8},{16,12},{20,16},{24,20},{28,24},{5,1},{9,5},{13... | collective-permute-start | bytes 491528 | tf_op jit(solution)/shard_map/ppermute | solution.py:301
  11.4 10.8 %collective-permute-start.14 = (bf16[16,64,128]{2,1,0:T(8,128)(2,1)S(1)}, bf16[16,64,128]{2,1,0:T(8,128)(2,1)S(1)}, u32[]{:S(2)}, u32[]{:S(2)}) collective-permute-start(bf16[16,64,128]{2,1,0:T(8,128)(2,1)S(1)} %get-tuple-element.32.near_in), channel_id=1, source_target_pairs={{0,2},{1,3},{2,0},{3,1},{4,6},{5,7},{6,4},{7,5},{8,10},{9,11},{10,... | collective-permute-start | bytes 786440 | tf_op jit(solution)/shard_map/ppermute | solution.py:290
  13.0 9.5 %collective-permute-start.2 = (bf16[16,64,128]{2,1,0:T(8,128)(2,1)S(1)}, bf16[16,64,128]{2,1,0:T(8,128)(2,1)S(1)}, u32[]{:S(2)}, u32[]{:S(2)}) collective-permute-start(bf16[16,64,128]{2,1,0:T(8,128)(2,1)S(1)} %get-tuple-element.32.near_in), channel_id=1, source_target_pairs={{0,1},{1,0},{2,3},{3,2},{4,5},{5,4},{6,7},{7,6},{8,9},{9,8},{10,11... | collective-permute-start | bytes 786440 | tf_op jit(solution)/shard_map/ppermute | solution.py:290
  17.0 5.5 %collective-permute-start.3 = (bf16[16,64,128]{2,1,0:T(8,128)(2,1)S(1)}, bf16[16,64,128]{2,1,0:T(8,128)(2,1)S(1)}, u32[]{:S(2)}, u32[]{:S(2)}) collective-permute-start(bf16[16,64,128]{2,1,0:T(8,128)(2,1)S(1)} %smooth_outer.1.after_ref.near_out), channel_id=1, source_target_pairs={{0,1},{1,0},{2,3},{3,2},{4,5},{5,4},{6,7},{7,6},{8,9},{9,8},{10,11... | collective-permute-start | bytes 786440 | tf_op jit(solution)/shard_map/ppermute | solution.py:290
  17.1 9.4 %collective-permute-start.4 = (bf16[16,64,128]{2,1,0:T(8,128)(2,1)S(1)}, bf16[16,64,128]{2,1,0:T(8,128)(2,1)S(1)}, u32[]{:S(2)}, u32[]{:S(2)}) collective-permute-start(bf16[16,64,128]{2,1,0:T(8,128)(2,1)S(1)} %smooth_outer.1.after_ref.near_out), channel_id=1, source_target_pairs={{0,2},{1,3},{2,0},{3,1},{4,6},{5,7},{6,4},{7,5},{8,10},{9,11},{10,... | collective-permute-start | bytes 786440 | tf_op jit(solution)/shard_map/ppermute | solution.py:290
  22.2 9.9 %collective-permute-start.15 = (bf16[16,64,128]{2,1,0:T(8,128)(2,1)S(1)}, bf16[16,64,128]{2,1,0:T(8,128)(2,1)S(1)}, u32[]{:S(2)}, u32[]{:S(2)}) collective-permute-start(bf16[16,64,128]{2,1,0:T(8,128)(2,1)S(1)} %collective-permute-done.14.near_in), channel_id=1, source_target_pairs={{0,1},{1,0},{2,3},{3,2},{4,5},{5,4},{6,7},{7,6},{8,9},{9,8},{10,11... | collective-permute-start | bytes 786440 | tf_op jit(solution)/shard_map/ppermute | solution.py:290
  26.5 5.7 %collective-permute-start.16 = (bf16[16,64,128]{2,1,0:T(8,128)(2,1)S(1)}, bf16[16,64,128]{2,1,0:T(8,128)(2,1)S(1)}, u32[]{:S(2)}, u32[]{:S(2)}) collective-permute-start(bf16[16,64,128]{2,1,0:T(8,128)(2,1)S(1)} %collective-permute-done.4.near_out), channel_id=1, source_target_pairs={{0,1},{1,0},{2,3},{3,2},{4,5},{5,4},{6,7},{7,6},{8,9},{9,8},{10,11... | collective-permute-start | bytes 786440 | tf_op jit(solution)/shard_map/ppermute | solution.py:290
  26.9 9.4 %collective-permute-start.5 = (bf16[8,128,128]{2,1,0:T(8,128)(2,1)S(1)}, bf16[8,128,128]{2,1,0:T(8,128)(2,1)S(1)}, u32[]{:S(2)}, u32[]{:S(2)}) collective-permute-start(bf16[8,128,128]{2,1,0:T(8,128)(2,1)S(1)} %get-tuple-element.35.after_ref), channel_id=1, source_target_pairs={{0,4},{4,0},{8,12},{12,8},{16,20},{20,16},{24,28},{28,24},{1,5},{5... | collective-permute-start | bytes 786440 | tf_op jit(solution)/shard_map/ppermute | solution.py:290
  36.3 8.2 %collective-permute-start.17 = (bf16[8,128,128]{2,1,0:T(8,128)(2,1)S(1)}, bf16[8,128,128]{2,1,0:T(8,128)(2,1)S(1)}, u32[]{:S(2)}, u32[]{:S(2)}) collective-permute-start(bf16[8,128,128]{2,1,0:T(8,128)(2,1)S(1)} %get-tuple-element.40), channel_id=1, source_target_pairs={{0,4},{4,0},{8,12},{12,8},{16,20},{20,16},{24,28},{28,24},{1,5},{5... | collective-permute-start | bytes 786440 | tf_op jit(solution)/shard_map/ppermute | solution.py:290
  36.5 11.4 %collective-permute-start.6 = (bf16[256,128]{1,0:T(8,128)(2,1)S(1)}, bf16[256,128]{1,0:T(8,128)(2,1)S(1)}, u32[]{:S(2)}, u32[]{:S(2)}) collective-permute-start(bf16[256,128]{1,0:T(8,128)(2,1)S(1)} %get-tuple-element.58), channel_id=1, source_target_pairs={{0,16},{4,20},{8,24},{12,28},{16,0},{20,4},{24,8},{28,12},{1,17},{... | collective-permute-start | bytes 196616 | tf_op jit(solution)/shard_map/ppermute | solution.py:290
  40.0 9.1 %collective-permute-start.8 = (bf16[256,128]{1,0:T(8,128)(2,1)S(1)}, bf16[256,128]{1,0:T(8,128)(2,1)S(1)}, u32[]{:S(2)}, u32[]{:S(2)}) collective-permute-start(bf16[256,128]{1,0:T(8,128)(2,1)S(1)} %get-tuple-element.59), channel_id=1, source_target_pairs={{0,8},{4,12},{8,0},{12,4},{16,24},{20,28},{24,16},{28,20},{1,9},{5... | collective-permute-start | bytes 196616 | tf_op jit(solution)/shard_map/ppermute | solution.py:290
  41.6 7.5 %collective-permute-start.7 = (bf16[256,128]{1,0:T(8,128)(2,1)S(1)}, bf16[256,128]{1,0:T(8,128)(2,1)S(1)}, u32[]{:S(2)}, u32[]{:S(2)}) collective-permute-start(bf16[256,128]{1,0:T(8,128)(2,1)S(1)} %get-tuple-element.60), channel_id=1, source_target_pairs={{0,24},{4,28},{8,16},{12,20},{16,8},{20,12},{24,0},{28,4},{1,25},{... | collective-permute-start | bytes 196616 | tf_op jit(solution)/shard_map/ppermute | solution.py:290
  44.6 5.4 %collective-permute-start.18 = (bf16[256,128]{1,0:T(8,128)(2,1)S(1)}, bf16[256,128]{1,0:T(8,128)(2,1)S(1)}, u32[]{:S(2)}, u32[]{:S(2)}) collective-permute-start(bf16[256,128]{1,0:T(8,128)(2,1)S(1)} %get-tuple-element.55), channel_id=1, source_target_pairs={{0,16},{4,20},{8,24},{12,28},{16,0},{20,4},{24,8},{28,12},{1,17},{... | collective-permute-start | bytes 196616 | tf_op jit(solution)/shard_map/ppermute | solution.py:290
  47.2 4.6 %collective-permute-start.20 = (bf16[256,128]{1,0:T(8,128)(2,1)S(1)}, bf16[256,128]{1,0:T(8,128)(2,1)S(1)}, u32[]{:S(2)}, u32[]{:S(2)}) collective-permute-start(bf16[256,128]{1,0:T(8,128)(2,1)S(1)} %get-tuple-element.56), channel_id=1, source_target_pairs={{0,8},{4,12},{8,0},{12,4},{16,24},{20,28},{24,16},{28,20},{1,9},{5... | collective-permute-start | bytes 196616 | tf_op jit(solution)/shard_map/ppermute | solution.py:290
  47.9 6.1 %collective-permute-start.19 = (bf16[256,128]{1,0:T(8,128)(2,1)S(1)}, bf16[256,128]{1,0:T(8,128)(2,1)S(1)}, u32[]{:S(2)}, u32[]{:S(2)}) collective-permute-start(bf16[256,128]{1,0:T(8,128)(2,1)S(1)} %get-tuple-element.57), channel_id=1, source_target_pairs={{0,24},{4,28},{8,16},{12,20},{16,8},{20,12},{24,0},{28,4},{1,25},{... | collective-permute-start | bytes 196616 | tf_op jit(solution)/shard_map/ppermute | solution.py:290
  54.1 6.4 %collective-permute-start.11 = (bf16[256,128]{1,0:T(8,128)(2,1)S(1)}, bf16[256,128]{1,0:T(8,128)(2,1)S(1)}, u32[]{:S(2)}, u32[]{:S(2)}) collective-permute-start(bf16[256,128]{1,0:T(8,128)(2,1)S(1)} %get-tuple-element.62.after_ref), channel_id=1, source_target_pairs={{0,24},{4,28},{8,16},{12,20},{16,8},{20,12},{24,0},{28,4},{1,25},{... | collective-permute-start | bytes 196616 | tf_op jit(solution)/shard_map/ppermute | solution.py:290
  55.3 8.5 %collective-permute-start.10 = (bf16[256,128]{1,0:T(8,128)(2,1)S(1)}, bf16[256,128]{1,0:T(8,128)(2,1)S(1)}, u32[]{:S(2)}, u32[]{:S(2)}) collective-permute-start(bf16[256,128]{1,0:T(8,128)(2,1)S(1)} %get-tuple-element.62.after_ref), channel_id=1, source_target_pairs={{0,16},{4,20},{8,24},{12,28},{16,0},{20,4},{24,8},{28,12},{1,17},{... | collective-permute-start | bytes 196616 | tf_op jit(solution)/shard_map/ppermute | solution.py:290
  55.4 8.5 %collective-permute-start.9 = (bf16[256,128]{1,0:T(8,128)(2,1)S(1)}, bf16[256,128]{1,0:T(8,128)(2,1)S(1)}, u32[]{:S(2)}, u32[]{:S(2)}) collective-permute-start(bf16[256,128]{1,0:T(8,128)(2,1)S(1)} %get-tuple-element.62.after_ref), channel_id=1, source_target_pairs={{0,8},{4,12},{8,0},{12,4},{16,24},{20,28},{24,16},{28,20},{1,9},{5... | collective-permute-start | bytes 196616 | tf_op jit(solution)/shard_map/ppermute | solution.py:290
  58.5 6.9 %collective-permute-start.23 = (bf16[256,128]{1,0:T(8,128)(2,1)S(1)}, bf16[256,128]{1,0:T(8,128)(2,1)S(1)}, u32[]{:S(2)}, u32[]{:S(2)}) collective-permute-start(bf16[256,128]{1,0:T(8,128)(2,1)S(1)} %get-tuple-element.61), channel_id=1, source_target_pairs={{0,24},{4,28},{8,16},{12,20},{16,8},{20,12},{24,0},{28,4},{1,25},{... | collective-permute-start | bytes 196616 | tf_op jit(solution)/shard_map/ppermute | solution.py:290
  59.7 7.0 %collective-permute-start.22 = (bf16[256,128]{1,0:T(8,128)(2,1)S(1)}, bf16[256,128]{1,0:T(8,128)(2,1)S(1)}, u32[]{:S(2)}, u32[]{:S(2)}) collective-permute-start(bf16[256,128]{1,0:T(8,128)(2,1)S(1)} %get-tuple-element.61), channel_id=1, source_target_pairs={{0,16},{4,20},{8,24},{12,28},{16,0},{20,4},{24,8},{28,12},{1,17},{... | collective-permute-start | bytes 196616 | tf_op jit(solution)/shard_map/ppermute | solution.py:290
  60.4 6.3 %collective-permute-start.21 = (bf16[256,128]{1,0:T(8,128)(2,1)S(1)}, bf16[256,128]{1,0:T(8,128)(2,1)S(1)}, u32[]{:S(2)}, u32[]{:S(2)}) collective-permute-start(bf16[256,128]{1,0:T(8,128)(2,1)S(1)} %get-tuple-element.61), channel_id=1, source_target_pairs={{0,8},{4,12},{8,0},{12,4},{16,24},{20,28},{24,16},{28,20},{1,9},{5... | collective-permute-start | bytes 196616 | tf_op jit(solution)/shard_map/ppermute | solution.py:290
  63.9 8.9 %collective-permute-start.12 = (bf16[4,256,128]{2,1,0:T(8,128)(2,1)S(1)}, bf16[4,256,128]{2,1,0:T(8,128)(2,1)S(1)}, u32[]{:S(2)}, u32[]{:S(2)}) collective-permute-start(bf16[4,256,128]{2,1,0:T(8,128)(2,1)S(1)} %pad_maximum_fusion.mine_ref), channel_id=1, source_target_pairs={{0,4},{4,0},{8,12},{12,8},{16,20},{20,16},{24,28},{28,24},{1,5},{5... | collective-permute-start | bytes 786440 | tf_op jit(solution)/shard_map/ppermute | solution.py:290
  66.8 9.8 %collective-permute-start.24 = (bf16[4,256,128]{2,1,0:T(8,128)(2,1)S(1)}, bf16[4,256,128]{2,1,0:T(8,128)(2,1)S(1)}, u32[]{:S(2)}, u32[]{:S(2)}) collective-permute-start(bf16[4,256,128]{2,1,0:T(8,128)(2,1)S(1)} %pad_maximum_fusion.1.mine_ref), channel_id=1, source_target_pairs={{0,4},{4,0},{8,12},{12,8},{16,20},{20,16},{24,28},{28,24},{1,5},{5... | collective-permute-start | bytes 786440 | tf_op jit(solution)/shard_map/ppermute | solution.py:290
  80.4 1.6 %collective-permute-start.25 = (bf16[16,64,128]{2,1,0:T(8,128)(2,1)S(1)}, bf16[16,64,128]{2,1,0:T(8,128)(2,1)S(1)}, u32[]{:S(2)}, u32[]{:S(2)}) collective-permute-start(bf16[16,64,128]{2,1,0:T(8,128)(2,1)S(1)} %get-tuple-element.46), channel_id=1, source_target_pairs={{0,1},{1,0},{2,3},{3,2},{4,5},{5,4},{6,7},{7,6},{8,9},{9,8},{10,11... | collective-permute-start | bytes 786440 | tf_op jit(solution)/shard_map/ppermute | solution.py:290
  80.5 1.9 %collective-permute-start.30 = (bf16[16,64,128]{2,1,0:T(8,128)(2,1)S(1)}, bf16[16,64,128]{2,1,0:T(8,128)(2,1)S(1)}, u32[]{:S(2)}, u32[]{:S(2)}) collective-permute-start(bf16[16,64,128]{2,1,0:T(8,128)(2,1)S(1)} %get-tuple-element.50), channel_id=1, source_target_pairs={{0,1},{1,0},{2,3},{3,2},{4,5},{5,4},{6,7},{7,6},{8,9},{9,8},{10,11... | collective-permute-start | bytes 786440 | tf_op jit(solution)/shard_map/ppermute | solution.py:290
  81.0 3.4 %collective-permute-start.13 = (bf16[16,64,128]{2,1,0:T(8,128)(2,1)S(1)}, bf16[16,64,128]{2,1,0:T(8,128)(2,1)S(1)}, u32[]{:S(2)}, u32[]{:S(2)}) collective-permute-start(bf16[16,64,128]{2,1,0:T(8,128)(2,1)S(1)} %get-tuple-element.37), channel_id=1, source_target_pairs={{0,1},{1,0},{2,3},{3,2},{4,5},{5,4},{6,7},{7,6},{8,9},{9,8},{10,11... | collective-permute-start | bytes 786440 | tf_op jit(solution)/shard_map/ppermute | solution.py:290
  82.1 9.2 %collective-permute-start.26 = (bf16[16,64,128]{2,1,0:T(8,128)(2,1)S(1)}, bf16[16,64,128]{2,1,0:T(8,128)(2,1)S(1)}, u32[]{:S(2)}, u32[]{:S(2)}) collective-permute-start(bf16[16,64,128]{2,1,0:T(8,128)(2,1)S(1)} %add_convert_fusion.2), channel_id=1, source_target_pairs={{0,2},{1,3},{2,0},{3,1},{4,6},{5,7},{6,4},{7,5},{8,10},{9,11},{10,... | collective-permute-start | bytes 786440 | tf_op jit(solution)/shard_map/ppermute | solution.py:290
  82.3 15.1 %collective-permute-start.29 = (bf16[16,64,128]{2,1,0:T(8,128)(2,1)S(1)}, bf16[16,64,128]{2,1,0:T(8,128)(2,1)S(1)}, u32[]{:S(2)}, u32[]{:S(2)}) collective-permute-start(bf16[16,64,128]{2,1,0:T(8,128)(2,1)S(1)} %get-tuple-element.48), channel_id=1, source_target_pairs={{0,1},{1,0},{2,3},{3,2},{4,5},{5,4},{6,7},{7,6},{8,9},{9,8},{10,11... | collective-permute-start | bytes 786440 | tf_op jit(solution)/shard_map/ppermute | solution.py:290
  82.5 14.9 %collective-permute-start.31 = (bf16[16,64,128]{2,1,0:T(8,128)(2,1)S(1)}, bf16[16,64,128]{2,1,0:T(8,128)(2,1)S(1)}, u32[]{:S(2)}, u32[]{:S(2)}) collective-permute-start(bf16[16,64,128]{2,1,0:T(8,128)(2,1)S(1)} %add_convert_fusion), channel_id=1, source_target_pairs={{0,2},{1,3},{2,0},{3,1},{4,6},{5,7},{6,4},{7,5},{8,10},{9,11},{10,... | collective-permute-start | bytes 786440 | tf_op jit(solution)/shard_map/ppermute | solution.py:290
  91.5 9.5 %collective-permute-start.28 = (bf16[8,64,128]{2,1,0:T(8,128)(2,1)S(1)}, bf16[8,64,128]{2,1,0:T(8,128)(2,1)S(1)}, u32[]{:S(2)}, u32[]{:S(2)}) collective-permute-start(bf16[8,64,128]{2,1,0:T(8,128)(2,1)S(1)} %get-tuple-element.53), channel_id=1, source_target_pairs={{4,0},{8,4},{12,8},{16,12},{20,16},{24,20},{28,24},{5,1},{9,5},{13... | collective-permute-start | bytes 393224 | tf_op jit(solution)/shard_map/ppermute | solution.py:301
  92.8 8.2 %collective-permute-start.27 = (bf16[8,64,128]{2,1,0:T(8,128)(2,1)S(1)}, bf16[8,64,128]{2,1,0:T(8,128)(2,1)S(1)}, u32[]{:S(2)}, u32[]{:S(2)}) collective-permute-start(bf16[8,64,128]{2,1,0:T(8,128)(2,1)S(1)} %get-tuple-element.54), channel_id=1, source_target_pairs={{0,4},{4,8},{8,12},{12,16},{16,20},{20,24},{24,28},{1,5},{5,9},{9,... | collective-permute-start | bytes 393224 | tf_op jit(solution)/shard_map/ppermute | solution.py:301
  (7 other events, 98.6 us)

commit v5 on v4

--- a/solution.py
+++ b/solution.py
@@ -11,9 +11,15 @@
 SUB = 8
 PIECES = 16
 GROUP = 32
+FETCHES = 4
 F32, BF16 = jnp.float32, jnp.bfloat16
 VMEM = pl.BlockSpec(memory_space=pltpu.VMEM)
 SMEM = pl.BlockSpec(memory_space=pltpu.SMEM)
+HBM = pl.BlockSpec(memory_space=pltpu.HBM)
+
+
+def in_hbm(x):
+    return pltpu.with_memory_space_constraint(x, pltpu.HBM)
 
 
 def params(mib=24):
@@ -27,17 +33,41 @@
 
 def one_row(wide, start, size, rows):
     at = pl.ds(start, size, stride=rows)
-    return jnp.concatenate([wide[h, at, :] for h in range(wide.shape[0])], axis=1)
-
-
-def edge_kernel(probes_ref, kappa_ref, north_ref, south_ref, wide):
+    return [wide[h, at, :] for h in range(wide.shape[0])]
+
+
+def split_row(row):
+    return [row[:, h * BLK : (h + 1) * BLK] for h in range(row.shape[1] // BLK)]
+
+
+def around(north, row, south, lane):
+    east = [pltpu.roll(x, 1, 1) for x in row]
+    west = [pltpu.roll(x, BLK - 1, 1) for x in row]
+    out = []
+    for h, x in enumerate(row):
+        left = jnp.where(lane > 0, east[h], east[h - 1] if h else 0.0)
+        right = jnp.where(lane < BLK - 1, west[h], west[h + 1] if h + 1 < len(row) else 0.0)
+        out.append(((north[h] + south[h]) + (left + right)) - 4.0 * x)
+    return out
+
+
+def edge_kernel(probes_hbm, kappa_hbm, north_ref, south_ref, probes_ref, kappa_ref, wide, arrived):
+    fetches = [
+        pltpu.make_async_copy(probes_hbm, probes_ref, arrived.at[0]),
+        pltpu.make_async_copy(kappa_hbm, kappa_ref, arrived.at[1]),
+    ]
+    for fetch in fetches:
+        fetch.start()
+    for fetch in fetches:
+        fetch.wait()
     rows, lon = kappa_ref.shape
     probe_local = probes_ref.shape[0] // rows
     widen(probes_ref, wide)
     place = lax.broadcasted_iota(jnp.int32, (PIECES, lon), 0)
     for out_ref, first in ((north_ref, 0), (south_ref, rows - SMOOTH)):
         for r in range(SMOOTH):
-            out_ref[r, :probe_local, :] = one_row(wide, first + r, probe_local, rows).astype(BF16)
+            for h, part in enumerate(one_row(wide, first + r, probe_local, rows)):
+                out_ref[r, :probe_local, h * BLK : (h + 1) * BLK] = part.astype(BF16)
             whole = kappa_ref[first + r : first + r + 1, :]
             high = whole.astype(BF16).astype(F32)
             rest = whole - high
@@ -61,30 +91,35 @@
 
 
 def put_row(ref, blk, at, row):
-    for h in range(row.shape[1] // BLK):
-        ref[blk + h, at, :] = row[:, h * BLK : (h + 1) * BLK]
-
-
-def smooth_step(f, coef, lon, r):
-    k, kl, kr = coef[0, r], coef[1, r], coef[2, r]
-    g = f[r]
-    return g + k * (f[r - 1] + f[r + 1] - 4.0 * g) + kl * pltpu.roll(g, 1, 1) + kr * pltpu.roll(g, lon - 1, 1)
-
-
-def smooth_coefficients(coef, kappas, lon):
-    lane = lax.broadcasted_iota(jnp.int32, (SUB, lon), 1)
-    for r, k in enumerate(kappas):
-        k = jnp.broadcast_to(k, (SUB, lon))
-        coef[0, r] = k
-        coef[1, r] = jnp.where(lane > 0, k, 0.0)
-        coef[2, r] = jnp.where(lane < lon - 1, k, 0.0)
+    for h, part in enumerate(row):
+        ref[blk + h, at, :] = part
+
+
+def smooth_step(f, coef, lane, r):
+    lap = around(f[r - 1], f[r], f[r + 1], lane)
+    return [x + coef[r, :, h * BLK : (h + 1) * BLK] * y for h, (x, y) in enumerate(zip(f[r], lap))]
+
+
+def coefficients(coef, kappas):
+    for r, k in kappas:
+        coef[r] = jnp.broadcast_to(k, coef.shape[1:])
+
+
+def lanes():
+    return lax.broadcasted_iota(jnp.int32, (SUB, BLK), 1)
 
 
 def keep_state(state_ref, step, f, at):
     rows = len(f)
-    for i in range(2):
-        state_ref[0, step, i, at, :] = f[step + i]
-        state_ref[1, step, i, at, :] = f[rows - 2 - step + i]
+    for side, first in ((0, step), (1, rows - 2 - step)):
+        for i in range(2):
+            for h, part in enumerate(f[first + i]):
+                state_ref[side, step, i, at, h * BLK : (h + 1) * BLK] = part
+
+
+def outer_rows(kappas):
+    total, reach = len(kappas), 2 * SMOOTH + 1
+    return [(r, k) for r, k in enumerate(kappas) if r < reach or r >= total - reach]
 
 
 def smooth_inner_kernel(probes_ref, kappa_ref, field_ref, state_ref, wide, coef, result):
@@ -92,16 +127,17 @@
     probe_local = probes_ref.shape[0] // rows
     halves = lon // BLK
     widen(probes_ref, wide)
-    smooth_coefficients(coef, [kappa_ref[r : r + 1, :] for r in range(rows)], lon)
-
-    @pl.loop(0, probe_local // SUB)
+    coefficients(coef, [(r, kappa_ref[r : r + 1, :]) for r in range(rows)])
+    lane = lanes()
+
+    @pl.loop(0, probe_local // SUB, unroll=2)
     def _(c):
         base = pl.multiple_of(c * SUB, SUB)
         at = pl.ds(base, SUB)
         f = [one_row(wide, base * rows + r, SUB, rows) for r in range(rows)]
         for step in range(SMOOTH):
             keep_state(state_ref, step, f, at)
-            f = [smooth_step(f, coef, lon, r) if step < r < rows - 1 - step else f[r] for r in range(rows)]
+            f = [smooth_step(f, coef, lane, r) if step < r < rows - 1 - step else f[r] for r in range(rows)]
         for r in range(SMOOTH, rows - SMOOTH):
             put_row(result, (r - SMOOTH) * halves, at, f[r])
 
@@ -109,7 +145,7 @@
 
 
 def side_rows(state_ref, side, step, mine, at):
-    inner = [state_ref[side, step, i, at, :] for i in range(2)]
+    inner = [split_row(state_ref[side, step, i, at, :]) for i in range(2)]
     return mine + inner if side == 0 else inner + mine
 
 
@@ -119,21 +155,22 @@
     halves = lon // BLK
     halos[0] = above_ref[:, :probe_local, :].astype(F32)
     halos[1] = below_ref[:, :probe_local, :].astype(F32)
-    smooth_coefficients(coef, kappa_rows(kappa_ref, above_ref, below_ref, probe_local), lon)
+    coefficients(coef, outer_rows(kappa_rows(kappa_ref, above_ref, below_ref, probe_local)))
+    lane = lanes()
     total = rows + 2 * SMOOTH
 
-    @pl.loop(0, probe_local // SUB)
+    @pl.loop(0, probe_local // SUB, unroll=2)
     def _(c):
         base = pl.multiple_of(c * SUB, SUB)
         at = pl.ds(base, SUB)
         for side in range(2):
-            mine = [halos[side, r, at, :] for r in range(SMOOTH)]
+            mine = [split_row(halos[side, r, at, :]) for r in range(SMOOTH)]
             for step in range(SMOOTH):
                 f = side_rows(state_ref, side, step, mine, at)
                 first = step if side == 0 else total - 6 - step
                 rows_at = dict(enumerate(f, first))
                 new = range(first + 1, first + 5)
-                mine = [smooth_step(rows_at, coef, lon, r) for r in new]
+                mine = [smooth_step(rows_at, coef, lane, r) for r in new]
             for r in range(SMOOTH):
                 put_row(result, (side * SMOOTH + r) * halves, at, mine[r])
 
@@ -154,8 +191,28 @@
 
 
 def forward_kernel(
-    sources, receptors, count, place, held, near_in, near_out, far_in, far_out, keep_ref, give_ref, turned, total
+    sources,
+    receptors,
+    count,
+    place,
+    blocks_ref,
+    near_in,
+    near_out,
+    far_in,
+    far_out,
+    keep_ref,
+    give_ref,
+    turned,
+    total,
+    held,
+    arrived,
 ):
+    fetches = []
+    size = held.shape[0] // FETCHES
+    for g in range(FETCHES):
+        at = pl.ds(g * size, size)
+        fetches.append(pltpu.make_async_copy(blocks_ref.at[at], held.at[at], arrived.at[g]))
+        fetches[g].start()
     total[...] = jnp.zeros_like(total)
     edge = near_out.shape[0] // 2
     for j in range(turned.shape[0]):
@@ -172,7 +229,10 @@
         b = jnp.where(n < count[0], receptors[n], spare)
         total[b] += jnp.dot(held[n], turned[sources[n]], preferred_element_type=F32)
 
-    each_slot(held.shape[0], slot)
+    for g, fetch in enumerate(fetches):
+        fetch.wait()
+        for i in range(size):
+            slot(g * size + i)
     half = keep_ref.shape[0]
     for out_ref, side in ((keep_ref, place[0]), (give_ref, 1 - place[0])):
         for b in range(half):
@@ -206,15 +266,12 @@
         out_ref[edge:] = total[spare - edge : spare, at].astype(BF16)
 
 
-def joined(ref, first, at, halves):
-    return jnp.concatenate([ref[first + h, at, :] for h in range(halves)], axis=1)
-
-
-def back_step(f, g, lane, r):
-    lon = lane.shape[1]
-    west = jnp.where(lane > 0, pltpu.roll(g[r], 1, 1), 0.0)
-    east = jnp.where(lane < lon - 1, pltpu.roll(g[r], lon - 1, 1), 0.0)
-    return g[r - 1] + g[r + 1] + west + east - 4.0 * g[r]
+def block_row(ref, first, at, halves):
+    return [ref[first + h, at, :] for h in range(halves)]
+
+
+def times_kappa(coef, f, r):
+    return [coef[r, :, h * BLK : (h + 1) * BLK] * x for h, x in enumerate(f[r])]
 
 
 def back_inner_kernel(
@@ -230,59 +287,74 @@
     terms[:edge] = outer[:edge]
     terms[edge : terms.shape[0] - edge] = inner
     terms[terms.shape[0] - edge :] = outer[edge:]
-    lane = lax.broadcasted_iota(jnp.int32, (SUB, lon), 1)
-    for r in range(rows):
-        coef[r] = jnp.broadcast_to(kappa_ref[r : r + 1, :], (SUB, lon))
-
-    @pl.loop(0, probe_local // SUB)
+    lane = lanes()
+    coefficients(coef, [(r, kappa_ref[r : r + 1, :]) for r in range(rows)])
+
+    @pl.loop(0, probe_local // SUB, unroll=2)
     def _(c):
         base = pl.multiple_of(c * SUB, SUB)
         at = pl.ds(base, SUB)
-        f = [joined(terms, r * halves, at, halves) for r in range(rows)]
+        f = [block_row(terms, r * halves, at, halves) for r in range(rows)]
         for step in range(SMOOTH):
             keep_state(state_ref, step, f, at)
-            g = {r: coef[r] * f[r] for r in range(step, rows - step)}
-            f = [f[r] + back_step(f, g, lane, r) if step < r < rows - 1 - step else f[r] for r in range(rows)]
+            g = {r: times_kappa(coef, f, r) for r in (step, step + 1)}
+            new = list(f)
+            for r in range(step + 1, rows - 1 - step):
+                g[r + 1] = times_kappa(coef, f, r + 1)
+                new[r] = [x + y for x, y in zip(f[r], around(g[r - 1], g[r], g[r + 1], lane))]
+            f = new
         for r in range(SMOOTH, rows - SMOOTH):
             for h in range(halves):
-                wide[h, pl.ds(base * rows + r, SUB, stride=rows), :] += f[r][:, h * BLK : (h + 1) * BLK]
+                wide[h, pl.ds(base * rows + r, SUB, stride=rows), :] += f[r][h]
 
 
 def back_outer_kernel(
-    inside, kappa_ref, above_ref, below_ref, top_ref, bottom_ref, state_ref, done_ref, out_ref, wide, coef, halos
+    inside, kappa_ref, above_ref, below_ref, top_ref, bottom_ref, state_ref, done_ref, out_hbm, wide, coef, halos, sent
 ):
     rows, lon = kappa_ref.shape
     probe_local = state_ref.shape[3]
     halves = lon // BLK
     total = rows + 2 * SMOOTH
-    wide[...] = done_ref[...]
     halos[0] = top_ref[...].astype(F32)
     halos[1] = bottom_ref[...].astype(F32)
-    lane = lax.broadcasted_iota(jnp.int32, (SUB, lon), 1)
-    for r, k in enumerate(kappa_rows(kappa_ref, above_ref, below_ref, probe_local)):
-        coef[r] = jnp.broadcast_to(k, (SUB, lon))
-
-    @pl.loop(0, probe_local // SUB)
+    lane = lanes()
+    coefficients(coef, outer_rows(kappa_rows(kappa_ref, above_ref, below_ref, probe_local)))
+
+    def sends(c):
+        lines = pl.ds(pl.multiple_of(c * SUB * rows, SUB * rows), SUB * rows)
+        return [
+            pltpu.make_async_copy(wide.at[h, lines], out_hbm.at[lines, h * BLK : (h + 1) * BLK], sent.at[c, h])
+            for h in range(halves)
+        ]
+
+    @pl.loop(0, probe_local // SUB, unroll=2)
     def _(c):
         base = pl.multiple_of(c * SUB, SUB)
         at = pl.ds(base, SUB)
+        lines = pl.ds(pl.multiple_of(base * rows, SUB * rows), SUB * rows)
+        wide[:, lines, :] = done_ref[:, lines, :]
         for side in range(2):
-            mine = [joined(halos.at[side], r * halves, at, halves) for r in range(SMOOTH)]
+            mine = [block_row(halos.at[side], r * halves, at, halves) for r in range(SMOOTH)]
             for step in range(SMOOTH):
                 first = step if side == 0 else total - 6 - step
                 f = dict(enumerate(side_rows(state_ref, side, step, mine, at), first))
-                g = {r: coef[r] * f[r] for r in f}
+                g = {r: times_kappa(coef, f, r) for r in f}
                 mine = []
                 for r in range(first + 1, first + 5):
-                    lap = back_step(f, g, lane, r)
-                    mine.append(f[r] + (lap if SMOOTH <= r < total - SMOOTH else lap * inside[side]))
+                    lap = around(g[r - 1], g[r], g[r + 1], lane)
+                    if not SMOOTH <= r < total - SMOOTH:
+                        lap = [x * inside[side] for x in lap]
+                    mine.append([x + y for x, y in zip(f[r], lap)])
             for r in range(SMOOTH):
                 row = r if side == 0 else rows - SMOOTH + r
                 for h in range(halves):
-                    wide[h, pl.ds(base * rows + row, SUB, stride=rows), :] += mine[r][:, h * BLK : (h + 1) * BLK]
-
-    for h in range(halves):
-        out_ref[:, h * BLK : (h + 1) * BLK] = wide[h]
+                    wide[h, pl.ds(base * rows + row, SUB, stride=rows), :] += mine[r][h]
+        for copy in sends(c):
+            copy.start()
+
+    for c in range(probe_local // SUB):
+        for copy in sends(c):
+            copy.wait()
 
 
 def swap(x, axis, distance):
@@ -313,28 +385,31 @@
     pair = 2 * probe_local
 
     edge = jax.ShapeDtypeStruct((SMOOTH, probe_local + PIECES, lon), BF16)
-    north, south = pl.pallas_call(
+    north, south, flat, kappa = pl.pallas_call(
         edge_kernel,
-        out_shape=(edge, edge),
-        in_specs=[VMEM, VMEM],
-        out_specs=(VMEM, VMEM),
-        scratch_shapes=[pltpu.VMEM((halves, probe_local * rows, BLK), F32)],
+        out_shape=(edge, edge, jax.ShapeDtypeStruct(flat.shape, BF16), jax.ShapeDtypeStruct(kappa.shape, F32)),
+        in_specs=[HBM, HBM],
+        out_specs=(VMEM,) * 4,
+        scratch_shapes=[
+            pltpu.VMEM((halves, probe_local * rows, BLK), F32),
+            pltpu.SemaphoreType.DMA((2,)),
+        ],
         compiler_params=params(),
         name="edges",
-    )(flat, kappa)
+    )(in_hbm(flat), in_hbm(kappa))
     above, below = exchange_edges(north, south)
 
     def hold(after):
         return pl.pallas_call(
             hold_kernel,
             out_shape=jax.ShapeDtypeStruct(blocks.shape, BF16),
-            in_specs=[pl.BlockSpec(memory_space=pltpu.HBM), pl.BlockSpec(memory_space=pl.ANY)],
+            in_specs=[HBM, pl.BlockSpec(memory_space=pl.ANY)],
             out_specs=VMEM,
             scratch_shapes=[pltpu.SemaphoreType.DMA],
             compiler_params=params(),
             cost_estimate=pl.CostEstimate(flops=0, bytes_accessed=4 * slots * BLK * BLK, transcendentals=0),
             name="hold",
-        )(pltpu.with_memory_space_constraint(blocks, pltpu.HBM), after)
+        )(in_hbm(blocks), after)
 
     edge_cells = SMOOTH * halves
     inner_part = jax.ShapeDtypeStruct((cells - 2 * edge_cells, probe_local, BLK), BF16)
@@ -349,7 +424,7 @@
         out_specs=(VMEM, VMEM),
         scratch_shapes=[
             pltpu.VMEM(by_half, F32),
-            pltpu.VMEM((3, rows, SUB, lon), F32),
+            pltpu.VMEM((rows, SUB, lon), F32),
             pltpu.VMEM(inner_part.shape, F32),
         ],
         compiler_params=params(),
@@ -361,7 +436,7 @@
         in_specs=[VMEM] * 4,
         out_specs=VMEM,
         scratch_shapes=[
-            pltpu.VMEM((3, halo_rows, SUB, lon), F32),
+            pltpu.VMEM((halo_rows, SUB, lon), F32),
             pltpu.VMEM((2, SMOOTH, probe_local, lon), F32),
             pltpu.VMEM(outer_part.shape, F32),
         ],
@@ -375,11 +450,11 @@
     spread_over = tiles // 2
     share = RB_LOC * pair // tiles
 
-    def over_slots(kernel, held, operands, outs, scratch):
+    def over_slots(kernel, footprints, footprints_spec, operands, outs, scratch):
         return pl.pallas_call(
             kernel,
             out_shape=outs,
-            in_specs=[SMEM] * len(scalars) + [VMEM] * (1 + len(operands)),
+            in_specs=[SMEM] * len(scalars) + [footprints_spec] + [VMEM] * len(operands),
             out_specs=jax.tree.map(lambda _: VMEM, outs),
             scratch_shapes=scratch,
             compiler_params=params(),
@@ -387,22 +462,29 @@
                 flops=2 * slots * BLK * BLK * pair, bytes_accessed=2 * slots * BLK * BLK, transcendentals=0
             ),
             name=kernel.__name__,
-        )(*scalars, held, *operands)
-
-    def forward(held, *fields):
+        )(*scalars, footprints, *operands)
+
+    def forward(*fields):
         half = jax.ShapeDtypeStruct((RB_LOC // 2, pair, BLK), BF16)
         return over_slots(
             forward_kernel,
-            held,
+            in_hbm(blocks),
+            HBM,
             fields,
             (half, half),
-            [pltpu.VMEM((cells, BLK, pair), BF16), pltpu.VMEM((RB_LOC + 1, BLK, pair), F32)],
+            [
+                pltpu.VMEM((cells, BLK, pair), BF16),
+                pltpu.VMEM((RB_LOC + 1, BLK, pair), F32),
+                pltpu.VMEM(blocks.shape, BF16),
+                pltpu.SemaphoreType.DMA((FETCHES,)),
+            ],
         )
 
     def adjoint(held, mine, theirs):
         return over_slots(
             adjoint_kernel,
             held,
+            VMEM,
             (mine, theirs),
             (inner_part, outer_part) * 2,
             [pltpu.VMEM((RB_LOC * pair, BLK), BF16), pltpu.VMEM((cells + 1, pair, BLK), F32)],
@@ -433,11 +515,10 @@
     own = (own_in, own_out)
     other = [swap(x, "rcv", 2) for x in own]
     beside = [swap(x, "rcv", 1) for x in own]
-    held = hold(own_out)
-    near_keep, near_give = forward(held, *own, *beside)
+    near_keep, near_give = forward(*own, *beside)
     other[1], near_give = lax.optimization_barrier((other[1], near_give))
     first = summed(near_keep, near_give)
-    second = summed(*forward(hold(near_give), *other, *[swap(x, "rcv", 1) for x in other]))
+    second = summed(*forward(*other, *[swap(x, "rcv", 1) for x in other]))
 
     held = hold(first)
     first_mine = gathered(first)
@@ -468,11 +549,12 @@
         back_outer_kernel,
         out_shape=jax.ShapeDtypeStruct((probe_local * rows, lon), F32),
         in_specs=[SMEM] + [VMEM] * 7,
-        out_specs=VMEM,
+        out_specs=HBM,
         scratch_shapes=[
             pltpu.VMEM(by_half, F32),
             pltpu.VMEM((halo_rows, SUB, lon), F32),
             pltpu.VMEM((2, edge_cells, probe_local, BLK), F32),
+            pltpu.SemaphoreType.DMA((probe_local // SUB, halves)),
         ],
         compiler_params=params(),
         name="back_outer",

time: 106 us -> 101 us (0.953)
  Pallas kernels: 37.8 us -> 31.9 us
  waiting for transfers between devices: 21.8 us -> 24.3 us
    pallas_call x3 -> x1, Pallas kernels: 8.4 us -> 2.79 us  [hold(): pl.pallas_call(hold_kernel, out_shape=jax.ShapeDtypeStruct(blocks.shape,...]
    ppermute x28, waiting for transfers between devices: 20.3 us -> 22.1 us  [swap(): return lax.ppermute(x, axis, [(i, i ^ distance) for i in range(size)])]
    pallas_call x4, Pallas kernels: 15.7 us -> 17.1 us  [over_slots(): pl.pallas_call(kernel, out_shape=outs, in_specs=[SMEM] * len(scalars) + [...]
    pallas_call x1, Pallas kernels: 0.29 us -> 1.39 us  [per_device(): pl.pallas_call(edge_kernel, out_shape=(edge, edge, jax.ShapeDtypeStruct(f...]
  transfers between devices with their start and end apart: 32 -> 32, of which waited for: 11 -> 14; matrix products, arithmetic and copies ran while one was open for 1% -> 1% of each run, Pallas kernels for 28% -> 23%
where the time goes in v5:
time: 101 us
  starting transfers between devices  41.2 us (41%)
  Pallas kernels  31.9 us (32%)
  waiting for transfers between devices  24.3 us (24%)
  local copies, waits for them, and re-layouts  1.44 us (1%)
    ppermute x28, starting transfers between devices, swap(): return lax.ppermute(x, axis, [(i, i ^ distance) for i in range(size)])  29.2 us
    ppermute x28, waiting for transfers between devices, swap(): return lax.ppermute(x, axis, [(i, i ^ distance) for i in range(size)])  22.1 us
    pallas_call x4, Pallas kernels, over_slots(): pl.pallas_call(kernel, out_shape=outs, in_specs=[SMEM] * len(scalars) + [...  17.1 us
    ppermute x4, starting transfers between devices, exchange_edges(): return (lax.ppermute(south, 'src', down), lax.ppermute(north, 'src', up))  12 us
    pallas_call x1, Pallas kernels, per_device(): pl.pallas_call(back_outer_kernel, out_shape=jax.ShapeDtypeStruct((probe_l...  3.36 us
    pallas_call x1, Pallas kernels, hold(): pl.pallas_call(hold_kernel, out_shape=jax.ShapeDtypeStruct(blocks.shape,...  2.79 us
    pallas_call x1, Pallas kernels, per_device(): pl.pallas_call(back_inner_kernel, out_shape=(jax.ShapeDtypeStruct(by_half...  2.61 us
    pallas_call x1, Pallas kernels, per_device(): pl.pallas_call(smooth_inner_kernel, out_shape=(inner_part, state), in_spe...  2.43 us
  transfers between devices with their start and end apart: 32, of which 14 were waited for; matrix products, arithmetic and copies ran while one was open for 1% of the time, Pallas kernels for 23%

profile of v5, /device:TPU:0, one launch (start us, length us, event | category | flops | bytes accessed | tf_op | source)
XLA Modules:
  0.0 100.5 jit_solution(14290064505318486287)
XLA Ops:
  0.0 1.4 %edges.1 = (bf16[4,80,256]{2,1,0:T(8,128)(2,1)S(1)}, bf16[4,80,256]{2,1,0:T(8,128)(2,1)S(1)}, bf16[1024,256]{1,0:T(8,128)(2,1)S(1)}, f32[16,256]{1,0:T(8,128)S(1)}) custom-call(bf16[1024,256]{1,0:T(8,128)(2,1)} %bitcast.69, f32[16,256]{1,0:T(8,128)} %kappa_hbm.1), custom_call_target="tpu_custom_call" | custom-call | tf_op jit(solution)/shard_map/edges/pallas_call | solution.py:388
  1.4 4.9 %collective-permute-start = (bf16[4,80,256]{2,1,0:T(8,128)(2,1)S(1)}, bf16[4,80,256]{2,1,0:T(8,128)(2,1)S(1)}, u32[]{:S(2)}, u32[]{:S(2)}) collective-permute-start(bf16[4,80,256]{2,1,0:T(8,128)(2,1)S(1)} %get-tuple-element.32), channel_id=1, source_target_pairs={{0,4},{4,8},{8,12},{12,16},{16,20},{20,24},{24,28},{1,5},{5,9},{9,... | collective-permute-start | bytes 491528 | tf_op jit(solution)/shard_map/ppermute | solution.py:373
  6.3 1.3 %collective-permute-start.1 = (bf16[4,80,256]{2,1,0:T(8,128)(2,1)S(1)}, bf16[4,80,256]{2,1,0:T(8,128)(2,1)S(1)}, u32[]{:S(2)}, u32[]{:S(2)}) collective-permute-start(bf16[4,80,256]{2,1,0:T(8,128)(2,1)S(1)} %get-tuple-element.33), channel_id=1, source_target_pairs={{4,0},{8,4},{12,8},{16,12},{20,16},{24,20},{28,24},{5,1},{9,5},{13... | collective-permute-start | bytes 491528 | tf_op jit(solution)/shard_map/ppermute | solution.py:373
  7.6 2.4 %smooth_inner.1 = (bf16[16,64,128]{2,1,0:T(8,128)(2,1)S(1)}, f32[2,4,2,64,256]{4,3,2,1,0:T(8,128)S(1)}) custom-call(bf16[1024,256]{1,0:T(8,128)(2,1)S(1)} %get-tuple-element.34.probes_ref, f32[16,256]{1,0:T(8,128)S(1)} %get-tuple-element.31.kappa_ref), custom_call_target="tpu_custom_call" | custom-call | tf_op jit(solution)/shard_map/smooth_inner/pallas_call | solution.py:420
  10.0 1.6 %collective-permute-start.14 = (bf16[16,64,128]{2,1,0:T(8,128)(2,1)S(1)}, bf16[16,64,128]{2,1,0:T(8,128)(2,1)S(1)}, u32[]{:S(2)}, u32[]{:S(2)}) collective-permute-start(bf16[16,64,128]{2,1,0:T(8,128)(2,1)S(1)} %get-tuple-element.35.near_in), channel_id=1, source_target_pairs={{0,2},{1,3},{2,0},{3,1},{4,6},{5,7},{6,4},{7,5},{8,10},{9,11},{10,... | collective-permute-start | bytes 786440 | tf_op jit(solution)/shard_map/ppermute | solution.py:362
  11.6 2.2 %collective-permute-done.1.below_ref = bf16[4,80,256]{2,1,0:T(8,128)(2,1)S(1)} collective-permute-done((bf16[4,80,256]{2,1,0:T(8,128)(2,1)S(1)}, bf16[4,80,256]{2,1,0:T(8,128)(2,1)S(1)}, u32[]{:S(2)}, u32[]{:S(2)}) %collective-permute-start.1) | collective-permute-done | bytes 163872 | tf_op jit(solution)/shard_map/ppermute | solution.py:373
  13.8 2.2 %smooth_outer.1.near_out = bf16[16,64,128]{2,1,0:T(8,128)(2,1)S(1)} custom-call(f32[16,256]{1,0:T(8,128)S(1)} %get-tuple-element.31.kappa_ref, bf16[4,80,256]{2,1,0:T(8,128)(2,1)S(1)} %collective-permute-done.above_ref, bf16[4,80,256]{2,1,0:T(8,128)(2,1)S(1)} %collective-permute-done.1.below_ref, f32[2,4,2,64,256]{4,3,2,1,0:T(8,128)S(1)} %get-tuple-element.36.state_ref), custom_call_target="tpu_custom_call" | custom-call | tf_op jit(solution)/shard_map/smooth_outer/pallas_call | solution.py:433
  16.1 1.6 %collective-permute-start.4 = (bf16[16,64,128]{2,1,0:T(8,128)(2,1)S(1)}, bf16[16,64,128]{2,1,0:T(8,128)(2,1)S(1)}, u32[]{:S(2)}, u32[]{:S(2)}) collective-permute-start(bf16[16,64,128]{2,1,0:T(8,128)(2,1)S(1)} %smooth_outer.1.near_out), channel_id=1, source_target_pairs={{0,2},{1,3},{2,0},{3,1},{4,6},{5,7},{6,4},{7,5},{8,10},{9,11},{10,... | collective-permute-start | bytes 786440 | tf_op jit(solution)/shard_map/ppermute | solution.py:362
  20.0 4.8 %forward_kernel.2 = (bf16[8,128,128]{2,1,0:T(8,128)(2,1)S(1)}, bf16[8,128,128]{2,1,0:T(8,128)(2,1)S(1)}) custom-call(s32[192]{0:T(256)S(1)} %bitcast.54, s32[192]{0:T(256)S(1)} %bitcast.58, s32[1]{0:T(128)} %bitcast.48.count, s32[2]{0:T(128)S(1)} %pad_add_fusion.place, bf16[192,128,128]{2,1,0:T(8,128)(2,1)} %bitcast.62, ...), custom_call_target="tpu_custom_call" | custom-call | flops 805306368 | bytes 6291456 | tf_op jit(solution)/shard_map/forward_kernel/pallas_call | solution.py:454
  25.2 2.4 %collective-permute-start.5 = (bf16[8,128,128]{2,1,0:T(8,128)(2,1)S(1)}, bf16[8,128,128]{2,1,0:T(8,128)(2,1)S(1)}, u32[]{:S(2)}, u32[]{:S(2)}) collective-permute-start(bf16[8,128,128]{2,1,0:T(8,128)(2,1)S(1)} %get-tuple-element.39), channel_id=1, source_target_pairs={{0,4},{4,0},{8,12},{12,8},{16,20},{20,16},{24,28},{28,24},{1,5},{5... | collective-permute-start | bytes 786440 | tf_op jit(solution)/shard_map/ppermute | solution.py:362
  27.6 4.8 %forward_kernel.3 = (bf16[8,128,128]{2,1,0:T(8,128)(2,1)S(1)}, bf16[8,128,128]{2,1,0:T(8,128)(2,1)S(1)}) custom-call(s32[192]{0:T(256)S(1)} %bitcast.55, s32[192]{0:T(256)S(1)} %bitcast.59, s32[1]{0:T(128)} %bitcast.50.count, s32[2]{0:T(128)S(1)} %pad_add_fusion.place, bf16[192,128,128]{2,1,0:T(8,128)(2,1)} %bitcast.63, ...), custom_call_target="tpu_custom_call" | custom-call | flops 805306368 | bytes 6291456 | tf_op jit(solution)/shard_map/forward_kernel/pallas_call | solution.py:454
  34.4 3.2 %collective-permute-start.6 = (bf16[256,128]{1,0:T(8,128)(2,1)S(1)}, bf16[256,128]{1,0:T(8,128)(2,1)S(1)}, u32[]{:S(2)}, u32[]{:S(2)}) collective-permute-start(bf16[256,128]{1,0:T(8,128)(2,1)S(1)} %get-tuple-element.62), channel_id=1, source_target_pairs={{0,16},{4,20},{8,24},{12,28},{16,0},{20,4},{24,8},{28,12},{1,17},{... | collective-permute-start | bytes 196616 | tf_op jit(solution)/shard_map/ppermute | solution.py:362
  37.6 1.6 %collective-permute-start.8 = (bf16[256,128]{1,0:T(8,128)(2,1)S(1)}, bf16[256,128]{1,0:T(8,128)(2,1)S(1)}, u32[]{:S(2)}, u32[]{:S(2)}) collective-permute-start(bf16[256,128]{1,0:T(8,128)(2,1)S(1)} %get-tuple-element.63), channel_id=1, source_target_pairs={{0,8},{4,12},{8,0},{12,4},{16,24},{20,28},{24,16},{28,20},{1,9},{5... | collective-permute-start | bytes 196616 | tf_op jit(solution)/shard_map/ppermute | solution.py:362
  39.2 1.4 %collective-permute-done.17 = bf16[8,128,128]{2,1,0:T(8,128)(2,1)S(1)} collective-permute-done((bf16[8,128,128]{2,1,0:T(8,128)(2,1)S(1)}, bf16[8,128,128]{2,1,0:T(8,128)(2,1)S(1)}, u32[]{:S(2)}, u32[]{:S(2)}) %collective-permute-start.17) | collective-permute-done | bytes 262176 | tf_op jit(solution)/shard_map/ppermute | solution.py:362
  40.7 3.1 %collective-permute-start.18 = (bf16[256,128]{1,0:T(8,128)(2,1)S(1)}, bf16[256,128]{1,0:T(8,128)(2,1)S(1)}, u32[]{:S(2)}, u32[]{:S(2)}) collective-permute-start(bf16[256,128]{1,0:T(8,128)(2,1)S(1)} %get-tuple-element.59), channel_id=1, source_target_pairs={{0,16},{4,20},{8,24},{12,28},{16,0},{20,4},{24,8},{28,12},{1,17},{... | collective-permute-start | bytes 196616 | tf_op jit(solution)/shard_map/ppermute | solution.py:362
  43.8 1.5 %collective-permute-start.20 = (bf16[256,128]{1,0:T(8,128)(2,1)S(1)}, bf16[256,128]{1,0:T(8,128)(2,1)S(1)}, u32[]{:S(2)}, u32[]{:S(2)}) collective-permute-start(bf16[256,128]{1,0:T(8,128)(2,1)S(1)} %get-tuple-element.60), channel_id=1, source_target_pairs={{0,8},{4,12},{8,0},{12,4},{16,24},{20,28},{24,16},{28,20},{1,9},{5... | collective-permute-start | bytes 196616 | tf_op jit(solution)/shard_map/ppermute | solution.py:362
  45.6 2.3 %collective-permute-done.18 = bf16[256,128]{1,0:T(8,128)(2,1)S(1)} collective-permute-done((bf16[256,128]{1,0:T(8,128)(2,1)S(1)}, bf16[256,128]{1,0:T(8,128)(2,1)S(1)}, u32[]{:S(2)}, u32[]{:S(2)}) %collective-permute-start.18) | collective-permute-done | bytes 65568 | tf_op jit(solution)/shard_map/ppermute | solution.py:362
  48.3 3.1 %collective-permute-done.19 = bf16[256,128]{1,0:T(8,128)(2,1)S(1)} collective-permute-done((bf16[256,128]{1,0:T(8,128)(2,1)S(1)}, bf16[256,128]{1,0:T(8,128)(2,1)S(1)}, u32[]{:S(2)}, u32[]{:S(2)}) %collective-permute-start.19) | collective-permute-done | bytes 65568 | tf_op jit(solution)/shard_map/ppermute | solution.py:362
  51.5 1.3 %collective-permute-start.11 = (bf16[256,128]{1,0:T(8,128)(2,1)S(1)}, bf16[256,128]{1,0:T(8,128)(2,1)S(1)}, u32[]{:S(2)}, u32[]{:S(2)}) collective-permute-start(bf16[256,128]{1,0:T(8,128)(2,1)S(1)} %get-tuple-element.66.after_ref), channel_id=1, source_target_pairs={{0,24},{4,28},{8,16},{12,20},{16,8},{20,12},{24,0},{28,4},{1,25},{... | collective-permute-start | bytes 196616 | tf_op jit(solution)/shard_map/ppermute | solution.py:362
  52.8 3.1 %collective-permute-start.9 = (bf16[256,128]{1,0:T(8,128)(2,1)S(1)}, bf16[256,128]{1,0:T(8,128)(2,1)S(1)}, u32[]{:S(2)}, u32[]{:S(2)}) collective-permute-start(bf16[256,128]{1,0:T(8,128)(2,1)S(1)} %get-tuple-element.66.after_ref), channel_id=1, source_target_pairs={{0,8},{4,12},{8,0},{12,4},{16,24},{20,28},{24,16},{28,20},{1,9},{5... | collective-permute-start | bytes 196616 | tf_op jit(solution)/shard_map/ppermute | solution.py:362
  58.2 2.2 %collective-permute-start.21 = (bf16[256,128]{1,0:T(8,128)(2,1)S(1)}, bf16[256,128]{1,0:T(8,128)(2,1)S(1)}, u32[]{:S(2)}, u32[]{:S(2)}) collective-permute-start(bf16[256,128]{1,0:T(8,128)(2,1)S(1)} %get-tuple-element.65), channel_id=1, source_target_pairs={{0,8},{4,12},{8,0},{12,4},{16,24},{20,28},{24,16},{28,20},{1,9},{5... | collective-permute-start | bytes 196616 | tf_op jit(solution)/shard_map/ppermute | solution.py:362
  62.2 2.2 %collective-permute-done.22 = bf16[256,128]{1,0:T(8,128)(2,1)S(1)} collective-permute-done((bf16[256,128]{1,0:T(8,128)(2,1)S(1)}, bf16[256,128]{1,0:T(8,128)(2,1)S(1)}, u32[]{:S(2)}, u32[]{:S(2)}) %collective-permute-start.22) | collective-permute-done | bytes 65568 | tf_op jit(solution)/shard_map/ppermute | solution.py:362
  65.0 2.8 %hold.1.held = bf16[192,128,128]{2,1,0:T(8,128)(2,1)S(1)} custom-call(bf16[192,128,128]{2,1,0:T(8,128)(2,1)} %bitcast.64, bf16[256,128]{1,0:T(8,128)(2,1)S(1)} %get-tuple-element.66.after_ref), custom_call_target="tpu_custom_call" | custom-call | bytes 12582912 | tf_op jit(solution)/shard_map/hold/pallas_call | solution.py:403
  67.8 2.2 %collective-permute-done.12.theirs_ref = bf16[4,256,128]{2,1,0:T(8,128)(2,1)S(1)} collective-permute-done((bf16[4,256,128]{2,1,0:T(8,128)(2,1)S(1)}, bf16[4,256,128]{2,1,0:T(8,128)(2,1)S(1)}, u32[]{:S(2)}, u32[]{:S(2)}) %collective-permute-start.12) | collective-permute-done | bytes 262176 | tf_op jit(solution)/shard_map/ppermute | solution.py:362
  69.9 3.8 %adjoint_kernel.2 = (bf16[16,64,128]{2,1,0:T(8,128)(2,1)S(1)}, bf16[16,64,128]{2,1,0:T(8,128)(2,1)S(1)}, bf16[16,64,128]{2,1,0:T(8,128)(2,1)S(1)}, bf16[16,64,128]{2,1,0:T(8,128)(2,1)S(1)}) custom-call(s32[192]{0:T(256)S(1)} %bitcast.56, s32[192]{0:T(256)S(1)} %bitcast.60, s32[1]{0:T(128)} %bitcast.49.count, s32[2]{0:T(128)S(1)} %pad_add_fusion.place, ...), custom_call_target="tpu_custom_call" | custom-call | flops 805306368 | bytes 6291456 | tf_op jit(solution)/shard_map/adjoint_kernel/pallas_call | solution.py:454
  73.7 3.8 %adjoint_kernel.3 = (bf16[16,64,128]{2,1,0:T(8,128)(2,1)S(1)}, bf16[16,64,128]{2,1,0:T(8,128)(2,1)S(1)}, bf16[16,64,128]{2,1,0:T(8,128)(2,1)S(1)}, bf16[16,64,128]{2,1,0:T(8,128)(2,1)S(1)}) custom-call(s32[192]{0:T(256)S(1)} %bitcast.57, s32[192]{0:T(256)S(1)} %bitcast.61, s32[1]{0:T(128)} %bitcast.51.count, s32[2]{0:T(128)S(1)} %pad_add_fusion.place, ...), custom_call_target="tpu_custom_call" | custom-call | flops 805306368 | bytes 6291456 | tf_op jit(solution)/shard_map/adjoint_kernel/pallas_call | solution.py:454
  79.2 1.8 %collective-permute-start.26 = (bf16[16,64,128]{2,1,0:T(8,128)(2,1)S(1)}, bf16[16,64,128]{2,1,0:T(8,128)(2,1)S(1)}, u32[]{:S(2)}, u32[]{:S(2)}) collective-permute-start(bf16[16,64,128]{2,1,0:T(8,128)(2,1)S(1)} %add_convert_fusion.2), channel_id=1, source_target_pairs={{0,2},{1,3},{2,0},{3,1},{4,6},{5,7},{6,4},{7,5},{8,10},{9,11},{10,... | collective-permute-start | bytes 786440 | tf_op jit(solution)/shard_map/ppermute | solution.py:362
  81.5 7.0 %collective-permute-done.26.far_out = bf16[16,64,128]{2,1,0:T(8,128)(2,1)S(1)} collective-permute-done((bf16[16,64,128]{2,1,0:T(8,128)(2,1)S(1)}, bf16[16,64,128]{2,1,0:T(8,128)(2,1)S(1)}, u32[]{:S(2)}, u32[]{:S(2)}) %collective-permute-start.26) | collective-permute-done | bytes 262176 | tf_op jit(solution)/shard_map/ppermute | solution.py:362
  88.6 1.3 %collective-permute-start.28 = (bf16[8,64,128]{2,1,0:T(8,128)(2,1)S(1)}, bf16[8,64,128]{2,1,0:T(8,128)(2,1)S(1)}, u32[]{:S(2)}, u32[]{:S(2)}) collective-permute-start(bf16[8,64,128]{2,1,0:T(8,128)(2,1)S(1)} %get-tuple-element.57), channel_id=1, source_target_pairs={{4,0},{8,4},{12,8},{16,12},{20,16},{24,20},{28,24},{5,1},{9,5},{13... | collective-permute-start | bytes 393224 | tf_op jit(solution)/shard_map/ppermute | solution.py:373
  89.9 4.6 %collective-permute-start.27 = (bf16[8,64,128]{2,1,0:T(8,128)(2,1)S(1)}, bf16[8,64,128]{2,1,0:T(8,128)(2,1)S(1)}, u32[]{:S(2)}, u32[]{:S(2)}) collective-permute-start(bf16[8,64,128]{2,1,0:T(8,128)(2,1)S(1)} %get-tuple-element.58), channel_id=1, source_target_pairs={{0,4},{4,8},{8,12},{12,16},{16,20},{20,24},{24,28},{1,5},{5,9},{9,... | collective-permute-start | bytes 393224 | tf_op jit(solution)/shard_map/ppermute | solution.py:373
  94.5 2.6 %back_inner.1 = (f32[2,1024,128]{2,1,0:T(8,128)S(1)}, f32[2,4,2,64,256]{4,3,2,1,0:T(8,128)S(1)}) custom-call(bf16[1024,256]{1,0:T(8,128)(2,1)S(1)} %get-tuple-element.34.probes_ref, f32[16,256]{1,0:T(8,128)S(1)} %get-tuple-element.31.kappa_ref, bf16[16,64,128]{2,1,0:T(8,128)(2,1)S(1)} %get-tuple-element.51.own_in, ...), custom_call_target="tpu_custom_call" | custom-call | tf_op jit(solution)/shard_map/back_inner/pallas_call | solution.py:539
  97.2 3.4 %back_outer.1 = f32[1024,256]{1,0:T(8,128)} custom-call(f32[2]{0:T(128)S(1)} %add_convert_fusion.5.inside, f32[16,256]{1,0:T(8,128)S(1)} %get-tuple-element.31.kappa_ref, bf16[4,80,256]{2,1,0:T(8,128)(2,1)S(1)} %collective-permute-done.above_ref, bf16[4,80,256]{2,1,0:T(8,128)(2,1)S(1)} %collective-permute-done.1.below_ref, ...), custom_call_target="tpu_custom_call" | custom-call | tf_op jit(solution)/shard_map/back_outer/pallas_call | solution.py:548
  (66 shorter events, 11.7 us)
Async XLA Ops:
  1.4 10.2 %collective-permute-start = (bf16[4,80,256]{2,1,0:T(8,128)(2,1)S(1)}, bf16[4,80,256]{2,1,0:T(8,128)(2,1)S(1)}, u32[]{:S(2)}, u32[]{:S(2)}) collective-permute-start(bf16[4,80,256]{2,1,0:T(8,128)(2,1)S(1)} %get-tuple-element.32), channel_id=1, source_target_pairs={{0,4},{4,8},{8,12},{12,16},{16,20},{20,24},{24,28},{1,5},{5,9},{9,... | collective-permute-start | bytes 491528 | tf_op jit(solution)/shard_map/ppermute | solution.py:373
  6.3 7.6 %collective-permute-start.1 = (bf16[4,80,256]{2,1,0:T(8,128)(2,1)S(1)}, bf16[4,80,256]{2,1,0:T(8,128)(2,1)S(1)}, u32[]{:S(2)}, u32[]{:S(2)}) collective-permute-start(bf16[4,80,256]{2,1,0:T(8,128)(2,1)S(1)} %get-tuple-element.33), channel_id=1, source_target_pairs={{4,0},{8,4},{12,8},{16,12},{20,16},{24,20},{28,24},{5,1},{9,5},{13... | collective-permute-start | bytes 491528 | tf_op jit(solution)/shard_map/ppermute | solution.py:373
  10.0 8.4 %collective-permute-start.14 = (bf16[16,64,128]{2,1,0:T(8,128)(2,1)S(1)}, bf16[16,64,128]{2,1,0:T(8,128)(2,1)S(1)}, u32[]{:S(2)}, u32[]{:S(2)}) collective-permute-start(bf16[16,64,128]{2,1,0:T(8,128)(2,1)S(1)} %get-tuple-element.35.near_in), channel_id=1, source_target_pairs={{0,2},{1,3},{2,0},{3,1},{4,6},{5,7},{6,4},{7,5},{8,10},{9,11},{10,... | collective-permute-start | bytes 786440 | tf_op jit(solution)/shard_map/ppermute | solution.py:362
  11.6 7.0 %collective-permute-start.2 = (bf16[16,64,128]{2,1,0:T(8,128)(2,1)S(1)}, bf16[16,64,128]{2,1,0:T(8,128)(2,1)S(1)}, u32[]{:S(2)}, u32[]{:S(2)}) collective-permute-start(bf16[16,64,128]{2,1,0:T(8,128)(2,1)S(1)} %get-tuple-element.35.near_in), channel_id=1, source_target_pairs={{0,1},{1,0},{2,3},{3,2},{4,5},{5,4},{6,7},{7,6},{8,9},{9,8},{10,11... | collective-permute-start | bytes 786440 | tf_op jit(solution)/shard_map/ppermute | solution.py:362
  16.0 2.6 %collective-permute-start.3 = (bf16[16,64,128]{2,1,0:T(8,128)(2,1)S(1)}, bf16[16,64,128]{2,1,0:T(8,128)(2,1)S(1)}, u32[]{:S(2)}, u32[]{:S(2)}) collective-permute-start(bf16[16,64,128]{2,1,0:T(8,128)(2,1)S(1)} %smooth_outer.1.near_out), channel_id=1, source_target_pairs={{0,1},{1,0},{2,3},{3,2},{4,5},{5,4},{6,7},{7,6},{8,9},{9,8},{10,11... | collective-permute-start | bytes 786440 | tf_op jit(solution)/shard_map/ppermute | solution.py:362
  16.1 8.7 %collective-permute-start.4 = (bf16[16,64,128]{2,1,0:T(8,128)(2,1)S(1)}, bf16[16,64,128]{2,1,0:T(8,128)(2,1)S(1)}, u32[]{:S(2)}, u32[]{:S(2)}) collective-permute-start(bf16[16,64,128]{2,1,0:T(8,128)(2,1)S(1)} %smooth_outer.1.near_out), channel_id=1, source_target_pairs={{0,2},{1,3},{2,0},{3,1},{4,6},{5,7},{6,4},{7,5},{8,10},{9,11},{10,... | collective-permute-start | bytes 786440 | tf_op jit(solution)/shard_map/ppermute | solution.py:362
  18.4 9.2 %collective-permute-start.15 = (bf16[16,64,128]{2,1,0:T(8,128)(2,1)S(1)}, bf16[16,64,128]{2,1,0:T(8,128)(2,1)S(1)}, u32[]{:S(2)}, u32[]{:S(2)}) collective-permute-start(bf16[16,64,128]{2,1,0:T(8,128)(2,1)S(1)} %collective-permute-done.14.near_in), channel_id=1, source_target_pairs={{0,1},{1,0},{2,3},{3,2},{4,5},{5,4},{6,7},{7,6},{8,9},{9,8},{10,11... | collective-permute-start | bytes 786440 | tf_op jit(solution)/shard_map/ppermute | solution.py:362
  24.8 2.8 %collective-permute-start.16 = (bf16[16,64,128]{2,1,0:T(8,128)(2,1)S(1)}, bf16[16,64,128]{2,1,0:T(8,128)(2,1)S(1)}, u32[]{:S(2)}, u32[]{:S(2)}) collective-permute-start(bf16[16,64,128]{2,1,0:T(8,128)(2,1)S(1)} %collective-permute-done.4.near_out), channel_id=1, source_target_pairs={{0,1},{1,0},{2,3},{3,2},{4,5},{5,4},{6,7},{7,6},{8,9},{9,8},{10,11... | collective-permute-start | bytes 786440 | tf_op jit(solution)/shard_map/ppermute | solution.py:362
  25.2 9.1 %collective-permute-start.5 = (bf16[8,128,128]{2,1,0:T(8,128)(2,1)S(1)}, bf16[8,128,128]{2,1,0:T(8,128)(2,1)S(1)}, u32[]{:S(2)}, u32[]{:S(2)}) collective-permute-start(bf16[8,128,128]{2,1,0:T(8,128)(2,1)S(1)} %get-tuple-element.39), channel_id=1, source_target_pairs={{0,4},{4,0},{8,12},{12,8},{16,20},{20,16},{24,28},{28,24},{1,5},{5... | collective-permute-start | bytes 786440 | tf_op jit(solution)/shard_map/ppermute | solution.py:362
  32.4 8.2 %collective-permute-start.17 = (bf16[8,128,128]{2,1,0:T(8,128)(2,1)S(1)}, bf16[8,128,128]{2,1,0:T(8,128)(2,1)S(1)}, u32[]{:S(2)}, u32[]{:S(2)}) collective-permute-start(bf16[8,128,128]{2,1,0:T(8,128)(2,1)S(1)} %get-tuple-element.44), channel_id=1, source_target_pairs={{0,4},{4,0},{8,12},{12,8},{16,20},{20,16},{24,28},{28,24},{1,5},{5... | collective-permute-start | bytes 786440 | tf_op jit(solution)/shard_map/ppermute | solution.py:362
  34.4 11.0 %collective-permute-start.6 = (bf16[256,128]{1,0:T(8,128)(2,1)S(1)}, bf16[256,128]{1,0:T(8,128)(2,1)S(1)}, u32[]{:S(2)}, u32[]{:S(2)}) collective-permute-start(bf16[256,128]{1,0:T(8,128)(2,1)S(1)} %get-tuple-element.62), channel_id=1, source_target_pairs={{0,16},{4,20},{8,24},{12,28},{16,0},{20,4},{24,8},{28,12},{1,17},{... | collective-permute-start | bytes 196616 | tf_op jit(solution)/shard_map/ppermute | solution.py:362
  37.6 8.0 %collective-permute-start.8 = (bf16[256,128]{1,0:T(8,128)(2,1)S(1)}, bf16[256,128]{1,0:T(8,128)(2,1)S(1)}, u32[]{:S(2)}, u32[]{:S(2)}) collective-permute-start(bf16[256,128]{1,0:T(8,128)(2,1)S(1)} %get-tuple-element.63), channel_id=1, source_target_pairs={{0,8},{4,12},{8,0},{12,4},{16,24},{20,28},{24,16},{28,20},{1,9},{5... | collective-permute-start | bytes 196616 | tf_op jit(solution)/shard_map/ppermute | solution.py:362
  39.2 6.4 %collective-permute-start.7 = (bf16[256,128]{1,0:T(8,128)(2,1)S(1)}, bf16[256,128]{1,0:T(8,128)(2,1)S(1)}, u32[]{:S(2)}, u32[]{:S(2)}) collective-permute-start(bf16[256,128]{1,0:T(8,128)(2,1)S(1)} %get-tuple-element.64), channel_id=1, source_target_pairs={{0,24},{4,28},{8,16},{12,20},{16,8},{20,12},{24,0},{28,4},{1,25},{... | collective-permute-start | bytes 196616 | tf_op jit(solution)/shard_map/ppermute | solution.py:362
  40.7 7.2 %collective-permute-start.18 = (bf16[256,128]{1,0:T(8,128)(2,1)S(1)}, bf16[256,128]{1,0:T(8,128)(2,1)S(1)}, u32[]{:S(2)}, u32[]{:S(2)}) collective-permute-start(bf16[256,128]{1,0:T(8,128)(2,1)S(1)} %get-tuple-element.59), channel_id=1, source_target_pairs={{0,16},{4,20},{8,24},{12,28},{16,0},{20,4},{24,8},{28,12},{1,17},{... | collective-permute-start | bytes 196616 | tf_op jit(solution)/shard_map/ppermute | solution.py:362
  43.8 4.5 %collective-permute-start.20 = (bf16[256,128]{1,0:T(8,128)(2,1)S(1)}, bf16[256,128]{1,0:T(8,128)(2,1)S(1)}, u32[]{:S(2)}, u32[]{:S(2)}) collective-permute-start(bf16[256,128]{1,0:T(8,128)(2,1)S(1)} %get-tuple-element.60), channel_id=1, source_target_pairs={{0,8},{4,12},{8,0},{12,4},{16,24},{20,28},{24,16},{28,20},{1,9},{5... | collective-permute-start | bytes 196616 | tf_op jit(solution)/shard_map/ppermute | solution.py:362
  45.4 6.1 %collective-permute-start.19 = (bf16[256,128]{1,0:T(8,128)(2,1)S(1)}, bf16[256,128]{1,0:T(8,128)(2,1)S(1)}, u32[]{:S(2)}, u32[]{:S(2)}) collective-permute-start(bf16[256,128]{1,0:T(8,128)(2,1)S(1)} %get-tuple-element.61), channel_id=1, source_target_pairs={{0,24},{4,28},{8,16},{12,20},{16,8},{20,12},{24,0},{28,4},{1,25},{... | collective-permute-start | bytes 196616 | tf_op jit(solution)/shard_map/ppermute | solution.py:362
  51.5 6.6 %collective-permute-start.11 = (bf16[256,128]{1,0:T(8,128)(2,1)S(1)}, bf16[256,128]{1,0:T(8,128)(2,1)S(1)}, u32[]{:S(2)}, u32[]{:S(2)}) collective-permute-start(bf16[256,128]{1,0:T(8,128)(2,1)S(1)} %get-tuple-element.66.after_ref), channel_id=1, source_target_pairs={{0,24},{4,28},{8,16},{12,20},{16,8},{20,12},{24,0},{28,4},{1,25},{... | collective-permute-start | bytes 196616 | tf_op jit(solution)/shard_map/ppermute | solution.py:362
  52.8 8.5 %collective-permute-start.10 = (bf16[256,128]{1,0:T(8,128)(2,1)S(1)}, bf16[256,128]{1,0:T(8,128)(2,1)S(1)}, u32[]{:S(2)}, u32[]{:S(2)}) collective-permute-start(bf16[256,128]{1,0:T(8,128)(2,1)S(1)} %get-tuple-element.66.after_ref), channel_id=1, source_target_pairs={{0,16},{4,20},{8,24},{12,28},{16,0},{20,4},{24,8},{28,12},{1,17},{... | collective-permute-start | bytes 196616 | tf_op jit(solution)/shard_map/ppermute | solution.py:362
  52.8 8.5 %collective-permute-start.9 = (bf16[256,128]{1,0:T(8,128)(2,1)S(1)}, bf16[256,128]{1,0:T(8,128)(2,1)S(1)}, u32[]{:S(2)}, u32[]{:S(2)}) collective-permute-start(bf16[256,128]{1,0:T(8,128)(2,1)S(1)} %get-tuple-element.66.after_ref), channel_id=1, source_target_pairs={{0,8},{4,12},{8,0},{12,4},{16,24},{20,28},{24,16},{28,20},{1,9},{5... | collective-permute-start | bytes 196616 | tf_op jit(solution)/shard_map/ppermute | solution.py:362
  56.0 6.2 %collective-permute-start.23 = (bf16[256,128]{1,0:T(8,128)(2,1)S(1)}, bf16[256,128]{1,0:T(8,128)(2,1)S(1)}, u32[]{:S(2)}, u32[]{:S(2)}) collective-permute-start(bf16[256,128]{1,0:T(8,128)(2,1)S(1)} %get-tuple-element.65), channel_id=1, source_target_pairs={{0,24},{4,28},{8,16},{12,20},{16,8},{20,12},{24,0},{28,4},{1,25},{... | collective-permute-start | bytes 196616 | tf_op jit(solution)/shard_map/ppermute | solution.py:362
  57.2 7.1 %collective-permute-start.22 = (bf16[256,128]{1,0:T(8,128)(2,1)S(1)}, bf16[256,128]{1,0:T(8,128)(2,1)S(1)}, u32[]{:S(2)}, u32[]{:S(2)}) collective-permute-start(bf16[256,128]{1,0:T(8,128)(2,1)S(1)} %get-tuple-element.65), channel_id=1, source_target_pairs={{0,16},{4,20},{8,24},{12,28},{16,0},{20,4},{24,8},{28,12},{1,17},{... | collective-permute-start | bytes 196616 | tf_op jit(solution)/shard_map/ppermute | solution.py:362
  58.2 6.2 %collective-permute-start.21 = (bf16[256,128]{1,0:T(8,128)(2,1)S(1)}, bf16[256,128]{1,0:T(8,128)(2,1)S(1)}, u32[]{:S(2)}, u32[]{:S(2)}) collective-permute-start(bf16[256,128]{1,0:T(8,128)(2,1)S(1)} %get-tuple-element.65), channel_id=1, source_target_pairs={{0,8},{4,12},{8,0},{12,4},{16,24},{20,28},{24,16},{28,20},{1,9},{5... | collective-permute-start | bytes 196616 | tf_op jit(solution)/shard_map/ppermute | solution.py:362
  61.4 8.6 %collective-permute-start.12 = (bf16[4,256,128]{2,1,0:T(8,128)(2,1)S(1)}, bf16[4,256,128]{2,1,0:T(8,128)(2,1)S(1)}, u32[]{:S(2)}, u32[]{:S(2)}) collective-permute-start(bf16[4,256,128]{2,1,0:T(8,128)(2,1)S(1)} %pad_maximum_fusion.mine_ref), channel_id=1, source_target_pairs={{0,4},{4,0},{8,12},{12,8},{16,20},{20,16},{24,28},{28,24},{1,5},{5... | collective-permute-start | bytes 786440 | tf_op jit(solution)/shard_map/ppermute | solution.py:362
  64.4 9.3 %collective-permute-start.24 = (bf16[4,256,128]{2,1,0:T(8,128)(2,1)S(1)}, bf16[4,256,128]{2,1,0:T(8,128)(2,1)S(1)}, u32[]{:S(2)}, u32[]{:S(2)}) collective-permute-start(bf16[4,256,128]{2,1,0:T(8,128)(2,1)S(1)} %pad_maximum_fusion.1.mine_ref), channel_id=1, source_target_pairs={{0,4},{4,0},{8,12},{12,8},{16,20},{20,16},{24,28},{28,24},{1,5},{5... | collective-permute-start | bytes 786440 | tf_op jit(solution)/shard_map/ppermute | solution.py:362
  77.5 1.6 %collective-permute-start.25 = (bf16[16,64,128]{2,1,0:T(8,128)(2,1)S(1)}, bf16[16,64,128]{2,1,0:T(8,128)(2,1)S(1)}, u32[]{:S(2)}, u32[]{:S(2)}) collective-permute-start(bf16[16,64,128]{2,1,0:T(8,128)(2,1)S(1)} %get-tuple-element.50), channel_id=1, source_target_pairs={{0,1},{1,0},{2,3},{3,2},{4,5},{5,4},{6,7},{7,6},{8,9},{9,8},{10,11... | collective-permute-start | bytes 786440 | tf_op jit(solution)/shard_map/ppermute | solution.py:362
  77.6 3.4 %collective-permute-start.30 = (bf16[16,64,128]{2,1,0:T(8,128)(2,1)S(1)}, bf16[16,64,128]{2,1,0:T(8,128)(2,1)S(1)}, u32[]{:S(2)}, u32[]{:S(2)}) collective-permute-start(bf16[16,64,128]{2,1,0:T(8,128)(2,1)S(1)} %get-tuple-element.54), channel_id=1, source_target_pairs={{0,1},{1,0},{2,3},{3,2},{4,5},{5,4},{6,7},{7,6},{8,9},{9,8},{10,11... | collective-permute-start | bytes 786440 | tf_op jit(solution)/shard_map/ppermute | solution.py:362
  78.1 3.4 %collective-permute-start.13 = (bf16[16,64,128]{2,1,0:T(8,128)(2,1)S(1)}, bf16[16,64,128]{2,1,0:T(8,128)(2,1)S(1)}, u32[]{:S(2)}, u32[]{:S(2)}) collective-permute-start(bf16[16,64,128]{2,1,0:T(8,128)(2,1)S(1)} %get-tuple-element.41), channel_id=1, source_target_pairs={{0,1},{1,0},{2,3},{3,2},{4,5},{5,4},{6,7},{7,6},{8,9},{9,8},{10,11... | collective-permute-start | bytes 786440 | tf_op jit(solution)/shard_map/ppermute | solution.py:362
  79.2 9.2 %collective-permute-start.26 = (bf16[16,64,128]{2,1,0:T(8,128)(2,1)S(1)}, bf16[16,64,128]{2,1,0:T(8,128)(2,1)S(1)}, u32[]{:S(2)}, u32[]{:S(2)}) collective-permute-start(bf16[16,64,128]{2,1,0:T(8,128)(2,1)S(1)} %add_convert_fusion.2), channel_id=1, source_target_pairs={{0,2},{1,3},{2,0},{3,1},{4,6},{5,7},{6,4},{7,5},{8,10},{9,11},{10,... | collective-permute-start | bytes 786440 | tf_op jit(solution)/shard_map/ppermute | solution.py:362
  81.0 13.5 %collective-permute-start.29 = (bf16[16,64,128]{2,1,0:T(8,128)(2,1)S(1)}, bf16[16,64,128]{2,1,0:T(8,128)(2,1)S(1)}, u32[]{:S(2)}, u32[]{:S(2)}) collective-permute-start(bf16[16,64,128]{2,1,0:T(8,128)(2,1)S(1)} %get-tuple-element.52), channel_id=1, source_target_pairs={{0,1},{1,0},{2,3},{3,2},{4,5},{5,4},{6,7},{7,6},{8,9},{9,8},{10,11... | collective-permute-start | bytes 786440 | tf_op jit(solution)/shard_map/ppermute | solution.py:362
  81.1 13.4 %collective-permute-start.31 = (bf16[16,64,128]{2,1,0:T(8,128)(2,1)S(1)}, bf16[16,64,128]{2,1,0:T(8,128)(2,1)S(1)}, u32[]{:S(2)}, u32[]{:S(2)}) collective-permute-start(bf16[16,64,128]{2,1,0:T(8,128)(2,1)S(1)} %add_convert_fusion), channel_id=1, source_target_pairs={{0,2},{1,3},{2,0},{3,1},{4,6},{5,7},{6,4},{7,5},{8,10},{9,11},{10,... | collective-permute-start | bytes 786440 | tf_op jit(solution)/shard_map/ppermute | solution.py:362
  88.6 8.6 %collective-permute-start.28 = (bf16[8,64,128]{2,1,0:T(8,128)(2,1)S(1)}, bf16[8,64,128]{2,1,0:T(8,128)(2,1)S(1)}, u32[]{:S(2)}, u32[]{:S(2)}) collective-permute-start(bf16[8,64,128]{2,1,0:T(8,128)(2,1)S(1)} %get-tuple-element.57), channel_id=1, source_target_pairs={{4,0},{8,4},{12,8},{16,12},{20,16},{24,20},{28,24},{5,1},{9,5},{13... | collective-permute-start | bytes 393224 | tf_op jit(solution)/shard_map/ppermute | solution.py:373
  89.9 7.3 %collective-permute-start.27 = (bf16[8,64,128]{2,1,0:T(8,128)(2,1)S(1)}, bf16[8,64,128]{2,1,0:T(8,128)(2,1)S(1)}, u32[]{:S(2)}, u32[]{:S(2)}) collective-permute-start(bf16[8,64,128]{2,1,0:T(8,128)(2,1)S(1)} %get-tuple-element.58), channel_id=1, source_target_pairs={{0,4},{4,8},{8,12},{12,16},{16,20},{20,24},{24,28},{1,5},{5,9},{9,... | collective-permute-start | bytes 393224 | tf_op jit(solution)/shard_map/ppermute | solution.py:373
  (5 other events, 102.1 us)

commit v6 on v5

--- a/solution.py
+++ b/solution.py
@@ -65,22 +65,24 @@
     widen(probes_ref, wide)
     place = lax.broadcasted_iota(jnp.int32, (PIECES, lon), 0)
     for out_ref, first in ((north_ref, 0), (south_ref, rows - SMOOTH)):
+        pieces = jnp.zeros((PIECES, lon), F32)
         for r in range(SMOOTH):
             for h, part in enumerate(one_row(wide, first + r, probe_local, rows)):
-                out_ref[r, :probe_local, h * BLK : (h + 1) * BLK] = part.astype(BF16)
+                out_ref[r * probe_local : (r + 1) * probe_local, h * BLK : (h + 1) * BLK] = part.astype(BF16)
             whole = kappa_ref[first + r : first + r + 1, :]
             high = whole.astype(BF16).astype(F32)
             rest = whole - high
             middle = rest.astype(BF16).astype(F32)
-            low = rest - middle
-            pieces = jnp.where(place == 0, high, jnp.where(place == 1, middle, jnp.where(place == 2, low, 0.0)))
-            out_ref[r, probe_local:, :] = pieces.astype(BF16)
+            for i, piece in enumerate((high, middle, rest - middle)):
+                pieces = jnp.where(place == i * SMOOTH + r, piece, pieces)
+        out_ref[SMOOTH * probe_local :, :] = pieces.astype(BF16)
 
 
 def kappa_rows(kappa_ref, above_ref, below_ref, probe_local):
     def halo(ref, r):
-        piece = ref[r, probe_local:, :].astype(F32)
-        return piece[0:1] + piece[1:2] + piece[2:3]
+        pieces = ref[SMOOTH * probe_local :, :].astype(F32)
+        high, middle, low = [pieces[i * SMOOTH + r : i * SMOOTH + r + 1] for i in range(3)]
+        return high + middle + low
 
     rows = kappa_ref.shape[0]
     return (
@@ -153,8 +155,9 @@
     rows, lon = kappa_ref.shape
     probe_local = state_ref.shape[3]
     halves = lon // BLK
-    halos[0] = above_ref[:, :probe_local, :].astype(F32)
-    halos[1] = below_ref[:, :probe_local, :].astype(F32)
+    for r in range(SMOOTH):
+        halos[0, r] = above_ref[r * probe_local : (r + 1) * probe_local, :].astype(F32)
+        halos[1, r] = below_ref[r * probe_local : (r + 1) * probe_local, :].astype(F32)
     coefficients(coef, outer_rows(kappa_rows(kappa_ref, above_ref, below_ref, probe_local)))
     lane = lanes()
     total = rows + 2 * SMOOTH
@@ -191,8 +194,8 @@
 
 
 def forward_kernel(
-    sources,
-    receptors,
+    sources_hbm,
+    receptors_hbm,
     count,
     place,
     blocks_ref,
@@ -206,7 +209,16 @@
     total,
     held,
     arrived,
+    sources,
+    receptors,
+    listed,
 ):
+    lists = [
+        pltpu.make_async_copy(sources_hbm, sources, listed.at[0]),
+        pltpu.make_async_copy(receptors_hbm, receptors, listed.at[1]),
+    ]
+    for fetch in lists:
+        fetch.start()
     fetches = []
     size = held.shape[0] // FETCHES
     for g in range(FETCHES):
@@ -229,6 +241,8 @@
         b = jnp.where(n < count[0], receptors[n], spare)
         total[b] += jnp.dot(held[n], turned[sources[n]], preferred_element_type=F32)
 
+    for fetch in lists:
+        fetch.wait()
     for g, fetch in enumerate(fetches):
         fetch.wait()
         for i in range(size):
@@ -384,7 +398,7 @@
     flat = probes.reshape(probe_local * rows, lon)
     pair = 2 * probe_local
 
-    edge = jax.ShapeDtypeStruct((SMOOTH, probe_local + PIECES, lon), BF16)
+    edge = jax.ShapeDtypeStruct((SMOOTH * probe_local + PIECES, lon), BF16)
     north, south, flat, kappa = pl.pallas_call(
         edge_kernel,
         out_shape=(edge, edge, jax.ShapeDtypeStruct(flat.shape, BF16), jax.ShapeDtypeStruct(kappa.shape, F32)),
@@ -446,15 +460,16 @@
 
     side, row = me % 2, me // 2
     place = jnp.stack([side, row]).astype(jnp.int32)
-    scalars = (block_source.reshape(-1), block_receptor.reshape(-1), block_count.reshape(-1), place)
+    lists = (block_source.reshape(-1), block_receptor.reshape(-1))
+    single = (block_count.reshape(-1), place)
     spread_over = tiles // 2
     share = RB_LOC * pair // tiles
 
-    def over_slots(kernel, footprints, footprints_spec, operands, outs, scratch):
+    def over_slots(kernel, list_spec, lists, footprints_spec, footprints, operands, outs, scratch):
         return pl.pallas_call(
             kernel,
             out_shape=outs,
-            in_specs=[SMEM] * len(scalars) + [footprints_spec] + [VMEM] * len(operands),
+            in_specs=[list_spec, list_spec, SMEM, SMEM, footprints_spec] + [VMEM] * len(operands),
             out_specs=jax.tree.map(lambda _: VMEM, outs),
             scratch_shapes=scratch,
             compiler_params=params(),
@@ -462,14 +477,16 @@
                 flops=2 * slots * BLK * BLK * pair, bytes_accessed=2 * slots * BLK * BLK, transcendentals=0
             ),
             name=kernel.__name__,
-        )(*scalars, footprints, *operands)
+        )(*lists, *single, footprints, *operands)
 
     def forward(*fields):
         half = jax.ShapeDtypeStruct((RB_LOC // 2, pair, BLK), BF16)
         return over_slots(
             forward_kernel,
+            HBM,
+            [in_hbm(x) for x in lists],
+            HBM,
             in_hbm(blocks),
-            HBM,
             fields,
             (half, half),
             [
@@ -477,14 +494,19 @@
                 pltpu.VMEM((RB_LOC + 1, BLK, pair), F32),
                 pltpu.VMEM(blocks.shape, BF16),
                 pltpu.SemaphoreType.DMA((FETCHES,)),
+                pltpu.SMEM((slots,), jnp.int32),
+                pltpu.SMEM((slots,), jnp.int32),
+                pltpu.SemaphoreType.DMA((2,)),
             ],
         )
 
     def adjoint(held, mine, theirs):
         return over_slots(
             adjoint_kernel,
+            SMEM,
+            lists,
+            VMEM,
             held,
-            VMEM,
             (mine, theirs),
             (inner_part, outer_part) * 2,
             [pltpu.VMEM((RB_LOC * pair, BLK), BF16), pltpu.VMEM((cells + 1, pair, BLK), F32)],
@@ -523,15 +545,16 @@
     held = hold(first)
     first_mine = gathered(first)
     second_mine = gathered(second)
-    second_mine, _ = lax.optimization_barrier((second_mine, first_mine))
-    mine_in, mine_out, *to_beside = adjoint(held, first_mine, swap(first_mine, "src", 1))
-    beside_in, beside_out = [swap(x, "rcv", 1) for x in to_beside]
     second_halves = (second_mine, swap(second_mine, "src", 1))
-    second_halves, mine_in = lax.optimization_barrier((second_halves, mine_in))
+    second_halves, _ = lax.optimization_barrier((second_halves, first_mine))
     other_in, other_out, diagonal_in, diagonal_out = adjoint(held, *second_halves)
     both = lambda here, there: (here.astype(F32) + swap(there, "rcv", 1).astype(F32)).astype(BF16)
-    far_out = swap(both(other_out, diagonal_out), "rcv", 2)
-    far_in = swap(both(other_in, diagonal_in), "rcv", 2)
+    to_far = [both(other_out, diagonal_out), both(other_in, diagonal_in)]
+    far_out, far_in = [swap(x, "rcv", 2) for x in to_far]
+    first_theirs = swap(first_mine, "src", 1)
+    first_theirs, _ = lax.optimization_barrier((first_theirs, to_far))
+    mine_in, mine_out, *to_beside = adjoint(held, first_mine, first_theirs)
+    beside_in, beside_out = [swap(x, "rcv", 1) for x in to_beside]
 
     edges = (mine_out.astype(F32) + beside_out.astype(F32) + far_out.astype(F32)).astype(BF16)
     top, bottom = exchange_edges(edges[:edge_cells], edges[edge_cells:])

time: 101 us -> 98.8 us (0.978)
  waiting for transfers between devices: 24.3 us -> 19 us
  starting transfers between devices: 41.2 us -> 45.6 us
  local copies, waits for them, and re-layouts: 1.44 us -> 0.09 us
    ppermute x28, waiting for transfers between devices: 22.1 us -> 17.2 us  [swap(): return lax.ppermute(x, axis, [(i, i ^ distance) for i in range(size)])]
    ppermute x28, starting transfers between devices: 29.2 us -> 33.6 us  [swap(): return lax.ppermute(x, axis, [(i, i ^ distance) for i in range(size)])]
    unnamed x10 -> x6, local copies, waits for them, and re-layouts: 1.37 us -> 0.01 us
  transfers between devices with their start and end apart: 32 -> 32, of which waited for: 14 -> 13; matrix products, arithmetic and copies ran while one was open for 1% -> 1% of each run, Pallas kernels for 23% -> 24%
where the time goes in v6:
time: 98.8 us; the launch traced here: 98.6 us
  starting transfers between devices  45.6 us (46%)
  Pallas kernels  32.2 us (33%)
  waiting for transfers between devices  19 us (19%)
    ppermute x28, starting transfers between devices, swap(): return lax.ppermute(x, axis, [(i, i ^ distance) for i in range(size)])  33.6 us
    pallas_call x4, Pallas kernels, over_slots(): pl.pallas_call(kernel, out_shape=outs, in_specs=[list_spec, list_spec, SM...  17.4 us
    ppermute x28, waiting for transfers between devices, swap(): return lax.ppermute(x, axis, [(i, i ^ distance) for i in range(size)])  17.2 us
    ppermute x4, starting transfers between devices, exchange_edges(): return (lax.ppermute(south, 'src', down), lax.ppermute(north, 'src', up))  12 us
    pallas_call x1, Pallas kernels, per_device(): pl.pallas_call(back_outer_kernel, out_shape=jax.ShapeDtypeStruct((probe_l...  3.36 us
    pallas_call x1, Pallas kernels, hold(): pl.pallas_call(hold_kernel, out_shape=jax.ShapeDtypeStruct(blocks.shape,...  2.79 us
    pallas_call x1, Pallas kernels, per_device(): pl.pallas_call(back_inner_kernel, out_shape=(jax.ShapeDtypeStruct(by_half...  2.61 us
    pallas_call x1, Pallas kernels, per_device(): pl.pallas_call(smooth_inner_kernel, out_shape=(inner_part, state), in_spe...  2.43 us
  transfers between devices with their start and end apart: 32, of which 13 were waited for; matrix products, arithmetic and copies ran while one was open for 1% of the time, Pallas kernels for 24%

profile of v6, /device:TPU:0, one launch (start us, length us, event | category | flops | bytes accessed | tf_op | source)
XLA Modules:
  0.0 98.6 jit_solution(13714911913918306258)
XLA Ops:
  0.0 1.4 %edges.1 = (bf16[272,256]{1,0:T(8,128)(2,1)S(1)}, bf16[272,256]{1,0:T(8,128)(2,1)S(1)}, bf16[1024,256]{1,0:T(8,128)(2,1)S(1)}, f32[16,256]{1,0:T(8,128)S(1)}) custom-call(bf16[1024,256]{1,0:T(8,128)(2,1)} %bitcast.69, f32[16,256]{1,0:T(8,128)} %kappa_hbm.1), custom_call_target="tpu_custom_call" | custom-call | tf_op jit(solution)/shard_map/edges/pallas_call | solution.py:402
  1.4 4.9 %collective-permute-start = (bf16[272,256]{1,0:T(8,128)(2,1)S(1)}, bf16[272,256]{1,0:T(8,128)(2,1)S(1)}, u32[]{:S(2)}, u32[]{:S(2)}) collective-permute-start(bf16[272,256]{1,0:T(8,128)(2,1)S(1)} %get-tuple-element.31), channel_id=1, source_target_pairs={{0,4},{4,8},{8,12},{12,16},{16,20},{20,24},{24,28},{1,5},{5,9},{9,... | collective-permute-start | bytes 417800 | tf_op jit(solution)/shard_map/ppermute | solution.py:387
  7.5 2.4 %smooth_inner.1 = (bf16[16,64,128]{2,1,0:T(8,128)(2,1)S(1)}, f32[2,4,2,64,256]{4,3,2,1,0:T(8,128)S(1)}) custom-call(bf16[1024,256]{1,0:T(8,128)(2,1)S(1)} %get-tuple-element.33.probes_ref, f32[16,256]{1,0:T(8,128)S(1)} %get-tuple-element.30.kappa_ref), custom_call_target="tpu_custom_call" | custom-call | tf_op jit(solution)/shard_map/smooth_inner/pallas_call | solution.py:434
  10.0 1.6 %collective-permute-start.13 = (bf16[16,64,128]{2,1,0:T(8,128)(2,1)S(1)}, bf16[16,64,128]{2,1,0:T(8,128)(2,1)S(1)}, u32[]{:S(2)}, u32[]{:S(2)}) collective-permute-start(bf16[16,64,128]{2,1,0:T(8,128)(2,1)S(1)} %get-tuple-element.34.near_in), channel_id=1, source_target_pairs={{0,2},{1,3},{2,0},{3,1},{4,6},{5,7},{6,4},{7,5},{8,10},{9,11},{10,... | collective-permute-start | bytes 786440 | tf_op jit(solution)/shard_map/ppermute | solution.py:376
  11.6 1.7 %collective-permute-done.1.below_ref = bf16[272,256]{1,0:T(8,128)(2,1)S(1)} collective-permute-done((bf16[272,256]{1,0:T(8,128)(2,1)S(1)}, bf16[272,256]{1,0:T(8,128)(2,1)S(1)}, u32[]{:S(2)}, u32[]{:S(2)}) %collective-permute-start.1) | collective-permute-done | bytes 139296 | tf_op jit(solution)/shard_map/ppermute | solution.py:387
  13.3 2.2 %smooth_outer.1.near_out = bf16[16,64,128]{2,1,0:T(8,128)(2,1)S(1)} custom-call(f32[16,256]{1,0:T(8,128)S(1)} %get-tuple-element.30.kappa_ref, bf16[272,256]{1,0:T(8,128)(2,1)S(1)} %collective-permute-done.above_ref, bf16[272,256]{1,0:T(8,128)(2,1)S(1)} %collective-permute-done.1.below_ref, f32[2,4,2,64,256]{4,3,2,1,0:T(8,128)S(1)} %get-tuple-element.35.state_ref), custom_call_target="tpu_custom_call" | custom-call | tf_op jit(solution)/shard_map/smooth_outer/pallas_call | solution.py:447
  15.6 1.6 %collective-permute-start.4 = (bf16[16,64,128]{2,1,0:T(8,128)(2,1)S(1)}, bf16[16,64,128]{2,1,0:T(8,128)(2,1)S(1)}, u32[]{:S(2)}, u32[]{:S(2)}) collective-permute-start(bf16[16,64,128]{2,1,0:T(8,128)(2,1)S(1)} %smooth_outer.1.near_out), channel_id=1, source_target_pairs={{0,2},{1,3},{2,0},{3,1},{4,6},{5,7},{6,4},{7,5},{8,10},{9,11},{10,... | collective-permute-start | bytes 786440 | tf_op jit(solution)/shard_map/ppermute | solution.py:376
  18.1 4.9 %forward_kernel.2 = (bf16[8,128,128]{2,1,0:T(8,128)(2,1)S(1)}, bf16[8,128,128]{2,1,0:T(8,128)(2,1)S(1)}) custom-call(s32[192]{0:T(256)} %bitcast.54, s32[192]{0:T(256)} %bitcast.58, s32[1]{0:T(128)} %bitcast.48.count, s32[2]{0:T(128)S(1)} %pad_add_fusion.place, bf16[192,128,128]{2,1,0:T(8,128)(2,1)} %bitcast.62, ...), custom_call_target="tpu_custom_call" | custom-call | flops 805306368 | bytes 6291456 | tf_op jit(solution)/shard_map/forward_kernel/pallas_call | solution.py:469
  24.3 2.4 %collective-permute-start.5 = (bf16[8,128,128]{2,1,0:T(8,128)(2,1)S(1)}, bf16[8,128,128]{2,1,0:T(8,128)(2,1)S(1)}, u32[]{:S(2)}, u32[]{:S(2)}) collective-permute-start(bf16[8,128,128]{2,1,0:T(8,128)(2,1)S(1)} %get-tuple-element.38), channel_id=1, source_target_pairs={{0,4},{4,0},{8,12},{12,8},{16,20},{20,16},{24,28},{28,24},{1,5},{5... | collective-permute-start | bytes 786440 | tf_op jit(solution)/shard_map/ppermute | solution.py:376
  26.7 4.9 %forward_kernel.3 = (bf16[8,128,128]{2,1,0:T(8,128)(2,1)S(1)}, bf16[8,128,128]{2,1,0:T(8,128)(2,1)S(1)}) custom-call(s32[192]{0:T(256)} %bitcast.55, s32[192]{0:T(256)} %bitcast.59, s32[1]{0:T(128)} %bitcast.49.count, s32[2]{0:T(128)S(1)} %pad_add_fusion.place, bf16[192,128,128]{2,1,0:T(8,128)(2,1)} %bitcast.63, ...), custom_call_target="tpu_custom_call" | custom-call | flops 805306368 | bytes 6291456 | tf_op jit(solution)/shard_map/forward_kernel/pallas_call | solution.py:469
  31.7 1.6 %collective-permute-start.16 = (bf16[8,128,128]{2,1,0:T(8,128)(2,1)S(1)}, bf16[8,128,128]{2,1,0:T(8,128)(2,1)S(1)}, u32[]{:S(2)}, u32[]{:S(2)}) collective-permute-start(bf16[8,128,128]{2,1,0:T(8,128)(2,1)S(1)} %get-tuple-element.41), channel_id=1, source_target_pairs={{0,4},{4,0},{8,12},{12,8},{16,20},{20,16},{24,28},{28,24},{1,5},{5... | collective-permute-start | bytes 786440 | tf_op jit(solution)/shard_map/ppermute | solution.py:376
  33.8 2.9 %collective-permute-start.6 = (bf16[256,128]{1,0:T(8,128)(2,1)S(1)}, bf16[256,128]{1,0:T(8,128)(2,1)S(1)}, u32[]{:S(2)}, u32[]{:S(2)}) collective-permute-start(bf16[256,128]{1,0:T(8,128)(2,1)S(1)} %get-tuple-element.60), channel_id=1, source_target_pairs={{0,16},{4,20},{8,24},{12,28},{16,0},{20,4},{24,8},{28,12},{1,17},{... | collective-permute-start | bytes 196616 | tf_op jit(solution)/shard_map/ppermute | solution.py:376
  36.7 1.6 %collective-permute-start.8 = (bf16[256,128]{1,0:T(8,128)(2,1)S(1)}, bf16[256,128]{1,0:T(8,128)(2,1)S(1)}, u32[]{:S(2)}, u32[]{:S(2)}) collective-permute-start(bf16[256,128]{1,0:T(8,128)(2,1)S(1)} %get-tuple-element.61), channel_id=1, source_target_pairs={{0,8},{4,12},{8,0},{12,4},{16,24},{20,28},{24,16},{28,20},{1,9},{5... | collective-permute-start | bytes 196616 | tf_op jit(solution)/shard_map/ppermute | solution.py:376
  38.3 1.9 %collective-permute-done.16 = bf16[8,128,128]{2,1,0:T(8,128)(2,1)S(1)} collective-permute-done((bf16[8,128,128]{2,1,0:T(8,128)(2,1)S(1)}, bf16[8,128,128]{2,1,0:T(8,128)(2,1)S(1)}, u32[]{:S(2)}, u32[]{:S(2)}) %collective-permute-start.16) | collective-permute-done | bytes 262176 | tf_op jit(solution)/shard_map/ppermute | solution.py:376
  40.3 2.7 %collective-permute-start.17 = (bf16[256,128]{1,0:T(8,128)(2,1)S(1)}, bf16[256,128]{1,0:T(8,128)(2,1)S(1)}, u32[]{:S(2)}, u32[]{:S(2)}) collective-permute-start(bf16[256,128]{1,0:T(8,128)(2,1)S(1)} %get-tuple-element.57), channel_id=1, source_target_pairs={{0,16},{4,20},{8,24},{12,28},{16,0},{20,4},{24,8},{28,12},{1,17},{... | collective-permute-start | bytes 196616 | tf_op jit(solution)/shard_map/ppermute | solution.py:376
  43.0 1.5 %collective-permute-start.19 = (bf16[256,128]{1,0:T(8,128)(2,1)S(1)}, bf16[256,128]{1,0:T(8,128)(2,1)S(1)}, u32[]{:S(2)}, u32[]{:S(2)}) collective-permute-start(bf16[256,128]{1,0:T(8,128)(2,1)S(1)} %get-tuple-element.58), channel_id=1, source_target_pairs={{0,8},{4,12},{8,0},{12,4},{16,24},{20,28},{24,16},{28,20},{1,9},{5... | collective-permute-start | bytes 196616 | tf_op jit(solution)/shard_map/ppermute | solution.py:376
  47.3 3.1 %collective-permute-done.18 = bf16[256,128]{1,0:T(8,128)(2,1)S(1)} collective-permute-done((bf16[256,128]{1,0:T(8,128)(2,1)S(1)}, bf16[256,128]{1,0:T(8,128)(2,1)S(1)}, u32[]{:S(2)}, u32[]{:S(2)}) %collective-permute-start.18) | collective-permute-done | bytes 65568 | tf_op jit(solution)/shard_map/ppermute | solution.py:376
  50.6 1.4 %collective-permute-start.22 = (bf16[256,128]{1,0:T(8,128)(2,1)S(1)}, bf16[256,128]{1,0:T(8,128)(2,1)S(1)}, u32[]{:S(2)}, u32[]{:S(2)}) collective-permute-start(bf16[256,128]{1,0:T(8,128)(2,1)S(1)} %get-tuple-element.63), channel_id=1, source_target_pairs={{0,24},{4,28},{8,16},{12,20},{16,8},{20,12},{24,0},{28,4},{1,25},{... | collective-permute-start | bytes 196616 | tf_op jit(solution)/shard_map/ppermute | solution.py:376
  52.0 3.0 %collective-permute-start.20 = (bf16[256,128]{1,0:T(8,128)(2,1)S(1)}, bf16[256,128]{1,0:T(8,128)(2,1)S(1)}, u32[]{:S(2)}, u32[]{:S(2)}) collective-permute-start(bf16[256,128]{1,0:T(8,128)(2,1)S(1)} %get-tuple-element.63), channel_id=1, source_target_pairs={{0,8},{4,12},{8,0},{12,4},{16,24},{20,28},{24,16},{28,20},{1,9},{5... | collective-permute-start | bytes 196616 | tf_op jit(solution)/shard_map/ppermute | solution.py:376
  55.0 1.7 %collective-permute-done.22 = bf16[256,128]{1,0:T(8,128)(2,1)S(1)} collective-permute-done((bf16[256,128]{1,0:T(8,128)(2,1)S(1)}, bf16[256,128]{1,0:T(8,128)(2,1)S(1)}, u32[]{:S(2)}, u32[]{:S(2)}) %collective-permute-start.22) | collective-permute-done | bytes 65568 | tf_op jit(solution)/shard_map/ppermute | solution.py:376
  56.7 1.4 %collective-permute-done.21 = bf16[256,128]{1,0:T(8,128)(2,1)S(1)} collective-permute-done((bf16[256,128]{1,0:T(8,128)(2,1)S(1)}, bf16[256,128]{1,0:T(8,128)(2,1)S(1)}, u32[]{:S(2)}, u32[]{:S(2)}) %collective-permute-start.21) | collective-permute-done | bytes 65568 | tf_op jit(solution)/shard_map/ppermute | solution.py:376
  59.0 1.5 %collective-permute-start.11 = (bf16[256,128]{1,0:T(8,128)(2,1)S(1)}, bf16[256,128]{1,0:T(8,128)(2,1)S(1)}, u32[]{:S(2)}, u32[]{:S(2)}) collective-permute-start(bf16[256,128]{1,0:T(8,128)(2,1)S(1)} %get-tuple-element.64.after_ref), channel_id=1, source_target_pairs={{0,24},{4,28},{8,16},{12,20},{16,8},{20,12},{24,0},{28,4},{1,25},{... | collective-permute-start | bytes 196616 | tf_op jit(solution)/shard_map/ppermute | solution.py:376
  61.7 1.7 %collective-permute-start.9 = (bf16[256,128]{1,0:T(8,128)(2,1)S(1)}, bf16[256,128]{1,0:T(8,128)(2,1)S(1)}, u32[]{:S(2)}, u32[]{:S(2)}) collective-permute-start(bf16[256,128]{1,0:T(8,128)(2,1)S(1)} %get-tuple-element.64.after_ref), channel_id=1, source_target_pairs={{0,8},{4,12},{8,0},{12,4},{16,24},{20,28},{24,16},{28,20},{1,9},{5... | collective-permute-start | bytes 196616 | tf_op jit(solution)/shard_map/ppermute | solution.py:376
  63.4 2.8 %hold.1.held = bf16[192,128,128]{2,1,0:T(8,128)(2,1)S(1)} custom-call(bf16[192,128,128]{2,1,0:T(8,128)(2,1)} %bitcast.64, bf16[256,128]{1,0:T(8,128)(2,1)S(1)} %get-tuple-element.64.after_ref), custom_call_target="tpu_custom_call" | custom-call | bytes 12582912 | tf_op jit(solution)/shard_map/hold/pallas_call | solution.py:417
  66.7 3.8 %adjoint_kernel.2 = (bf16[16,64,128]{2,1,0:T(8,128)(2,1)S(1)}, bf16[16,64,128]{2,1,0:T(8,128)(2,1)S(1)}, bf16[16,64,128]{2,1,0:T(8,128)(2,1)S(1)}, bf16[16,64,128]{2,1,0:T(8,128)(2,1)S(1)}) custom-call(s32[192]{0:T(256)S(1)} %bitcast.56, s32[192]{0:T(256)S(1)} %bitcast.60, s32[1]{0:T(128)} %bitcast.50.count, s32[2]{0:T(128)S(1)} %pad_add_fusion.place, ...), custom_call_target="tpu_custom_call" | custom-call | flops 805306368 | bytes 6291456 | tf_op jit(solution)/shard_map/adjoint_kernel/pallas_call | solution.py:469
  72.4 2.2 %collective-permute-start.27 = (bf16[16,64,128]{2,1,0:T(8,128)(2,1)S(1)}, bf16[16,64,128]{2,1,0:T(8,128)(2,1)S(1)}, u32[]{:S(2)}, u32[]{:S(2)}) collective-permute-start(bf16[16,64,128]{2,1,0:T(8,128)(2,1)S(1)} %add_convert_fusion.2), channel_id=1, source_target_pairs={{0,2},{1,3},{2,0},{3,1},{4,6},{5,7},{6,4},{7,5},{8,10},{9,11},{10,... | collective-permute-start | bytes 786440 | tf_op jit(solution)/shard_map/ppermute | solution.py:376
  74.6 4.7 %collective-permute-done.12.theirs_ref = bf16[4,256,128]{2,1,0:T(8,128)(2,1)S(1)} collective-permute-done((bf16[4,256,128]{2,1,0:T(8,128)(2,1)S(1)}, bf16[4,256,128]{2,1,0:T(8,128)(2,1)S(1)}, u32[]{:S(2)}, u32[]{:S(2)}) %collective-permute-start.12) | collective-permute-done | bytes 262176 | tf_op jit(solution)/shard_map/ppermute | solution.py:376
  79.3 3.8 %adjoint_kernel.3 = (bf16[16,64,128]{2,1,0:T(8,128)(2,1)S(1)}, bf16[16,64,128]{2,1,0:T(8,128)(2,1)S(1)}, bf16[16,64,128]{2,1,0:T(8,128)(2,1)S(1)}, bf16[16,64,128]{2,1,0:T(8,128)(2,1)S(1)}) custom-call(s32[192]{0:T(256)S(1)} %bitcast.57, s32[192]{0:T(256)S(1)} %bitcast.61, s32[1]{0:T(128)} %bitcast.51.count, s32[2]{0:T(128)S(1)} %pad_add_fusion.place, ...), custom_call_target="tpu_custom_call" | custom-call | flops 805306368 | bytes 6291456 | tf_op jit(solution)/shard_map/adjoint_kernel/pallas_call | solution.py:469
  83.2 2.4 %collective-permute-start.31 = (bf16[16,64,128]{2,1,0:T(8,128)(2,1)S(1)}, bf16[16,64,128]{2,1,0:T(8,128)(2,1)S(1)}, u32[]{:S(2)}, u32[]{:S(2)}) collective-permute-start(bf16[16,64,128]{2,1,0:T(8,128)(2,1)S(1)} %add_convert_fusion.1), channel_id=1, source_target_pairs={{0,2},{1,3},{2,0},{3,1},{4,6},{5,7},{6,4},{7,5},{8,10},{9,11},{10,... | collective-permute-start | bytes 786440 | tf_op jit(solution)/shard_map/ppermute | solution.py:376
  87.2 4.6 %collective-permute-start.28 = (bf16[8,64,128]{2,1,0:T(8,128)(2,1)S(1)}, bf16[8,64,128]{2,1,0:T(8,128)(2,1)S(1)}, u32[]{:S(2)}, u32[]{:S(2)}) collective-permute-start(bf16[8,64,128]{2,1,0:T(8,128)(2,1)S(1)} %get-tuple-element.56), channel_id=1, source_target_pairs={{0,4},{4,8},{8,12},{12,16},{16,20},{20,24},{24,28},{1,5},{5,9},{9,... | collective-permute-start | bytes 393224 | tf_op jit(solution)/shard_map/ppermute | solution.py:387
  92.5 2.6 %back_inner.1 = (f32[2,1024,128]{2,1,0:T(8,128)S(1)}, f32[2,4,2,64,256]{4,3,2,1,0:T(8,128)S(1)}) custom-call(bf16[1024,256]{1,0:T(8,128)(2,1)S(1)} %get-tuple-element.33.probes_ref, f32[16,256]{1,0:T(8,128)S(1)} %get-tuple-element.30.kappa_ref, bf16[16,64,128]{2,1,0:T(8,128)(2,1)S(1)} %get-tuple-element.51.own_in, ...), custom_call_target="tpu_custom_call" | custom-call | tf_op jit(solution)/shard_map/back_inner/pallas_call | solution.py:562
  95.2 3.4 %back_outer.1 = f32[1024,256]{1,0:T(8,128)} custom-call(f32[2]{0:T(128)S(1)} %add_convert_fusion.5.inside, f32[16,256]{1,0:T(8,128)S(1)} %get-tuple-element.30.kappa_ref, bf16[272,256]{1,0:T(8,128)(2,1)S(1)} %collective-permute-done.above_ref, bf16[272,256]{1,0:T(8,128)(2,1)S(1)} %collective-permute-done.1.below_ref, ...), custom_call_target="tpu_custom_call" | custom-call | tf_op jit(solution)/shard_map/back_outer/pallas_call | solution.py:571
  (62 shorter events, 13.4 us)
Async XLA Ops:
  1.4 10.2 %collective-permute-start = (bf16[272,256]{1,0:T(8,128)(2,1)S(1)}, bf16[272,256]{1,0:T(8,128)(2,1)S(1)}, u32[]{:S(2)}, u32[]{:S(2)}) collective-permute-start(bf16[272,256]{1,0:T(8,128)(2,1)S(1)} %get-tuple-element.31), channel_id=1, source_target_pairs={{0,4},{4,8},{8,12},{12,16},{16,20},{20,24},{24,28},{1,5},{5,9},{9,... | collective-permute-start | bytes 417800 | tf_op jit(solution)/shard_map/ppermute | solution.py:387
  6.2 7.0 %collective-permute-start.1 = (bf16[272,256]{1,0:T(8,128)(2,1)S(1)}, bf16[272,256]{1,0:T(8,128)(2,1)S(1)}, u32[]{:S(2)}, u32[]{:S(2)}) collective-permute-start(bf16[272,256]{1,0:T(8,128)(2,1)S(1)} %get-tuple-element.32), channel_id=1, source_target_pairs={{4,0},{8,4},{12,8},{16,12},{20,16},{24,20},{28,24},{5,1},{9,5},{13... | collective-permute-start | bytes 417800 | tf_op jit(solution)/shard_map/ppermute | solution.py:387
  10.0 7.9 %collective-permute-start.13 = (bf16[16,64,128]{2,1,0:T(8,128)(2,1)S(1)}, bf16[16,64,128]{2,1,0:T(8,128)(2,1)S(1)}, u32[]{:S(2)}, u32[]{:S(2)}) collective-permute-start(bf16[16,64,128]{2,1,0:T(8,128)(2,1)S(1)} %get-tuple-element.34.near_in), channel_id=1, source_target_pairs={{0,2},{1,3},{2,0},{3,1},{4,6},{5,7},{6,4},{7,5},{8,10},{9,11},{10,... | collective-permute-start | bytes 786440 | tf_op jit(solution)/shard_map/ppermute | solution.py:376
  11.6 6.5 %collective-permute-start.2 = (bf16[16,64,128]{2,1,0:T(8,128)(2,1)S(1)}, bf16[16,64,128]{2,1,0:T(8,128)(2,1)S(1)}, u32[]{:S(2)}, u32[]{:S(2)}) collective-permute-start(bf16[16,64,128]{2,1,0:T(8,128)(2,1)S(1)} %get-tuple-element.34.near_in), channel_id=1, source_target_pairs={{0,1},{1,0},{2,3},{3,2},{4,5},{5,4},{6,7},{7,6},{8,9},{9,8},{10,11... | collective-permute-start | bytes 786440 | tf_op jit(solution)/shard_map/ppermute | solution.py:376
  15.5 2.6 %collective-permute-start.3 = (bf16[16,64,128]{2,1,0:T(8,128)(2,1)S(1)}, bf16[16,64,128]{2,1,0:T(8,128)(2,1)S(1)}, u32[]{:S(2)}, u32[]{:S(2)}) collective-permute-start(bf16[16,64,128]{2,1,0:T(8,128)(2,1)S(1)} %smooth_outer.1.near_out), channel_id=1, source_target_pairs={{0,1},{1,0},{2,3},{3,2},{4,5},{5,4},{6,7},{7,6},{8,9},{9,8},{10,11... | collective-permute-start | bytes 786440 | tf_op jit(solution)/shard_map/ppermute | solution.py:376
  15.6 8.7 %collective-permute-start.4 = (bf16[16,64,128]{2,1,0:T(8,128)(2,1)S(1)}, bf16[16,64,128]{2,1,0:T(8,128)(2,1)S(1)}, u32[]{:S(2)}, u32[]{:S(2)}) collective-permute-start(bf16[16,64,128]{2,1,0:T(8,128)(2,1)S(1)} %smooth_outer.1.near_out), channel_id=1, source_target_pairs={{0,2},{1,3},{2,0},{3,1},{4,6},{5,7},{6,4},{7,5},{8,10},{9,11},{10,... | collective-permute-start | bytes 786440 | tf_op jit(solution)/shard_map/ppermute | solution.py:376
  17.9 8.9 %collective-permute-start.14 = (bf16[16,64,128]{2,1,0:T(8,128)(2,1)S(1)}, bf16[16,64,128]{2,1,0:T(8,128)(2,1)S(1)}, u32[]{:S(2)}, u32[]{:S(2)}) collective-permute-start(bf16[16,64,128]{2,1,0:T(8,128)(2,1)S(1)} %collective-permute-done.13.near_in), channel_id=1, source_target_pairs={{0,1},{1,0},{2,3},{3,2},{4,5},{5,4},{6,7},{7,6},{8,9},{9,8},{10,11... | collective-permute-start | bytes 786440 | tf_op jit(solution)/shard_map/ppermute | solution.py:376
  24.3 2.5 %collective-permute-start.15 = (bf16[16,64,128]{2,1,0:T(8,128)(2,1)S(1)}, bf16[16,64,128]{2,1,0:T(8,128)(2,1)S(1)}, u32[]{:S(2)}, u32[]{:S(2)}) collective-permute-start(bf16[16,64,128]{2,1,0:T(8,128)(2,1)S(1)} %collective-permute-done.4.near_out), channel_id=1, source_target_pairs={{0,1},{1,0},{2,3},{3,2},{4,5},{5,4},{6,7},{7,6},{8,9},{9,8},{10,11... | collective-permute-start | bytes 786440 | tf_op jit(solution)/shard_map/ppermute | solution.py:376
  24.3 9.4 %collective-permute-start.5 = (bf16[8,128,128]{2,1,0:T(8,128)(2,1)S(1)}, bf16[8,128,128]{2,1,0:T(8,128)(2,1)S(1)}, u32[]{:S(2)}, u32[]{:S(2)}) collective-permute-start(bf16[8,128,128]{2,1,0:T(8,128)(2,1)S(1)} %get-tuple-element.38), channel_id=1, source_target_pairs={{0,4},{4,0},{8,12},{12,8},{16,20},{20,16},{24,28},{28,24},{1,5},{5... | collective-permute-start | bytes 786440 | tf_op jit(solution)/shard_map/ppermute | solution.py:376
  31.7 8.5 %collective-permute-start.16 = (bf16[8,128,128]{2,1,0:T(8,128)(2,1)S(1)}, bf16[8,128,128]{2,1,0:T(8,128)(2,1)S(1)}, u32[]{:S(2)}, u32[]{:S(2)}) collective-permute-start(bf16[8,128,128]{2,1,0:T(8,128)(2,1)S(1)} %get-tuple-element.41), channel_id=1, source_target_pairs={{0,4},{4,0},{8,12},{12,8},{16,20},{20,16},{24,28},{28,24},{1,5},{5... | collective-permute-start | bytes 786440 | tf_op jit(solution)/shard_map/ppermute | solution.py:376
  33.8 10.6 %collective-permute-start.6 = (bf16[256,128]{1,0:T(8,128)(2,1)S(1)}, bf16[256,128]{1,0:T(8,128)(2,1)S(1)}, u32[]{:S(2)}, u32[]{:S(2)}) collective-permute-start(bf16[256,128]{1,0:T(8,128)(2,1)S(1)} %get-tuple-element.60), channel_id=1, source_target_pairs={{0,16},{4,20},{8,24},{12,28},{16,0},{20,4},{24,8},{28,12},{1,17},{... | collective-permute-start | bytes 196616 | tf_op jit(solution)/shard_map/ppermute | solution.py:376
  36.7 9.0 %collective-permute-start.8 = (bf16[256,128]{1,0:T(8,128)(2,1)S(1)}, bf16[256,128]{1,0:T(8,128)(2,1)S(1)}, u32[]{:S(2)}, u32[]{:S(2)}) collective-permute-start(bf16[256,128]{1,0:T(8,128)(2,1)S(1)} %get-tuple-element.61), channel_id=1, source_target_pairs={{0,8},{4,12},{8,0},{12,4},{16,24},{20,28},{24,16},{28,20},{1,9},{5... | collective-permute-start | bytes 196616 | tf_op jit(solution)/shard_map/ppermute | solution.py:376
  38.2 7.4 %collective-permute-start.7 = (bf16[256,128]{1,0:T(8,128)(2,1)S(1)}, bf16[256,128]{1,0:T(8,128)(2,1)S(1)}, u32[]{:S(2)}, u32[]{:S(2)}) collective-permute-start(bf16[256,128]{1,0:T(8,128)(2,1)S(1)} %get-tuple-element.62), channel_id=1, source_target_pairs={{0,24},{4,28},{8,16},{12,20},{16,8},{20,12},{24,0},{28,4},{1,25},{... | collective-permute-start | bytes 196616 | tf_op jit(solution)/shard_map/ppermute | solution.py:376
  40.3 6.6 %collective-permute-start.17 = (bf16[256,128]{1,0:T(8,128)(2,1)S(1)}, bf16[256,128]{1,0:T(8,128)(2,1)S(1)}, u32[]{:S(2)}, u32[]{:S(2)}) collective-permute-start(bf16[256,128]{1,0:T(8,128)(2,1)S(1)} %get-tuple-element.57), channel_id=1, source_target_pairs={{0,16},{4,20},{8,24},{12,28},{16,0},{20,4},{24,8},{28,12},{1,17},{... | collective-permute-start | bytes 196616 | tf_op jit(solution)/shard_map/ppermute | solution.py:376
  43.0 4.4 %collective-permute-start.19 = (bf16[256,128]{1,0:T(8,128)(2,1)S(1)}, bf16[256,128]{1,0:T(8,128)(2,1)S(1)}, u32[]{:S(2)}, u32[]{:S(2)}) collective-permute-start(bf16[256,128]{1,0:T(8,128)(2,1)S(1)} %get-tuple-element.58), channel_id=1, source_target_pairs={{0,8},{4,12},{8,0},{12,4},{16,24},{20,28},{24,16},{28,20},{1,9},{5... | collective-permute-start | bytes 196616 | tf_op jit(solution)/shard_map/ppermute | solution.py:376
  44.4 6.1 %collective-permute-start.18 = (bf16[256,128]{1,0:T(8,128)(2,1)S(1)}, bf16[256,128]{1,0:T(8,128)(2,1)S(1)}, u32[]{:S(2)}, u32[]{:S(2)}) collective-permute-start(bf16[256,128]{1,0:T(8,128)(2,1)S(1)} %get-tuple-element.59), channel_id=1, source_target_pairs={{0,24},{4,28},{8,16},{12,20},{16,8},{20,12},{24,0},{28,4},{1,25},{... | collective-permute-start | bytes 196616 | tf_op jit(solution)/shard_map/ppermute | solution.py:376
  50.6 6.2 %collective-permute-start.22 = (bf16[256,128]{1,0:T(8,128)(2,1)S(1)}, bf16[256,128]{1,0:T(8,128)(2,1)S(1)}, u32[]{:S(2)}, u32[]{:S(2)}) collective-permute-start(bf16[256,128]{1,0:T(8,128)(2,1)S(1)} %get-tuple-element.63), channel_id=1, source_target_pairs={{0,24},{4,28},{8,16},{12,20},{16,8},{20,12},{24,0},{28,4},{1,25},{... | collective-permute-start | bytes 196616 | tf_op jit(solution)/shard_map/ppermute | solution.py:376
  52.0 6.1 %collective-permute-start.21 = (bf16[256,128]{1,0:T(8,128)(2,1)S(1)}, bf16[256,128]{1,0:T(8,128)(2,1)S(1)}, u32[]{:S(2)}, u32[]{:S(2)}) collective-permute-start(bf16[256,128]{1,0:T(8,128)(2,1)S(1)} %get-tuple-element.63), channel_id=1, source_target_pairs={{0,16},{4,20},{8,24},{12,28},{16,0},{20,4},{24,8},{28,12},{1,17},{... | collective-permute-start | bytes 196616 | tf_op jit(solution)/shard_map/ppermute | solution.py:376
  52.0 6.1 %collective-permute-start.20 = (bf16[256,128]{1,0:T(8,128)(2,1)S(1)}, bf16[256,128]{1,0:T(8,128)(2,1)S(1)}, u32[]{:S(2)}, u32[]{:S(2)}) collective-permute-start(bf16[256,128]{1,0:T(8,128)(2,1)S(1)} %get-tuple-element.63), channel_id=1, source_target_pairs={{0,8},{4,12},{8,0},{12,4},{16,24},{20,28},{24,16},{28,20},{1,9},{5... | collective-permute-start | bytes 196616 | tf_op jit(solution)/shard_map/ppermute | solution.py:376
  58.1 8.5 %collective-permute-start.23 = (bf16[4,256,128]{2,1,0:T(8,128)(2,1)S(1)}, bf16[4,256,128]{2,1,0:T(8,128)(2,1)S(1)}, u32[]{:S(2)}, u32[]{:S(2)}) collective-permute-start(bf16[4,256,128]{2,1,0:T(8,128)(2,1)S(1)} %pad_maximum_fusion.1.mine_ref), channel_id=1, source_target_pairs={{0,4},{4,0},{8,12},{12,8},{16,20},{20,16},{24,28},{28,24},{1,5},{5... | collective-permute-start | bytes 786440 | tf_op jit(solution)/shard_map/ppermute | solution.py:376
  59.0 7.2 %collective-permute-start.11 = (bf16[256,128]{1,0:T(8,128)(2,1)S(1)}, bf16[256,128]{1,0:T(8,128)(2,1)S(1)}, u32[]{:S(2)}, u32[]{:S(2)}) collective-permute-start(bf16[256,128]{1,0:T(8,128)(2,1)S(1)} %get-tuple-element.64.after_ref), channel_id=1, source_target_pairs={{0,24},{4,28},{8,16},{12,20},{16,8},{20,12},{24,0},{28,4},{1,25},{... | collective-permute-start | bytes 196616 | tf_op jit(solution)/shard_map/ppermute | solution.py:376
  60.6 6.0 %collective-permute-start.10 = (bf16[256,128]{1,0:T(8,128)(2,1)S(1)}, bf16[256,128]{1,0:T(8,128)(2,1)S(1)}, u32[]{:S(2)}, u32[]{:S(2)}) collective-permute-start(bf16[256,128]{1,0:T(8,128)(2,1)S(1)} %get-tuple-element.64.after_ref), channel_id=1, source_target_pairs={{0,16},{4,20},{8,24},{12,28},{16,0},{20,4},{24,8},{28,12},{1,17},{... | collective-permute-start | bytes 196616 | tf_op jit(solution)/shard_map/ppermute | solution.py:376
  61.7 5.0 %collective-permute-start.9 = (bf16[256,128]{1,0:T(8,128)(2,1)S(1)}, bf16[256,128]{1,0:T(8,128)(2,1)S(1)}, u32[]{:S(2)}, u32[]{:S(2)}) collective-permute-start(bf16[256,128]{1,0:T(8,128)(2,1)S(1)} %get-tuple-element.64.after_ref), channel_id=1, source_target_pairs={{0,8},{4,12},{8,0},{12,4},{16,24},{20,28},{24,16},{28,20},{1,9},{5... | collective-permute-start | bytes 196616 | tf_op jit(solution)/shard_map/ppermute | solution.py:376
  70.5 1.8 %collective-permute-start.24 = (bf16[16,64,128]{2,1,0:T(8,128)(2,1)S(1)}, bf16[16,64,128]{2,1,0:T(8,128)(2,1)S(1)}, u32[]{:S(2)}, u32[]{:S(2)}) collective-permute-start(bf16[16,64,128]{2,1,0:T(8,128)(2,1)S(1)} %get-tuple-element.45), channel_id=1, source_target_pairs={{0,1},{1,0},{2,3},{3,2},{4,5},{5,4},{6,7},{7,6},{8,9},{9,8},{10,11... | collective-permute-start | bytes 786440 | tf_op jit(solution)/shard_map/ppermute | solution.py:376
  70.6 4.0 %collective-permute-start.25 = (bf16[16,64,128]{2,1,0:T(8,128)(2,1)S(1)}, bf16[16,64,128]{2,1,0:T(8,128)(2,1)S(1)}, u32[]{:S(2)}, u32[]{:S(2)}) collective-permute-start(bf16[16,64,128]{2,1,0:T(8,128)(2,1)S(1)} %get-tuple-element.47), channel_id=1, source_target_pairs={{0,1},{1,0},{2,3},{3,2},{4,5},{5,4},{6,7},{7,6},{8,9},{9,8},{10,11... | collective-permute-start | bytes 786440 | tf_op jit(solution)/shard_map/ppermute | solution.py:376
  71.1 8.3 %collective-permute-start.12 = (bf16[4,256,128]{2,1,0:T(8,128)(2,1)S(1)}, bf16[4,256,128]{2,1,0:T(8,128)(2,1)S(1)}, u32[]{:S(2)}, u32[]{:S(2)}) collective-permute-start(bf16[4,256,128]{2,1,0:T(8,128)(2,1)S(1)} %pad_maximum_fusion.mine_ref), channel_id=1, source_target_pairs={{0,4},{4,0},{8,12},{12,8},{16,20},{20,16},{24,28},{28,24},{1,5},{5... | collective-permute-start | bytes 786440 | tf_op jit(solution)/shard_map/ppermute | solution.py:376
  72.4 13.4 %collective-permute-start.27 = (bf16[16,64,128]{2,1,0:T(8,128)(2,1)S(1)}, bf16[16,64,128]{2,1,0:T(8,128)(2,1)S(1)}, u32[]{:S(2)}, u32[]{:S(2)}) collective-permute-start(bf16[16,64,128]{2,1,0:T(8,128)(2,1)S(1)} %add_convert_fusion.2), channel_id=1, source_target_pairs={{0,2},{1,3},{2,0},{3,1},{4,6},{5,7},{6,4},{7,5},{8,10},{9,11},{10,... | collective-permute-start | bytes 786440 | tf_op jit(solution)/shard_map/ppermute | solution.py:376
  83.1 2.7 %collective-permute-start.26 = (bf16[16,64,128]{2,1,0:T(8,128)(2,1)S(1)}, bf16[16,64,128]{2,1,0:T(8,128)(2,1)S(1)}, u32[]{:S(2)}, u32[]{:S(2)}) collective-permute-start(bf16[16,64,128]{2,1,0:T(8,128)(2,1)S(1)} %get-tuple-element.50), channel_id=1, source_target_pairs={{0,1},{1,0},{2,3},{3,2},{4,5},{5,4},{6,7},{7,6},{8,9},{9,8},{10,11... | collective-permute-start | bytes 786440 | tf_op jit(solution)/shard_map/ppermute | solution.py:376
  83.2 9.3 %collective-permute-start.31 = (bf16[16,64,128]{2,1,0:T(8,128)(2,1)S(1)}, bf16[16,64,128]{2,1,0:T(8,128)(2,1)S(1)}, u32[]{:S(2)}, u32[]{:S(2)}) collective-permute-start(bf16[16,64,128]{2,1,0:T(8,128)(2,1)S(1)} %add_convert_fusion.1), channel_id=1, source_target_pairs={{0,2},{1,3},{2,0},{3,1},{4,6},{5,7},{6,4},{7,5},{8,10},{9,11},{10,... | collective-permute-start | bytes 786440 | tf_op jit(solution)/shard_map/ppermute | solution.py:376
  85.6 6.3 %collective-permute-start.30 = (bf16[16,64,128]{2,1,0:T(8,128)(2,1)S(1)}, bf16[16,64,128]{2,1,0:T(8,128)(2,1)S(1)}, u32[]{:S(2)}, u32[]{:S(2)}) collective-permute-start(bf16[16,64,128]{2,1,0:T(8,128)(2,1)S(1)} %get-tuple-element.52), channel_id=1, source_target_pairs={{0,1},{1,0},{2,3},{3,2},{4,5},{5,4},{6,7},{7,6},{8,9},{9,8},{10,11... | collective-permute-start | bytes 786440 | tf_op jit(solution)/shard_map/ppermute | solution.py:376
  85.9 9.2 %collective-permute-start.29 = (bf16[8,64,128]{2,1,0:T(8,128)(2,1)S(1)}, bf16[8,64,128]{2,1,0:T(8,128)(2,1)S(1)}, u32[]{:S(2)}, u32[]{:S(2)}) collective-permute-start(bf16[8,64,128]{2,1,0:T(8,128)(2,1)S(1)} %get-tuple-element.55), channel_id=1, source_target_pairs={{4,0},{8,4},{12,8},{16,12},{20,16},{24,20},{28,24},{5,1},{9,5},{13... | collective-permute-start | bytes 393224 | tf_op jit(solution)/shard_map/ppermute | solution.py:387
  87.2 8.0 %collective-permute-start.28 = (bf16[8,64,128]{2,1,0:T(8,128)(2,1)S(1)}, bf16[8,64,128]{2,1,0:T(8,128)(2,1)S(1)}, u32[]{:S(2)}, u32[]{:S(2)}) collective-permute-start(bf16[8,64,128]{2,1,0:T(8,128)(2,1)S(1)} %get-tuple-element.56), channel_id=1, source_target_pairs={{0,4},{4,8},{8,12},{12,16},{16,20},{20,24},{24,28},{1,5},{5,9},{9,... | collective-permute-start | bytes 393224 | tf_op jit(solution)/shard_map/ppermute | solution.py:387
  (3 other events, 61.0 us)

commit v7 on v6

--- a/solution.py
+++ b/solution.py
@@ -10,8 +10,8 @@
 SMOOTH = 4
 SUB = 8
 PIECES = 16
-GROUP = 32
-FETCHES = 4
+GROUP = 96
+FETCHES = 3
 F32, BF16 = jnp.float32, jnp.bfloat16
 VMEM = pl.BlockSpec(memory_space=pltpu.VMEM)
 SMEM = pl.BlockSpec(memory_space=pltpu.SMEM)

time: 98.8 us -> 98.2 us (level)
  no operation moved by 1% of the time
where the time goes in v7:
time: 98.2 us; the launch traced here: 98 us
  starting transfers between devices  45.5 us (46%)
  Pallas kernels  31.4 us (32%)
  waiting for transfers between devices  19.2 us (20%)
  between operations  1.1 us (1%)
    ppermute x28, starting transfers between devices, swap(): return lax.ppermute(x, axis, [(i, i ^ distance) for i in range(size)])  33.5 us
    ppermute x28, waiting for transfers between devices, swap(): return lax.ppermute(x, axis, [(i, i ^ distance) for i in range(size)])  17.3 us
    pallas_call x4, Pallas kernels, over_slots(): pl.pallas_call(kernel, out_shape=outs, in_specs=[list_spec, list_spec, SM...  16.6 us
    ppermute x4, starting transfers between devices, exchange_edges(): return (lax.ppermute(south, 'src', down), lax.ppermute(north, 'src', up))  12 us
    pallas_call x1, Pallas kernels, per_device(): pl.pallas_call(back_outer_kernel, out_shape=jax.ShapeDtypeStruct((probe_l...  3.36 us
    pallas_call x1, Pallas kernels, hold(): pl.pallas_call(hold_kernel, out_shape=jax.ShapeDtypeStruct(blocks.shape,...  2.79 us
    pallas_call x1, Pallas kernels, per_device(): pl.pallas_call(back_inner_kernel, out_shape=(jax.ShapeDtypeStruct(by_half...  2.61 us
    pallas_call x1, Pallas kernels, per_device(): pl.pallas_call(smooth_inner_kernel, out_shape=(inner_part, state), in_spe...  2.43 us
  transfers between devices with their start and end apart: 32, of which 13 were waited for; matrix products, arithmetic and copies ran while one was open for 1% of the time, Pallas kernels for 24%

profile of v7, /device:TPU:0, one launch (start us, length us, event | category | flops | bytes accessed | tf_op | source)
XLA Modules:
  0.0 98.0 jit_solution(8110030355233952087)
XLA Ops:
  1.4 4.9 %collective-permute-start = (bf16[272,256]{1,0:T(8,128)(2,1)S(1)}, bf16[272,256]{1,0:T(8,128)(2,1)S(1)}, u32[]{:S(2)}, u32[]{:S(2)}) collective-permute-start(bf16[272,256]{1,0:T(8,128)(2,1)S(1)} %get-tuple-element.31), channel_id=1, source_target_pairs={{0,4},{4,8},{8,12},{12,16},{16,20},{20,24},{24,28},{1,5},{5,9},{9,... | collective-permute-start | bytes 417800 | tf_op jit(solution)/shard_map/ppermute | solution.py:387
  7.5 2.4 %smooth_inner.1 = (bf16[16,64,128]{2,1,0:T(8,128)(2,1)S(1)}, f32[2,4,2,64,256]{4,3,2,1,0:T(8,128)S(1)}) custom-call(bf16[1024,256]{1,0:T(8,128)(2,1)S(1)} %get-tuple-element.33.probes_ref, f32[16,256]{1,0:T(8,128)S(1)} %get-tuple-element.30.kappa_ref), custom_call_target="tpu_custom_call" | custom-call | tf_op jit(solution)/shard_map/smooth_inner/pallas_call | solution.py:434
  10.0 1.6 %collective-permute-start.13 = (bf16[16,64,128]{2,1,0:T(8,128)(2,1)S(1)}, bf16[16,64,128]{2,1,0:T(8,128)(2,1)S(1)}, u32[]{:S(2)}, u32[]{:S(2)}) collective-permute-start(bf16[16,64,128]{2,1,0:T(8,128)(2,1)S(1)} %get-tuple-element.34.near_in), channel_id=1, source_target_pairs={{0,2},{1,3},{2,0},{3,1},{4,6},{5,7},{6,4},{7,5},{8,10},{9,11},{10,... | collective-permute-start | bytes 786440 | tf_op jit(solution)/shard_map/ppermute | solution.py:376
  11.6 1.7 %collective-permute-done.1.below_ref = bf16[272,256]{1,0:T(8,128)(2,1)S(1)} collective-permute-done((bf16[272,256]{1,0:T(8,128)(2,1)S(1)}, bf16[272,256]{1,0:T(8,128)(2,1)S(1)}, u32[]{:S(2)}, u32[]{:S(2)}) %collective-permute-start.1) | collective-permute-done | bytes 139296 | tf_op jit(solution)/shard_map/ppermute | solution.py:387
  13.3 2.2 %smooth_outer.1.near_out = bf16[16,64,128]{2,1,0:T(8,128)(2,1)S(1)} custom-call(f32[16,256]{1,0:T(8,128)S(1)} %get-tuple-element.30.kappa_ref, bf16[272,256]{1,0:T(8,128)(2,1)S(1)} %collective-permute-done.above_ref, bf16[272,256]{1,0:T(8,128)(2,1)S(1)} %collective-permute-done.1.below_ref, f32[2,4,2,64,256]{4,3,2,1,0:T(8,128)S(1)} %get-tuple-element.35.state_ref), custom_call_target="tpu_custom_call" | custom-call | tf_op jit(solution)/shard_map/smooth_outer/pallas_call | solution.py:447
  15.6 1.6 %collective-permute-start.4 = (bf16[16,64,128]{2,1,0:T(8,128)(2,1)S(1)}, bf16[16,64,128]{2,1,0:T(8,128)(2,1)S(1)}, u32[]{:S(2)}, u32[]{:S(2)}) collective-permute-start(bf16[16,64,128]{2,1,0:T(8,128)(2,1)S(1)} %smooth_outer.1.near_out), channel_id=1, source_target_pairs={{0,2},{1,3},{2,0},{3,1},{4,6},{5,7},{6,4},{7,5},{8,10},{9,11},{10,... | collective-permute-start | bytes 786440 | tf_op jit(solution)/shard_map/ppermute | solution.py:376
  18.1 4.8 %forward_kernel.2 = (bf16[8,128,128]{2,1,0:T(8,128)(2,1)S(1)}, bf16[8,128,128]{2,1,0:T(8,128)(2,1)S(1)}) custom-call(s32[192]{0:T(256)} %bitcast.54, s32[192]{0:T(256)} %bitcast.58, s32[1]{0:T(128)} %bitcast.48.count, s32[2]{0:T(128)S(1)} %pad_add_fusion.place, bf16[192,128,128]{2,1,0:T(8,128)(2,1)} %bitcast.62, ...), custom_call_target="tpu_custom_call" | custom-call | flops 805306368 | bytes 6291456 | tf_op jit(solution)/shard_map/forward_kernel/pallas_call | solution.py:469
  22.9 1.4 %collective-permute-done.4.near_out = bf16[16,64,128]{2,1,0:T(8,128)(2,1)S(1)} collective-permute-done((bf16[16,64,128]{2,1,0:T(8,128)(2,1)S(1)}, bf16[16,64,128]{2,1,0:T(8,128)(2,1)S(1)}, u32[]{:S(2)}, u32[]{:S(2)}) %collective-permute-start.4) | collective-permute-done | bytes 262176 | tf_op jit(solution)/shard_map/ppermute | solution.py:376
  24.3 2.4 %collective-permute-start.5 = (bf16[8,128,128]{2,1,0:T(8,128)(2,1)S(1)}, bf16[8,128,128]{2,1,0:T(8,128)(2,1)S(1)}, u32[]{:S(2)}, u32[]{:S(2)}) collective-permute-start(bf16[8,128,128]{2,1,0:T(8,128)(2,1)S(1)} %get-tuple-element.38), channel_id=1, source_target_pairs={{0,4},{4,0},{8,12},{12,8},{16,20},{20,16},{24,28},{28,24},{1,5},{5... | collective-permute-start | bytes 786440 | tf_op jit(solution)/shard_map/ppermute | solution.py:376
  26.7 4.8 %forward_kernel.3 = (bf16[8,128,128]{2,1,0:T(8,128)(2,1)S(1)}, bf16[8,128,128]{2,1,0:T(8,128)(2,1)S(1)}) custom-call(s32[192]{0:T(256)} %bitcast.55, s32[192]{0:T(256)} %bitcast.59, s32[1]{0:T(128)} %bitcast.49.count, s32[2]{0:T(128)S(1)} %pad_add_fusion.place, bf16[192,128,128]{2,1,0:T(8,128)(2,1)} %bitcast.63, ...), custom_call_target="tpu_custom_call" | custom-call | flops 805306368 | bytes 6291456 | tf_op jit(solution)/shard_map/forward_kernel/pallas_call | solution.py:469
  31.6 1.6 %collective-permute-start.16 = (bf16[8,128,128]{2,1,0:T(8,128)(2,1)S(1)}, bf16[8,128,128]{2,1,0:T(8,128)(2,1)S(1)}, u32[]{:S(2)}, u32[]{:S(2)}) collective-permute-start(bf16[8,128,128]{2,1,0:T(8,128)(2,1)S(1)} %get-tuple-element.41), channel_id=1, source_target_pairs={{0,4},{4,0},{8,12},{12,8},{16,20},{20,16},{24,28},{28,24},{1,5},{5... | collective-permute-start | bytes 786440 | tf_op jit(solution)/shard_map/ppermute | solution.py:376
  33.8 2.9 %collective-permute-start.6 = (bf16[256,128]{1,0:T(8,128)(2,1)S(1)}, bf16[256,128]{1,0:T(8,128)(2,1)S(1)}, u32[]{:S(2)}, u32[]{:S(2)}) collective-permute-start(bf16[256,128]{1,0:T(8,128)(2,1)S(1)} %get-tuple-element.60), channel_id=1, source_target_pairs={{0,16},{4,20},{8,24},{12,28},{16,0},{20,4},{24,8},{28,12},{1,17},{... | collective-permute-start | bytes 196616 | tf_op jit(solution)/shard_map/ppermute | solution.py:376
  36.7 1.6 %collective-permute-start.8 = (bf16[256,128]{1,0:T(8,128)(2,1)S(1)}, bf16[256,128]{1,0:T(8,128)(2,1)S(1)}, u32[]{:S(2)}, u32[]{:S(2)}) collective-permute-start(bf16[256,128]{1,0:T(8,128)(2,1)S(1)} %get-tuple-element.61), channel_id=1, source_target_pairs={{0,8},{4,12},{8,0},{12,4},{16,24},{20,28},{24,16},{28,20},{1,9},{5... | collective-permute-start | bytes 196616 | tf_op jit(solution)/shard_map/ppermute | solution.py:376
  38.3 1.8 %collective-permute-done.16 = bf16[8,128,128]{2,1,0:T(8,128)(2,1)S(1)} collective-permute-done((bf16[8,128,128]{2,1,0:T(8,128)(2,1)S(1)}, bf16[8,128,128]{2,1,0:T(8,128)(2,1)S(1)}, u32[]{:S(2)}, u32[]{:S(2)}) %collective-permute-start.16) | collective-permute-done | bytes 262176 | tf_op jit(solution)/shard_map/ppermute | solution.py:376
  40.2 2.7 %collective-permute-start.17 = (bf16[256,128]{1,0:T(8,128)(2,1)S(1)}, bf16[256,128]{1,0:T(8,128)(2,1)S(1)}, u32[]{:S(2)}, u32[]{:S(2)}) collective-permute-start(bf16[256,128]{1,0:T(8,128)(2,1)S(1)} %get-tuple-element.57), channel_id=1, source_target_pairs={{0,16},{4,20},{8,24},{12,28},{16,0},{20,4},{24,8},{28,12},{1,17},{... | collective-permute-start | bytes 196616 | tf_op jit(solution)/shard_map/ppermute | solution.py:376
  42.9 1.5 %collective-permute-start.19 = (bf16[256,128]{1,0:T(8,128)(2,1)S(1)}, bf16[256,128]{1,0:T(8,128)(2,1)S(1)}, u32[]{:S(2)}, u32[]{:S(2)}) collective-permute-start(bf16[256,128]{1,0:T(8,128)(2,1)S(1)} %get-tuple-element.58), channel_id=1, source_target_pairs={{0,8},{4,12},{8,0},{12,4},{16,24},{20,28},{24,16},{28,20},{1,9},{5... | collective-permute-start | bytes 196616 | tf_op jit(solution)/shard_map/ppermute | solution.py:376
  47.3 3.1 %collective-permute-done.18 = bf16[256,128]{1,0:T(8,128)(2,1)S(1)} collective-permute-done((bf16[256,128]{1,0:T(8,128)(2,1)S(1)}, bf16[256,128]{1,0:T(8,128)(2,1)S(1)}, u32[]{:S(2)}, u32[]{:S(2)}) %collective-permute-start.18) | collective-permute-done | bytes 65568 | tf_op jit(solution)/shard_map/ppermute | solution.py:376
  50.5 1.5 %collective-permute-start.22 = (bf16[256,128]{1,0:T(8,128)(2,1)S(1)}, bf16[256,128]{1,0:T(8,128)(2,1)S(1)}, u32[]{:S(2)}, u32[]{:S(2)}) collective-permute-start(bf16[256,128]{1,0:T(8,128)(2,1)S(1)} %get-tuple-element.63), channel_id=1, source_target_pairs={{0,24},{4,28},{8,16},{12,20},{16,8},{20,12},{24,0},{28,4},{1,25},{... | collective-permute-start | bytes 196616 | tf_op jit(solution)/shard_map/ppermute | solution.py:376
  52.0 2.9 %collective-permute-start.20 = (bf16[256,128]{1,0:T(8,128)(2,1)S(1)}, bf16[256,128]{1,0:T(8,128)(2,1)S(1)}, u32[]{:S(2)}, u32[]{:S(2)}) collective-permute-start(bf16[256,128]{1,0:T(8,128)(2,1)S(1)} %get-tuple-element.63), channel_id=1, source_target_pairs={{0,8},{4,12},{8,0},{12,4},{16,24},{20,28},{24,16},{28,20},{1,9},{5... | collective-permute-start | bytes 196616 | tf_op jit(solution)/shard_map/ppermute | solution.py:376
  54.9 1.7 %collective-permute-done.22 = bf16[256,128]{1,0:T(8,128)(2,1)S(1)} collective-permute-done((bf16[256,128]{1,0:T(8,128)(2,1)S(1)}, bf16[256,128]{1,0:T(8,128)(2,1)S(1)}, u32[]{:S(2)}, u32[]{:S(2)}) %collective-permute-start.22) | collective-permute-done | bytes 65568 | tf_op jit(solution)/shard_map/ppermute | solution.py:376
  56.6 1.4 %collective-permute-done.21 = bf16[256,128]{1,0:T(8,128)(2,1)S(1)} collective-permute-done((bf16[256,128]{1,0:T(8,128)(2,1)S(1)}, bf16[256,128]{1,0:T(8,128)(2,1)S(1)}, u32[]{:S(2)}, u32[]{:S(2)}) %collective-permute-start.21) | collective-permute-done | bytes 65568 | tf_op jit(solution)/shard_map/ppermute | solution.py:376
  58.8 1.6 %collective-permute-start.11 = (bf16[256,128]{1,0:T(8,128)(2,1)S(1)}, bf16[256,128]{1,0:T(8,128)(2,1)S(1)}, u32[]{:S(2)}, u32[]{:S(2)}) collective-permute-start(bf16[256,128]{1,0:T(8,128)(2,1)S(1)} %get-tuple-element.64.after_ref), channel_id=1, source_target_pairs={{0,24},{4,28},{8,16},{12,20},{16,8},{20,12},{24,0},{28,4},{1,25},{... | collective-permute-start | bytes 196616 | tf_op jit(solution)/shard_map/ppermute | solution.py:376
  61.4 1.7 %collective-permute-start.9 = (bf16[256,128]{1,0:T(8,128)(2,1)S(1)}, bf16[256,128]{1,0:T(8,128)(2,1)S(1)}, u32[]{:S(2)}, u32[]{:S(2)}) collective-permute-start(bf16[256,128]{1,0:T(8,128)(2,1)S(1)} %get-tuple-element.64.after_ref), channel_id=1, source_target_pairs={{0,8},{4,12},{8,0},{12,4},{16,24},{20,28},{24,16},{28,20},{1,9},{5... | collective-permute-start | bytes 196616 | tf_op jit(solution)/shard_map/ppermute | solution.py:376
  63.2 2.8 %hold.1.held = bf16[192,128,128]{2,1,0:T(8,128)(2,1)S(1)} custom-call(bf16[192,128,128]{2,1,0:T(8,128)(2,1)} %bitcast.64, bf16[256,128]{1,0:T(8,128)(2,1)S(1)} %get-tuple-element.64.after_ref), custom_call_target="tpu_custom_call" | custom-call | bytes 12582912 | tf_op jit(solution)/shard_map/hold/pallas_call | solution.py:417
  66.5 3.4 %adjoint_kernel.2 = (bf16[16,64,128]{2,1,0:T(8,128)(2,1)S(1)}, bf16[16,64,128]{2,1,0:T(8,128)(2,1)S(1)}, bf16[16,64,128]{2,1,0:T(8,128)(2,1)S(1)}, bf16[16,64,128]{2,1,0:T(8,128)(2,1)S(1)}) custom-call(s32[192]{0:T(256)S(1)} %bitcast.56, s32[192]{0:T(256)S(1)} %bitcast.60, s32[1]{0:T(128)} %bitcast.50.count, s32[2]{0:T(128)S(1)} %pad_add_fusion.place, ...), custom_call_target="tpu_custom_call" | custom-call | flops 805306368 | bytes 6291456 | tf_op jit(solution)/shard_map/adjoint_kernel/pallas_call | solution.py:469
  71.8 2.1 %collective-permute-start.27 = (bf16[16,64,128]{2,1,0:T(8,128)(2,1)S(1)}, bf16[16,64,128]{2,1,0:T(8,128)(2,1)S(1)}, u32[]{:S(2)}, u32[]{:S(2)}) collective-permute-start(bf16[16,64,128]{2,1,0:T(8,128)(2,1)S(1)} %add_convert_fusion.2), channel_id=1, source_target_pairs={{0,2},{1,3},{2,0},{3,1},{4,6},{5,7},{6,4},{7,5},{8,10},{9,11},{10,... | collective-permute-start | bytes 786440 | tf_op jit(solution)/shard_map/ppermute | solution.py:376
  74.0 4.7 %collective-permute-done.12.theirs_ref = bf16[4,256,128]{2,1,0:T(8,128)(2,1)S(1)} collective-permute-done((bf16[4,256,128]{2,1,0:T(8,128)(2,1)S(1)}, bf16[4,256,128]{2,1,0:T(8,128)(2,1)S(1)}, u32[]{:S(2)}, u32[]{:S(2)}) %collective-permute-start.12) | collective-permute-done | bytes 262176 | tf_op jit(solution)/shard_map/ppermute | solution.py:376
  78.7 3.5 %adjoint_kernel.3 = (bf16[16,64,128]{2,1,0:T(8,128)(2,1)S(1)}, bf16[16,64,128]{2,1,0:T(8,128)(2,1)S(1)}, bf16[16,64,128]{2,1,0:T(8,128)(2,1)S(1)}, bf16[16,64,128]{2,1,0:T(8,128)(2,1)S(1)}) custom-call(s32[192]{0:T(256)S(1)} %bitcast.57, s32[192]{0:T(256)S(1)} %bitcast.61, s32[1]{0:T(128)} %bitcast.51.count, s32[2]{0:T(128)S(1)} %pad_add_fusion.place, ...), custom_call_target="tpu_custom_call" | custom-call | flops 805306368 | bytes 6291456 | tf_op jit(solution)/shard_map/adjoint_kernel/pallas_call | solution.py:469
  82.4 2.4 %collective-permute-start.31 = (bf16[16,64,128]{2,1,0:T(8,128)(2,1)S(1)}, bf16[16,64,128]{2,1,0:T(8,128)(2,1)S(1)}, u32[]{:S(2)}, u32[]{:S(2)}) collective-permute-start(bf16[16,64,128]{2,1,0:T(8,128)(2,1)S(1)} %add_convert_fusion.1), channel_id=1, source_target_pairs={{0,2},{1,3},{2,0},{3,1},{4,6},{5,7},{6,4},{7,5},{8,10},{9,11},{10,... | collective-permute-start | bytes 786440 | tf_op jit(solution)/shard_map/ppermute | solution.py:376
  86.3 4.6 %collective-permute-start.28 = (bf16[8,64,128]{2,1,0:T(8,128)(2,1)S(1)}, bf16[8,64,128]{2,1,0:T(8,128)(2,1)S(1)}, u32[]{:S(2)}, u32[]{:S(2)}) collective-permute-start(bf16[8,64,128]{2,1,0:T(8,128)(2,1)S(1)} %get-tuple-element.56), channel_id=1, source_target_pairs={{0,4},{4,8},{8,12},{12,16},{16,20},{20,24},{24,28},{1,5},{5,9},{9,... | collective-permute-start | bytes 393224 | tf_op jit(solution)/shard_map/ppermute | solution.py:387
  91.6 2.6 %back_inner.1 = (f32[2,1024,128]{2,1,0:T(8,128)S(1)}, f32[2,4,2,64,256]{4,3,2,1,0:T(8,128)S(1)}) custom-call(bf16[1024,256]{1,0:T(8,128)(2,1)S(1)} %get-tuple-element.33.probes_ref, f32[16,256]{1,0:T(8,128)S(1)} %get-tuple-element.30.kappa_ref, bf16[16,64,128]{2,1,0:T(8,128)(2,1)S(1)} %get-tuple-element.51.own_in, ...), custom_call_target="tpu_custom_call" | custom-call | tf_op jit(solution)/shard_map/back_inner/pallas_call | solution.py:562
  94.5 3.4 %back_outer.1 = f32[1024,256]{1,0:T(8,128)} custom-call(f32[2]{0:T(128)S(1)} %add_convert_fusion.5.inside, f32[16,256]{1,0:T(8,128)S(1)} %get-tuple-element.30.kappa_ref, bf16[272,256]{1,0:T(8,128)(2,1)S(1)} %collective-permute-done.above_ref, bf16[272,256]{1,0:T(8,128)(2,1)S(1)} %collective-permute-done.1.below_ref, ...), custom_call_target="tpu_custom_call" | custom-call | tf_op jit(solution)/shard_map/back_outer/pallas_call | solution.py:571
  (62 shorter events, 13.7 us)
Async XLA Ops:
  1.4 10.2 %collective-permute-start = (bf16[272,256]{1,0:T(8,128)(2,1)S(1)}, bf16[272,256]{1,0:T(8,128)(2,1)S(1)}, u32[]{:S(2)}, u32[]{:S(2)}) collective-permute-start(bf16[272,256]{1,0:T(8,128)(2,1)S(1)} %get-tuple-element.31), channel_id=1, source_target_pairs={{0,4},{4,8},{8,12},{12,16},{16,20},{20,24},{24,28},{1,5},{5,9},{9,... | collective-permute-start | bytes 417800 | tf_op jit(solution)/shard_map/ppermute | solution.py:387
  6.2 7.0 %collective-permute-start.1 = (bf16[272,256]{1,0:T(8,128)(2,1)S(1)}, bf16[272,256]{1,0:T(8,128)(2,1)S(1)}, u32[]{:S(2)}, u32[]{:S(2)}) collective-permute-start(bf16[272,256]{1,0:T(8,128)(2,1)S(1)} %get-tuple-element.32), channel_id=1, source_target_pairs={{4,0},{8,4},{12,8},{16,12},{20,16},{24,20},{28,24},{5,1},{9,5},{13... | collective-permute-start | bytes 417800 | tf_op jit(solution)/shard_map/ppermute | solution.py:387
  10.0 7.9 %collective-permute-start.13 = (bf16[16,64,128]{2,1,0:T(8,128)(2,1)S(1)}, bf16[16,64,128]{2,1,0:T(8,128)(2,1)S(1)}, u32[]{:S(2)}, u32[]{:S(2)}) collective-permute-start(bf16[16,64,128]{2,1,0:T(8,128)(2,1)S(1)} %get-tuple-element.34.near_in), channel_id=1, source_target_pairs={{0,2},{1,3},{2,0},{3,1},{4,6},{5,7},{6,4},{7,5},{8,10},{9,11},{10,... | collective-permute-start | bytes 786440 | tf_op jit(solution)/shard_map/ppermute | solution.py:376
  11.6 6.5 %collective-permute-start.2 = (bf16[16,64,128]{2,1,0:T(8,128)(2,1)S(1)}, bf16[16,64,128]{2,1,0:T(8,128)(2,1)S(1)}, u32[]{:S(2)}, u32[]{:S(2)}) collective-permute-start(bf16[16,64,128]{2,1,0:T(8,128)(2,1)S(1)} %get-tuple-element.34.near_in), channel_id=1, source_target_pairs={{0,1},{1,0},{2,3},{3,2},{4,5},{5,4},{6,7},{7,6},{8,9},{9,8},{10,11... | collective-permute-start | bytes 786440 | tf_op jit(solution)/shard_map/ppermute | solution.py:376
  15.5 2.6 %collective-permute-start.3 = (bf16[16,64,128]{2,1,0:T(8,128)(2,1)S(1)}, bf16[16,64,128]{2,1,0:T(8,128)(2,1)S(1)}, u32[]{:S(2)}, u32[]{:S(2)}) collective-permute-start(bf16[16,64,128]{2,1,0:T(8,128)(2,1)S(1)} %smooth_outer.1.near_out), channel_id=1, source_target_pairs={{0,1},{1,0},{2,3},{3,2},{4,5},{5,4},{6,7},{7,6},{8,9},{9,8},{10,11... | collective-permute-start | bytes 786440 | tf_op jit(solution)/shard_map/ppermute | solution.py:376
  15.6 8.7 %collective-permute-start.4 = (bf16[16,64,128]{2,1,0:T(8,128)(2,1)S(1)}, bf16[16,64,128]{2,1,0:T(8,128)(2,1)S(1)}, u32[]{:S(2)}, u32[]{:S(2)}) collective-permute-start(bf16[16,64,128]{2,1,0:T(8,128)(2,1)S(1)} %smooth_outer.1.near_out), channel_id=1, source_target_pairs={{0,2},{1,3},{2,0},{3,1},{4,6},{5,7},{6,4},{7,5},{8,10},{9,11},{10,... | collective-permute-start | bytes 786440 | tf_op jit(solution)/shard_map/ppermute | solution.py:376
  17.9 8.9 %collective-permute-start.14 = (bf16[16,64,128]{2,1,0:T(8,128)(2,1)S(1)}, bf16[16,64,128]{2,1,0:T(8,128)(2,1)S(1)}, u32[]{:S(2)}, u32[]{:S(2)}) collective-permute-start(bf16[16,64,128]{2,1,0:T(8,128)(2,1)S(1)} %collective-permute-done.13.near_in), channel_id=1, source_target_pairs={{0,1},{1,0},{2,3},{3,2},{4,5},{5,4},{6,7},{7,6},{8,9},{9,8},{10,11... | collective-permute-start | bytes 786440 | tf_op jit(solution)/shard_map/ppermute | solution.py:376
  24.3 2.5 %collective-permute-start.15 = (bf16[16,64,128]{2,1,0:T(8,128)(2,1)S(1)}, bf16[16,64,128]{2,1,0:T(8,128)(2,1)S(1)}, u32[]{:S(2)}, u32[]{:S(2)}) collective-permute-start(bf16[16,64,128]{2,1,0:T(8,128)(2,1)S(1)} %collective-permute-done.4.near_out), channel_id=1, source_target_pairs={{0,1},{1,0},{2,3},{3,2},{4,5},{5,4},{6,7},{7,6},{8,9},{9,8},{10,11... | collective-permute-start | bytes 786440 | tf_op jit(solution)/shard_map/ppermute | solution.py:376
  24.3 9.4 %collective-permute-start.5 = (bf16[8,128,128]{2,1,0:T(8,128)(2,1)S(1)}, bf16[8,128,128]{2,1,0:T(8,128)(2,1)S(1)}, u32[]{:S(2)}, u32[]{:S(2)}) collective-permute-start(bf16[8,128,128]{2,1,0:T(8,128)(2,1)S(1)} %get-tuple-element.38), channel_id=1, source_target_pairs={{0,4},{4,0},{8,12},{12,8},{16,20},{20,16},{24,28},{28,24},{1,5},{5... | collective-permute-start | bytes 786440 | tf_op jit(solution)/shard_map/ppermute | solution.py:376
  31.6 8.5 %collective-permute-start.16 = (bf16[8,128,128]{2,1,0:T(8,128)(2,1)S(1)}, bf16[8,128,128]{2,1,0:T(8,128)(2,1)S(1)}, u32[]{:S(2)}, u32[]{:S(2)}) collective-permute-start(bf16[8,128,128]{2,1,0:T(8,128)(2,1)S(1)} %get-tuple-element.41), channel_id=1, source_target_pairs={{0,4},{4,0},{8,12},{12,8},{16,20},{20,16},{24,28},{28,24},{1,5},{5... | collective-permute-start | bytes 786440 | tf_op jit(solution)/shard_map/ppermute | solution.py:376
  33.8 10.5 %collective-permute-start.6 = (bf16[256,128]{1,0:T(8,128)(2,1)S(1)}, bf16[256,128]{1,0:T(8,128)(2,1)S(1)}, u32[]{:S(2)}, u32[]{:S(2)}) collective-permute-start(bf16[256,128]{1,0:T(8,128)(2,1)S(1)} %get-tuple-element.60), channel_id=1, source_target_pairs={{0,16},{4,20},{8,24},{12,28},{16,0},{20,4},{24,8},{28,12},{1,17},{... | collective-permute-start | bytes 196616 | tf_op jit(solution)/shard_map/ppermute | solution.py:376
  36.7 9.0 %collective-permute-start.8 = (bf16[256,128]{1,0:T(8,128)(2,1)S(1)}, bf16[256,128]{1,0:T(8,128)(2,1)S(1)}, u32[]{:S(2)}, u32[]{:S(2)}) collective-permute-start(bf16[256,128]{1,0:T(8,128)(2,1)S(1)} %get-tuple-element.61), channel_id=1, source_target_pairs={{0,8},{4,12},{8,0},{12,4},{16,24},{20,28},{24,16},{28,20},{1,9},{5... | collective-permute-start | bytes 196616 | tf_op jit(solution)/shard_map/ppermute | solution.py:376
  38.2 7.4 %collective-permute-start.7 = (bf16[256,128]{1,0:T(8,128)(2,1)S(1)}, bf16[256,128]{1,0:T(8,128)(2,1)S(1)}, u32[]{:S(2)}, u32[]{:S(2)}) collective-permute-start(bf16[256,128]{1,0:T(8,128)(2,1)S(1)} %get-tuple-element.62), channel_id=1, source_target_pairs={{0,24},{4,28},{8,16},{12,20},{16,8},{20,12},{24,0},{28,4},{1,25},{... | collective-permute-start | bytes 196616 | tf_op jit(solution)/shard_map/ppermute | solution.py:376
  40.2 6.7 %collective-permute-start.17 = (bf16[256,128]{1,0:T(8,128)(2,1)S(1)}, bf16[256,128]{1,0:T(8,128)(2,1)S(1)}, u32[]{:S(2)}, u32[]{:S(2)}) collective-permute-start(bf16[256,128]{1,0:T(8,128)(2,1)S(1)} %get-tuple-element.57), channel_id=1, source_target_pairs={{0,16},{4,20},{8,24},{12,28},{16,0},{20,4},{24,8},{28,12},{1,17},{... | collective-permute-start | bytes 196616 | tf_op jit(solution)/shard_map/ppermute | solution.py:376
  42.9 4.4 %collective-permute-start.19 = (bf16[256,128]{1,0:T(8,128)(2,1)S(1)}, bf16[256,128]{1,0:T(8,128)(2,1)S(1)}, u32[]{:S(2)}, u32[]{:S(2)}) collective-permute-start(bf16[256,128]{1,0:T(8,128)(2,1)S(1)} %get-tuple-element.58), channel_id=1, source_target_pairs={{0,8},{4,12},{8,0},{12,4},{16,24},{20,28},{24,16},{28,20},{1,9},{5... | collective-permute-start | bytes 196616 | tf_op jit(solution)/shard_map/ppermute | solution.py:376
  44.3 6.1 %collective-permute-start.18 = (bf16[256,128]{1,0:T(8,128)(2,1)S(1)}, bf16[256,128]{1,0:T(8,128)(2,1)S(1)}, u32[]{:S(2)}, u32[]{:S(2)}) collective-permute-start(bf16[256,128]{1,0:T(8,128)(2,1)S(1)} %get-tuple-element.59), channel_id=1, source_target_pairs={{0,24},{4,28},{8,16},{12,20},{16,8},{20,12},{24,0},{28,4},{1,25},{... | collective-permute-start | bytes 196616 | tf_op jit(solution)/shard_map/ppermute | solution.py:376
  50.5 6.2 %collective-permute-start.22 = (bf16[256,128]{1,0:T(8,128)(2,1)S(1)}, bf16[256,128]{1,0:T(8,128)(2,1)S(1)}, u32[]{:S(2)}, u32[]{:S(2)}) collective-permute-start(bf16[256,128]{1,0:T(8,128)(2,1)S(1)} %get-tuple-element.63), channel_id=1, source_target_pairs={{0,24},{4,28},{8,16},{12,20},{16,8},{20,12},{24,0},{28,4},{1,25},{... | collective-permute-start | bytes 196616 | tf_op jit(solution)/shard_map/ppermute | solution.py:376
  52.0 6.0 %collective-permute-start.21 = (bf16[256,128]{1,0:T(8,128)(2,1)S(1)}, bf16[256,128]{1,0:T(8,128)(2,1)S(1)}, u32[]{:S(2)}, u32[]{:S(2)}) collective-permute-start(bf16[256,128]{1,0:T(8,128)(2,1)S(1)} %get-tuple-element.63), channel_id=1, source_target_pairs={{0,16},{4,20},{8,24},{12,28},{16,0},{20,4},{24,8},{28,12},{1,17},{... | collective-permute-start | bytes 196616 | tf_op jit(solution)/shard_map/ppermute | solution.py:376
  52.0 6.0 %collective-permute-start.20 = (bf16[256,128]{1,0:T(8,128)(2,1)S(1)}, bf16[256,128]{1,0:T(8,128)(2,1)S(1)}, u32[]{:S(2)}, u32[]{:S(2)}) collective-permute-start(bf16[256,128]{1,0:T(8,128)(2,1)S(1)} %get-tuple-element.63), channel_id=1, source_target_pairs={{0,8},{4,12},{8,0},{12,4},{16,24},{20,28},{24,16},{28,20},{1,9},{5... | collective-permute-start | bytes 196616 | tf_op jit(solution)/shard_map/ppermute | solution.py:376
  58.1 8.4 %collective-permute-start.23 = (bf16[4,256,128]{2,1,0:T(8,128)(2,1)S(1)}, bf16[4,256,128]{2,1,0:T(8,128)(2,1)S(1)}, u32[]{:S(2)}, u32[]{:S(2)}) collective-permute-start(bf16[4,256,128]{2,1,0:T(8,128)(2,1)S(1)} %pad_maximum_fusion.1.mine_ref), channel_id=1, source_target_pairs={{0,4},{4,0},{8,12},{12,8},{16,20},{20,16},{24,28},{28,24},{1,5},{5... | collective-permute-start | bytes 786440 | tf_op jit(solution)/shard_map/ppermute | solution.py:376
  58.8 7.2 %collective-permute-start.11 = (bf16[256,128]{1,0:T(8,128)(2,1)S(1)}, bf16[256,128]{1,0:T(8,128)(2,1)S(1)}, u32[]{:S(2)}, u32[]{:S(2)}) collective-permute-start(bf16[256,128]{1,0:T(8,128)(2,1)S(1)} %get-tuple-element.64.after_ref), channel_id=1, source_target_pairs={{0,24},{4,28},{8,16},{12,20},{16,8},{20,12},{24,0},{28,4},{1,25},{... | collective-permute-start | bytes 196616 | tf_op jit(solution)/shard_map/ppermute | solution.py:376
  60.4 6.0 %collective-permute-start.10 = (bf16[256,128]{1,0:T(8,128)(2,1)S(1)}, bf16[256,128]{1,0:T(8,128)(2,1)S(1)}, u32[]{:S(2)}, u32[]{:S(2)}) collective-permute-start(bf16[256,128]{1,0:T(8,128)(2,1)S(1)} %get-tuple-element.64.after_ref), channel_id=1, source_target_pairs={{0,16},{4,20},{8,24},{12,28},{16,0},{20,4},{24,8},{28,12},{1,17},{... | collective-permute-start | bytes 196616 | tf_op jit(solution)/shard_map/ppermute | solution.py:376
  61.4 5.0 %collective-permute-start.9 = (bf16[256,128]{1,0:T(8,128)(2,1)S(1)}, bf16[256,128]{1,0:T(8,128)(2,1)S(1)}, u32[]{:S(2)}, u32[]{:S(2)}) collective-permute-start(bf16[256,128]{1,0:T(8,128)(2,1)S(1)} %get-tuple-element.64.after_ref), channel_id=1, source_target_pairs={{0,8},{4,12},{8,0},{12,4},{16,24},{20,28},{24,16},{28,20},{1,9},{5... | collective-permute-start | bytes 196616 | tf_op jit(solution)/shard_map/ppermute | solution.py:376
  69.9 1.9 %collective-permute-start.24 = (bf16[16,64,128]{2,1,0:T(8,128)(2,1)S(1)}, bf16[16,64,128]{2,1,0:T(8,128)(2,1)S(1)}, u32[]{:S(2)}, u32[]{:S(2)}) collective-permute-start(bf16[16,64,128]{2,1,0:T(8,128)(2,1)S(1)} %get-tuple-element.45), channel_id=1, source_target_pairs={{0,1},{1,0},{2,3},{3,2},{4,5},{5,4},{6,7},{7,6},{8,9},{9,8},{10,11... | collective-permute-start | bytes 786440 | tf_op jit(solution)/shard_map/ppermute | solution.py:376
  69.9 4.0 %collective-permute-start.25 = (bf16[16,64,128]{2,1,0:T(8,128)(2,1)S(1)}, bf16[16,64,128]{2,1,0:T(8,128)(2,1)S(1)}, u32[]{:S(2)}, u32[]{:S(2)}) collective-permute-start(bf16[16,64,128]{2,1,0:T(8,128)(2,1)S(1)} %get-tuple-element.47), channel_id=1, source_target_pairs={{0,1},{1,0},{2,3},{3,2},{4,5},{5,4},{6,7},{7,6},{8,9},{9,8},{10,11... | collective-permute-start | bytes 786440 | tf_op jit(solution)/shard_map/ppermute | solution.py:376
  70.4 8.3 %collective-permute-start.12 = (bf16[4,256,128]{2,1,0:T(8,128)(2,1)S(1)}, bf16[4,256,128]{2,1,0:T(8,128)(2,1)S(1)}, u32[]{:S(2)}, u32[]{:S(2)}) collective-permute-start(bf16[4,256,128]{2,1,0:T(8,128)(2,1)S(1)} %pad_maximum_fusion.mine_ref), channel_id=1, source_target_pairs={{0,4},{4,0},{8,12},{12,8},{16,20},{20,16},{24,28},{28,24},{1,5},{5... | collective-permute-start | bytes 786440 | tf_op jit(solution)/shard_map/ppermute | solution.py:376
  71.8 13.0 %collective-permute-start.27 = (bf16[16,64,128]{2,1,0:T(8,128)(2,1)S(1)}, bf16[16,64,128]{2,1,0:T(8,128)(2,1)S(1)}, u32[]{:S(2)}, u32[]{:S(2)}) collective-permute-start(bf16[16,64,128]{2,1,0:T(8,128)(2,1)S(1)} %add_convert_fusion.2), channel_id=1, source_target_pairs={{0,2},{1,3},{2,0},{3,1},{4,6},{5,7},{6,4},{7,5},{8,10},{9,11},{10,... | collective-permute-start | bytes 786440 | tf_op jit(solution)/shard_map/ppermute | solution.py:376
  82.3 2.6 %collective-permute-start.26 = (bf16[16,64,128]{2,1,0:T(8,128)(2,1)S(1)}, bf16[16,64,128]{2,1,0:T(8,128)(2,1)S(1)}, u32[]{:S(2)}, u32[]{:S(2)}) collective-permute-start(bf16[16,64,128]{2,1,0:T(8,128)(2,1)S(1)} %get-tuple-element.50), channel_id=1, source_target_pairs={{0,1},{1,0},{2,3},{3,2},{4,5},{5,4},{6,7},{7,6},{8,9},{9,8},{10,11... | collective-permute-start | bytes 786440 | tf_op jit(solution)/shard_map/ppermute | solution.py:376
  82.4 9.3 %collective-permute-start.31 = (bf16[16,64,128]{2,1,0:T(8,128)(2,1)S(1)}, bf16[16,64,128]{2,1,0:T(8,128)(2,1)S(1)}, u32[]{:S(2)}, u32[]{:S(2)}) collective-permute-start(bf16[16,64,128]{2,1,0:T(8,128)(2,1)S(1)} %add_convert_fusion.1), channel_id=1, source_target_pairs={{0,2},{1,3},{2,0},{3,1},{4,6},{5,7},{6,4},{7,5},{8,10},{9,11},{10,... | collective-permute-start | bytes 786440 | tf_op jit(solution)/shard_map/ppermute | solution.py:376
  84.7 6.3 %collective-permute-start.30 = (bf16[16,64,128]{2,1,0:T(8,128)(2,1)S(1)}, bf16[16,64,128]{2,1,0:T(8,128)(2,1)S(1)}, u32[]{:S(2)}, u32[]{:S(2)}) collective-permute-start(bf16[16,64,128]{2,1,0:T(8,128)(2,1)S(1)} %get-tuple-element.52), channel_id=1, source_target_pairs={{0,1},{1,0},{2,3},{3,2},{4,5},{5,4},{6,7},{7,6},{8,9},{9,8},{10,11... | collective-permute-start | bytes 786440 | tf_op jit(solution)/shard_map/ppermute | solution.py:376
  85.0 9.2 %collective-permute-start.29 = (bf16[8,64,128]{2,1,0:T(8,128)(2,1)S(1)}, bf16[8,64,128]{2,1,0:T(8,128)(2,1)S(1)}, u32[]{:S(2)}, u32[]{:S(2)}) collective-permute-start(bf16[8,64,128]{2,1,0:T(8,128)(2,1)S(1)} %get-tuple-element.55), channel_id=1, source_target_pairs={{4,0},{8,4},{12,8},{16,12},{20,16},{24,20},{28,24},{5,1},{9,5},{13... | collective-permute-start | bytes 393224 | tf_op jit(solution)/shard_map/ppermute | solution.py:387
  86.3 8.1 %collective-permute-start.28 = (bf16[8,64,128]{2,1,0:T(8,128)(2,1)S(1)}, bf16[8,64,128]{2,1,0:T(8,128)(2,1)S(1)}, u32[]{:S(2)}, u32[]{:S(2)}) collective-permute-start(bf16[8,64,128]{2,1,0:T(8,128)(2,1)S(1)} %get-tuple-element.56), channel_id=1, source_target_pairs={{0,4},{4,8},{8,12},{12,16},{16,20},{20,24},{24,28},{1,5},{5,9},{9,... | collective-permute-start | bytes 393224 | tf_op jit(solution)/shard_map/ppermute | solution.py:387
  (3 other events, 61.0 us)

commit v8 on v7

--- a/solution.py
+++ b/solution.py
@@ -132,7 +132,7 @@
     coefficients(coef, [(r, kappa_ref[r : r + 1, :]) for r in range(rows)])
     lane = lanes()
 
-    @pl.loop(0, probe_local // SUB, unroll=2)
+    @pl.loop(0, probe_local // SUB, unroll=4)
     def _(c):
         base = pl.multiple_of(c * SUB, SUB)
         at = pl.ds(base, SUB)
@@ -304,7 +304,7 @@
     lane = lanes()
     coefficients(coef, [(r, kappa_ref[r : r + 1, :]) for r in range(rows)])
 
-    @pl.loop(0, probe_local // SUB, unroll=2)
+    @pl.loop(0, probe_local // SUB, unroll=4)
     def _(c):
         base = pl.multiple_of(c * SUB, SUB)
         at = pl.ds(base, SUB)

time: 98.2 us -> 98.1 us (level)
  no operation moved by 1% of the time
where the time goes in v8:
time: 98.1 us; the launch traced here: 97.9 us
  starting transfers between devices  45.5 us (46%)
  Pallas kernels  31.2 us (32%)
  waiting for transfers between devices  19.2 us (20%)
  between operations  1.1 us (1%)
    ppermute x28, starting transfers between devices, swap(): return lax.ppermute(x, axis, [(i, i ^ distance) for i in range(size)])  33.6 us
    ppermute x28, waiting for transfers between devices, swap(): return lax.ppermute(x, axis, [(i, i ^ distance) for i in range(size)])  17.2 us
    pallas_call x4, Pallas kernels, over_slots(): pl.pallas_call(kernel, out_shape=outs, in_specs=[list_spec, list_spec, SM...  16.6 us
    ppermute x4, starting transfers between devices, exchange_edges(): return (lax.ppermute(south, 'src', down), lax.ppermute(north, 'src', up))  12 us
    pallas_call x1, Pallas kernels, per_device(): pl.pallas_call(back_outer_kernel, out_shape=jax.ShapeDtypeStruct((probe_l...  3.36 us
    pallas_call x1, Pallas kernels, hold(): pl.pallas_call(hold_kernel, out_shape=jax.ShapeDtypeStruct(blocks.shape,...  2.79 us
    pallas_call x1, Pallas kernels, per_device(): pl.pallas_call(back_inner_kernel, out_shape=(jax.ShapeDtypeStruct(by_half...  2.53 us
    pallas_call x1, Pallas kernels, per_device(): pl.pallas_call(smooth_inner_kernel, out_shape=(inner_part, state), in_spe...  2.36 us
  transfers between devices with their start and end apart: 32, of which 13 were waited for; matrix products, arithmetic and copies ran while one was open for 1% of the time, Pallas kernels for 24%

profile of v8, /device:TPU:0, one launch (start us, length us, event | category | flops | bytes accessed | tf_op | source)
XLA Modules:
  0.0 97.9 jit_solution(1105843328011104493)
XLA Ops:
  1.4 4.9 %collective-permute-start = (bf16[272,256]{1,0:T(8,128)(2,1)S(1)}, bf16[272,256]{1,0:T(8,128)(2,1)S(1)}, u32[]{:S(2)}, u32[]{:S(2)}) collective-permute-start(bf16[272,256]{1,0:T(8,128)(2,1)S(1)} %get-tuple-element.31), channel_id=1, source_target_pairs={{0,4},{4,8},{8,12},{12,16},{16,20},{20,24},{24,28},{1,5},{5,9},{9,... | collective-permute-start | bytes 417800 | tf_op jit(solution)/shard_map/ppermute | solution.py:387
  7.5 2.4 %smooth_inner.1 = (bf16[16,64,128]{2,1,0:T(8,128)(2,1)S(1)}, f32[2,4,2,64,256]{4,3,2,1,0:T(8,128)S(1)}) custom-call(bf16[1024,256]{1,0:T(8,128)(2,1)S(1)} %get-tuple-element.33.probes_ref, f32[16,256]{1,0:T(8,128)S(1)} %get-tuple-element.30.kappa_ref), custom_call_target="tpu_custom_call" | custom-call | tf_op jit(solution)/shard_map/smooth_inner/pallas_call | solution.py:434
  9.9 1.6 %collective-permute-start.13 = (bf16[16,64,128]{2,1,0:T(8,128)(2,1)S(1)}, bf16[16,64,128]{2,1,0:T(8,128)(2,1)S(1)}, u32[]{:S(2)}, u32[]{:S(2)}) collective-permute-start(bf16[16,64,128]{2,1,0:T(8,128)(2,1)S(1)} %get-tuple-element.34.near_in), channel_id=1, source_target_pairs={{0,2},{1,3},{2,0},{3,1},{4,6},{5,7},{6,4},{7,5},{8,10},{9,11},{10,... | collective-permute-start | bytes 786440 | tf_op jit(solution)/shard_map/ppermute | solution.py:376
  11.5 1.8 %collective-permute-done.1.below_ref = bf16[272,256]{1,0:T(8,128)(2,1)S(1)} collective-permute-done((bf16[272,256]{1,0:T(8,128)(2,1)S(1)}, bf16[272,256]{1,0:T(8,128)(2,1)S(1)}, u32[]{:S(2)}, u32[]{:S(2)}) %collective-permute-start.1) | collective-permute-done | bytes 139296 | tf_op jit(solution)/shard_map/ppermute | solution.py:387
  13.3 2.2 %smooth_outer.1.near_out = bf16[16,64,128]{2,1,0:T(8,128)(2,1)S(1)} custom-call(f32[16,256]{1,0:T(8,128)S(1)} %get-tuple-element.30.kappa_ref, bf16[272,256]{1,0:T(8,128)(2,1)S(1)} %collective-permute-done.above_ref, bf16[272,256]{1,0:T(8,128)(2,1)S(1)} %collective-permute-done.1.below_ref, f32[2,4,2,64,256]{4,3,2,1,0:T(8,128)S(1)} %get-tuple-element.35.state_ref), custom_call_target="tpu_custom_call" | custom-call | tf_op jit(solution)/shard_map/smooth_outer/pallas_call | solution.py:447
  15.6 1.6 %collective-permute-start.4 = (bf16[16,64,128]{2,1,0:T(8,128)(2,1)S(1)}, bf16[16,64,128]{2,1,0:T(8,128)(2,1)S(1)}, u32[]{:S(2)}, u32[]{:S(2)}) collective-permute-start(bf16[16,64,128]{2,1,0:T(8,128)(2,1)S(1)} %smooth_outer.1.near_out), channel_id=1, source_target_pairs={{0,2},{1,3},{2,0},{3,1},{4,6},{5,7},{6,4},{7,5},{8,10},{9,11},{10,... | collective-permute-start | bytes 786440 | tf_op jit(solution)/shard_map/ppermute | solution.py:376
  18.1 4.8 %forward_kernel.2 = (bf16[8,128,128]{2,1,0:T(8,128)(2,1)S(1)}, bf16[8,128,128]{2,1,0:T(8,128)(2,1)S(1)}) custom-call(s32[192]{0:T(256)} %bitcast.54, s32[192]{0:T(256)} %bitcast.58, s32[1]{0:T(128)} %bitcast.48.count, s32[2]{0:T(128)S(1)} %pad_add_fusion.place, bf16[192,128,128]{2,1,0:T(8,128)(2,1)} %bitcast.62, ...), custom_call_target="tpu_custom_call" | custom-call | flops 805306368 | bytes 6291456 | tf_op jit(solution)/shard_map/forward_kernel/pallas_call | solution.py:469
  22.9 1.4 %collective-permute-done.4.near_out = bf16[16,64,128]{2,1,0:T(8,128)(2,1)S(1)} collective-permute-done((bf16[16,64,128]{2,1,0:T(8,128)(2,1)S(1)}, bf16[16,64,128]{2,1,0:T(8,128)(2,1)S(1)}, u32[]{:S(2)}, u32[]{:S(2)}) %collective-permute-start.4) | collective-permute-done | bytes 262176 | tf_op jit(solution)/shard_map/ppermute | solution.py:376
  24.3 2.4 %collective-permute-start.5 = (bf16[8,128,128]{2,1,0:T(8,128)(2,1)S(1)}, bf16[8,128,128]{2,1,0:T(8,128)(2,1)S(1)}, u32[]{:S(2)}, u32[]{:S(2)}) collective-permute-start(bf16[8,128,128]{2,1,0:T(8,128)(2,1)S(1)} %get-tuple-element.38), channel_id=1, source_target_pairs={{0,4},{4,0},{8,12},{12,8},{16,20},{20,16},{24,28},{28,24},{1,5},{5... | collective-permute-start | bytes 786440 | tf_op jit(solution)/shard_map/ppermute | solution.py:376
  26.7 4.8 %forward_kernel.3 = (bf16[8,128,128]{2,1,0:T(8,128)(2,1)S(1)}, bf16[8,128,128]{2,1,0:T(8,128)(2,1)S(1)}) custom-call(s32[192]{0:T(256)} %bitcast.55, s32[192]{0:T(256)} %bitcast.59, s32[1]{0:T(128)} %bitcast.49.count, s32[2]{0:T(128)S(1)} %pad_add_fusion.place, bf16[192,128,128]{2,1,0:T(8,128)(2,1)} %bitcast.63, ...), custom_call_target="tpu_custom_call" | custom-call | flops 805306368 | bytes 6291456 | tf_op jit(solution)/shard_map/forward_kernel/pallas_call | solution.py:469
  31.6 1.6 %collective-permute-start.16 = (bf16[8,128,128]{2,1,0:T(8,128)(2,1)S(1)}, bf16[8,128,128]{2,1,0:T(8,128)(2,1)S(1)}, u32[]{:S(2)}, u32[]{:S(2)}) collective-permute-start(bf16[8,128,128]{2,1,0:T(8,128)(2,1)S(1)} %get-tuple-element.41), channel_id=1, source_target_pairs={{0,4},{4,0},{8,12},{12,8},{16,20},{20,16},{24,28},{28,24},{1,5},{5... | collective-permute-start | bytes 786440 | tf_op jit(solution)/shard_map/ppermute | solution.py:376
  33.8 2.8 %collective-permute-start.6 = (bf16[256,128]{1,0:T(8,128)(2,1)S(1)}, bf16[256,128]{1,0:T(8,128)(2,1)S(1)}, u32[]{:S(2)}, u32[]{:S(2)}) collective-permute-start(bf16[256,128]{1,0:T(8,128)(2,1)S(1)} %get-tuple-element.60), channel_id=1, source_target_pairs={{0,16},{4,20},{8,24},{12,28},{16,0},{20,4},{24,8},{28,12},{1,17},{... | collective-permute-start | bytes 196616 | tf_op jit(solution)/shard_map/ppermute | solution.py:376
  36.6 1.6 %collective-permute-start.8 = (bf16[256,128]{1,0:T(8,128)(2,1)S(1)}, bf16[256,128]{1,0:T(8,128)(2,1)S(1)}, u32[]{:S(2)}, u32[]{:S(2)}) collective-permute-start(bf16[256,128]{1,0:T(8,128)(2,1)S(1)} %get-tuple-element.61), channel_id=1, source_target_pairs={{0,8},{4,12},{8,0},{12,4},{16,24},{20,28},{24,16},{28,20},{1,9},{5... | collective-permute-start | bytes 196616 | tf_op jit(solution)/shard_map/ppermute | solution.py:376
  38.3 1.8 %collective-permute-done.16 = bf16[8,128,128]{2,1,0:T(8,128)(2,1)S(1)} collective-permute-done((bf16[8,128,128]{2,1,0:T(8,128)(2,1)S(1)}, bf16[8,128,128]{2,1,0:T(8,128)(2,1)S(1)}, u32[]{:S(2)}, u32[]{:S(2)}) %collective-permute-start.16) | collective-permute-done | bytes 262176 | tf_op jit(solution)/shard_map/ppermute | solution.py:376
  40.2 2.7 %collective-permute-start.17 = (bf16[256,128]{1,0:T(8,128)(2,1)S(1)}, bf16[256,128]{1,0:T(8,128)(2,1)S(1)}, u32[]{:S(2)}, u32[]{:S(2)}) collective-permute-start(bf16[256,128]{1,0:T(8,128)(2,1)S(1)} %get-tuple-element.57), channel_id=1, source_target_pairs={{0,16},{4,20},{8,24},{12,28},{16,0},{20,4},{24,8},{28,12},{1,17},{... | collective-permute-start | bytes 196616 | tf_op jit(solution)/shard_map/ppermute | solution.py:376
  42.9 1.4 %collective-permute-start.19 = (bf16[256,128]{1,0:T(8,128)(2,1)S(1)}, bf16[256,128]{1,0:T(8,128)(2,1)S(1)}, u32[]{:S(2)}, u32[]{:S(2)}) collective-permute-start(bf16[256,128]{1,0:T(8,128)(2,1)S(1)} %get-tuple-element.58), channel_id=1, source_target_pairs={{0,8},{4,12},{8,0},{12,4},{16,24},{20,28},{24,16},{28,20},{1,9},{5... | collective-permute-start | bytes 196616 | tf_op jit(solution)/shard_map/ppermute | solution.py:376
  47.3 3.0 %collective-permute-done.18 = bf16[256,128]{1,0:T(8,128)(2,1)S(1)} collective-permute-done((bf16[256,128]{1,0:T(8,128)(2,1)S(1)}, bf16[256,128]{1,0:T(8,128)(2,1)S(1)}, u32[]{:S(2)}, u32[]{:S(2)}) %collective-permute-start.18) | collective-permute-done | bytes 65568 | tf_op jit(solution)/shard_map/ppermute | solution.py:376
  50.4 1.5 %collective-permute-start.22 = (bf16[256,128]{1,0:T(8,128)(2,1)S(1)}, bf16[256,128]{1,0:T(8,128)(2,1)S(1)}, u32[]{:S(2)}, u32[]{:S(2)}) collective-permute-start(bf16[256,128]{1,0:T(8,128)(2,1)S(1)} %get-tuple-element.63), channel_id=1, source_target_pairs={{0,24},{4,28},{8,16},{12,20},{16,8},{20,12},{24,0},{28,4},{1,25},{... | collective-permute-start | bytes 196616 | tf_op jit(solution)/shard_map/ppermute | solution.py:376
  51.9 2.9 %collective-permute-start.20 = (bf16[256,128]{1,0:T(8,128)(2,1)S(1)}, bf16[256,128]{1,0:T(8,128)(2,1)S(1)}, u32[]{:S(2)}, u32[]{:S(2)}) collective-permute-start(bf16[256,128]{1,0:T(8,128)(2,1)S(1)} %get-tuple-element.63), channel_id=1, source_target_pairs={{0,8},{4,12},{8,0},{12,4},{16,24},{20,28},{24,16},{28,20},{1,9},{5... | collective-permute-start | bytes 196616 | tf_op jit(solution)/shard_map/ppermute | solution.py:376
  54.8 1.7 %collective-permute-done.22 = bf16[256,128]{1,0:T(8,128)(2,1)S(1)} collective-permute-done((bf16[256,128]{1,0:T(8,128)(2,1)S(1)}, bf16[256,128]{1,0:T(8,128)(2,1)S(1)}, u32[]{:S(2)}, u32[]{:S(2)}) %collective-permute-start.22) | collective-permute-done | bytes 65568 | tf_op jit(solution)/shard_map/ppermute | solution.py:376
  56.5 1.4 %collective-permute-done.21 = bf16[256,128]{1,0:T(8,128)(2,1)S(1)} collective-permute-done((bf16[256,128]{1,0:T(8,128)(2,1)S(1)}, bf16[256,128]{1,0:T(8,128)(2,1)S(1)}, u32[]{:S(2)}, u32[]{:S(2)}) %collective-permute-start.21) | collective-permute-done | bytes 65568 | tf_op jit(solution)/shard_map/ppermute | solution.py:376
  58.7 1.7 %collective-permute-start.11 = (bf16[256,128]{1,0:T(8,128)(2,1)S(1)}, bf16[256,128]{1,0:T(8,128)(2,1)S(1)}, u32[]{:S(2)}, u32[]{:S(2)}) collective-permute-start(bf16[256,128]{1,0:T(8,128)(2,1)S(1)} %get-tuple-element.64.after_ref), channel_id=1, source_target_pairs={{0,24},{4,28},{8,16},{12,20},{16,8},{20,12},{24,0},{28,4},{1,25},{... | collective-permute-start | bytes 196616 | tf_op jit(solution)/shard_map/ppermute | solution.py:376
  61.3 1.7 %collective-permute-start.9 = (bf16[256,128]{1,0:T(8,128)(2,1)S(1)}, bf16[256,128]{1,0:T(8,128)(2,1)S(1)}, u32[]{:S(2)}, u32[]{:S(2)}) collective-permute-start(bf16[256,128]{1,0:T(8,128)(2,1)S(1)} %get-tuple-element.64.after_ref), channel_id=1, source_target_pairs={{0,8},{4,12},{8,0},{12,4},{16,24},{20,28},{24,16},{28,20},{1,9},{5... | collective-permute-start | bytes 196616 | tf_op jit(solution)/shard_map/ppermute | solution.py:376
  63.1 2.8 %hold.1.held = bf16[192,128,128]{2,1,0:T(8,128)(2,1)S(1)} custom-call(bf16[192,128,128]{2,1,0:T(8,128)(2,1)} %bitcast.64, bf16[256,128]{1,0:T(8,128)(2,1)S(1)} %get-tuple-element.64.after_ref), custom_call_target="tpu_custom_call" | custom-call | bytes 12582912 | tf_op jit(solution)/shard_map/hold/pallas_call | solution.py:417
  66.4 3.4 %adjoint_kernel.2 = (bf16[16,64,128]{2,1,0:T(8,128)(2,1)S(1)}, bf16[16,64,128]{2,1,0:T(8,128)(2,1)S(1)}, bf16[16,64,128]{2,1,0:T(8,128)(2,1)S(1)}, bf16[16,64,128]{2,1,0:T(8,128)(2,1)S(1)}) custom-call(s32[192]{0:T(256)S(1)} %bitcast.56, s32[192]{0:T(256)S(1)} %bitcast.60, s32[1]{0:T(128)} %bitcast.50.count, s32[2]{0:T(128)S(1)} %pad_add_fusion.place, ...), custom_call_target="tpu_custom_call" | custom-call | flops 805306368 | bytes 6291456 | tf_op jit(solution)/shard_map/adjoint_kernel/pallas_call | solution.py:469
  71.8 2.1 %collective-permute-start.27 = (bf16[16,64,128]{2,1,0:T(8,128)(2,1)S(1)}, bf16[16,64,128]{2,1,0:T(8,128)(2,1)S(1)}, u32[]{:S(2)}, u32[]{:S(2)}) collective-permute-start(bf16[16,64,128]{2,1,0:T(8,128)(2,1)S(1)} %add_convert_fusion.2), channel_id=1, source_target_pairs={{0,2},{1,3},{2,0},{3,1},{4,6},{5,7},{6,4},{7,5},{8,10},{9,11},{10,... | collective-permute-start | bytes 786440 | tf_op jit(solution)/shard_map/ppermute | solution.py:376
  73.9 4.7 %collective-permute-done.12.theirs_ref = bf16[4,256,128]{2,1,0:T(8,128)(2,1)S(1)} collective-permute-done((bf16[4,256,128]{2,1,0:T(8,128)(2,1)S(1)}, bf16[4,256,128]{2,1,0:T(8,128)(2,1)S(1)}, u32[]{:S(2)}, u32[]{:S(2)}) %collective-permute-start.12) | collective-permute-done | bytes 262176 | tf_op jit(solution)/shard_map/ppermute | solution.py:376
  78.6 3.5 %adjoint_kernel.3 = (bf16[16,64,128]{2,1,0:T(8,128)(2,1)S(1)}, bf16[16,64,128]{2,1,0:T(8,128)(2,1)S(1)}, bf16[16,64,128]{2,1,0:T(8,128)(2,1)S(1)}, bf16[16,64,128]{2,1,0:T(8,128)(2,1)S(1)}) custom-call(s32[192]{0:T(256)S(1)} %bitcast.57, s32[192]{0:T(256)S(1)} %bitcast.61, s32[1]{0:T(128)} %bitcast.51.count, s32[2]{0:T(128)S(1)} %pad_add_fusion.place, ...), custom_call_target="tpu_custom_call" | custom-call | flops 805306368 | bytes 6291456 | tf_op jit(solution)/shard_map/adjoint_kernel/pallas_call | solution.py:469
  82.3 2.4 %collective-permute-start.31 = (bf16[16,64,128]{2,1,0:T(8,128)(2,1)S(1)}, bf16[16,64,128]{2,1,0:T(8,128)(2,1)S(1)}, u32[]{:S(2)}, u32[]{:S(2)}) collective-permute-start(bf16[16,64,128]{2,1,0:T(8,128)(2,1)S(1)} %add_convert_fusion.1), channel_id=1, source_target_pairs={{0,2},{1,3},{2,0},{3,1},{4,6},{5,7},{6,4},{7,5},{8,10},{9,11},{10,... | collective-permute-start | bytes 786440 | tf_op jit(solution)/shard_map/ppermute | solution.py:376
  86.3 4.6 %collective-permute-start.28 = (bf16[8,64,128]{2,1,0:T(8,128)(2,1)S(1)}, bf16[8,64,128]{2,1,0:T(8,128)(2,1)S(1)}, u32[]{:S(2)}, u32[]{:S(2)}) collective-permute-start(bf16[8,64,128]{2,1,0:T(8,128)(2,1)S(1)} %get-tuple-element.56), channel_id=1, source_target_pairs={{0,4},{4,8},{8,12},{12,16},{16,20},{20,24},{24,28},{1,5},{5,9},{9,... | collective-permute-start | bytes 393224 | tf_op jit(solution)/shard_map/ppermute | solution.py:387
  91.6 2.5 %back_inner.1 = (f32[2,1024,128]{2,1,0:T(8,128)S(1)}, f32[2,4,2,64,256]{4,3,2,1,0:T(8,128)S(1)}) custom-call(bf16[1024,256]{1,0:T(8,128)(2,1)S(1)} %get-tuple-element.33.probes_ref, f32[16,256]{1,0:T(8,128)S(1)} %get-tuple-element.30.kappa_ref, bf16[16,64,128]{2,1,0:T(8,128)(2,1)S(1)} %get-tuple-element.51.own_in, ...), custom_call_target="tpu_custom_call" | custom-call | tf_op jit(solution)/shard_map/back_inner/pallas_call | solution.py:562
  94.4 3.4 %back_outer.1 = f32[1024,256]{1,0:T(8,128)} custom-call(f32[2]{0:T(128)S(1)} %add_convert_fusion.5.inside, f32[16,256]{1,0:T(8,128)S(1)} %get-tuple-element.30.kappa_ref, bf16[272,256]{1,0:T(8,128)(2,1)S(1)} %collective-permute-done.above_ref, bf16[272,256]{1,0:T(8,128)(2,1)S(1)} %collective-permute-done.1.below_ref, ...), custom_call_target="tpu_custom_call" | custom-call | tf_op jit(solution)/shard_map/back_outer/pallas_call | solution.py:571
  (62 shorter events, 13.8 us)
Async XLA Ops:
  1.4 10.1 %collective-permute-start = (bf16[272,256]{1,0:T(8,128)(2,1)S(1)}, bf16[272,256]{1,0:T(8,128)(2,1)S(1)}, u32[]{:S(2)}, u32[]{:S(2)}) collective-permute-start(bf16[272,256]{1,0:T(8,128)(2,1)S(1)} %get-tuple-element.31), channel_id=1, source_target_pairs={{0,4},{4,8},{8,12},{12,16},{16,20},{20,24},{24,28},{1,5},{5,9},{9,... | collective-permute-start | bytes 417800 | tf_op jit(solution)/shard_map/ppermute | solution.py:387
  6.2 7.0 %collective-permute-start.1 = (bf16[272,256]{1,0:T(8,128)(2,1)S(1)}, bf16[272,256]{1,0:T(8,128)(2,1)S(1)}, u32[]{:S(2)}, u32[]{:S(2)}) collective-permute-start(bf16[272,256]{1,0:T(8,128)(2,1)S(1)} %get-tuple-element.32), channel_id=1, source_target_pairs={{4,0},{8,4},{12,8},{16,12},{20,16},{24,20},{28,24},{5,1},{9,5},{13... | collective-permute-start | bytes 417800 | tf_op jit(solution)/shard_map/ppermute | solution.py:387
  9.9 8.0 %collective-permute-start.13 = (bf16[16,64,128]{2,1,0:T(8,128)(2,1)S(1)}, bf16[16,64,128]{2,1,0:T(8,128)(2,1)S(1)}, u32[]{:S(2)}, u32[]{:S(2)}) collective-permute-start(bf16[16,64,128]{2,1,0:T(8,128)(2,1)S(1)} %get-tuple-element.34.near_in), channel_id=1, source_target_pairs={{0,2},{1,3},{2,0},{3,1},{4,6},{5,7},{6,4},{7,5},{8,10},{9,11},{10,... | collective-permute-start | bytes 786440 | tf_op jit(solution)/shard_map/ppermute | solution.py:376
  11.5 6.6 %collective-permute-start.2 = (bf16[16,64,128]{2,1,0:T(8,128)(2,1)S(1)}, bf16[16,64,128]{2,1,0:T(8,128)(2,1)S(1)}, u32[]{:S(2)}, u32[]{:S(2)}) collective-permute-start(bf16[16,64,128]{2,1,0:T(8,128)(2,1)S(1)} %get-tuple-element.34.near_in), channel_id=1, source_target_pairs={{0,1},{1,0},{2,3},{3,2},{4,5},{5,4},{6,7},{7,6},{8,9},{9,8},{10,11... | collective-permute-start | bytes 786440 | tf_op jit(solution)/shard_map/ppermute | solution.py:376
  15.5 2.6 %collective-permute-start.3 = (bf16[16,64,128]{2,1,0:T(8,128)(2,1)S(1)}, bf16[16,64,128]{2,1,0:T(8,128)(2,1)S(1)}, u32[]{:S(2)}, u32[]{:S(2)}) collective-permute-start(bf16[16,64,128]{2,1,0:T(8,128)(2,1)S(1)} %smooth_outer.1.near_out), channel_id=1, source_target_pairs={{0,1},{1,0},{2,3},{3,2},{4,5},{5,4},{6,7},{7,6},{8,9},{9,8},{10,11... | collective-permute-start | bytes 786440 | tf_op jit(solution)/shard_map/ppermute | solution.py:376
  15.6 8.7 %collective-permute-start.4 = (bf16[16,64,128]{2,1,0:T(8,128)(2,1)S(1)}, bf16[16,64,128]{2,1,0:T(8,128)(2,1)S(1)}, u32[]{:S(2)}, u32[]{:S(2)}) collective-permute-start(bf16[16,64,128]{2,1,0:T(8,128)(2,1)S(1)} %smooth_outer.1.near_out), channel_id=1, source_target_pairs={{0,2},{1,3},{2,0},{3,1},{4,6},{5,7},{6,4},{7,5},{8,10},{9,11},{10,... | collective-permute-start | bytes 786440 | tf_op jit(solution)/shard_map/ppermute | solution.py:376
  17.9 8.9 %collective-permute-start.14 = (bf16[16,64,128]{2,1,0:T(8,128)(2,1)S(1)}, bf16[16,64,128]{2,1,0:T(8,128)(2,1)S(1)}, u32[]{:S(2)}, u32[]{:S(2)}) collective-permute-start(bf16[16,64,128]{2,1,0:T(8,128)(2,1)S(1)} %collective-permute-done.13.near_in), channel_id=1, source_target_pairs={{0,1},{1,0},{2,3},{3,2},{4,5},{5,4},{6,7},{7,6},{8,9},{9,8},{10,11... | collective-permute-start | bytes 786440 | tf_op jit(solution)/shard_map/ppermute | solution.py:376
  24.3 2.5 %collective-permute-start.15 = (bf16[16,64,128]{2,1,0:T(8,128)(2,1)S(1)}, bf16[16,64,128]{2,1,0:T(8,128)(2,1)S(1)}, u32[]{:S(2)}, u32[]{:S(2)}) collective-permute-start(bf16[16,64,128]{2,1,0:T(8,128)(2,1)S(1)} %collective-permute-done.4.near_out), channel_id=1, source_target_pairs={{0,1},{1,0},{2,3},{3,2},{4,5},{5,4},{6,7},{7,6},{8,9},{9,8},{10,11... | collective-permute-start | bytes 786440 | tf_op jit(solution)/shard_map/ppermute | solution.py:376
  24.3 9.4 %collective-permute-start.5 = (bf16[8,128,128]{2,1,0:T(8,128)(2,1)S(1)}, bf16[8,128,128]{2,1,0:T(8,128)(2,1)S(1)}, u32[]{:S(2)}, u32[]{:S(2)}) collective-permute-start(bf16[8,128,128]{2,1,0:T(8,128)(2,1)S(1)} %get-tuple-element.38), channel_id=1, source_target_pairs={{0,4},{4,0},{8,12},{12,8},{16,20},{20,16},{24,28},{28,24},{1,5},{5... | collective-permute-start | bytes 786440 | tf_op jit(solution)/shard_map/ppermute | solution.py:376
  31.6 8.5 %collective-permute-start.16 = (bf16[8,128,128]{2,1,0:T(8,128)(2,1)S(1)}, bf16[8,128,128]{2,1,0:T(8,128)(2,1)S(1)}, u32[]{:S(2)}, u32[]{:S(2)}) collective-permute-start(bf16[8,128,128]{2,1,0:T(8,128)(2,1)S(1)} %get-tuple-element.41), channel_id=1, source_target_pairs={{0,4},{4,0},{8,12},{12,8},{16,20},{20,16},{24,28},{28,24},{1,5},{5... | collective-permute-start | bytes 786440 | tf_op jit(solution)/shard_map/ppermute | solution.py:376
  33.8 10.4 %collective-permute-start.6 = (bf16[256,128]{1,0:T(8,128)(2,1)S(1)}, bf16[256,128]{1,0:T(8,128)(2,1)S(1)}, u32[]{:S(2)}, u32[]{:S(2)}) collective-permute-start(bf16[256,128]{1,0:T(8,128)(2,1)S(1)} %get-tuple-element.60), channel_id=1, source_target_pairs={{0,16},{4,20},{8,24},{12,28},{16,0},{20,4},{24,8},{28,12},{1,17},{... | collective-permute-start | bytes 196616 | tf_op jit(solution)/shard_map/ppermute | solution.py:376
  36.6 9.0 %collective-permute-start.8 = (bf16[256,128]{1,0:T(8,128)(2,1)S(1)}, bf16[256,128]{1,0:T(8,128)(2,1)S(1)}, u32[]{:S(2)}, u32[]{:S(2)}) collective-permute-start(bf16[256,128]{1,0:T(8,128)(2,1)S(1)} %get-tuple-element.61), channel_id=1, source_target_pairs={{0,8},{4,12},{8,0},{12,4},{16,24},{20,28},{24,16},{28,20},{1,9},{5... | collective-permute-start | bytes 196616 | tf_op jit(solution)/shard_map/ppermute | solution.py:376
  38.2 7.4 %collective-permute-start.7 = (bf16[256,128]{1,0:T(8,128)(2,1)S(1)}, bf16[256,128]{1,0:T(8,128)(2,1)S(1)}, u32[]{:S(2)}, u32[]{:S(2)}) collective-permute-start(bf16[256,128]{1,0:T(8,128)(2,1)S(1)} %get-tuple-element.62), channel_id=1, source_target_pairs={{0,24},{4,28},{8,16},{12,20},{16,8},{20,12},{24,0},{28,4},{1,25},{... | collective-permute-start | bytes 196616 | tf_op jit(solution)/shard_map/ppermute | solution.py:376
  40.2 6.7 %collective-permute-start.17 = (bf16[256,128]{1,0:T(8,128)(2,1)S(1)}, bf16[256,128]{1,0:T(8,128)(2,1)S(1)}, u32[]{:S(2)}, u32[]{:S(2)}) collective-permute-start(bf16[256,128]{1,0:T(8,128)(2,1)S(1)} %get-tuple-element.57), channel_id=1, source_target_pairs={{0,16},{4,20},{8,24},{12,28},{16,0},{20,4},{24,8},{28,12},{1,17},{... | collective-permute-start | bytes 196616 | tf_op jit(solution)/shard_map/ppermute | solution.py:376
  42.9 4.4 %collective-permute-start.19 = (bf16[256,128]{1,0:T(8,128)(2,1)S(1)}, bf16[256,128]{1,0:T(8,128)(2,1)S(1)}, u32[]{:S(2)}, u32[]{:S(2)}) collective-permute-start(bf16[256,128]{1,0:T(8,128)(2,1)S(1)} %get-tuple-element.58), channel_id=1, source_target_pairs={{0,8},{4,12},{8,0},{12,4},{16,24},{20,28},{24,16},{28,20},{1,9},{5... | collective-permute-start | bytes 196616 | tf_op jit(solution)/shard_map/ppermute | solution.py:376
  44.2 6.1 %collective-permute-start.18 = (bf16[256,128]{1,0:T(8,128)(2,1)S(1)}, bf16[256,128]{1,0:T(8,128)(2,1)S(1)}, u32[]{:S(2)}, u32[]{:S(2)}) collective-permute-start(bf16[256,128]{1,0:T(8,128)(2,1)S(1)} %get-tuple-element.59), channel_id=1, source_target_pairs={{0,24},{4,28},{8,16},{12,20},{16,8},{20,12},{24,0},{28,4},{1,25},{... | collective-permute-start | bytes 196616 | tf_op jit(solution)/shard_map/ppermute | solution.py:376
  50.4 6.2 %collective-permute-start.22 = (bf16[256,128]{1,0:T(8,128)(2,1)S(1)}, bf16[256,128]{1,0:T(8,128)(2,1)S(1)}, u32[]{:S(2)}, u32[]{:S(2)}) collective-permute-start(bf16[256,128]{1,0:T(8,128)(2,1)S(1)} %get-tuple-element.63), channel_id=1, source_target_pairs={{0,24},{4,28},{8,16},{12,20},{16,8},{20,12},{24,0},{28,4},{1,25},{... | collective-permute-start | bytes 196616 | tf_op jit(solution)/shard_map/ppermute | solution.py:376
  51.9 6.0 %collective-permute-start.21 = (bf16[256,128]{1,0:T(8,128)(2,1)S(1)}, bf16[256,128]{1,0:T(8,128)(2,1)S(1)}, u32[]{:S(2)}, u32[]{:S(2)}) collective-permute-start(bf16[256,128]{1,0:T(8,128)(2,1)S(1)} %get-tuple-element.63), channel_id=1, source_target_pairs={{0,16},{4,20},{8,24},{12,28},{16,0},{20,4},{24,8},{28,12},{1,17},{... | collective-permute-start | bytes 196616 | tf_op jit(solution)/shard_map/ppermute | solution.py:376
  51.9 6.0 %collective-permute-start.20 = (bf16[256,128]{1,0:T(8,128)(2,1)S(1)}, bf16[256,128]{1,0:T(8,128)(2,1)S(1)}, u32[]{:S(2)}, u32[]{:S(2)}) collective-permute-start(bf16[256,128]{1,0:T(8,128)(2,1)S(1)} %get-tuple-element.63), channel_id=1, source_target_pairs={{0,8},{4,12},{8,0},{12,4},{16,24},{20,28},{24,16},{28,20},{1,9},{5... | collective-permute-start | bytes 196616 | tf_op jit(solution)/shard_map/ppermute | solution.py:376
  58.0 8.4 %collective-permute-start.23 = (bf16[4,256,128]{2,1,0:T(8,128)(2,1)S(1)}, bf16[4,256,128]{2,1,0:T(8,128)(2,1)S(1)}, u32[]{:S(2)}, u32[]{:S(2)}) collective-permute-start(bf16[4,256,128]{2,1,0:T(8,128)(2,1)S(1)} %pad_maximum_fusion.1.mine_ref), channel_id=1, source_target_pairs={{0,4},{4,0},{8,12},{12,8},{16,20},{20,16},{24,28},{28,24},{1,5},{5... | collective-permute-start | bytes 786440 | tf_op jit(solution)/shard_map/ppermute | solution.py:376
  58.7 7.2 %collective-permute-start.11 = (bf16[256,128]{1,0:T(8,128)(2,1)S(1)}, bf16[256,128]{1,0:T(8,128)(2,1)S(1)}, u32[]{:S(2)}, u32[]{:S(2)}) collective-permute-start(bf16[256,128]{1,0:T(8,128)(2,1)S(1)} %get-tuple-element.64.after_ref), channel_id=1, source_target_pairs={{0,24},{4,28},{8,16},{12,20},{16,8},{20,12},{24,0},{28,4},{1,25},{... | collective-permute-start | bytes 196616 | tf_op jit(solution)/shard_map/ppermute | solution.py:376
  60.4 5.9 %collective-permute-start.10 = (bf16[256,128]{1,0:T(8,128)(2,1)S(1)}, bf16[256,128]{1,0:T(8,128)(2,1)S(1)}, u32[]{:S(2)}, u32[]{:S(2)}) collective-permute-start(bf16[256,128]{1,0:T(8,128)(2,1)S(1)} %get-tuple-element.64.after_ref), channel_id=1, source_target_pairs={{0,16},{4,20},{8,24},{12,28},{16,0},{20,4},{24,8},{28,12},{1,17},{... | collective-permute-start | bytes 196616 | tf_op jit(solution)/shard_map/ppermute | solution.py:376
  61.3 5.0 %collective-permute-start.9 = (bf16[256,128]{1,0:T(8,128)(2,1)S(1)}, bf16[256,128]{1,0:T(8,128)(2,1)S(1)}, u32[]{:S(2)}, u32[]{:S(2)}) collective-permute-start(bf16[256,128]{1,0:T(8,128)(2,1)S(1)} %get-tuple-element.64.after_ref), channel_id=1, source_target_pairs={{0,8},{4,12},{8,0},{12,4},{16,24},{20,28},{24,16},{28,20},{1,9},{5... | collective-permute-start | bytes 196616 | tf_op jit(solution)/shard_map/ppermute | solution.py:376
  69.8 1.9 %collective-permute-start.24 = (bf16[16,64,128]{2,1,0:T(8,128)(2,1)S(1)}, bf16[16,64,128]{2,1,0:T(8,128)(2,1)S(1)}, u32[]{:S(2)}, u32[]{:S(2)}) collective-permute-start(bf16[16,64,128]{2,1,0:T(8,128)(2,1)S(1)} %get-tuple-element.45), channel_id=1, source_target_pairs={{0,1},{1,0},{2,3},{3,2},{4,5},{5,4},{6,7},{7,6},{8,9},{9,8},{10,11... | collective-permute-start | bytes 786440 | tf_op jit(solution)/shard_map/ppermute | solution.py:376
  69.8 4.0 %collective-permute-start.25 = (bf16[16,64,128]{2,1,0:T(8,128)(2,1)S(1)}, bf16[16,64,128]{2,1,0:T(8,128)(2,1)S(1)}, u32[]{:S(2)}, u32[]{:S(2)}) collective-permute-start(bf16[16,64,128]{2,1,0:T(8,128)(2,1)S(1)} %get-tuple-element.47), channel_id=1, source_target_pairs={{0,1},{1,0},{2,3},{3,2},{4,5},{5,4},{6,7},{7,6},{8,9},{9,8},{10,11... | collective-permute-start | bytes 786440 | tf_op jit(solution)/shard_map/ppermute | solution.py:376
  70.3 8.3 %collective-permute-start.12 = (bf16[4,256,128]{2,1,0:T(8,128)(2,1)S(1)}, bf16[4,256,128]{2,1,0:T(8,128)(2,1)S(1)}, u32[]{:S(2)}, u32[]{:S(2)}) collective-permute-start(bf16[4,256,128]{2,1,0:T(8,128)(2,1)S(1)} %pad_maximum_fusion.mine_ref), channel_id=1, source_target_pairs={{0,4},{4,0},{8,12},{12,8},{16,20},{20,16},{24,28},{28,24},{1,5},{5... | collective-permute-start | bytes 786440 | tf_op jit(solution)/shard_map/ppermute | solution.py:376
  71.8 13.1 %collective-permute-start.27 = (bf16[16,64,128]{2,1,0:T(8,128)(2,1)S(1)}, bf16[16,64,128]{2,1,0:T(8,128)(2,1)S(1)}, u32[]{:S(2)}, u32[]{:S(2)}) collective-permute-start(bf16[16,64,128]{2,1,0:T(8,128)(2,1)S(1)} %add_convert_fusion.2), channel_id=1, source_target_pairs={{0,2},{1,3},{2,0},{3,1},{4,6},{5,7},{6,4},{7,5},{8,10},{9,11},{10,... | collective-permute-start | bytes 786440 | tf_op jit(solution)/shard_map/ppermute | solution.py:376
  82.2 2.7 %collective-permute-start.26 = (bf16[16,64,128]{2,1,0:T(8,128)(2,1)S(1)}, bf16[16,64,128]{2,1,0:T(8,128)(2,1)S(1)}, u32[]{:S(2)}, u32[]{:S(2)}) collective-permute-start(bf16[16,64,128]{2,1,0:T(8,128)(2,1)S(1)} %get-tuple-element.50), channel_id=1, source_target_pairs={{0,1},{1,0},{2,3},{3,2},{4,5},{5,4},{6,7},{7,6},{8,9},{9,8},{10,11... | collective-permute-start | bytes 786440 | tf_op jit(solution)/shard_map/ppermute | solution.py:376
  82.3 9.3 %collective-permute-start.31 = (bf16[16,64,128]{2,1,0:T(8,128)(2,1)S(1)}, bf16[16,64,128]{2,1,0:T(8,128)(2,1)S(1)}, u32[]{:S(2)}, u32[]{:S(2)}) collective-permute-start(bf16[16,64,128]{2,1,0:T(8,128)(2,1)S(1)} %add_convert_fusion.1), channel_id=1, source_target_pairs={{0,2},{1,3},{2,0},{3,1},{4,6},{5,7},{6,4},{7,5},{8,10},{9,11},{10,... | collective-permute-start | bytes 786440 | tf_op jit(solution)/shard_map/ppermute | solution.py:376
  84.7 6.3 %collective-permute-start.30 = (bf16[16,64,128]{2,1,0:T(8,128)(2,1)S(1)}, bf16[16,64,128]{2,1,0:T(8,128)(2,1)S(1)}, u32[]{:S(2)}, u32[]{:S(2)}) collective-permute-start(bf16[16,64,128]{2,1,0:T(8,128)(2,1)S(1)} %get-tuple-element.52), channel_id=1, source_target_pairs={{0,1},{1,0},{2,3},{3,2},{4,5},{5,4},{6,7},{7,6},{8,9},{9,8},{10,11... | collective-permute-start | bytes 786440 | tf_op jit(solution)/shard_map/ppermute | solution.py:376
  85.0 9.1 %collective-permute-start.29 = (bf16[8,64,128]{2,1,0:T(8,128)(2,1)S(1)}, bf16[8,64,128]{2,1,0:T(8,128)(2,1)S(1)}, u32[]{:S(2)}, u32[]{:S(2)}) collective-permute-start(bf16[8,64,128]{2,1,0:T(8,128)(2,1)S(1)} %get-tuple-element.55), channel_id=1, source_target_pairs={{4,0},{8,4},{12,8},{16,12},{20,16},{24,20},{28,24},{5,1},{9,5},{13... | collective-permute-start | bytes 393224 | tf_op jit(solution)/shard_map/ppermute | solution.py:387
  86.3 8.1 %collective-permute-start.28 = (bf16[8,64,128]{2,1,0:T(8,128)(2,1)S(1)}, bf16[8,64,128]{2,1,0:T(8,128)(2,1)S(1)}, u32[]{:S(2)}, u32[]{:S(2)}) collective-permute-start(bf16[8,64,128]{2,1,0:T(8,128)(2,1)S(1)} %get-tuple-element.56), channel_id=1, source_target_pairs={{0,4},{4,8},{8,12},{12,16},{16,20},{20,24},{24,28},{1,5},{5,9},{9,... | collective-permute-start | bytes 393224 | tf_op jit(solution)/shard_map/ppermute | solution.py:387
  (3 other events, 60.9 us)
